TPU v7x, 32 devices: a whole 2x2x4 slice. The times are simulated.
32 devices in a mesh: dp: 4 (over y, x), ctx: 8 (over z, core).
Axes of the slice: x: 2, y: 2, z: 4, core: 2. Of those that a mesh axis runs over, the one named last changes fastest.
Arguments:
- tokens: bfloat16 [4, 32768, 768], P('dp', 'ctx'), may hold values from -6 to 6
- cotangent: bfloat16 [4, 32768, 768], P('dp', 'ctx'), may hold values from -6 to 6
- first_factor: bfloat16 [256, 256], replicated, may hold values from -0.375 to 0.375
- second_factor: bfloat16 [128, 128], replicated, may hold values from -0.5 to 0.5
- twiddle: float32 [256, 128], P('ctx'), may hold values from -4 to 4
- gate_gain: float32 [768], replicated, may hold values from 0.5 to 2
- gate_bias: float32 [768], replicated, may hold values from -1 to 1
- skip_gain: float32 [768], replicated, may hold values from -4 to 4
Outputs:
- grad_tokens: bfloat16 [4, 32768, 768], P('dp', 'ctx')
- grad_first: float32 [256, 256], replicated
- grad_second: float32 [128, 128], replicated
- grad_twiddle: float32 [256, 128], P('ctx')
- grad_gain: float32 [768], replicated
- grad_bias: float32 [768], replicated
- grad_skip: float32 [768], replicated
All inputs are finite; a program needn't handle non-finite values.
Results may differ from a plain program's by a relative error of at most 0.0059.
Values may be sent and summed in bfloat16 or wider, within the bound.
No kernel may reach another device: no remote copies, remote signals or barrier semaphores. Data moves between devices by JAX's collectives and lax.ppermute only.
A program may use at most 192 MiB of HBM per device.

v0:
```python
import math

import jax
import jax.numpy as jnp
from jax import lax
from jax.sharding import PartitionSpec as P

A = 256
B = 128


def token_body(
    tokens, cotangent, first_factor, second_factor, twiddle, gate_gain, gate_bias, skip_gain
):
    seq_count, tok_rows, width = tokens.shape
    local_rows = tok_rows // B
    blocks_in = tokens.reshape(seq_count, local_rows, B, width)
    inputs = blocks_in.astype(jnp.float32)
    upstream = cotangent.reshape(seq_count, local_rows, B, width).astype(jnp.float32)
    gate_vals = jax.nn.sigmoid(gate_gain * inputs + gate_bias)
    inner = jnp.einsum(
        "pb,sabc->sapc", second_factor, blocks_in, preferred_element_type=jnp.float32
    )
    scaled = (inner * twiddle[None, :, :, None]).astype(jnp.bfloat16)
    grad_hidden = upstream * gate_vals
    grad_outer = grad_hidden.astype(jnp.bfloat16)
    scaled_cols = lax.all_to_all(scaled, "ctx", split_axis=2, concat_axis=1, tiled=True)
    outer_cols = jnp.einsum(
        "qa,sapc->sqpc", first_factor, scaled_cols, preferred_element_type=jnp.float32
    ).astype(jnp.bfloat16)
    outer_back = lax.all_to_all(outer_cols, "ctx", split_axis=1, concat_axis=2, tiled=True)
    grad_cols = lax.all_to_all(grad_outer, "ctx", split_axis=2, concat_axis=1, tiled=True)
    grad_scaled_cols = jnp.einsum(
        "qa,sqpc->sapc", first_factor, grad_cols, preferred_element_type=jnp.float32
    ).astype(jnp.bfloat16)
    grad_scaled = lax.all_to_all(grad_scaled_cols, "ctx", split_axis=1, concat_axis=2, tiled=True)
    first_term = jnp.einsum(
        "sqpc,sapc->qa", grad_cols, scaled_cols, preferred_element_type=jnp.float32
    )
    hidden = outer_back.astype(jnp.float32) + skip_gain * inputs
    grad_pre = upstream * hidden * gate_vals * (1.0 - gate_vals)
    grad_scaled_wide = grad_scaled.astype(jnp.float32)
    twiddle_term = jnp.sum(grad_scaled_wide * inner, axis=(0, 3))
    grad_inner = (grad_scaled_wide * twiddle[None, :, :, None]).astype(jnp.bfloat16)
    second_term = jnp.einsum(
        "sapc,sabc->pb", grad_inner, blocks_in, preferred_element_type=jnp.float32
    )
    grad_in = jnp.einsum(
        "pb,sapc->sabc", second_factor, grad_inner, preferred_element_type=jnp.float32
    )
    grad_in = grad_in + grad_hidden * skip_gain + grad_pre * gate_gain
    gain_term = jnp.sum(grad_pre * inputs, axis=(0, 1, 2))
    bias_term = jnp.sum(grad_pre, axis=(0, 1, 2))
    skip_term = jnp.sum(grad_hidden * inputs, axis=(0, 1, 2))
    first_sum, second_sum, gain_sum, bias_sum, skip_sum = lax.psum(
        (first_term, second_term, gain_term, bias_term, skip_term), ("dp", "ctx")
    )
    twiddle_sum = lax.psum(twiddle_term, "dp")
    total_seqs = seq_count * lax.axis_size("dp")
    first_norm = math.sqrt(total_seqs * B * width)
    second_norm = math.sqrt(total_seqs * A * width)
    twiddle_norm = math.sqrt(total_seqs * width)
    channel_norm = math.sqrt(total_seqs * A * B)
    grad_tokens = grad_in.astype(jnp.bfloat16).reshape(seq_count, tok_rows, width)
    return (
        grad_tokens,
        first_sum / first_norm,
        second_sum / second_norm,
        twiddle_sum / twiddle_norm,
        gain_sum / channel_norm,
        bias_sum / channel_norm,
        skip_sum / channel_norm,
    )


def body(tokens, cotangent, first_factor, second_factor, twiddle, gate_gain, gate_bias, skip_gain):
    return token_body(
        tokens, cotangent, first_factor, second_factor, twiddle, gate_gain, gate_bias, skip_gain
    )


def solution(mesh):
    return jax.shard_map(
        body,
        mesh=mesh,
        in_specs=(
            P("dp", "ctx", None),
            P("dp", "ctx", None),
            P(),
            P(),
            P("ctx", None),
            P(),
            P(),
            P(),
        ),
        out_specs=(P("dp", "ctx", None), P(), P(), P("ctx", None), P(), P(), P()),
        check_vma=False,
    )
```

profile of v0, /device:TPU:0, one launch (start us, length us, event | category | flops | bytes accessed | tf_op | source)
XLA Modules:
  0.0 872.5 jit_solution(16891300255420700217)
XLA Ops:
  7.2 14.3 %fusion.19 = (bf16[1,32,128,768]{3,2,1,0:T(8,128)(2,1)S(1)}, f32[1,32,128,768]{3,2,1,0:T(8,128)}, f32[1,32,128,768]{3,2,1,0:T(8,128)}) fusion(f32[768]{0:T(1024)} %param.14, f32[768]{0:T(1024)} %param.13, bf16[1,32,128,768]{3,2,1,0:T(8,128)(2,1)} %bitcast.97, bf16[1,32,128,768]{3,2,1,0:T(8,128)(2,1)} %bitcast.113), kind=kLoop, calls=%fused_computation.33 | loop fusion | flops 28311552 | bytes 44046336 | tf_op jit(solution)/shard_map/convert_element_type | solution.py:26
  21.5 3.6 copy.83
  25.0 145.5 %all_to_all.48 = bf16[1,32,128,768]{3,1,0,2:T(8,128)(2,1)S(1)} all-to-all(bf16[1,32,128,768]{3,1,0,2:T(8,128)(2,1)S(1)} %copy.83), channel_id=1, replica_groups=mesh['dp'=4,'ctx'=8] {'ctx'}, dimensions={2} | all-to-all | bytes 12582912 | tf_op jit(solution)/shard_map/all_to_all | solution.py:32
  170.5 3.6 copy.84
  174.6 2.6 copy-done.4
  177.2 7.4 convert_bitcast_fusion.3
  184.7 9.0 %copy.87 = bf16[1,256,16,768]{3,2,0,1:T(8,128)(2,1)} copy(bf16[1,256,16,768]{1,3,2,0:T(8,128)(2,1)} %convert_bitcast_fusion.3) | data formatting | bytes 12582912 | tf_op jit(solution)/shard_map/convert_element_type | solution.py:35
  193.7 143.2 %all_to_all.49 = bf16[1,256,16,768]{3,2,0,1:T(8,128)(2,1)S(1)} all-to-all(bf16[1,256,16,768]{3,2,0,1:T(8,128)(2,1)} %copy.87), channel_id=1, replica_groups=mesh['dp'=4,'ctx'=8] {'ctx'}, dimensions={1} | all-to-all | bytes 12582912 | tf_op jit(solution)/shard_map/all_to_all | solution.py:36
  336.9 2.6 copy-done.2
  339.4 6.2 convert_bitcast_fusion.1
  345.7 11.0 %copy.89 = f32[1,32,8,16,768]{4,3,2,1,0:T(8,128)} copy(f32[1,32,8,16,768]{4,3,1,2,0:T(8,128)} %convert_bitcast_fusion.1) | data formatting | bytes 25165824 | tf_op jit(solution)/shard_map/convert_element_type | solution.py:42
  356.7 12.6 %copy.105 = f32[1,32,128,768]{2,3,1,0:T(8,128)} copy(f32[1,32,128,768]{3,2,1,0:T(8,128)} %bitcast.104) | data formatting | bytes 25165824 | tf_op jit(solution)/shard_map/convert_element_type | solution.py:42
  369.3 11.2 %fusion.6 = (f32[32,128]{1,0:T(8,128)S(1)}, bf16[1,32,128,768]{2,3,1,0:T(8,128)(2,1)}) fusion(f32[1,32,128,768]{2,3,1,0:T(8,128)} %copy.105, f32[32,128]{1,0:T(8,128)S(1)} %copy-done.5, bf16[32,128,768]{2,1,0:T(8,128)(2,1)} %bitcast.98, bf16[128,128]{1,0:T(8,128)(2,1)S(1)} %copy-done.6), kind=kOutput, calls=%fused_computation.11 | convolution fusion | flops 817885184 | bytes 25231360 | tf_op jit(solution)/shard_map/pb,sabc->sapc/dot_general | solution.py:21
  380.5 9.1 %copy.92 = bf16[1,32,128,768]{3,1,0,2:T(8,128)(2,1)} copy(bf16[1,32,128,768]{2,3,1,0:T(8,128)(2,1)} %get-tuple-element.19) | data formatting | bytes 12582912 | tf_op jit(solution)/shard_map/convert_element_type | solution.py:24
  389.5 142.8 %all_to_all.50 = bf16[1,32,128,768]{3,1,0,2:T(8,128)(2,1)S(1)} all-to-all(bf16[1,32,128,768]{3,1,0,2:T(8,128)(2,1)} %copy.92), channel_id=1, replica_groups=mesh['dp'=4,'ctx'=8] {'ctx'}, dimensions={2} | all-to-all | bytes 12582912 | tf_op jit(solution)/shard_map/all_to_all | solution.py:27
  532.3 3.6 copy.93
  536.5 2.6 copy-done.3
  539.1 7.4 convert_bitcast_fusion.2
  546.5 9.0 %copy.96 = bf16[1,256,16,768]{3,2,0,1:T(8,128)(2,1)} copy(bf16[1,256,16,768]{1,3,2,0:T(8,128)(2,1)} %convert_bitcast_fusion.2) | data formatting | bytes 12582912 | tf_op jit(solution)/shard_map/convert_element_type | solution.py:30
  555.5 4.7 all-to-all-start.3
  560.5 3.9 multiply_convert_fusion
  564.4 3.4 copy.103
  567.8 16.3 %psum.44 = f32[32,128]{1,0:T(8,128)S(1)} all-reduce(f32[32,128]{1,0:T(8,128)S(1)} %get-tuple-element.18), channel_id=1, replica_groups=mesh['dp'=4,'ctx'=8] {'dp'}, use_global_device_ids=true, to_apply=%region_3.0 | all-reduce | flops 4096 | bytes 32768 | tf_op jit(solution)/shard_map/psum | solution.py:58
  584.1 7.2 convolution_bitcast_fusion
  591.3 10.1 %fusion.33 = f32[256,256]{1,0:T(8,128)} fusion(bf16[256,16,768]{2,1,0:T(8,128)(2,1)S(1)} %bitcast.109, bf16[256,16,768]{2,1,0:T(8,128)(2,1)} %bitcast.115), kind=kOutput, calls=%fused_computation.45 | convolution fusion | flops 1610612736 | bytes 12845056 | tf_op jit(solution)/shard_map/sqpc,sapc->qa/dot_general | solution.py:37
  602.0 164.5 %all-reduce.4.cloned.1.call-done = (f32[256,256]{1,0:T(8,128)}, f32[128,128]{1,0:T(8,128)}) async-done(((f32[256,256]{1,0:T(8,128)}, f32[128,128]{1,0:T(8,128)}), (f32[256,256]{1,0:T(8,128)}, f32[128,128]{1,0:T(8,128)})) %all-reduce.4.cloned.1.call-update) | async-done | bytes 327696 | tf_op jit(solution)/shard_map/psum | solution.py:55
  768.0 1.7 broadcast_multiply_fusion
  769.7 9.2 %convert_bitcast_fusion = f32[1,32,8,16,768]{4,3,1,2,0:T(8,128)} fusion(bf16[1,8,32,16,768]{4,3,2,1,0:T(8,128)(2,1)} %bitcast.36), kind=kLoop, calls=%fused_computation.7 | loop fusion | flops 3145728 | bytes 18874368 | tf_op jit(solution)/shard_map/convert_element_type | solution.py:40
  778.8 11.0 %copy.98 = f32[1,32,8,16,768]{4,3,2,1,0:T(8,128)} copy(f32[1,32,8,16,768]{4,3,1,2,0:T(8,128)} %convert_bitcast_fusion) | data formatting | bytes 25165824 | tf_op jit(solution)/shard_map/convert_element_type | solution.py:40
  789.9 11.4 %fusion.43 = (f32[768]{0:T(1024)S(1)}, f32[768]{0:T(1024)S(1)}, f32[768]{0:T(1024)S(1)}) fusion(bf16[1,4096,768]{2,1,0:T(8,128)(2,1)S(1)} %bitcast.101, f32[768]{0:T(1024)S(1)} %copy-done.7, f32[768]{0:T(1024)S(1)} %copy-done.8, bf16[1,4096,768]{2,1,0:T(8,128)(2,1)} %param.9, f32[768]{0:T(1024)S(1)} %copy-done.9, f32[1,32,8,16,768]{4,3,2,1,0:T(8,128)} %copy.98), kind=kLoop, calls=%fused_computation.58 | loop fusion | flops 59766528 | bytes 25184256 | tf_op jit(solution)/shard_map/reduce_sum | solution.py:53
  801.3 41.4 %all-reduce = (f32[768]{0:T(1024)S(1)}, f32[768]{0:T(1024)S(1)}, f32[768]{0:T(1024)S(1)}) all-reduce(f32[768]{0:T(1024)S(1)} %get-tuple-element.8, f32[768]{0:T(1024)S(1)} %get-tuple-element.7, f32[768]{0:T(1024)S(1)} %get-tuple-element.9), channel_id=1, replica_groups=mesh['dp'=4,'ctx'=8] {'dp','ctx'}, use_global_device_ids=true, to_apply=%region_5.0 | all-reduce | flops 2304 | bytes 18432 | tf_op jit(solution)/shard_map/psum | solution.py:55
  843.9 21.5 %fusion.1 = bf16[1,32,128,768]{3,2,1,0:T(8,128)(2,1)} fusion(f32[1,32,128,768]{3,2,1,0:T(8,128)} %get-tuple-element.17, f32[1,32,8,16,768]{4,3,2,1,0:T(8,128)} %copy.98, f32[1,32,128,768]{3,2,1,0:T(8,128)} %get-tuple-element.16, f32[768]{0:T(1024)S(1)} %copy-done.9, f32[768]{0:T(1024)S(1)} %copy-done.7, f32[768]{0:T(1024)S(1)} %copy-done.8, ...), kind=kOutput, calls=%fused_computation.2 | convolution fusion | flops 865075200 | bytes 56681472 | tf_op jit(solution)/shard_map/pb,sapc->sabc/dot_general | solution.py:48
  (38 shorter events, 4.8 us)
Async XLA Ops:
  7.2 170.1 %copy-start = (bf16[256,256]{1,0:T(8,128)(2,1)S(1)}, bf16[256,256]{1,0:T(8,128)(2,1)}, u32[]{:S(2)}) copy-start(bf16[256,256]{1,0:T(8,128)(2,1)} %param.10) | copy-start | bytes 393220
  174.6 2.6 copy-start.4
  336.9 2.6 copy-start.2
  356.7 12.6 %copy-start.5 = (f32[32,128]{1,0:T(8,128)S(1)}, f32[32,128]{1,0:T(8,128)}, u32[]{:S(2)}) copy-start(f32[32,128]{1,0:T(8,128)} %param.12) | copy-start | bytes 49156
  356.7 12.6 %copy-start.6 = (bf16[128,128]{1,0:T(8,128)(2,1)S(1)}, bf16[128,128]{1,0:T(8,128)(2,1)}, u32[]{:S(2)}) copy-start(bf16[128,128]{1,0:T(8,128)(2,1)} %param.11) | copy-start | bytes 98308
  536.5 2.6 copy-start.3
  555.5 214.1 %all-to-all-start.3 = ((bf16[1,256,16,768]{3,2,0,1:T(8,128)(2,1)}), bf16[1,256,16,768]{3,2,0,1:T(8,128)(2,1)}, u32[]{:S(2)}, u32[]{:S(2)}) async-start(bf16[1,256,16,768]{3,2,0,1:T(8,128)(2,1)} %copy.96), calls=%async_computation.3 | async-start | bytes 12582912 | tf_op jit(solution)/shard_map/all_to_all | solution.py:31
  560.3 206.2 %all-reduce.4.cloned.1.call-start = ((), (), s32[]{:S(2)}) async-start(), calls=%async_computation.4 | async-start | bytes 655360 | tf_op jit(solution)/shard_map/psum | solution.py:55
  564.4 26.9 %slice-start.2 = ((s8[6291456]{0:T(1024)(128)(4,1)}), s8[2097152]{0:T(1024)(128)(4,1)S(1)}, s32[]{:S(2)}) async-start(s8[6291456]{0:T(1024)(128)(4,1)} %bitcast.107), calls=%async_computation.7 | async-start | bytes 4194304
  584.1 7.2 slice-start.3
  769.7 20.2 %slice-start = ((s8[6291456]{0:T(1024)(128)(4,1)}), s8[4194304]{0:T(1024)(128)(4,1)S(1)}, s32[]{:S(2)}) async-start(s8[6291456]{0:T(1024)(128)(4,1)} %bitcast.100), calls=%async_computation.5 | async-start | bytes 8388608
  778.8 11.0 %slice-start.1 = ((s8[6291456]{0:T(1024)(128)(4,1)}), s8[2097152]{0:T(1024)(128)(4,1)S(1)}, s32[]{:S(2)}) async-start(s8[6291456]{0:T(1024)(128)(4,1)} %bitcast.100), calls=%async_computation.6 | async-start | bytes 4194304
  778.8 11.0 %copy-start.7 = (f32[768]{0:T(1024)S(1)}, f32[768]{0:T(1024)}, u32[]{:S(2)}) copy-start(f32[768]{0:T(1024)} %param.14) | copy-start | bytes 9220
  778.8 11.0 %copy-start.8 = (f32[768]{0:T(1024)S(1)}, f32[768]{0:T(1024)}, u32[]{:S(2)}) copy-start(f32[768]{0:T(1024)} %param.13) | copy-start | bytes 9220
  778.8 11.0 %copy-start.9 = (f32[768]{0:T(1024)S(1)}, f32[768]{0:T(1024)}, u32[]{:S(2)}) copy-start(f32[768]{0:T(1024)} %param.15) | copy-start | bytes 9220
  843.9 21.5 %copy-start.1 = (bf16[256,256]{1,0:T(8,128)(2,1)S(1)}, bf16[256,256]{1,0:T(8,128)(2,1)}, u32[]{:S(2)}) copy-start(bf16[256,256]{1,0:T(8,128)(2,1)} %param.10) | copy-start | bytes 393220
Sparse Core Ops, SparseCore 0:
  601.5 164.9 all-reduce.3
where the time goes:
time: 878 us; the launch traced here: 872 us
  blocking collectives  489 us (56%)
  waiting for transfers between devices  164 us (19%)
  local copies, waits for them, and re-layouts  84.9 us (10%)
  matrix products  64.8 us (7%)
  other arithmetic  49.9 us (6%)
  between operations  14.4 us (2%)
    psum x1, waiting for transfers between devices, token_body(): lax.psum((first_term, second_term, gain_term, bias_term, skip_term), ('dp...  164 us
    all_to_all x1, blocking collectives, token_body(): lax.all_to_all(grad_outer, 'ctx', split_axis=2, concat_axis=1, tiled=True)  145 us
    all_to_all x1, blocking collectives, token_body(): lax.all_to_all(grad_scaled_cols, 'ctx', split_axis=1, concat_axis=2, tile...  143 us
    all_to_all x1, blocking collectives, token_body(): lax.all_to_all(scaled, 'ctx', split_axis=2, concat_axis=1, tiled=True)  143 us
    psum x1, blocking collectives, token_body(): lax.psum((first_term, second_term, gain_term, bias_term, skip_term), ('dp...  41.4 us
    convert_element_type x2, local copies, waits for them, and re-layouts, token_body(): grad_scaled_wide = grad_scaled.astype(jnp.float32)  23.6 us
    dot_general x1, matrix products, token_body(): jnp.einsum('pb,sapc->sabc', second_factor, grad_inner, preferred_element_...  21.5 us
  transfers between devices with their start and end apart: 2, of which 1 were waited for; matrix products, arithmetic and copies ran while one was open for 3% of the time, Pallas kernels for 0%

commit v1 on v0

v1 whole, which is shorter than its diff:
```python
import functools
import math

import jax
import jax.numpy as jnp
from jax import lax
from jax.experimental import pallas as pl
from jax.experimental.pallas import tpu as pltpu
from jax.sharding import PartitionSpec as P

A = 256
B = 128
LANES = 128
VMEM_BYTES = 48 * 1024 * 1024


def dot(left, right, left_dim, right_dim):
    return lax.dot_general(
        left, right, (((left_dim,), (right_dim,)), ((), ())), preferred_element_type=jnp.float32
    )


def split_kernel(tok_ref, cot_ref, out_ref, swap_ref):
    rows = tok_ref.shape[0]
    share = out_ref.shape[2]
    for which, ref in enumerate((tok_ref, cot_ref)):
        for row in range(rows):
            swap_ref[row * LANES : (row + 1) * LANES, :] = ref[row].astype(jnp.float32).T
        for channel in range(LANES):
            out_ref[channel // share, which, channel % share] = swap_ref[
                pl.ds(channel, rows, stride=LANES), :
            ].astype(jnp.bfloat16)


def split_channels(tokens, cotangent, tile, ctx_size):
    rows = tokens.shape[0]
    step = min(16, rows)
    share = LANES // ctx_size
    block = pl.BlockSpec((step, B, LANES), lambda i: (i, 0, tile))
    return pl.pallas_call(
        split_kernel,
        grid=(rows // step,),
        in_specs=[block, block],
        out_specs=pl.BlockSpec((ctx_size, 2, share, step, B), lambda i: (0, 0, 0, i, 0)),
        out_shape=jax.ShapeDtypeStruct((ctx_size, 2, share, rows, B), jnp.bfloat16),
        scratch_shapes=[pltpu.VMEM((step * LANES, B), jnp.float32)],
        compiler_params=pltpu.CompilerParams(vmem_limit_bytes=VMEM_BYTES),
        cost_estimate=pl.CostEstimate(
            flops=0, bytes_accessed=8 * rows * B * LANES * 4, transcendentals=0
        ),
    )(tokens, cotangent)


def merge_kernel(part_ref, *rest):
    out_ref, swap_ref = rest[-2:]
    devices, share, rows, _ = part_ref.shape
    for device in range(devices):
        for channel in range(share):
            at = (device * share + channel) * rows
            swap_ref[at : at + rows, :] = part_ref[device, channel].astype(jnp.float32)
    for row in range(rows):
        out_ref[row] = swap_ref[pl.ds(row, LANES, stride=rows), :].T.astype(jnp.bfloat16)


def merge_channels(parts, held, tile, width):
    devices, share, rows, _ = parts.shape
    step = min(16, rows)
    given = [parts] if held is None else [parts, held]
    specs = [pl.BlockSpec((devices, share, step, B), lambda i: (0, 0, i, 0))]
    if held is not None:
        specs.append(pl.BlockSpec(memory_space=pl.ANY))
    return pl.pallas_call(
        merge_kernel,
        grid=(rows // step,),
        in_specs=specs,
        out_specs=pl.BlockSpec((step, B, LANES), lambda i: (i, 0, tile)),
        out_shape=jax.ShapeDtypeStruct((rows, B, width), jnp.bfloat16),
        scratch_shapes=[pltpu.VMEM((step * LANES, B), jnp.float32)],
        input_output_aliases={} if held is None else {1: 0},
        compiler_params=pltpu.CompilerParams(vmem_limit_bytes=VMEM_BYTES),
        cost_estimate=pl.CostEstimate(
            flops=0, bytes_accessed=4 * rows * B * LANES * 4, transcendentals=0
        ),
    )(*given)


def mix_kernel(
    base_ref, gain_ref, bias_ref, skip_ref, part_ref, first_ref, first_t_ref, second_ref,
    second_t_ref, twiddle_ref, first_in, second_in, twiddle_in,
    out_ref, first_out, second_out, twiddle_out, sums_out,
):
    step = pl.program_id(0)

    @pl.when(step == 0)
    def _():
        first_out[...] = first_in[...]
        second_out[...] = second_in[...]
        twiddle_out[...] = twiddle_in[...]

    devices, _, pair, rows, _ = part_ref.shape
    at = base_ref[0] + step * pair

    def together(which):
        return jnp.concatenate(
            [part_ref[:, which, c].reshape(A, B) for c in range(pair)], axis=1
        )

    def spread(ref):
        lane = lax.broadcasted_iota(jnp.int32, (1, pair * B), 1)
        row = jnp.full((1, pair * B), ref[at], jnp.float32)
        for c in range(1, pair):
            row = jnp.where(lane >= c * B, ref[at + c], row)
        return row

    gain, bias, skip = spread(gain_ref), spread(bias_ref), spread(skip_ref)
    tok = together(0)
    inputs = tok.astype(jnp.float32)
    upstream = together(1).astype(jnp.float32)
    twiddle = jnp.concatenate([twiddle_ref[...]] * pair, axis=1)
    inner = dot(tok, second_t_ref[...], 1, 0)
    scaled = (inner * twiddle).astype(jnp.bfloat16)
    gate = jax.nn.sigmoid(gain * inputs + bias)
    grad_hidden = upstream * gate
    grad_outer = grad_hidden.astype(jnp.bfloat16)
    outer = dot(first_ref[...], scaled, 1, 0).astype(jnp.bfloat16).astype(jnp.float32)
    grad_scaled = dot(first_t_ref[...], grad_outer, 1, 0).astype(jnp.bfloat16).astype(jnp.float32)
    first_out[...] += dot(grad_outer, scaled, 1, 1)
    hidden = outer + skip * inputs
    grad_pre = upstream * hidden * gate * (1.0 - gate)
    product = grad_scaled * inner
    twiddle_out[...] += sum(product[:, c * B : (c + 1) * B] for c in range(pair))
    grad_inner = (grad_scaled * twiddle).astype(jnp.bfloat16)
    second_out[...] += dot(grad_inner, tok, 0, 0)
    grad_in = dot(grad_inner, second_ref[...], 1, 0)
    grad_in = (grad_in + grad_hidden * skip + grad_pre * gain).astype(jnp.bfloat16)
    for c in range(pair):
        out_ref[:, c] = grad_in[:, c * B : (c + 1) * B].reshape(devices, rows, B)
    rows_of = (grad_pre * inputs, grad_pre, grad_hidden * inputs)
    for which, value in enumerate(rows_of):
        total = jnp.sum(value, axis=0, keepdims=True)
        for c in range(pair):
            sums_out[c, which : which + 1] = total[:, c * B : (c + 1) * B]


def mix(parts, base, gain, bias, skip, first, first_t, second, second_t, twiddle, totals):
    devices, _, share, rows, _ = parts.shape
    pair = second.shape[0] // B
    whole = lambda shape: pl.BlockSpec(shape, lambda i: (0,) * len(shape))
    smem = pl.BlockSpec(memory_space=pltpu.SMEM)
    total_specs = [whole(t.shape) for t in totals]
    return pl.pallas_call(
        mix_kernel,
        grid=(share // pair,),
        in_specs=[smem] * 4
        + [pl.BlockSpec((devices, 2, pair, rows, B), lambda i: (0, 0, i, 0, 0))]
        + [whole(t.shape) for t in (first, first_t, second, second_t, twiddle)]
        + total_specs,
        out_specs=[pl.BlockSpec((devices, pair, rows, B), lambda i: (0, i, 0, 0))]
        + total_specs
        + [pl.BlockSpec((pair, 8, B), lambda i: (i, 0, 0))],
        out_shape=[jax.ShapeDtypeStruct((devices, share, rows, B), jnp.bfloat16)]
        + [jax.ShapeDtypeStruct(t.shape, t.dtype) for t in totals]
        + [jax.ShapeDtypeStruct((share, 8, B), jnp.float32)],
        compiler_params=pltpu.CompilerParams(vmem_limit_bytes=VMEM_BYTES),
        cost_estimate=pl.CostEstimate(
            flops=share * A * B * 2 * 2304,
            bytes_accessed=share * A * B * 6,
            transcendentals=share * A * B * 2,
        ),
    )(base, gain, bias, skip, parts, first, first_t, second, second_t, twiddle, *totals)


def block_diagonal(square, count):
    zero = jnp.zeros_like(square)
    return jnp.concatenate(
        [
            jnp.concatenate([square if i == j else zero for j in range(count)], axis=1)
            for i in range(count)
        ],
        axis=0,
    )


def body(tokens, cotangent, first_factor, second_factor, twiddle, gate_gain, gate_bias, skip_gain):
    seq_count, tok_rows, width = tokens.shape
    ctx_size = lax.axis_size("ctx")
    me = lax.axis_index("ctx")
    share = LANES // ctx_size
    local_rows = tok_rows // B
    pair = 2
    tiles = width // LANES

    first_t = first_factor.T
    second = block_diagonal(second_factor, pair)
    second_t = block_diagonal(second_factor.T, pair)
    twiddle_all = lax.all_gather(twiddle, "ctx", axis=0, tiled=True)
    totals = [
        jnp.zeros((A, A), jnp.float32),
        jnp.zeros((pair * B, pair * B), jnp.float32),
        jnp.zeros((A, B), jnp.float32),
    ]
    grads = []
    channel_sums = [[] for _ in range(tiles)]
    for seq in range(seq_count):
        tok_blocks = tokens[seq].reshape(local_rows, B, width)
        cot_blocks = cotangent[seq].reshape(local_rows, B, width)
        arrived = []
        for tile in range(tiles):
            parts = split_channels(tok_blocks, cot_blocks, tile, ctx_size)
            arrived.append(
                lax.all_to_all(parts, "ctx", split_axis=0, concat_axis=0, tiled=True)
            )
        held = None
        for tile in range(tiles):
            base = (tile * LANES + me * share).astype(jnp.int32).reshape(1)
            grad_parts, *totals, sums = mix(
                arrived[tile], base, gate_gain, gate_bias, skip_gain, first_factor, first_t,
                second, second_t, twiddle_all, totals,
            )
            channel_sums[tile].append(jnp.sum(sums, axis=2))
            back = lax.all_to_all(grad_parts, "ctx", split_axis=0, concat_axis=0, tiled=True)
            held = merge_channels(back, held, tile, width)
        grads.append(held.reshape(tok_rows, width))
    grad_tokens = jnp.stack(grads)

    first_term, second_wide, twiddle_term = totals
    second_term = sum(
        second_wide[c * B : (c + 1) * B, c * B : (c + 1) * B] for c in range(pair)
    )
    own = jnp.stack([sum(s)[:, :3] for s in channel_sums])
    spread = jnp.zeros((tiles, ctx_size, share, 3), jnp.float32)
    spread = lax.dynamic_update_slice(spread, own[:, None], (0, me, 0, 0))
    channel_terms = spread.reshape(width, 3).T
    first_sum, second_sum, channel_sum = lax.psum(
        (first_term, second_term, channel_terms), ("dp", "ctx")
    )
    twiddle_sum = lax.psum(
        lax.psum_scatter(twiddle_term, "ctx", scatter_dimension=0, tiled=True), "dp"
    )
    total_seqs = seq_count * lax.axis_size("dp")
    first_norm = math.sqrt(total_seqs * B * width)
    second_norm = math.sqrt(total_seqs * A * width)
    twiddle_norm = math.sqrt(total_seqs * width)
    channel_norm = math.sqrt(total_seqs * A * B)
    return (
        grad_tokens,
        first_sum / first_norm,
        second_sum / second_norm,
        twiddle_sum / twiddle_norm,
        channel_sum[0] / channel_norm,
        channel_sum[1] / channel_norm,
        channel_sum[2] / channel_norm,
    )


def solution(mesh):
    return jax.shard_map(
        body,
        mesh=mesh,
        in_specs=(
            P("dp", "ctx", None),
            P("dp", "ctx", None),
            P(),
            P(),
            P("ctx", None),
            P(),
            P(),
            P(),
        ),
        out_specs=(P("dp", "ctx", None), P(), P(), P("ctx", None), P(), P(), P()),
        check_vma=False,
    )
```

time: 878 us -> 694 us (0.79)
  blocking collectives: 489 us -> 120 us
  waiting for transfers between devices: 164 us -> 348 us
  Pallas kernels: 0 us -> 80.1 us
  matrix products: 64.8 us -> 0 us
  starting transfers between devices: 4.76 us -> 49.1 us
  other arithmetic: 49.9 us -> 14.5 us
  local copies, waits for them, and re-layouts: 84.9 us -> 64 us
    all_to_all x3 -> x0, blocking collectives: 431 us -> none  [the longest x1 145 us: token_body(): lax.all_to_all(grad_outer, 'ctx', split_axis=2, concat_axis=1, tiled=True)]
    all_to_all x1 -> x12, waiting for transfers between devices: 0.01 us -> 267 us  [the longest x6 218 us: body(): lax.all_to_all(parts, 'ctx', split_axis=0, concat_axis=0, tiled=True)]
    psum x1, waiting for transfers between devices: 164 us -> 80.2 us  [body(): lax.psum((first_term, second_term, channel_terms), ('dp', 'ctx'))]
    pallas_call x0 -> x18, Pallas kernels: none -> 80.1 us  [the longest x6 34.9 us: mix(): pl.pallas_call(mix_kernel, grid=(share // pair,), in_specs=[smem] * 4 + [...]
    convert_element_type x8 -> x0, local copies, waits for them, and re-layouts: 68.6 us -> none  [the longest x2 23.6 us: token_body(): grad_scaled_wide = grad_scaled.astype(jnp.float32)]
    dot_general x6 -> x0, matrix products: 64.8 us -> none  [the longest x1 21.5 us: token_body(): jnp.einsum('pb,sapc->sabc', second_factor, grad_inner, preferred_element_...]
    all_gather x0 -> x1, blocking collectives: none -> 55 us  [body(): twiddle_all = lax.all_gather(twiddle, 'ctx', axis=0, tiled=True)]
    unnamed x29 -> x159, local copies, waits for them, and re-layouts: 7.9 us -> 57.5 us
  transfers between devices with their start and end apart: 2 -> 14, of which waited for: 1 -> 10; matrix products, arithmetic and copies ran while one was open for 3% -> 3% of each run, Pallas kernels for 0% -> 10%
where the time goes in v1:
time: 694 us; the launch traced here: 692 us
  waiting for transfers between devices  348 us (50%)
  blocking collectives  120 us (17%)
  Pallas kernels  80.1 us (12%)
  local copies, waits for them, and re-layouts  64 us (9%)
  starting transfers between devices  49.1 us (7%)
  between operations  16 us (2%)
  other arithmetic  14.5 us (2%)
    all_to_all x6, waiting for transfers between devices, body(): lax.all_to_all(parts, 'ctx', split_axis=0, concat_axis=0, tiled=True)  218 us
    psum x1, waiting for transfers between devices, body(): lax.psum((first_term, second_term, channel_terms), ('dp', 'ctx'))  80.2 us
    unnamed x159, local copies, waits for them, and re-layouts  57.5 us
    all_gather x1, blocking collectives, body(): twiddle_all = lax.all_gather(twiddle, 'ctx', axis=0, tiled=True)  55 us
    all_to_all x6, waiting for transfers between devices, body(): lax.all_to_all(grad_parts, 'ctx', split_axis=0, concat_axis=0, tiled=True)  49.1 us
    psum x1, blocking collectives, body(): lax.psum((first_term, second_term, channel_terms), ('dp', 'ctx'))  49.1 us
    pallas_call x6, Pallas kernels, mix(): pl.pallas_call(mix_kernel, grid=(share // pair,), in_specs=[smem] * 4 + [...  34.9 us
    pallas_call x6, Pallas kernels, split_channels(): pl.pallas_call(split_kernel, grid=(rows // step,), in_specs=[block, block...  32 us
  transfers between devices with their start and end apart: 14, of which 10 were waited for; matrix products, arithmetic and copies ran while one was open for 3% of the time, Pallas kernels for 10%

profile of v1, /device:TPU:0, one launch (start us, length us, event | category | flops | bytes accessed | tf_op | source)
XLA Modules:
  0.0 691.7 jit_solution(11103487317169672811)
XLA Ops:
  8.0 5.4 shard_map.140
  13.4 6.3 all-to-all-start.5
  19.7 5.3 shard_map.139
  25.0 43.8 %all-to-all-done.5.part_ref = bf16[8,2,16,32,128]{4,3,2,1,0:T(8,128)(2,1)S(1)} async-done(((bf16[8,2,16,32,128]{4,3,2,1,0:T(8,128)(2,1)}), bf16[8,2,16,32,128]{4,3,2,1,0:T(8,128)(2,1)S(1)}, u32[]{:S(2)}, u32[]{:S(2)}) %all-to-all-start.5) | async-done | bytes 2097184 | tf_op jit(solution)/shard_map/all_to_all | solution.py:211
  70.1 3.6 all-to-all-start.4
  73.7 5.4 shard_map.138
  79.0 43.6 %all-to-all-done.4.part_ref = bf16[8,2,16,32,128]{4,3,2,1,0:T(8,128)(2,1)S(1)} async-done(((bf16[8,2,16,32,128]{4,3,2,1,0:T(8,128)(2,1)}), bf16[8,2,16,32,128]{4,3,2,1,0:T(8,128)(2,1)S(1)}, u32[]{:S(2)}, u32[]{:S(2)}) %all-to-all-start.4) | async-done | bytes 2097184 | tf_op jit(solution)/shard_map/all_to_all | solution.py:211
  127.7 5.3 shard_map.137
  133.0 43.7 %all-to-all-done.3.part_ref = bf16[8,2,16,32,128]{4,3,2,1,0:T(8,128)(2,1)S(1)} async-done(((bf16[8,2,16,32,128]{4,3,2,1,0:T(8,128)(2,1)}), bf16[8,2,16,32,128]{4,3,2,1,0:T(8,128)(2,1)S(1)}, u32[]{:S(2)}, u32[]{:S(2)}) %all-to-all-start.3) | async-done | bytes 2097184 | tf_op jit(solution)/shard_map/all_to_all | solution.py:211
  181.6 5.4 shard_map.136
  187.0 43.6 %all-to-all-done.2.part_ref = bf16[8,2,16,32,128]{4,3,2,1,0:T(8,128)(2,1)S(1)} async-done(((bf16[8,2,16,32,128]{4,3,2,1,0:T(8,128)(2,1)}), bf16[8,2,16,32,128]{4,3,2,1,0:T(8,128)(2,1)S(1)}, u32[]{:S(2)}, u32[]{:S(2)}) %all-to-all-start.2) | async-done | bytes 2097184 | tf_op jit(solution)/shard_map/all_to_all | solution.py:211
  235.6 5.3 shard_map.135
  240.9 43.6 %all-to-all-done.1.part_ref = bf16[8,2,16,32,128]{4,3,2,1,0:T(8,128)(2,1)S(1)} async-done(((bf16[8,2,16,32,128]{4,3,2,1,0:T(8,128)(2,1)}), bf16[8,2,16,32,128]{4,3,2,1,0:T(8,128)(2,1)S(1)}, u32[]{:S(2)}, u32[]{:S(2)}) %all-to-all-start.1) | async-done | bytes 2097184 | tf_op jit(solution)/shard_map/all_to_all | solution.py:211
  289.8 55.0 %all_gather.3.twiddle_ref = f32[256,128]{1,0:T(8,128)S(1)} all-gather(f32[32,128]{1,0:T(8,128)S(1)} %copy-done.72), channel_id=1, replica_groups=mesh['dp'=4,'ctx'=8] {'ctx'}, dimensions={0}, use_global_device_ids=true | all-gather | bytes 147456 | tf_op jit(solution)/shard_map/all_gather | solution.py:196
  347.1 5.7 shard_map.141
  357.8 4.0 all-to-all-start.11
  366.5 5.7 shard_map.142
  375.9 12.6 %all-to-all-done.11.part_ref = bf16[8,16,32,128]{3,2,1,0:T(8,128)(2,1)S(1)} async-done(((bf16[8,16,32,128]{3,2,1,0:T(8,128)(2,1)}), bf16[8,16,32,128]{3,2,1,0:T(8,128)(2,1)S(1)}, u32[]{:S(2)}, u32[]{:S(2)}) %all-to-all-start.11) | async-done | bytes 1048608 | tf_op jit(solution)/shard_map/all_to_all | solution.py:221
  388.4 3.7 all-to-all-start.10
  394.7 5.7 shard_map.143
  404.1 14.6 %all-to-all-done.10.part_ref = bf16[8,16,32,128]{3,2,1,0:T(8,128)(2,1)S(1)} async-done(((bf16[8,16,32,128]{3,2,1,0:T(8,128)(2,1)}), bf16[8,16,32,128]{3,2,1,0:T(8,128)(2,1)S(1)}, u32[]{:S(2)}, u32[]{:S(2)}) %all-to-all-start.10) | async-done | bytes 1048608 | tf_op jit(solution)/shard_map/all_to_all | solution.py:221
  428.4 5.7 shard_map.144
  437.8 11.0 %all-to-all-done.9.part_ref = bf16[8,16,32,128]{3,2,1,0:T(8,128)(2,1)S(1)} async-done(((bf16[8,16,32,128]{3,2,1,0:T(8,128)(2,1)}), bf16[8,16,32,128]{3,2,1,0:T(8,128)(2,1)S(1)}, u32[]{:S(2)}, u32[]{:S(2)}) %all-to-all-start.9) | async-done | bytes 1048608 | tf_op jit(solution)/shard_map/all_to_all | solution.py:221
  448.7 4.2 all-to-all-start.8
  459.2 5.7 shard_map.145
  468.6 11.0 %all-to-all-done.8.part_ref = bf16[8,16,32,128]{3,2,1,0:T(8,128)(2,1)} async-done(((bf16[8,16,32,128]{3,2,1,0:T(8,128)(2,1)}), bf16[8,16,32,128]{3,2,1,0:T(8,128)(2,1)}, u32[]{:S(2)}, u32[]{:S(2)}) %all-to-all-start.8) | async-done | bytes 1048608 | tf_op jit(solution)/shard_map/all_to_all | solution.py:221
  479.6 4.2 all-to-all-start.7
  503.9 6.5 shard_map.146
  515.9 5.0 all-to-all-start.6
  521.4 49.1 %psum.31 = f32[3,768]{1,0:T(4,128)S(1)} all-reduce(f32[3,768]{1,0:T(4,128)S(1)} %bitcast.55), channel_id=1, replica_groups=mesh['dp'=4,'ctx'=8] {'dp','ctx'}, use_global_device_ids=true, to_apply=%region_10.0 | all-reduce | flops 2304 | bytes 18432 | tf_op jit(solution)/shard_map/psum | solution.py:234
  571.1 80.2 %all-reduce.7.cloned.1.call-done = (f32[256,256]{1,0:T(8,128)}, f32[128,128]{1,0:T(8,128)}) async-done(((f32[256,256]{1,0:T(8,128)}, f32[128,128]{1,0:T(8,128)}), (f32[256,256]{1,0:T(8,128)}, f32[128,128]{1,0:T(8,128)})) %all-reduce.7.cloned.1.call-update) | async-done | bytes 327696 | tf_op jit(solution)/shard_map/psum | solution.py:234
  654.5 16.0 %psum.30 = f32[32,128]{1,0:T(8,128)S(1)} all-reduce(f32[32,128]{1,0:T(8,128)} %reduce-scatter.2.cloned.1.call-done), channel_id=1, replica_groups=mesh['dp'=4,'ctx'=8] {'dp'}, use_global_device_ids=true, to_apply=%region_3.0 | all-reduce | flops 4096 | bytes 32768 | tf_op jit(solution)/shard_map/psum | solution.py:237
  (203 shorter events, 109.9 us)
Async XLA Ops:
  13.4 55.4 %all-to-all-start.5 = ((bf16[8,2,16,32,128]{4,3,2,1,0:T(8,128)(2,1)}), bf16[8,2,16,32,128]{4,3,2,1,0:T(8,128)(2,1)S(1)}, u32[]{:S(2)}, u32[]{:S(2)}) async-start(bf16[8,2,16,32,128]{4,3,2,1,0:T(8,128)(2,1)} %shard_map.140), calls=%async_computation.5 | async-start | bytes 4194304 | tf_op jit(solution)/shard_map/all_to_all | solution.py:211
  70.1 52.6 %all-to-all-start.4 = ((bf16[8,2,16,32,128]{4,3,2,1,0:T(8,128)(2,1)}), bf16[8,2,16,32,128]{4,3,2,1,0:T(8,128)(2,1)S(1)}, u32[]{:S(2)}, u32[]{:S(2)}) async-start(bf16[8,2,16,32,128]{4,3,2,1,0:T(8,128)(2,1)} %shard_map.139), calls=%async_computation.4 | async-start | bytes 4194304 | tf_op jit(solution)/shard_map/all_to_all | solution.py:211
  124.1 52.6 %all-to-all-start.3 = ((bf16[8,2,16,32,128]{4,3,2,1,0:T(8,128)(2,1)}), bf16[8,2,16,32,128]{4,3,2,1,0:T(8,128)(2,1)S(1)}, u32[]{:S(2)}, u32[]{:S(2)}) async-start(bf16[8,2,16,32,128]{4,3,2,1,0:T(8,128)(2,1)} %shard_map.138), calls=%async_computation.3 | async-start | bytes 4194304 | tf_op jit(solution)/shard_map/all_to_all | solution.py:211
  178.0 52.6 %all-to-all-start.2 = ((bf16[8,2,16,32,128]{4,3,2,1,0:T(8,128)(2,1)}), bf16[8,2,16,32,128]{4,3,2,1,0:T(8,128)(2,1)S(1)}, u32[]{:S(2)}, u32[]{:S(2)}) async-start(bf16[8,2,16,32,128]{4,3,2,1,0:T(8,128)(2,1)} %shard_map.137), calls=%async_computation.2 | async-start | bytes 4194304 | tf_op jit(solution)/shard_map/all_to_all | solution.py:211
  232.0 52.6 %all-to-all-start.1 = ((bf16[8,2,16,32,128]{4,3,2,1,0:T(8,128)(2,1)}), bf16[8,2,16,32,128]{4,3,2,1,0:T(8,128)(2,1)S(1)}, u32[]{:S(2)}, u32[]{:S(2)}) async-start(bf16[8,2,16,32,128]{4,3,2,1,0:T(8,128)(2,1)} %shard_map.136), calls=%async_computation.1 | async-start | bytes 4194304 | tf_op jit(solution)/shard_map/all_to_all | solution.py:211
  240.9 48.6 %copy-start.71 = (bf16[128,128]{1,0:T(8,128)(2,1)S(1)}, bf16[128,128]{1,0:T(8,128)(2,1)}, u32[]{:S(2)}) copy-start(bf16[128,128]{1,0:T(8,128)(2,1)} %param.11) | copy-start | bytes 98308
  240.9 48.7 %copy-start.18 = (bf16[256,256]{1,0:T(8,128)(2,1)S(1)}, bf16[256,256]{1,0:T(8,128)(2,1)}, u32[]{:S(2)}) copy-start(bf16[256,256]{1,0:T(8,128)(2,1)} %first_ref.11) | copy-start | bytes 393220
  240.9 48.8 %copy-start.72 = (f32[32,128]{1,0:T(8,128)S(1)}, f32[32,128]{1,0:T(8,128)}, u32[]{:S(2)}) copy-start(f32[32,128]{1,0:T(8,128)} %param.12) | copy-start | bytes 49156
  240.9 104.6 %copy-start.38 = (f32[768]{0:T(1024)S(1)}, f32[768]{0:T(1024)}, u32[]{:S(2)}) copy-start(f32[768]{0:T(1024)} %gain_ref.11) | copy-start | bytes 9220
  240.9 104.6 %copy-start.39 = (f32[768]{0:T(1024)S(1)}, f32[768]{0:T(1024)}, u32[]{:S(2)}) copy-start(f32[768]{0:T(1024)} %bias_ref.11) | copy-start | bytes 9220
  240.9 104.6 %copy-start.40 = (f32[768]{0:T(1024)S(1)}, f32[768]{0:T(1024)}, u32[]{:S(2)}) copy-start(f32[768]{0:T(1024)} %skip_ref.11) | copy-start | bytes 9220
  285.9 70.6 %all-to-all-start = ((bf16[8,2,16,32,128]{4,3,2,1,0:T(8,128)(2,1)}), bf16[8,2,16,32,128]{4,3,2,1,0:T(8,128)(2,1)S(1)}, u32[]{:S(2)}, u32[]{:S(2)}) async-start(bf16[8,2,16,32,128]{4,3,2,1,0:T(8,128)(2,1)} %shard_map.135), calls=%async_computation | async-start | bytes 4194304 | tf_op jit(solution)/shard_map/all_to_all | solution.py:211
  345.5 1.6 copy-start.11
  357.8 4.0 copy-start.9
  357.8 30.6 %all-to-all-start.11 = ((bf16[8,16,32,128]{3,2,1,0:T(8,128)(2,1)}), bf16[8,16,32,128]{3,2,1,0:T(8,128)(2,1)S(1)}, u32[]{:S(2)}, u32[]{:S(2)}) async-start(bf16[8,16,32,128]{3,2,1,0:T(8,128)(2,1)} %copy-done.17), calls=%async_computation.11 | async-start | bytes 2097152 | tf_op jit(solution)/shard_map/all_to_all | solution.py:221
  375.9 16.3 %copy-start.21 = (bf16[256,256]{1,0:T(8,128)(2,1)S(1)}, bf16[256,256]{1,0:T(8,128)(2,1)}, u32[]{:S(2)}) copy-start(bf16[256,256]{1,0:T(8,128)(2,1)} %copy-done.19) | copy-start | bytes 393220
  375.9 16.3 %copy-start.27 = (bf16[256,256]{1,0:T(8,128)(2,1)S(1)}, bf16[256,256]{1,0:T(8,128)(2,1)}, u32[]{:S(2)}) copy-start(bf16[256,256]{1,0:T(8,128)(2,1)} %copy-done.25) | copy-start | bytes 393220
  388.4 3.7 copy-start.46
  388.4 3.7 copy-start.48
  388.4 30.2 %all-to-all-start.10 = ((bf16[8,16,32,128]{3,2,1,0:T(8,128)(2,1)}), bf16[8,16,32,128]{3,2,1,0:T(8,128)(2,1)S(1)}, u32[]{:S(2)}, u32[]{:S(2)}) async-start(bf16[8,16,32,128]{3,2,1,0:T(8,128)(2,1)} %copy-done.14), calls=%async_computation.10 | async-start | bytes 2097152 | tf_op jit(solution)/shard_map/all_to_all | solution.py:221
  392.2 1.6 copy-start.7
  418.6 30.1 %all-to-all-start.9 = ((bf16[8,16,32,128]{3,2,1,0:T(8,128)(2,1)}), bf16[8,16,32,128]{3,2,1,0:T(8,128)(2,1)S(1)}, u32[]{:S(2)}, u32[]{:S(2)}) async-start(bf16[8,16,32,128]{3,2,1,0:T(8,128)(2,1)} %copy-done.15), calls=%async_computation.9 | async-start | bytes 2097152 | tf_op jit(solution)/shard_map/all_to_all | solution.py:221
  422.2 1.6 copy-start.5
  448.7 30.8 %all-to-all-start.8 = ((bf16[8,16,32,128]{3,2,1,0:T(8,128)(2,1)}), bf16[8,16,32,128]{3,2,1,0:T(8,128)(2,1)}, u32[]{:S(2)}, u32[]{:S(2)}) async-start(bf16[8,16,32,128]{3,2,1,0:T(8,128)(2,1)} %copy-done.16), calls=%async_computation.8 | async-start | bytes 2097152 | tf_op jit(solution)/shard_map/all_to_all | solution.py:221
  453.0 1.6 copy-start.3
  479.6 36.3 %all-to-all-start.7 = ((bf16[8,16,32,128]{3,2,1,0:T(8,128)(2,1)}), bf16[8,16,32,128]{3,2,1,0:T(8,128)(2,1)}, u32[]{:S(2)}, u32[]{:S(2)}) async-start(bf16[8,16,32,128]{3,2,1,0:T(8,128)(2,1)} %copy-done.13), calls=%async_computation.7 | async-start | bytes 2097152 | tf_op jit(solution)/shard_map/all_to_all | solution.py:221
  483.8 167.5 %all-reduce.7.cloned.1.call-start = ((), (), s32[]{:S(2)}) async-start(), calls=%async_computation.14 | async-start | bytes 655360 | tf_op jit(solution)/shard_map/psum | solution.py:234
  512.6 8.3 %copy-start.73 = (f32[16,3]{0,1:T(4,128)S(1)}, f32[16,3]{0,1:T(4,128)}, u32[]{:S(2)}) copy-start(f32[16,3]{0,1:T(4,128)} %copy.29) | copy-start | bytes 580
  512.6 8.3 %copy-start.74 = (f32[16,3]{0,1:T(4,128)S(1)}, f32[16,3]{0,1:T(4,128)}, u32[]{:S(2)}) copy-start(f32[16,3]{0,1:T(4,128)} %copy.30) | copy-start | bytes 580
  512.6 8.3 %copy-start.75 = (f32[16,3]{0,1:T(4,128)S(1)}, f32[16,3]{0,1:T(4,128)}, u32[]{:S(2)}) copy-start(f32[16,3]{0,1:T(4,128)} %copy.31) | copy-start | bytes 580
  515.9 165.7 %all-to-all-start.6 = ((bf16[8,16,32,128]{3,2,1,0:T(8,128)(2,1)}), bf16[8,16,32,128]{3,2,1,0:T(8,128)(2,1)}, u32[]{:S(2)}, u32[]{:S(2)}) async-start(bf16[8,16,32,128]{3,2,1,0:T(8,128)(2,1)} %copy-done.12), calls=%async_computation.6 | async-start | bytes 2097152 | tf_op jit(solution)/shard_map/all_to_all | solution.py:221
  520.8 133.7 %reduce-scatter.2.cloned.1.call-start = ((), (), s32[]{:S(2)}) async-start(), calls=%async_computation.13 | async-start | bytes 147456 | tf_op jit(solution)/shard_map/reduce_scatter | solution.py:238
  (58 other events, 50.9 us)
Sparse Core Ops, SparseCore 0:
  515.3 135.9 all-reduce.6
Sparse Core Ops, SparseCore 1:
  523.6 32.3 reduce-scatter.1

commit v2 on v1

v2 whole, which is shorter than its diff:
```python
import functools
import math

import jax
import jax.numpy as jnp
from jax import lax
from jax.experimental import pallas as pl
from jax.experimental.pallas import tpu as pltpu
from jax.sharding import PartitionSpec as P

A = 256
B = 128
LANES = 128
VMEM_BYTES = 48 * 1024 * 1024


def dot(left, right, left_dim, right_dim):
    return lax.dot_general(
        left, right, (((left_dim,), (right_dim,)), ((), ())), preferred_element_type=jnp.float32
    )


def split_tile(tok_ref, cot_ref, out_ref, swap_ref, first_at, second_at):
    rows = tok_ref.shape[0]
    share = LANES // out_ref.shape[0]
    for at, ref in ((first_at, tok_ref), (second_at, cot_ref)):
        for row in range(rows):
            swap_ref[row * LANES : (row + 1) * LANES, :] = ref[row].astype(jnp.float32).T
        for channel in range(LANES):
            out_ref[channel // share, at + channel % share] = swap_ref[
                pl.ds(channel, rows, stride=LANES), :
            ].astype(jnp.bfloat16)


def split_kernel(tok_ref, cot_ref, out_ref, swap_ref):
    share = LANES // out_ref.shape[0]
    split_tile(tok_ref, cot_ref, out_ref, swap_ref, 0, share)


def split_twiddle_kernel(tok_ref, cot_ref, twiddle_ref, out_ref, swap_ref):
    share = LANES // out_ref.shape[0]
    split_tile(tok_ref, cot_ref, out_ref, swap_ref, 0, share)
    left = twiddle_ref[...]
    for plane in range(3):
        part = left.astype(jnp.bfloat16)
        left = left - part.astype(jnp.float32)
        for device in range(out_ref.shape[0]):
            out_ref[device, 2 * share + plane] = part


def split_channels(tokens, cotangent, tile, tiles, ctx_size, twiddle=None):
    rows = tokens.shape[0]
    step = min(16, rows)
    share = LANES // ctx_size
    block = pl.BlockSpec((step, B, LANES), lambda t, i: (i, 0, tile + t))
    if twiddle is None:
        kernel, given, specs = split_kernel, [tokens, cotangent], [block, block]
        planes = 2 * share
    else:
        kernel, given = split_twiddle_kernel, [tokens, cotangent, twiddle]
        specs = [block, block, pl.BlockSpec((step, B), lambda t, i: (i, 0))]
        planes = 2 * share + 3
    return pl.pallas_call(
        kernel,
        grid=(tiles, rows // step),
        in_specs=specs,
        out_specs=pl.BlockSpec((ctx_size, planes, step, B), lambda t, i: (0, t, i, 0)),
        out_shape=jax.ShapeDtypeStruct((ctx_size, tiles * planes, rows, B), jnp.bfloat16),
        scratch_shapes=[pltpu.VMEM((step * LANES, B), jnp.float32)],
        compiler_params=pltpu.CompilerParams(vmem_limit_bytes=VMEM_BYTES),
        cost_estimate=pl.CostEstimate(
            flops=0, bytes_accessed=8 * rows * B * LANES * tiles, transcendentals=0
        ),
    )(*given)


def merge_kernel(part_ref, *rest):
    out_ref, swap_ref = rest[-2:]
    devices, share, rows, _ = part_ref.shape
    for device in range(devices):
        for channel in range(share):
            at = (device * share + channel) * rows
            swap_ref[at : at + rows, :] = part_ref[device, channel].astype(jnp.float32)
    for row in range(rows):
        out_ref[row] = swap_ref[pl.ds(row, LANES, stride=rows), :].T.astype(jnp.bfloat16)


def merge_channels(parts, held, tile, width):
    devices, channels, rows, _ = parts.shape
    step = min(16, rows)
    share = LANES // devices
    tiles = channels // share
    given = [parts] if held is None else [parts, held]
    specs = [pl.BlockSpec((devices, share, step, B), lambda t, i: (0, t, i, 0))]
    if held is not None:
        specs.append(pl.BlockSpec(memory_space=pl.ANY))
    return pl.pallas_call(
        merge_kernel,
        grid=(tiles, rows // step),
        in_specs=specs,
        out_specs=pl.BlockSpec((step, B, LANES), lambda t, i: (i, 0, tile + t)),
        out_shape=jax.ShapeDtypeStruct((rows, B, width), jnp.bfloat16),
        scratch_shapes=[pltpu.VMEM((step * LANES, B), jnp.float32)],
        input_output_aliases={} if held is None else {1: 0},
        compiler_params=pltpu.CompilerParams(vmem_limit_bytes=VMEM_BYTES),
        cost_estimate=pl.CostEstimate(
            flops=0, bytes_accessed=4 * rows * B * LANES * tiles, transcendentals=0
        ),
    )(*given)


SECOND_AT = 2 * A
TWIDDLE_AT = SECOND_AT + B
CHANNEL_AT = TWIDDLE_AT + A


def mix_kernel(
    place_ref, gain_ref, bias_ref, skip_ref, tok_ref, cot_ref, first_ref, first_t_ref, second_ref,
    second_t_ref, twiddle_ref, *rest, tile, tile_count, has_sums,
):
    out_ref, sums_ref = rest[-2:]
    t, step = pl.program_id(0), pl.program_id(1)

    @pl.when((t == 0) & (step == 0))
    def _():
        sums_ref[...] = rest[0][...] if has_sums else jnp.zeros(sums_ref.shape, jnp.float32)

    devices, pair, rows, _ = tok_ref.shape
    lane_at = place_ref[0] + step * pair
    at = (tile + t) * LANES + lane_at

    def together(ref):
        return jnp.concatenate([ref[:, c].reshape(A, B) for c in range(pair)], axis=1)

    def spread(ref):
        lane = lax.broadcasted_iota(jnp.int32, (1, pair * B), 1)
        row = jnp.full((1, pair * B), ref[at], jnp.float32)
        for c in range(1, pair):
            row = jnp.where(lane >= c * B, ref[at + c], row)
        return row

    gain, bias, skip = spread(gain_ref), spread(bias_ref), spread(skip_ref)
    tok = together(tok_ref)
    inputs = tok.astype(jnp.float32)
    upstream = together(cot_ref).astype(jnp.float32)
    twiddle = jnp.concatenate([twiddle_ref[...]] * pair, axis=1)
    inner = dot(tok, second_t_ref[...], 1, 0)
    scaled = (inner * twiddle).astype(jnp.bfloat16)
    gate = jax.nn.sigmoid(gain * inputs + bias)
    grad_hidden = upstream * gate
    grad_outer = grad_hidden.astype(jnp.bfloat16)
    outer = dot(first_ref[...], scaled, 1, 0).astype(jnp.bfloat16).astype(jnp.float32)
    grad_scaled = dot(first_t_ref[...], grad_outer, 1, 0).astype(jnp.bfloat16).astype(jnp.float32)
    first_term = dot(grad_outer, scaled, 1, 1)
    for half in range(A // B):
        sums_ref[half * A : (half + 1) * A] += first_term[:, half * B : (half + 1) * B]
    hidden = outer + skip * inputs
    grad_pre = upstream * hidden * gate * (1.0 - gate)
    product = grad_scaled * inner
    sums_ref[TWIDDLE_AT:CHANNEL_AT] += sum(product[:, c * B : (c + 1) * B] for c in range(pair))
    grad_inner = (grad_scaled * twiddle).astype(jnp.bfloat16)
    second_term = dot(grad_inner, tok, 0, 0)
    sums_ref[SECOND_AT:TWIDDLE_AT] += sum(
        second_term[c * B : (c + 1) * B, c * B : (c + 1) * B] for c in range(pair)
    )
    grad_in = dot(grad_inner, second_ref[...], 1, 0)
    grad_in = (grad_in + grad_hidden * skip + grad_pre * gain).astype(jnp.bfloat16)
    for c in range(pair):
        out_ref[:, c] = grad_in[:, c * B : (c + 1) * B].reshape(devices, rows, B)
    lane = lax.broadcasted_iota(jnp.int32, (1, LANES), 1)
    for which, value in enumerate((grad_pre * inputs, grad_pre, grad_hidden * inputs)):
        total = jnp.sum(value, axis=0, keepdims=True)
        row = jnp.zeros((1, LANES), jnp.float32)
        for c in range(pair):
            channel = jnp.sum(total[:, c * B : (c + 1) * B], axis=1, keepdims=True)
            row = jnp.where(lane == lane_at + c, channel, row)
        sums_ref[pl.ds(CHANNEL_AT + which * tile_count + tile + t, 1), :] += row


def mix(parts, tile, tiles, planes, place, vectors, factors, sums, sum_rows, out_tiles, out_at, held):
    devices, _, rows, _ = parts.shape
    share = LANES // devices
    pair = factors[2].shape[0] // B
    steps = share // pair
    whole = lambda array: pl.BlockSpec(array.shape, lambda t, i: (0,) * array.ndim)
    tok_at = lambda t, i: (0, t * (planes // pair) + i, 0, 0)
    cot_at = lambda t, i: (0, t * (planes // pair) + steps + i, 0, 0)
    block = (devices, pair, rows, B)
    given = [place, *vectors, parts, parts, *factors]
    specs = [pl.BlockSpec(memory_space=pltpu.SMEM)] * 4
    specs += [pl.BlockSpec(block, tok_at), pl.BlockSpec(block, cot_at)]
    specs += [whole(f) for f in factors]
    aliases = {}
    if sums is not None:
        given.append(sums)
        specs.append(whole(sums))
    if held is not None:
        aliases[len(given)] = 0
        given.append(held)
        specs.append(pl.BlockSpec(memory_space=pl.ANY))
    tile_count = vectors[0].shape[0] // LANES
    return pl.pallas_call(
        functools.partial(
            mix_kernel, tile=tile, tile_count=tile_count, has_sums=sums is not None
        ),
        grid=(tiles, steps),
        in_specs=specs,
        out_specs=[
            pl.BlockSpec(block, lambda t, i: (0, (out_at + t) * steps + i, 0, 0)),
            pl.BlockSpec((sum_rows, LANES), lambda t, i: (0, 0)),
        ],
        out_shape=[
            jax.ShapeDtypeStruct((devices, out_tiles * share, rows, B), jnp.bfloat16),
            jax.ShapeDtypeStruct((sum_rows, LANES), jnp.float32),
        ],
        input_output_aliases=aliases,
        compiler_params=pltpu.CompilerParams(vmem_limit_bytes=VMEM_BYTES),
        cost_estimate=pl.CostEstimate(
            flops=tiles * share * A * B * 2 * 2304,
            bytes_accessed=tiles * share * A * B * 6,
            transcendentals=tiles * share * A * B * 2,
        ),
    )(*given)


def block_diagonal(square, count):
    zero = jnp.zeros_like(square)
    return jnp.concatenate(
        [
            jnp.concatenate([square if i == j else zero for j in range(count)], axis=1)
            for i in range(count)
        ],
        axis=0,
    )


def body(tokens, cotangent, first_factor, second_factor, twiddle, gate_gain, gate_bias, skip_gain):
    seq_count, tok_rows, width = tokens.shape
    ctx_size = lax.axis_size("ctx")
    dp_size = lax.axis_size("dp")
    share = LANES // ctx_size
    local_rows = tok_rows // B
    tiles = width // LANES
    pair = 2
    sent = [1, tiles - 2, 1]
    returned = [tiles - 1, 1]

    place = (lax.axis_index("ctx") * share).astype(jnp.int32).reshape(1)
    second = block_diagonal(second_factor, pair)
    second_t = block_diagonal(second_factor.T, pair)
    vectors = [gate_gain, gate_bias, skip_gain]
    used_rows = CHANNEL_AT + 3 * tiles
    sum_rows = -(-used_rows // (8 * dp_size)) * 8 * dp_size

    def exchange(parts):
        return lax.all_to_all(parts, "ctx", split_axis=0, concat_axis=0, tiled=True)

    sums = None
    factors = None
    grads = []
    for seq in range(seq_count):
        tok_blocks = tokens[seq].reshape(local_rows, B, width)
        cot_blocks = cotangent[seq].reshape(local_rows, B, width)
        arrived = []
        at = 0
        for count in sent:
            own = twiddle if at == 0 else None
            parts = exchange(split_channels(tok_blocks, cot_blocks, at, count, ctx_size, own))
            arrived.append((at, count, parts))
            at += count
        planes = arrived[0][2][:, 2 * share :].astype(jnp.float32)
        twiddle_all = (planes[:, 0] + planes[:, 1] + planes[:, 2]).reshape(A, B)
        factors = [first_factor, first_factor.T, second, second_t, twiddle_all]
        leaving = [None] * len(returned)
        for at, count, parts in arrived:
            back = 0 if at < returned[0] else 1
            out_at = at - back * returned[0]
            leaving[back], sums = mix(
                parts, at, count, 2 * share, place, vectors, factors, sums, sum_rows,
                returned[back], out_at, leaving[back],
            )
        held = None
        at = 0
        for count, grad_parts in zip(returned, leaving):
            held = merge_channels(exchange(grad_parts), held, at, width)
            at += count
        grads.append(held.reshape(tok_rows, width))
    grad_tokens = jnp.stack(grads)

    sums = lax.psum_scatter(sums, "dp", scatter_dimension=0, tiled=True)
    sums = lax.psum(sums, "ctx")
    sums = lax.all_gather(sums, "dp", axis=0, tiled=True)
    total_seqs = seq_count * dp_size
    first_norm = math.sqrt(total_seqs * B * width)
    second_norm = math.sqrt(total_seqs * A * width)
    twiddle_norm = math.sqrt(total_seqs * width)
    channel_norm = math.sqrt(total_seqs * A * B)
    first_sum = jnp.concatenate([sums[half * A : (half + 1) * A] for half in range(A // B)], axis=1)
    mine = TWIDDLE_AT + lax.axis_index("ctx") * local_rows
    twiddle_sum = lax.dynamic_slice_in_dim(sums, mine, local_rows, 0)
    channel_sum = sums[CHANNEL_AT:used_rows].reshape(3, width)
    return (
        grad_tokens,
        first_sum / first_norm,
        sums[SECOND_AT:TWIDDLE_AT] / second_norm,
        twiddle_sum / twiddle_norm,
        channel_sum[0] / channel_norm,
        channel_sum[1] / channel_norm,
        channel_sum[2] / channel_norm,
    )


def solution(mesh):
    return jax.shard_map(
        body,
        mesh=mesh,
        in_specs=(
            P("dp", "ctx", None),
            P("dp", "ctx", None),
            P(),
            P(),
            P("ctx", None),
            P(),
            P(),
            P(),
        ),
        out_specs=(P("dp", "ctx", None), P(), P(), P("ctx", None), P(), P(), P()),
        check_vma=False,
    )
```

time: 694 us -> 538 us (0.78)
  blocking collectives: 120 us -> 11.2 us
  local copies, waits for them, and re-layouts: 64 us -> 0.96 us
  waiting for transfers between devices: 348 us -> 402 us
  starting transfers between devices: 49.1 us -> 24 us
  other arithmetic: 14.5 us -> 2.67 us
    all_to_all x12 -> x5, waiting for transfers between devices: 267 us -> 339 us  [exchange(): return lax.all_to_all(parts, 'ctx', split_axis=0, concat_axis=0, tiled=True)]
    psum x2 -> x0, blocking collectives: 65.1 us -> none  [the longest x1 49.1 us: body(): lax.psum((first_term, second_term, channel_terms), ('dp', 'ctx'))]
    unnamed x159 -> x14, local copies, waits for them, and re-layouts: 57.5 us -> 0.94 us
    all_gather x1, blocking collectives: 55 us -> 11.2 us  [body(): sums = lax.all_gather(sums, 'dp', axis=0, tiled=True)]
    all_to_all x12 -> x5, starting transfers between devices: 49.1 us -> 23.9 us  [exchange(): return lax.all_to_all(parts, 'ctx', split_axis=0, concat_axis=0, tiled=True)]
    psum x1, waiting for transfers between devices: 80.2 us -> 63 us  [body(): sums = lax.psum(sums, 'ctx')]
    reduce_sum x6 -> x0, other arithmetic: 8.6 us -> none  [body(): channel_sums[tile].append(jnp.sum(sums, axis=2))]
    pallas_call x18 -> x8, Pallas kernels: 80.1 us -> 80.1 us  [the longest x3 43.2 us: mix(): pl.pallas_call(functools.partial(mix_kernel, tile=tile, tile_count=tile_c...]
  transfers between devices with their start and end apart: 14 -> 7, of which waited for: 10 -> 5; matrix products, arithmetic and copies ran while one was open for 3% -> 1% of each run, Pallas kernels for 10% -> 14%
where the time goes in v2:
time: 538 us; the launch traced here: 536 us
  waiting for transfers between devices  402 us (75%)
  Pallas kernels  80.1 us (15%)
  starting transfers between devices  24 us (4%)
  between operations  14.2 us (3%)
  blocking collectives  11.2 us (2%)
    all_to_all x5, waiting for transfers between devices, exchange(): return lax.all_to_all(parts, 'ctx', split_axis=0, concat_axis=0, tiled=True)  339 us
    psum x1, waiting for transfers between devices, body(): sums = lax.psum(sums, 'ctx')  63 us
    pallas_call x3, Pallas kernels, mix(): pl.pallas_call(functools.partial(mix_kernel, tile=tile, tile_count=tile_c...  43.2 us
    pallas_call x3, Pallas kernels, split_channels(): pl.pallas_call(kernel, grid=(tiles, rows // step), in_specs=specs, out_sp...  25.6 us
    all_to_all x5, starting transfers between devices, exchange(): return lax.all_to_all(parts, 'ctx', split_axis=0, concat_axis=0, tiled=True)  23.9 us
    pallas_call x2, Pallas kernels, merge_channels(): pl.pallas_call(merge_kernel, grid=(tiles, rows // step), in_specs=specs,...  11.3 us
    all_gather x1, blocking collectives, body(): sums = lax.all_gather(sums, 'dp', axis=0, tiled=True)  11.2 us
  transfers between devices with their start and end apart: 7, of which 5 were waited for; matrix products, arithmetic and copies ran while one was open for 1% of the time, Pallas kernels for 14%

profile of v2, /device:TPU:0, one launch (start us, length us, event | category | flops | bytes accessed | tf_op | source)
XLA Modules:
  0.0 535.6 jit_solution(263816068612917365)
XLA Ops:
  7.2 0.7 copy-done.1
  7.9 5.3 shard_map.136
  13.2 6.3 %all-to-all-start.1 = ((bf16[8,35,32,128]{3,2,1,0:T(8,128)(2,1)}), bf16[8,35,32,128]{3,2,1,0:T(8,128)(2,1)S(1)}, u32[]{:S(2)}, u32[]{:S(2)}) async-start(bf16[8,35,32,128]{3,2,1,0:T(8,128)(2,1)} %shard_map.136), calls=%async_computation.1 | async-start | bytes 4587520 | tf_op jit(solution)/shard_map/all_to_all | solution.py:256
  19.5 14.9 %shard_map.137 = bf16[8,128,32,128]{3,2,1,0:T(8,128)(2,1)} custom-call(bf16[32,128,768]{2,1,0:T(8,128)(2,1)} %bitcast.21, bf16[32,128,768]{2,1,0:T(8,128)(2,1)} %bitcast.24), custom_call_target="tpu_custom_call" | custom-call | bytes 16777216 | tf_op jit(solution)/shard_map/pallas_call | solution.py:63
  34.4 38.4 %all-to-all-done.1.tok_ref.cot_ref = bf16[8,35,32,128]{3,2,1,0:T(8,128)(2,1)S(1)} async-done(((bf16[8,35,32,128]{3,2,1,0:T(8,128)(2,1)}), bf16[8,35,32,128]{3,2,1,0:T(8,128)(2,1)S(1)}, u32[]{:S(2)}, u32[]{:S(2)}) %all-to-all-start.1) | async-done | bytes 2293792 | tf_op jit(solution)/shard_map/all_to_all | solution.py:256
  72.8 5.0 all-to-all-start.2
  77.8 0.0 copy-start.5
  77.8 5.4 %shard_map.135 = bf16[8,32,32,128]{3,2,1,0:T(8,128)(2,1)} custom-call(bf16[32,128,768]{2,1,0:T(8,128)(2,1)} %bitcast.22, bf16[32,128,768]{2,1,0:T(8,128)(2,1)} %bitcast.25), custom_call_target="tpu_custom_call" | custom-call | bytes 4194304 | tf_op jit(solution)/shard_map/pallas_call | solution.py:63
  83.2 178.5 %all-to-all-done.2.tok_ref.cot_ref = bf16[8,128,32,128]{3,2,1,0:T(8,128)(2,1)} async-done(((bf16[8,128,32,128]{3,2,1,0:T(8,128)(2,1)}), bf16[8,128,32,128]{3,2,1,0:T(8,128)(2,1)}, u32[]{:S(2)}, u32[]{:S(2)}) %all-to-all-start.2) | async-done | bytes 8388640 | tf_op jit(solution)/shard_map/all_to_all | solution.py:256
  261.7 4.4 all-to-all-start
  266.1 0.1 copy.19
  266.2 0.1 copy.20
  266.5 7.0 %shard_map.138 = (bf16[8,80,32,128]{3,2,1,0:T(8,128)(2,1)}, f32[928,128]{1,0:T(8,128)S(1)}) custom-call(s32[1]{0:T(128)} %bitcast.place_ref, f32[768]{0:T(1024)S(1)} %copy-done.2, f32[768]{0:T(1024)S(1)} %copy-done.3, f32[768]{0:T(1024)S(1)} %copy-done.4, bf16[8,35,32,128]{3,2,1,0:T(8,128)(2,1)S(1)} %all-to-all-done.1.tok_ref.cot_ref, ...), custom_call_target="tpu_custom_call" | custom-call | flops 2415919104 | bytes 3145728 | tf_op jit(solution)/shard_map/pallas_call | solution.py:202
  273.4 28.1 %shard_map.139 = (bf16[8,80,32,128]{3,2,1,0:T(8,128)(2,1)}, f32[928,128]{1,0:T(8,128)S(1)}) custom-call(s32[1]{0:T(128)} %bitcast.place_ref, f32[768]{0:T(1024)S(1)} %copy-done.2, f32[768]{0:T(1024)S(1)} %copy-done.3, f32[768]{0:T(1024)S(1)} %copy-done.4, bf16[8,128,32,128]{3,2,1,0:T(8,128)(2,1)} %all-to-all-done.2.tok_ref.cot_ref, ...), custom_call_target="tpu_custom_call", output_to_operand_aliasing={{0}: (12, {})} | custom-call | flops 9663676416 | bytes 12582912 | tf_op jit(solution)/shard_map/pallas_call | solution.py:202
  301.6 13.6 %all-to-all-done.tok_ref.cot_ref = bf16[8,32,32,128]{3,2,1,0:T(8,128)(2,1)} async-done(((bf16[8,32,32,128]{3,2,1,0:T(8,128)(2,1)}), bf16[8,32,32,128]{3,2,1,0:T(8,128)(2,1)}, u32[]{:S(2)}, u32[]{:S(2)}) %all-to-all-start) | async-done | bytes 2097184 | tf_op jit(solution)/shard_map/all_to_all | solution.py:256
  315.1 4.7 all-to-all-start.4
  319.8 0.0 reduce-scatter.4.cloned.1.call-start
  319.9 8.1 %shard_map.140 = (bf16[8,16,32,128]{3,2,1,0:T(8,128)(2,1)}, f32[928,128]{1,0:T(8,128)}) custom-call(s32[1]{0:T(128)} %bitcast.place_ref, f32[768]{0:T(1024)S(1)} %copy-done.2, f32[768]{0:T(1024)S(1)} %copy-done.3, f32[768]{0:T(1024)S(1)} %copy-done.4, bf16[8,32,32,128]{3,2,1,0:T(8,128)(2,1)} %all-to-all-done.tok_ref.cot_ref, ...), custom_call_target="tpu_custom_call" | custom-call | flops 2415919104 | bytes 3145728 | tf_op jit(solution)/shard_map/pallas_call | solution.py:202
  328.0 0.0 reduce-scatter.4.cloned.1.call-update
  328.0 108.3 %all-to-all-done.4.part_ref = bf16[8,80,32,128]{3,2,1,0:T(8,128)(2,1)} async-done(((bf16[8,80,32,128]{3,2,1,0:T(8,128)(2,1)}), bf16[8,80,32,128]{3,2,1,0:T(8,128)(2,1)}, u32[]{:S(2)}, u32[]{:S(2)}) %all-to-all-start.4) | async-done | bytes 5242912 | tf_op jit(solution)/shard_map/all_to_all | solution.py:256
  436.3 3.6 all-to-all-start.3
  439.9 0.0 all-reduce.7.cloned.1.call-start
  439.9 0.0 reduce-scatter.4.cloned.1.call-done
  439.9 0.7 all-reduce.7.cloned.1.call-update
  440.6 63.0 %all-reduce.7.cloned.1.call-done = f32[232,128]{1,0:T(8,128)} async-done(((f32[232,128]{1,0:T(8,128)}), f32[232,128]{1,0:T(8,128)}) %all-reduce.7.cloned.1.call-update) | async-done | bytes 118800 | tf_op jit(solution)/shard_map/psum | solution.py:291
  503.6 11.2 %all_gather.3 = f32[928,128]{1,0:T(8,128)S(1)} all-gather(f32[232,128]{1,0:T(8,128)} %all-reduce.7.cloned.1.call-done), channel_id=1, replica_groups=mesh['dp'=4,'ctx'=8] {'dp'}, dimensions={0}, use_global_device_ids=true | all-gather | bytes 593920 | tf_op jit(solution)/shard_map/all_gather | solution.py:292
  514.9 0.6 dynamic-slice_multiply_fusion
  515.5 0.7 maximum_multiply_fusion
  516.2 0.6 fusion.6
  516.8 0.6 slice_multiply_fusion
  517.5 9.6 %shard_map.141.rest_0_ = bf16[32,128,768]{2,1,0:T(8,128)(2,1)} custom-call(bf16[8,80,32,128]{3,2,1,0:T(8,128)(2,1)} %all-to-all-done.4.part_ref), custom_call_target="tpu_custom_call" | custom-call | bytes 10485760 | tf_op jit(solution)/shard_map/pallas_call | solution.py:97
  527.1 1.7 shard_map.142
  (15 shorter events, 0.1 us)
Async XLA Ops:
  7.2 0.7 copy-start.1
  13.2 59.6 %all-to-all-start.1 = ((bf16[8,35,32,128]{3,2,1,0:T(8,128)(2,1)}), bf16[8,35,32,128]{3,2,1,0:T(8,128)(2,1)S(1)}, u32[]{:S(2)}, u32[]{:S(2)}) async-start(bf16[8,35,32,128]{3,2,1,0:T(8,128)(2,1)} %shard_map.136), calls=%async_computation.1 | async-start | bytes 4587520 | tf_op jit(solution)/shard_map/all_to_all | solution.py:256
  72.8 188.9 %all-to-all-start.2 = ((bf16[8,128,32,128]{3,2,1,0:T(8,128)(2,1)}), bf16[8,128,32,128]{3,2,1,0:T(8,128)(2,1)}, u32[]{:S(2)}, u32[]{:S(2)}) async-start(bf16[8,128,32,128]{3,2,1,0:T(8,128)(2,1)} %shard_map.137), calls=%async_computation.2 | async-start | bytes 16777216 | tf_op jit(solution)/shard_map/all_to_all | solution.py:256
  77.8 188.3 %copy-start = (bf16[256,256]{1,0:T(8,128)(2,1)S(1)}, bf16[256,256]{1,0:T(8,128)(2,1)}, u32[]{:S(2)}) copy-start(bf16[256,256]{1,0:T(8,128)(2,1)} %first_ref.5) | copy-start | bytes 393220
  77.8 188.4 %copy-start.5 = (bf16[128,128]{1,0:T(8,128)(2,1)S(1)}, bf16[128,128]{1,0:T(8,128)(2,1)}, u32[]{:S(2)}) copy-start(bf16[128,128]{1,0:T(8,128)(2,1)} %param.11) | copy-start | bytes 98308
  83.2 183.2 %copy-start.2 = (f32[768]{0:T(1024)S(1)}, f32[768]{0:T(1024)}, u32[]{:S(2)}) copy-start(f32[768]{0:T(1024)} %gain_ref.5) | copy-start | bytes 9220
  83.2 183.2 %copy-start.3 = (f32[768]{0:T(1024)S(1)}, f32[768]{0:T(1024)}, u32[]{:S(2)}) copy-start(f32[768]{0:T(1024)} %bias_ref.5) | copy-start | bytes 9220
  83.2 183.2 %copy-start.4 = (f32[768]{0:T(1024)S(1)}, f32[768]{0:T(1024)}, u32[]{:S(2)}) copy-start(f32[768]{0:T(1024)} %skip_ref.5) | copy-start | bytes 9220
  261.7 53.4 %all-to-all-start = ((bf16[8,32,32,128]{3,2,1,0:T(8,128)(2,1)}), bf16[8,32,32,128]{3,2,1,0:T(8,128)(2,1)}, u32[]{:S(2)}, u32[]{:S(2)}) async-start(bf16[8,32,32,128]{3,2,1,0:T(8,128)(2,1)} %shard_map.135), calls=%async_computation | async-start | bytes 4194304 | tf_op jit(solution)/shard_map/all_to_all | solution.py:256
  315.1 121.2 %all-to-all-start.4 = ((bf16[8,80,32,128]{3,2,1,0:T(8,128)(2,1)}), bf16[8,80,32,128]{3,2,1,0:T(8,128)(2,1)}, u32[]{:S(2)}, u32[]{:S(2)}) async-start(bf16[8,80,32,128]{3,2,1,0:T(8,128)(2,1)} %get-tuple-element.17), calls=%async_computation.4 | async-start | bytes 10485760 | tf_op jit(solution)/shard_map/all_to_all | solution.py:256
  319.8 120.1 %reduce-scatter.4.cloned.1.call-start = ((), (), s32[]{:S(2)}) async-start(), calls=%async_computation.7 | async-start | bytes 593920
  436.3 90.8 %all-to-all-start.3 = ((bf16[8,16,32,128]{3,2,1,0:T(8,128)(2,1)}), bf16[8,16,32,128]{3,2,1,0:T(8,128)(2,1)S(1)}, u32[]{:S(2)}, u32[]{:S(2)}) async-start(bf16[8,16,32,128]{3,2,1,0:T(8,128)(2,1)} %get-tuple-element.16), calls=%async_computation.3 | async-start | bytes 2097152 | tf_op jit(solution)/shard_map/all_to_all | solution.py:256
  439.9 63.8 %all-reduce.7.cloned.1.call-start = ((), (), s32[]{:S(2)}) async-start(), calls=%async_computation.6 | async-start | bytes 237568 | tf_op jit(solution)/shard_map/psum | solution.py:291
Sparse Core Ops, SparseCore 0:
  328.2 25.6 reduce-scatter.3
  443.0 60.5 all-reduce.6

commit v3 on v2

--- a/solution.py
+++ b/solution.py
@@ -287,8 +287,11 @@
         grads.append(held.reshape(tok_rows, width))
     grad_tokens = jnp.stack(grads)
 
-    sums = lax.psum_scatter(sums, "dp", scatter_dimension=0, tiled=True)
-    sums = lax.psum(sums, "ctx")
+    own_rows = sum_rows // dp_size
+    sums = lax.dynamic_slice_in_dim(
+        lax.all_gather(sums, "dp"), lax.axis_index("dp") * own_rows, own_rows, 1
+    )
+    sums = jnp.sum(lax.all_gather(jnp.sum(sums, axis=0), "ctx"), axis=0)
     sums = lax.all_gather(sums, "dp", axis=0, tiled=True)
     total_seqs = seq_count * dp_size
     first_norm = math.sqrt(total_seqs * B * width)

time: 538 us -> 509 us (0.946)
  waiting for transfers between devices: 402 us -> 339 us
  blocking collectives: 11.2 us -> 45.6 us
    psum x1 -> x0, waiting for transfers between devices: 63 us -> none  [body(): sums = lax.psum(sums, 'ctx')]
    all_gather x0 -> x1, blocking collectives: none -> 35.5 us  [body(): sums = jnp.sum(lax.all_gather(jnp.sum(sums, axis=0), 'ctx'), axis=0)]
  transfers between devices with their start and end apart: 7 -> 6, of which waited for: 5 -> 4; matrix products, arithmetic and copies ran while one was open for 1% -> 1% of each run, Pallas kernels for 14% -> 14%
where the time goes in v3:
time: 509 us; the launch traced here: 507 us
  waiting for transfers between devices  339 us (67%)
  Pallas kernels  80.1 us (16%)
  blocking collectives  45.6 us (9%)
  starting transfers between devices  23.9 us (5%)
  between operations  14.2 us (3%)
    all_to_all x5, waiting for transfers between devices, exchange(): return lax.all_to_all(parts, 'ctx', split_axis=0, concat_axis=0, tiled=True)  339 us
    pallas_call x3, Pallas kernels, mix(): pl.pallas_call(functools.partial(mix_kernel, tile=tile, tile_count=tile_c...  43.2 us
    all_gather x1, blocking collectives, body(): sums = jnp.sum(lax.all_gather(jnp.sum(sums, axis=0), 'ctx'), axis=0)  35.5 us
    pallas_call x3, Pallas kernels, split_channels(): pl.pallas_call(kernel, grid=(tiles, rows // step), in_specs=specs, out_sp...  25.6 us
    all_to_all x5, starting transfers between devices, exchange(): return lax.all_to_all(parts, 'ctx', split_axis=0, concat_axis=0, tiled=True)  23.8 us
    pallas_call x2, Pallas kernels, merge_channels(): pl.pallas_call(merge_kernel, grid=(tiles, rows // step), in_specs=specs,...  11.3 us
  transfers between devices with their start and end apart: 6, of which 4 were waited for; matrix products, arithmetic and copies ran while one was open for 1% of the time, Pallas kernels for 14%

profile of v3, /device:TPU:0, one launch (start us, length us, event | category | flops | bytes accessed | tf_op | source)
XLA Modules:
  0.0 507.3 jit_solution(10807791634432729583)
XLA Ops:
  7.2 0.7 copy-done.1
  7.9 5.3 %shard_map.136 = bf16[8,35,32,128]{3,2,1,0:T(8,128)(2,1)} custom-call(bf16[32,128,768]{2,1,0:T(8,128)(2,1)} %bitcast.21, bf16[32,128,768]{2,1,0:T(8,128)(2,1)} %bitcast.24, f32[32,128]{1,0:T(8,128)S(1)} %copy-done.1), custom_call_target="tpu_custom_call" | custom-call | bytes 4194304 | tf_op jit(solution)/shard_map/pallas_call | solution.py:63
  13.2 6.3 %all-to-all-start.1 = ((bf16[8,35,32,128]{3,2,1,0:T(8,128)(2,1)}), bf16[8,35,32,128]{3,2,1,0:T(8,128)(2,1)S(1)}, u32[]{:S(2)}, u32[]{:S(2)}) async-start(bf16[8,35,32,128]{3,2,1,0:T(8,128)(2,1)} %shard_map.136), calls=%async_computation.1 | async-start | bytes 4587520 | tf_op jit(solution)/shard_map/all_to_all | solution.py:256
  19.5 14.8 %shard_map.137 = bf16[8,128,32,128]{3,2,1,0:T(8,128)(2,1)} custom-call(bf16[32,128,768]{2,1,0:T(8,128)(2,1)} %bitcast.22, bf16[32,128,768]{2,1,0:T(8,128)(2,1)} %bitcast.25), custom_call_target="tpu_custom_call" | custom-call | bytes 16777216 | tf_op jit(solution)/shard_map/pallas_call | solution.py:63
  34.4 38.4 %all-to-all-done.1.tok_ref.cot_ref = bf16[8,35,32,128]{3,2,1,0:T(8,128)(2,1)S(1)} async-done(((bf16[8,35,32,128]{3,2,1,0:T(8,128)(2,1)}), bf16[8,35,32,128]{3,2,1,0:T(8,128)(2,1)S(1)}, u32[]{:S(2)}, u32[]{:S(2)}) %all-to-all-start.1) | async-done | bytes 2293792 | tf_op jit(solution)/shard_map/all_to_all | solution.py:256
  72.8 5.0 all-to-all-start.2
  77.8 0.0 copy-start
  77.8 0.0 copy-start.5
  77.8 5.4 %shard_map.135 = bf16[8,32,32,128]{3,2,1,0:T(8,128)(2,1)} custom-call(bf16[32,128,768]{2,1,0:T(8,128)(2,1)} %bitcast.23, bf16[32,128,768]{2,1,0:T(8,128)(2,1)} %bitcast.26), custom_call_target="tpu_custom_call" | custom-call | bytes 4194304 | tf_op jit(solution)/shard_map/pallas_call | solution.py:63
  83.2 178.5 %all-to-all-done.2.tok_ref.cot_ref = bf16[8,128,32,128]{3,2,1,0:T(8,128)(2,1)} async-done(((bf16[8,128,32,128]{3,2,1,0:T(8,128)(2,1)}), bf16[8,128,32,128]{3,2,1,0:T(8,128)(2,1)}, u32[]{:S(2)}, u32[]{:S(2)}) %all-to-all-start.2) | async-done | bytes 8388640 | tf_op jit(solution)/shard_map/all_to_all | solution.py:256
  261.7 4.4 all-to-all-start
  266.0 0.1 copy.19
  266.2 0.1 copy.20
  266.4 7.0 %shard_map.138 = (bf16[8,80,32,128]{3,2,1,0:T(8,128)(2,1)}, f32[928,128]{1,0:T(8,128)S(1)}) custom-call(s32[1]{0:T(128)} %bitcast.place_ref, f32[768]{0:T(1024)S(1)} %copy-done.2, f32[768]{0:T(1024)S(1)} %copy-done.3, f32[768]{0:T(1024)S(1)} %copy-done.4, bf16[8,35,32,128]{3,2,1,0:T(8,128)(2,1)S(1)} %all-to-all-done.1.tok_ref.cot_ref, ...), custom_call_target="tpu_custom_call" | custom-call | flops 2415919104 | bytes 3145728 | tf_op jit(solution)/shard_map/pallas_call | solution.py:202
  273.4 28.1 %shard_map.139 = (bf16[8,80,32,128]{3,2,1,0:T(8,128)(2,1)}, f32[928,128]{1,0:T(8,128)S(1)}) custom-call(s32[1]{0:T(128)} %bitcast.place_ref, f32[768]{0:T(1024)S(1)} %copy-done.2, f32[768]{0:T(1024)S(1)} %copy-done.3, f32[768]{0:T(1024)S(1)} %copy-done.4, bf16[8,128,32,128]{3,2,1,0:T(8,128)(2,1)} %all-to-all-done.2.tok_ref.cot_ref, ...), custom_call_target="tpu_custom_call", output_to_operand_aliasing={{0}: (12, {})} | custom-call | flops 9663676416 | bytes 12582912 | tf_op jit(solution)/shard_map/pallas_call | solution.py:202
  301.5 13.6 %all-to-all-done.tok_ref.cot_ref = bf16[8,32,32,128]{3,2,1,0:T(8,128)(2,1)} async-done(((bf16[8,32,32,128]{3,2,1,0:T(8,128)(2,1)}), bf16[8,32,32,128]{3,2,1,0:T(8,128)(2,1)}, u32[]{:S(2)}, u32[]{:S(2)}) %all-to-all-start) | async-done | bytes 2097184 | tf_op jit(solution)/shard_map/all_to_all | solution.py:256
  315.1 4.7 all-to-all-start.4
  319.8 0.0 all-gather.4.cloned.1.call-start
  319.8 8.1 %shard_map.140 = (bf16[8,16,32,128]{3,2,1,0:T(8,128)(2,1)}, f32[928,128]{1,0:T(8,128)}) custom-call(s32[1]{0:T(128)} %bitcast.place_ref, f32[768]{0:T(1024)S(1)} %copy-done.2, f32[768]{0:T(1024)S(1)} %copy-done.3, f32[768]{0:T(1024)S(1)} %copy-done.4, bf16[8,32,32,128]{3,2,1,0:T(8,128)(2,1)} %all-to-all-done.tok_ref.cot_ref, ...), custom_call_target="tpu_custom_call" | custom-call | flops 2415919104 | bytes 3145728 | tf_op jit(solution)/shard_map/pallas_call | solution.py:202
  327.9 0.0 all-gather.4.cloned.1.call-update
  328.0 108.3 %all-to-all-done.4.part_ref = bf16[8,80,32,128]{3,2,1,0:T(8,128)(2,1)} async-done(((bf16[8,80,32,128]{3,2,1,0:T(8,128)(2,1)}), bf16[8,80,32,128]{3,2,1,0:T(8,128)(2,1)}, u32[]{:S(2)}, u32[]{:S(2)}) %all-to-all-start.4) | async-done | bytes 5242912 | tf_op jit(solution)/shard_map/all_to_all | solution.py:256
  436.2 3.6 all-to-all-start.3
  439.8 0.0 all-gather.4.cloned.1.call-done
  439.8 1.1 dynamic-slice_reduce_fusion
  440.9 35.5 %all-gather.1 = f32[1856,128]{1,0:T(8,128)S(1)} all-gather(f32[232,128]{1,0:T(8,128)S(1)} %dynamic-slice_reduce_fusion), channel_id=3, replica_groups=mesh['dp'=4,'ctx'=8] {'ctx'}, dimensions={0}, use_global_device_ids=true | all-gather | bytes 1069056 | tf_op jit(solution)/shard_map/all_gather | solution.py:294
  476.5 10.1 %all_gather.19 = f32[928,128]{1,0:T(8,128)S(1)} all-gather(f32[232,128]{1,0:T(8,128)S(1)} %reduce_sum.19), channel_id=1, replica_groups=mesh['dp'=4,'ctx'=8] {'dp'}, dimensions={0}, use_global_device_ids=true | all-gather | bytes 593920 | tf_op jit(solution)/shard_map/all_gather | solution.py:295
  486.6 0.6 dynamic-slice_multiply_fusion
  487.2 0.7 maximum_multiply_fusion
  488.0 0.6 fusion.6
  488.6 0.6 slice_multiply_fusion
  489.2 9.6 %shard_map.141.rest_0_ = bf16[32,128,768]{2,1,0:T(8,128)(2,1)} custom-call(bf16[8,80,32,128]{3,2,1,0:T(8,128)(2,1)} %all-to-all-done.4.part_ref), custom_call_target="tpu_custom_call" | custom-call | bytes 10485760 | tf_op jit(solution)/shard_map/pallas_call | solution.py:97
  498.8 1.7 shard_map.142
  (15 shorter events, 0.2 us)
Async XLA Ops:
  7.2 0.7 copy-start.1
  13.2 59.6 %all-to-all-start.1 = ((bf16[8,35,32,128]{3,2,1,0:T(8,128)(2,1)}), bf16[8,35,32,128]{3,2,1,0:T(8,128)(2,1)S(1)}, u32[]{:S(2)}, u32[]{:S(2)}) async-start(bf16[8,35,32,128]{3,2,1,0:T(8,128)(2,1)} %shard_map.136), calls=%async_computation.1 | async-start | bytes 4587520 | tf_op jit(solution)/shard_map/all_to_all | solution.py:256
  72.8 188.8 %all-to-all-start.2 = ((bf16[8,128,32,128]{3,2,1,0:T(8,128)(2,1)}), bf16[8,128,32,128]{3,2,1,0:T(8,128)(2,1)}, u32[]{:S(2)}, u32[]{:S(2)}) async-start(bf16[8,128,32,128]{3,2,1,0:T(8,128)(2,1)} %shard_map.137), calls=%async_computation.2 | async-start | bytes 16777216 | tf_op jit(solution)/shard_map/all_to_all | solution.py:256
  77.8 188.3 %copy-start = (bf16[256,256]{1,0:T(8,128)(2,1)S(1)}, bf16[256,256]{1,0:T(8,128)(2,1)}, u32[]{:S(2)}) copy-start(bf16[256,256]{1,0:T(8,128)(2,1)} %first_ref.5) | copy-start | bytes 393220
  77.8 188.4 %copy-start.5 = (bf16[128,128]{1,0:T(8,128)(2,1)S(1)}, bf16[128,128]{1,0:T(8,128)(2,1)}, u32[]{:S(2)}) copy-start(bf16[128,128]{1,0:T(8,128)(2,1)} %param.11) | copy-start | bytes 98308
  83.2 183.2 %copy-start.2 = (f32[768]{0:T(1024)S(1)}, f32[768]{0:T(1024)}, u32[]{:S(2)}) copy-start(f32[768]{0:T(1024)} %gain_ref.5) | copy-start | bytes 9220
  83.2 183.2 %copy-start.3 = (f32[768]{0:T(1024)S(1)}, f32[768]{0:T(1024)}, u32[]{:S(2)}) copy-start(f32[768]{0:T(1024)} %bias_ref.5) | copy-start | bytes 9220
  83.2 183.2 %copy-start.4 = (f32[768]{0:T(1024)S(1)}, f32[768]{0:T(1024)}, u32[]{:S(2)}) copy-start(f32[768]{0:T(1024)} %skip_ref.5) | copy-start | bytes 9220
  261.7 53.4 %all-to-all-start = ((bf16[8,32,32,128]{3,2,1,0:T(8,128)(2,1)}), bf16[8,32,32,128]{3,2,1,0:T(8,128)(2,1)}, u32[]{:S(2)}, u32[]{:S(2)}) async-start(bf16[8,32,32,128]{3,2,1,0:T(8,128)(2,1)} %shard_map.135), calls=%async_computation | async-start | bytes 4194304 | tf_op jit(solution)/shard_map/all_to_all | solution.py:256
  315.1 121.1 %all-to-all-start.4 = ((bf16[8,80,32,128]{3,2,1,0:T(8,128)(2,1)}), bf16[8,80,32,128]{3,2,1,0:T(8,128)(2,1)}, u32[]{:S(2)}, u32[]{:S(2)}) async-start(bf16[8,80,32,128]{3,2,1,0:T(8,128)(2,1)} %get-tuple-element.17), calls=%async_computation.4 | async-start | bytes 10485760 | tf_op jit(solution)/shard_map/all_to_all | solution.py:256
  319.8 120.1 %all-gather.4.cloned.1.call-start = ((), (), s32[]{:S(2)}) async-start(), calls=%async_computation.5 | async-start | bytes 2375680 | tf_op jit(solution)/shard_map/all_gather | solution.py:292
  436.2 62.5 %all-to-all-start.3 = ((bf16[8,16,32,128]{3,2,1,0:T(8,128)(2,1)}), bf16[8,16,32,128]{3,2,1,0:T(8,128)(2,1)S(1)}, u32[]{:S(2)}, u32[]{:S(2)}) async-start(bf16[8,16,32,128]{3,2,1,0:T(8,128)(2,1)} %get-tuple-element.16), calls=%async_computation.3 | async-start | bytes 2097152 | tf_op jit(solution)/shard_map/all_to_all | solution.py:256
Sparse Core Ops, SparseCore 0:
  328.1 34.9 all-gather.3

commit v4 on v2

v4 whole, which is shorter than its diff:
```python
import functools
import math

import jax
import jax.numpy as jnp
from jax import lax
from jax.experimental import pallas as pl
from jax.experimental.pallas import tpu as pltpu
from jax.sharding import PartitionSpec as P

A = 256
B = 128
LANES = 128
VMEM_BYTES = 48 * 1024 * 1024


def dot(left, right, left_dim, right_dim):
    return lax.dot_general(
        left, right, (((left_dim,), (right_dim,)), ((), ())), preferred_element_type=jnp.float32
    )


def split_tile(first_channel, tok_ref, cot_ref, out_refs, swap_ref):
    rows = tok_ref.shape[0]
    share = LANES // len(out_refs)
    for which, ref in enumerate((tok_ref, cot_ref)):
        for row in range(rows):
            swap_ref[row * LANES : (row + 1) * LANES, :] = ref[row].astype(jnp.float32).T
        for shift, out_ref in enumerate(out_refs):
            start = (first_channel + shift * share) % LANES
            for channel in range(share):
                out_ref[which * share + channel] = swap_ref[
                    pl.ds(start + channel, rows, stride=LANES), :
                ].astype(jnp.bfloat16)


def split_kernel(place_ref, tok_ref, cot_ref, *rest):
    split_tile(place_ref[0], tok_ref, cot_ref, rest[:-1], rest[-1])


def split_twiddle_kernel(place_ref, tok_ref, cot_ref, twiddle_ref, *rest):
    out_refs = rest[:-1]
    split_tile(place_ref[0], tok_ref, cot_ref, out_refs, rest[-1])
    share = LANES // len(out_refs)
    left = twiddle_ref[...]
    for plane in range(3):
        part = left.astype(jnp.bfloat16)
        left = left - part.astype(jnp.float32)
        for out_ref in out_refs:
            out_ref[2 * share + plane] = part


def split_channels(place, tokens, cotangent, tile, tiles, ctx_size, twiddle=None):
    rows = tokens.shape[0]
    step = min(16, rows)
    share = LANES // ctx_size
    block = pl.BlockSpec((step, B, LANES), lambda t, i: (i, 0, tile + t))
    specs = [pl.BlockSpec(memory_space=pltpu.SMEM), block, block]
    if twiddle is None:
        kernel, given = split_kernel, [place, tokens, cotangent]
        planes = 2 * share
    else:
        kernel, given = split_twiddle_kernel, [place, tokens, cotangent, twiddle]
        specs.append(pl.BlockSpec((step, B), lambda t, i: (i, 0)))
        planes = 2 * share + 3
    return pl.pallas_call(
        kernel,
        grid=(tiles, rows // step),
        in_specs=specs,
        out_specs=[pl.BlockSpec((planes, step, B), lambda t, i: (t, i, 0))] * ctx_size,
        out_shape=[jax.ShapeDtypeStruct((tiles * planes, rows, B), jnp.bfloat16)] * ctx_size,
        scratch_shapes=[pltpu.VMEM((step * LANES, B), jnp.float32)],
        compiler_params=pltpu.CompilerParams(vmem_limit_bytes=VMEM_BYTES),
        cost_estimate=pl.CostEstimate(
            flops=0, bytes_accessed=8 * rows * B * LANES * tiles, transcendentals=0
        ),
    )(*given)


def merge_kernel(devices, place_ref, *rest):
    part_refs, out_ref, swap_ref = rest[:devices], rest[-2], rest[-1]
    share, rows, _ = part_refs[0].shape
    for shift, part_ref in enumerate(part_refs):
        start = (place_ref[0] + shift * share) % LANES
        for channel in range(share):
            at = pl.multiple_of((start + channel) * rows, rows)
            swap_ref[pl.ds(at, rows), :] = part_ref[channel].astype(jnp.float32)
    for row in range(rows):
        out_ref[row] = swap_ref[pl.ds(row, LANES, stride=rows), :].T.astype(jnp.bfloat16)


def merge_channels(place, parts, held, tile, width):
    devices = len(parts)
    channels, rows, _ = parts[0].shape
    step = min(16, rows)
    share = LANES // devices
    tiles = channels // share
    given = [place, *parts]
    specs = [pl.BlockSpec(memory_space=pltpu.SMEM)]
    specs += [pl.BlockSpec((share, step, B), lambda t, i: (t, i, 0))] * devices
    if held is not None:
        given.append(held)
        specs.append(pl.BlockSpec(memory_space=pl.ANY))
    return pl.pallas_call(
        functools.partial(merge_kernel, devices),
        grid=(tiles, rows // step),
        in_specs=specs,
        out_specs=pl.BlockSpec((step, B, LANES), lambda t, i: (i, 0, tile + t)),
        out_shape=jax.ShapeDtypeStruct((rows, B, width), jnp.bfloat16),
        scratch_shapes=[pltpu.VMEM((step * LANES, B), jnp.float32)],
        input_output_aliases={} if held is None else {devices + 1: 0},
        compiler_params=pltpu.CompilerParams(vmem_limit_bytes=VMEM_BYTES),
        cost_estimate=pl.CostEstimate(
            flops=0, bytes_accessed=4 * rows * B * LANES * tiles, transcendentals=0
        ),
    )(*given)


SECOND_AT = 2 * A
TWIDDLE_AT = SECOND_AT + B
CHANNEL_AT = TWIDDLE_AT + A


def mix_kernel(
    place_ref, gain_ref, bias_ref, skip_ref, *rest, devices, tile, tile_count, has_sums
):
    tok_refs, cot_refs, rest = rest[:devices], rest[devices : 2 * devices], rest[2 * devices :]
    first_ref, first_t_ref, second_ref, second_t_ref, twiddle_ref, *rest = rest
    out_refs, (sums_ref, tok_all, cot_all) = rest[-3 - devices : -3], rest[-3:]
    t, step = pl.program_id(0), pl.program_id(1)

    @pl.when((t == 0) & (step == 0))
    def _():
        sums_ref[...] = rest[0][...] if has_sums else jnp.zeros(sums_ref.shape, jnp.float32)

    pair, rows, _ = tok_refs[0].shape
    share = LANES // devices
    lane_at = place_ref[0] + step * pair
    at = (tile + t) * LANES + lane_at

    def rows_from(shift):
        source = (place_ref[0] // share - shift + devices) % devices
        return pl.ds(pl.multiple_of(source * rows, rows), rows)

    for refs, whole in ((tok_refs, tok_all), (cot_refs, cot_all)):
        for shift, ref in enumerate(refs):
            for c in range(pair):
                whole[rows_from(shift), c * B : (c + 1) * B] = ref[c].astype(jnp.float32)

    def spread(ref):
        lane = lax.broadcasted_iota(jnp.int32, (1, pair * B), 1)
        row = jnp.full((1, pair * B), ref[at], jnp.float32)
        for c in range(1, pair):
            row = jnp.where(lane >= c * B, ref[at + c], row)
        return row

    gain, bias, skip = spread(gain_ref), spread(bias_ref), spread(skip_ref)
    inputs = tok_all[...]
    tok = inputs.astype(jnp.bfloat16)
    upstream = cot_all[...]
    twiddle = jnp.concatenate([twiddle_ref[...]] * pair, axis=1)
    inner = dot(tok, second_t_ref[...], 1, 0)
    scaled = (inner * twiddle).astype(jnp.bfloat16)
    gate = jax.nn.sigmoid(gain * inputs + bias)
    grad_hidden = upstream * gate
    grad_outer = grad_hidden.astype(jnp.bfloat16)
    outer = dot(first_ref[...], scaled, 1, 0).astype(jnp.bfloat16).astype(jnp.float32)
    grad_scaled = dot(first_t_ref[...], grad_outer, 1, 0).astype(jnp.bfloat16).astype(jnp.float32)
    first_term = dot(grad_outer, scaled, 1, 1)
    for half in range(A // B):
        sums_ref[half * A : (half + 1) * A] += first_term[:, half * B : (half + 1) * B]
    hidden = outer + skip * inputs
    grad_pre = upstream * hidden * gate * (1.0 - gate)
    product = grad_scaled * inner
    sums_ref[TWIDDLE_AT:CHANNEL_AT] += sum(product[:, c * B : (c + 1) * B] for c in range(pair))
    grad_inner = (grad_scaled * twiddle).astype(jnp.bfloat16)
    second_term = dot(grad_inner, tok, 0, 0)
    sums_ref[SECOND_AT:TWIDDLE_AT] += sum(
        second_term[c * B : (c + 1) * B, c * B : (c + 1) * B] for c in range(pair)
    )
    lane = lax.broadcasted_iota(jnp.int32, (1, LANES), 1)
    for which, value in enumerate((grad_pre * inputs, grad_pre, grad_hidden * inputs)):
        total = jnp.sum(value, axis=0, keepdims=True)
        row = jnp.zeros((1, LANES), jnp.float32)
        for c in range(pair):
            channel = jnp.sum(total[:, c * B : (c + 1) * B], axis=1, keepdims=True)
            row = jnp.where(lane == lane_at + c, channel, row)
        sums_ref[pl.ds(CHANNEL_AT + which * tile_count + tile + t, 1), :] += row
    grad_in = dot(grad_inner, second_ref[...], 1, 0)
    tok_all[...] = grad_in + grad_hidden * skip + grad_pre * gain
    for shift, out_ref in enumerate(out_refs):
        for c in range(pair):
            out_ref[c] = tok_all[rows_from(shift), c * B : (c + 1) * B].astype(jnp.bfloat16)


def mix(parts, tile, tiles, planes, place, vectors, factors, sums, sum_rows, out_tiles, out_at, held):
    devices = len(parts)
    rows = parts[0].shape[1]
    share = LANES // devices
    pair = factors[2].shape[0] // B
    steps = share // pair
    whole = lambda array: pl.BlockSpec(array.shape, lambda t, i: (0,) * array.ndim)
    tok_at = lambda t, i: (t * (planes // pair) + i, 0, 0)
    cot_at = lambda t, i: (t * (planes // pair) + steps + i, 0, 0)
    block = (pair, rows, B)
    given = [place, *vectors, *parts, *parts, *factors]
    specs = [pl.BlockSpec(memory_space=pltpu.SMEM)] * 4
    specs += [pl.BlockSpec(block, tok_at)] * devices + [pl.BlockSpec(block, cot_at)] * devices
    specs += [whole(f) for f in factors]
    aliases = {}
    if sums is not None:
        given.append(sums)
        specs.append(whole(sums))
    if held is not None:
        for shift, array in enumerate(held):
            aliases[len(given)] = shift
            given.append(array)
            specs.append(pl.BlockSpec(memory_space=pl.ANY))
    tile_count = vectors[0].shape[0] // LANES
    *leaving, sums = pl.pallas_call(
        functools.partial(
            mix_kernel, devices=devices, tile=tile, tile_count=tile_count,
            has_sums=sums is not None,
        ),
        grid=(tiles, steps),
        in_specs=specs,
        out_specs=[pl.BlockSpec(block, lambda t, i: ((out_at + t) * steps + i, 0, 0))] * devices
        + [pl.BlockSpec((sum_rows, LANES), lambda t, i: (0, 0))],
        out_shape=[jax.ShapeDtypeStruct((out_tiles * share, rows, B), jnp.bfloat16)] * devices
        + [jax.ShapeDtypeStruct((sum_rows, LANES), jnp.float32)],
        scratch_shapes=[pltpu.VMEM((A, pair * B), jnp.float32)] * 2,
        input_output_aliases=aliases,
        compiler_params=pltpu.CompilerParams(vmem_limit_bytes=VMEM_BYTES),
        cost_estimate=pl.CostEstimate(
            flops=tiles * share * A * B * 2 * 2304,
            bytes_accessed=tiles * share * A * B * 6,
            transcendentals=tiles * share * A * B * 2,
        ),
    )(*given)
    return leaving, sums


def block_diagonal(square, count):
    zero = jnp.zeros_like(square)
    return jnp.concatenate(
        [
            jnp.concatenate([square if i == j else zero for j in range(count)], axis=1)
            for i in range(count)
        ],
        axis=0,
    )


def body(tokens, cotangent, first_factor, second_factor, twiddle, gate_gain, gate_bias, skip_gain):
    seq_count, tok_rows, width = tokens.shape
    ctx_size = lax.axis_size("ctx")
    dp_size = lax.axis_size("dp")
    share = LANES // ctx_size
    local_rows = tok_rows // B
    tiles = width // LANES
    pair = 2
    sent = [1, tiles - 2, 1]
    returned = [tiles - 1, 1]

    place = (lax.axis_index("ctx") * share).astype(jnp.int32).reshape(1)
    second = block_diagonal(second_factor, pair)
    second_t = block_diagonal(second_factor.T, pair)
    vectors = [gate_gain, gate_bias, skip_gain]
    used_rows = CHANNEL_AT + 3 * tiles
    sum_rows = -(-used_rows // (8 * dp_size)) * 8 * dp_size

    def exchange(parts, sign):
        moved = [parts[0]]
        for shift in range(1, ctx_size):
            pairs = [(i, (i + sign * shift) % ctx_size) for i in range(ctx_size)]
            moved.append(lax.ppermute(parts[shift], "ctx", pairs))
        return moved

    sums = None
    factors = None
    grads = []
    for seq in range(seq_count):
        tok_blocks = tokens[seq].reshape(local_rows, B, width)
        cot_blocks = cotangent[seq].reshape(local_rows, B, width)
        arrived = []
        at = 0
        for count in sent:
            own = twiddle if at == 0 else None
            parts = split_channels(place, tok_blocks, cot_blocks, at, count, ctx_size, own)
            arrived.append((at, count, exchange(parts, 1)))
            at += count
        planes = jnp.stack([part[2 * share :] for part in arrived[0][2]]).astype(jnp.float32)
        planes = (planes[:, 0] + planes[:, 1] + planes[:, 2]).reshape(A, B)
        planes = planes.reshape(ctx_size, local_rows, B)[::-1]
        planes = jnp.concatenate([planes, planes], axis=0)
        turn = ctx_size - 1 - lax.axis_index("ctx")
        twiddle_all = lax.dynamic_slice_in_dim(planes, turn, ctx_size, 0).reshape(A, B)
        factors = [first_factor, first_factor.T, second, second_t, twiddle_all]
        leaving = [None] * len(returned)
        for at, count, parts in arrived:
            back = 0 if at < returned[0] else 1
            out_at = at - back * returned[0]
            leaving[back], sums = mix(
                parts, at, count, 2 * share, place, vectors, factors, sums, sum_rows,
                returned[back], out_at, leaving[back],
            )
        held = None
        at = 0
        for count, grad_parts in zip(returned, leaving):
            held = merge_channels(place, exchange(grad_parts, -1), held, at, width)
            at += count
        grads.append(held.reshape(tok_rows, width))
    grad_tokens = jnp.stack(grads)

    own_rows = sum_rows // dp_size
    bit = 1
    while bit < dp_size:
        sums = sums + lax.ppermute(sums, "dp", [(i, i ^ bit) for i in range(dp_size)])
        bit *= 2
    sums = lax.dynamic_slice_in_dim(sums, lax.axis_index("dp") * own_rows, own_rows, 0)
    sums = jnp.sum(lax.all_gather(sums, "ctx"), axis=0)
    sums = lax.all_gather(sums, "dp", axis=0, tiled=True)
    total_seqs = seq_count * dp_size
    first_norm = math.sqrt(total_seqs * B * width)
    second_norm = math.sqrt(total_seqs * A * width)
    twiddle_norm = math.sqrt(total_seqs * width)
    channel_norm = math.sqrt(total_seqs * A * B)
    first_sum = jnp.concatenate([sums[half * A : (half + 1) * A] for half in range(A // B)], axis=1)
    mine = TWIDDLE_AT + lax.axis_index("ctx") * local_rows
    twiddle_sum = lax.dynamic_slice_in_dim(sums, mine, local_rows, 0)
    channel_sum = sums[CHANNEL_AT:used_rows].reshape(3, width)
    return (
        grad_tokens,
        first_sum / first_norm,
        sums[SECOND_AT:TWIDDLE_AT] / second_norm,
        twiddle_sum / twiddle_norm,
        channel_sum[0] / channel_norm,
        channel_sum[1] / channel_norm,
        channel_sum[2] / channel_norm,
    )


def solution(mesh):
    return jax.shard_map(
        body,
        mesh=mesh,
        in_specs=(
            P("dp", "ctx", None),
            P("dp", "ctx", None),
            P(),
            P(),
            P("ctx", None),
            P(),
            P(),
            P(),
        ),
        out_specs=(P("dp", "ctx", None), P(), P(), P("ctx", None), P(), P(), P()),
        check_vma=False,
    )
```

time: 538 us -> 505 us (0.939)
  waiting for transfers between devices: 402 us -> 174 us
  starting transfers between devices: 24 us -> 194 us
  local copies, waits for them, and re-layouts: 0.96 us -> 25.3 us
  blocking collectives: 11.2 us -> 27.3 us
  between operations: 14.2 us -> 0.99 us
    all_to_all x5 -> x0, waiting for transfers between devices: 339 us -> none  [exchange(): return lax.all_to_all(parts, 'ctx', split_axis=0, concat_axis=0, tiled=True)]
    ppermute x0 -> x37, starting transfers between devices: none -> 194 us  [the longest x35 191 us: exchange(): moved.append(lax.ppermute(parts[shift], 'ctx', pairs))]
    ppermute x0 -> x37, waiting for transfers between devices: none -> 174 us  [the longest x35 174 us: exchange(): moved.append(lax.ppermute(parts[shift], 'ctx', pairs))]
    psum x1 -> x0, waiting for transfers between devices: 63 us -> none  [body(): sums = lax.psum(sums, 'ctx')]
    all_to_all x5 -> x0, starting transfers between devices: 23.9 us -> none  [exchange(): return lax.all_to_all(parts, 'ctx', split_axis=0, concat_axis=0, tiled=True)]
    unnamed x14 -> x101, local copies, waits for them, and re-layouts: 0.94 us -> 24.6 us
    all_gather x0 -> x1, blocking collectives: none -> 17.1 us  [body(): sums = jnp.sum(lax.all_gather(sums, 'ctx'), axis=0)]
  transfers between devices with their start and end apart: 7 -> 37, of which waited for: 5 -> 11; matrix products, arithmetic and copies ran while one was open for 1% -> 1% of each run, Pallas kernels for 14% -> 14%
where the time goes in v4:
time: 505 us; the launch traced here: 502 us
  starting transfers between devices  194 us (38%)
  waiting for transfers between devices  174 us (34%)
  Pallas kernels  74.9 us (15%)
  blocking collectives  27.3 us (5%)
  local copies, waits for them, and re-layouts  25.3 us (5%)
  other arithmetic  5.49 us (1%)
    ppermute x35, starting transfers between devices, exchange(): moved.append(lax.ppermute(parts[shift], 'ctx', pairs))  191 us
    ppermute x35, waiting for transfers between devices, exchange(): moved.append(lax.ppermute(parts[shift], 'ctx', pairs))  174 us
    pallas_call x3, Pallas kernels, mix(): pl.pallas_call(functools.partial(mix_kernel, devices=devices, tile=tile,...  40.3 us
    pallas_call x3, Pallas kernels, split_channels(): pl.pallas_call(kernel, grid=(tiles, rows // step), in_specs=specs, out_sp...  25 us
    unnamed x101, local copies, waits for them, and re-layouts  24.6 us
    all_gather x1, blocking collectives, body(): sums = jnp.sum(lax.all_gather(sums, 'ctx'), axis=0)  17.1 us
    all_gather x1, blocking collectives, body(): sums = lax.all_gather(sums, 'dp', axis=0, tiled=True)  10.1 us
  transfers between devices with their start and end apart: 37, of which 11 were waited for; matrix products, arithmetic and copies ran while one was open for 1% of the time, Pallas kernels for 14%

profile of v4, /device:TPU:0, one launch (start us, length us, event | category | flops | bytes accessed | tf_op | source)
XLA Modules:
  0.0 501.8 jit_solution(7913385704722013454)
XLA Ops:
  1.4 5.1 %shard_map.136 = (bf16[35,32,128]{2,1,0:T(8,128)(2,1)S(1)}, bf16[35,32,128]{2,1,0:T(8,128)(2,1)S(1)}, bf16[35,32,128]{2,1,0:T(8,128)(2,1)S(1)}, bf16[35,32,128]{...) custom-call(s32[1]{0:T(128)} %bitcast.place_ref, ...), custom_call_target="tpu_custom_call" | custom-call | bytes 4194304 | tf_op jit(solution)/shard_map/pallas_call | solution.py:66
  9.6 14.8 %shard_map.137 = (bf16[128,32,128]{2,1,0:T(8,128)(2,1)S(1)}, bf16[128,32,128]{2,1,0:T(8,128)(2,1)}, bf16[128,32,128]{2,1,0:T(8,128)(2,1)}, bf16[128,32,128]{2,1,...) custom-call(s32[1]{0:T(128)} %bitcast.place_ref, ...), custom_call_target="tpu_custom_call" | custom-call | bytes 16777216 | tf_op jit(solution)/shard_map/pallas_call | solution.py:66
  28.4 5.0 shard_map.135
  40.4 26.5 %collective-permute-done.rest_1_.rest_9_ = bf16[32,32,128]{2,1,0:T(8,128)(2,1)S(1)} collective-permute-done((bf16[32,32,128]{2,1,0:T(8,128)(2,1)}, bf16[32,32,128]{2,1,0:T(8,128)(2,1)S(1)}, u32[]{:S(2)}, u32[]{:S(2)}) %collective-permute-start) | collective-permute-done | bytes 262176 | tf_op jit(solution)/shard_map/ppermute | solution.py:276
  70.3 17.2 %collective-permute-done.1.rest_2_.rest_10_ = bf16[32,32,128]{2,1,0:T(8,128)(2,1)S(1)} collective-permute-done((bf16[32,32,128]{2,1,0:T(8,128)(2,1)}, bf16[32,32,128]{2,1,0:T(8,128)(2,1)S(1)}, u32[]{:S(2)}, u32[]{:S(2)}) %collective-permute-start.1) | collective-permute-done | bytes 262176 | tf_op jit(solution)/shard_map/ppermute | solution.py:276
  88.2 12.5 %collective-permute-start.11 = (bf16[35,32,128]{2,1,0:T(8,128)(2,1)}, bf16[35,32,128]{2,1,0:T(8,128)(2,1)S(1)}, u32[]{:S(2)}, u32[]{:S(2)}) collective-permute-start(bf16[35,32,128]{2,1,0:T(8,128)(2,1)} %get-tuple-element.71), channel_id=1, source_target_pairs={{0,5},{1,6},{2,7},{3,0},{4,1},{5,2},{6,3},{7,4},{8,13},{9,14},{10,... | collective-permute-start | bytes 860168 | tf_op jit(solution)/shard_map/ppermute | solution.py:276
  103.3 4.1 collective-permute-done.11.rest_5_.rest_13_
  109.2 3.7 collective-permute-done.12.rest_6_.rest_14_
  112.9 6.3 %collective-permute-start.17 = (bf16[128,32,128]{2,1,0:T(8,128)(2,1)}, bf16[128,32,128]{2,1,0:T(8,128)(2,1)}, u32[]{:S(2)}, u32[]{:S(2)}) collective-permute-start(bf16[128,32,128]{2,1,0:T(8,128)(2,1)} %copy-done.13), channel_id=1, source_target_pairs={{0,4},{1,5},{2,6},{3,7},{4,0},{5,1},{6,2},{7,3},{8,12},{9,13},{10,... | collective-permute-start | bytes 3145736 | tf_op jit(solution)/shard_map/ppermute | solution.py:276
  119.2 2.7 collective-permute-start.18
  121.9 49.5 %collective-permute-start.19 = (bf16[128,32,128]{2,1,0:T(8,128)(2,1)}, bf16[128,32,128]{2,1,0:T(8,128)(2,1)}, u32[]{:S(2)}, u32[]{:S(2)}) collective-permute-start(bf16[128,32,128]{2,1,0:T(8,128)(2,1)} %get-tuple-element.80), channel_id=1, source_target_pairs={{0,6},{1,7},{2,0},{3,1},{4,2},{5,3},{6,4},{7,5},{8,14},{9,15},{10,... | collective-permute-start | bytes 3145736 | tf_op jit(solution)/shard_map/ppermute | solution.py:276
  174.3 6.8 %shard_map.138 = (bf16[80,32,128]{2,1,0:T(8,128)(2,1)S(1)}, bf16[80,32,128]{2,1,0:T(8,128)(2,1)S(1)}, bf16[80,32,128]{2,1,0:T(8,128)(2,1)S(1)}, bf16[80,32,128]{...) custom-call(s32[1]{0:T(128)} %bitcast.place_ref, ...), custom_call_target="tpu_custom_call" | custom-call | flops 2415919104 | bytes 3145728 | tf_op jit(solution)/shard_map/pallas_call | solution.py:220
  181.1 14.8 %collective-permute-done.16.rest_3_.rest_11_ = bf16[128,32,128]{2,1,0:T(8,128)(2,1)} collective-permute-done((bf16[128,32,128]{2,1,0:T(8,128)(2,1)}, bf16[128,32,128]{2,1,0:T(8,128)(2,1)}, u32[]{:S(2)}, u32[]{:S(2)}) %collective-permute-start.16) | collective-permute-done | bytes 1048608 | tf_op jit(solution)/shard_map/ppermute | solution.py:276
  195.9 34.8 %collective-permute-start.2 = (bf16[32,32,128]{2,1,0:T(8,128)(2,1)S(1)}, bf16[32,32,128]{2,1,0:T(8,128)(2,1)S(1)}, u32[]{:S(2)}, u32[]{:S(2)}) collective-permute-start(bf16[32,32,128]{2,1,0:T(8,128)(2,1)S(1)} %copy-done.37), channel_id=1, source_target_pairs={{0,3},{1,4},{2,5},{3,6},{4,7},{5,0},{6,1},{7,2},{8,11},{9,12},{10,... | collective-permute-start | bytes 786440 | tf_op jit(solution)/shard_map/ppermute | solution.py:276
  232.9 12.8 %collective-permute-start.4 = (bf16[32,32,128]{2,1,0:T(8,128)(2,1)S(1)}, bf16[32,32,128]{2,1,0:T(8,128)(2,1)S(1)}, u32[]{:S(2)}, u32[]{:S(2)}) collective-permute-start(bf16[32,32,128]{2,1,0:T(8,128)(2,1)S(1)} %copy-done.33), channel_id=1, source_target_pairs={{0,5},{1,6},{2,7},{3,0},{4,1},{5,2},{6,3},{7,4},{8,13},{9,14},{10,... | collective-permute-start | bytes 786440 | tf_op jit(solution)/shard_map/ppermute | solution.py:276
  245.7 21.4 %collective-permute-start.5 = (bf16[32,32,128]{2,1,0:T(8,128)(2,1)S(1)}, bf16[32,32,128]{2,1,0:T(8,128)(2,1)S(1)}, u32[]{:S(2)}, u32[]{:S(2)}) collective-permute-start(bf16[32,32,128]{2,1,0:T(8,128)(2,1)S(1)} %copy-done.31), channel_id=1, source_target_pairs={{0,6},{1,7},{2,0},{3,1},{4,2},{5,3},{6,4},{7,5},{8,14},{9,15},{10,... | collective-permute-start | bytes 786440 | tf_op jit(solution)/shard_map/ppermute | solution.py:276
  267.1 19.8 %collective-permute-start.6 = (bf16[32,32,128]{2,1,0:T(8,128)(2,1)S(1)}, bf16[32,32,128]{2,1,0:T(8,128)(2,1)S(1)}, u32[]{:S(2)}, u32[]{:S(2)}) collective-permute-start(bf16[32,32,128]{2,1,0:T(8,128)(2,1)S(1)} %copy-done.29), channel_id=1, source_target_pairs={{0,7},{1,0},{2,1},{3,2},{4,3},{5,4},{6,5},{7,6},{8,15},{9,8},{10,9... | collective-permute-start | bytes 786440 | tf_op jit(solution)/shard_map/ppermute | solution.py:276
  290.1 26.7 %shard_map.139 = (bf16[80,32,128]{2,1,0:T(8,128)(2,1)S(1)}, bf16[80,32,128]{2,1,0:T(8,128)(2,1)S(1)}, bf16[80,32,128]{2,1,0:T(8,128)(2,1)S(1)}, bf16[80,32,128]{...) custom-call(s32[1]{0:T(128)} %bitcast.place_ref, ...), custom_call_target="tpu_custom_call", output_to_operand_aliasing={{0}: (26, {}), {1}: (27, {}), {2}: (28, {}), {3}: (29, {}),... | custom-call | flops 9663676416 | bytes 12582912 | tf_op jit(solution)/shard_map/pallas_call | solution.py:220
  319.5 3.4 collective-permute-start.29
  322.9 6.8 %shard_map.140 = (bf16[16,32,128]{2,1,0:T(8,128)(2,1)S(1)}, bf16[16,32,128]{2,1,0:T(8,128)(2,1)S(1)}, bf16[16,32,128]{2,1,0:T(8,128)(2,1)S(1)}, bf16[16,32,128]{...) custom-call(s32[1]{0:T(128)} %bitcast.place_ref, ...), custom_call_target="tpu_custom_call" | custom-call | flops 2415919104 | bytes 3145728 | tf_op jit(solution)/shard_map/pallas_call | solution.py:220
  331.3 18.7 %collective-permute-done.21.rest_1_ = bf16[16,32,128]{2,1,0:T(8,128)(2,1)S(1)} collective-permute-done((bf16[16,32,128]{2,1,0:T(8,128)(2,1)S(1)}, bf16[16,32,128]{2,1,0:T(8,128)(2,1)S(1)}, u32[]{:S(2)}, u32[]{:S(2)}) %collective-permute-start.21) | collective-permute-done | bytes 131104 | tf_op jit(solution)/shard_map/ppermute | solution.py:276
  349.9 3.1 collective-permute-start.22
  353.0 6.8 %collective-permute-done.22.rest_2_ = bf16[16,32,128]{2,1,0:T(8,128)(2,1)S(1)} collective-permute-done((bf16[16,32,128]{2,1,0:T(8,128)(2,1)S(1)}, bf16[16,32,128]{2,1,0:T(8,128)(2,1)S(1)}, u32[]{:S(2)}, u32[]{:S(2)}) %collective-permute-start.22) | collective-permute-done | bytes 131104 | tf_op jit(solution)/shard_map/ppermute | solution.py:276
  360.4 3.0 collective-permute-start.23
  363.4 6.0 %collective-permute-done.23.rest_3_ = bf16[16,32,128]{2,1,0:T(8,128)(2,1)S(1)} collective-permute-done((bf16[16,32,128]{2,1,0:T(8,128)(2,1)S(1)}, bf16[16,32,128]{2,1,0:T(8,128)(2,1)S(1)}, u32[]{:S(2)}, u32[]{:S(2)}) %collective-permute-start.23) | collective-permute-done | bytes 131104 | tf_op jit(solution)/shard_map/ppermute | solution.py:276
  370.0 6.0 %collective-permute-start.31 = (bf16[80,32,128]{2,1,0:T(8,128)(2,1)S(1)}, bf16[80,32,128]{2,1,0:T(8,128)(2,1)S(1)}, u32[]{:S(2)}, u32[]{:S(2)}) collective-permute-start(bf16[80,32,128]{2,1,0:T(8,128)(2,1)S(1)} %copy-done.17), channel_id=1, source_target_pairs={{0,4},{1,5},{2,6},{3,7},{4,0},{5,1},{6,2},{7,3},{8,12},{9,13},{10,... | collective-permute-start | bytes 1966088 | tf_op jit(solution)/shard_map/ppermute | solution.py:276
  382.3 62.5 %collective-permute-done.31.rest_4_ = bf16[80,32,128]{2,1,0:T(8,128)(2,1)S(1)} collective-permute-done((bf16[80,32,128]{2,1,0:T(8,128)(2,1)S(1)}, bf16[80,32,128]{2,1,0:T(8,128)(2,1)S(1)}, u32[]{:S(2)}, u32[]{:S(2)}) %collective-permute-start.31) | collective-permute-done | bytes 655392 | tf_op jit(solution)/shard_map/ppermute | solution.py:276
  444.7 11.6 %collective-permute-done.32.rest_5_ = bf16[80,32,128]{2,1,0:T(8,128)(2,1)S(1)} collective-permute-done((bf16[80,32,128]{2,1,0:T(8,128)(2,1)S(1)}, bf16[80,32,128]{2,1,0:T(8,128)(2,1)S(1)}, u32[]{:S(2)}, u32[]{:S(2)}) %collective-permute-start.32) | collective-permute-done | bytes 655392 | tf_op jit(solution)/shard_map/ppermute | solution.py:276
  461.3 6.9 %shard_map.141.rest_8_ = bf16[32,128,768]{2,1,0:T(8,128)(2,1)} custom-call(s32[1]{0:T(128)} %bitcast.place_ref, bf16[80,32,128]{2,1,0:T(8,128)(2,1)S(1)} %copy-done.5, bf16[80,32,128]{2,1,0:T(8,128)(2,1)S(1)} %collective-permute-done.28.rest_1_, bf16[80,32,128]{2,1,0:T(8,128)(2,1)S(1)} %collective-permute-done.29.rest_2_, ...), custom_call_target="tpu_custom_call" | custom-call | bytes 10485760 | tf_op jit(solution)/shard_map/pallas_call | solution.py:104
  468.2 2.7 shard_map.142
  471.9 17.1 %all-gather = f32[1856,128]{1,0:T(8,128)S(1)} all-gather(f32[232,128]{1,0:T(8,128)S(1)} %dynamic-slice_add_fusion), channel_id=2, replica_groups=mesh['dp'=4,'ctx'=8] {'ctx'}, dimensions={0}, use_global_device_ids=true | all-gather | bytes 1069056 | tf_op jit(solution)/shard_map/all_gather | solution.py:321
  489.1 10.1 %all_gather.11 = f32[928,128]{1,0:T(8,128)S(1)} all-gather(f32[232,128]{1,0:T(8,128)S(1)} %reduce_sum.9), channel_id=1, replica_groups=mesh['dp'=4,'ctx'=8] {'dp'}, dimensions={0}, use_global_device_ids=true | all-gather | bytes 593920 | tf_op jit(solution)/shard_map/all_gather | solution.py:322
  (167 shorter events, 51.7 us)
Async XLA Ops:
  6.5 61.1 %collective-permute-start.7 = (bf16[35,32,128]{2,1,0:T(8,128)(2,1)S(1)}, bf16[35,32,128]{2,1,0:T(8,128)(2,1)S(1)}, u32[]{:S(2)}, u32[]{:S(2)}) collective-permute-start(bf16[35,32,128]{2,1,0:T(8,128)(2,1)S(1)} %get-tuple-element.67), channel_id=1, source_target_pairs={{0,1},{1,2},{2,3},{3,4},{4,5},{5,6},{6,7},{7,0},{8,9},{9,10},{10,1... | collective-permute-start | bytes 860168 | tf_op jit(solution)/shard_map/ppermute | solution.py:276
  7.0 61.5 %collective-permute-start.8 = (bf16[35,32,128]{2,1,0:T(8,128)(2,1)S(1)}, bf16[35,32,128]{2,1,0:T(8,128)(2,1)S(1)}, u32[]{:S(2)}, u32[]{:S(2)}) collective-permute-start(bf16[35,32,128]{2,1,0:T(8,128)(2,1)S(1)} %get-tuple-element.68), channel_id=1, source_target_pairs={{0,2},{1,3},{2,4},{3,5},{4,6},{5,7},{6,0},{7,1},{8,10},{9,11},{10,... | collective-permute-start | bytes 860168 | tf_op jit(solution)/shard_map/ppermute | solution.py:276
  25.4 96.5 %collective-permute-start.14 = (bf16[128,32,128]{2,1,0:T(8,128)(2,1)}, bf16[128,32,128]{2,1,0:T(8,128)(2,1)}, u32[]{:S(2)}, u32[]{:S(2)}) collective-permute-start(bf16[128,32,128]{2,1,0:T(8,128)(2,1)} %get-tuple-element.75), channel_id=1, source_target_pairs={{0,1},{1,2},{2,3},{3,4},{4,5},{5,6},{6,7},{7,0},{8,9},{9,10},{10,1... | collective-permute-start | bytes 3145736 | tf_op jit(solution)/shard_map/ppermute | solution.py:276
  26.8 144.5 %collective-permute-start.15 = (bf16[128,32,128]{2,1,0:T(8,128)(2,1)}, bf16[128,32,128]{2,1,0:T(8,128)(2,1)}, u32[]{:S(2)}, u32[]{:S(2)}) collective-permute-start(bf16[128,32,128]{2,1,0:T(8,128)(2,1)} %get-tuple-element.76), channel_id=1, source_target_pairs={{0,2},{1,3},{2,4},{3,5},{4,6},{5,7},{6,0},{7,1},{8,10},{9,11},{10,... | collective-permute-start | bytes 3145736 | tf_op jit(solution)/shard_map/ppermute | solution.py:276
  38.4 28.5 %collective-permute-start = (bf16[32,32,128]{2,1,0:T(8,128)(2,1)}, bf16[32,32,128]{2,1,0:T(8,128)(2,1)S(1)}, u32[]{:S(2)}, u32[]{:S(2)}) collective-permute-start(bf16[32,32,128]{2,1,0:T(8,128)(2,1)} %get-tuple-element.59), channel_id=1, source_target_pairs={{0,1},{1,2},{2,3},{3,4},{4,5},{5,6},{6,7},{7,0},{8,9},{9,10},{10,1... | collective-permute-start | bytes 786440 | tf_op jit(solution)/shard_map/ppermute | solution.py:276
  67.6 33.1 %collective-permute-start.9 = (bf16[35,32,128]{2,1,0:T(8,128)(2,1)S(1)}, bf16[35,32,128]{2,1,0:T(8,128)(2,1)S(1)}, u32[]{:S(2)}, u32[]{:S(2)}) collective-permute-start(bf16[35,32,128]{2,1,0:T(8,128)(2,1)S(1)} %get-tuple-element.69), channel_id=1, source_target_pairs={{0,3},{1,4},{2,5},{3,6},{4,7},{5,0},{6,1},{7,2},{8,11},{9,12},{10,... | collective-permute-start | bytes 860168 | tf_op jit(solution)/shard_map/ppermute | solution.py:276
  67.6 33.9 %collective-permute-start.10 = (bf16[35,32,128]{2,1,0:T(8,128)(2,1)S(1)}, bf16[35,32,128]{2,1,0:T(8,128)(2,1)S(1)}, u32[]{:S(2)}, u32[]{:S(2)}) collective-permute-start(bf16[35,32,128]{2,1,0:T(8,128)(2,1)S(1)} %get-tuple-element.70), channel_id=1, source_target_pairs={{0,4},{1,5},{2,6},{3,7},{4,0},{5,1},{6,2},{7,3},{8,12},{9,13},{10,... | collective-permute-start | bytes 860168 | tf_op jit(solution)/shard_map/ppermute | solution.py:276
  68.4 19.1 %collective-permute-start.1 = (bf16[32,32,128]{2,1,0:T(8,128)(2,1)}, bf16[32,32,128]{2,1,0:T(8,128)(2,1)S(1)}, u32[]{:S(2)}, u32[]{:S(2)}) collective-permute-start(bf16[32,32,128]{2,1,0:T(8,128)(2,1)} %copy-done.40), channel_id=1, source_target_pairs={{0,2},{1,3},{2,4},{3,5},{4,6},{5,7},{6,0},{7,1},{8,10},{9,11},{10,... | collective-permute-start | bytes 786440 | tf_op jit(solution)/shard_map/ppermute | solution.py:276
  88.2 19.2 %collective-permute-start.11 = (bf16[35,32,128]{2,1,0:T(8,128)(2,1)}, bf16[35,32,128]{2,1,0:T(8,128)(2,1)S(1)}, u32[]{:S(2)}, u32[]{:S(2)}) collective-permute-start(bf16[35,32,128]{2,1,0:T(8,128)(2,1)} %get-tuple-element.71), channel_id=1, source_target_pairs={{0,5},{1,6},{2,7},{3,0},{4,1},{5,2},{6,3},{7,4},{8,13},{9,14},{10,... | collective-permute-start | bytes 860168 | tf_op jit(solution)/shard_map/ppermute | solution.py:276
  100.7 12.2 %collective-permute-start.12 = (bf16[35,32,128]{2,1,0:T(8,128)(2,1)}, bf16[35,32,128]{2,1,0:T(8,128)(2,1)S(1)}, u32[]{:S(2)}, u32[]{:S(2)}) collective-permute-start(bf16[35,32,128]{2,1,0:T(8,128)(2,1)} %get-tuple-element.72), channel_id=1, source_target_pairs={{0,6},{1,7},{2,0},{3,1},{4,2},{5,3},{6,4},{7,5},{8,14},{9,15},{10,... | collective-permute-start | bytes 860168 | tf_op jit(solution)/shard_map/ppermute | solution.py:276
  101.5 17.6 %collective-permute-start.13 = (bf16[35,32,128]{2,1,0:T(8,128)(2,1)S(1)}, bf16[35,32,128]{2,1,0:T(8,128)(2,1)S(1)}, u32[]{:S(2)}, u32[]{:S(2)}) collective-permute-start(bf16[35,32,128]{2,1,0:T(8,128)(2,1)S(1)} %get-tuple-element.73), channel_id=1, source_target_pairs={{0,7},{1,0},{2,1},{3,2},{4,3},{5,4},{6,5},{7,6},{8,15},{9,8},{10,9... | collective-permute-start | bytes 860168 | tf_op jit(solution)/shard_map/ppermute | solution.py:276
  107.4 88.4 %collective-permute-start.16 = (bf16[128,32,128]{2,1,0:T(8,128)(2,1)}, bf16[128,32,128]{2,1,0:T(8,128)(2,1)}, u32[]{:S(2)}, u32[]{:S(2)}) collective-permute-start(bf16[128,32,128]{2,1,0:T(8,128)(2,1)} %copy-done.14), channel_id=1, source_target_pairs={{0,3},{1,4},{2,5},{3,6},{4,7},{5,0},{6,1},{7,2},{8,11},{9,12},{10,... | collective-permute-start | bytes 3145736 | tf_op jit(solution)/shard_map/ppermute | solution.py:276
  112.9 117.8 %collective-permute-start.17 = (bf16[128,32,128]{2,1,0:T(8,128)(2,1)}, bf16[128,32,128]{2,1,0:T(8,128)(2,1)}, u32[]{:S(2)}, u32[]{:S(2)}) collective-permute-start(bf16[128,32,128]{2,1,0:T(8,128)(2,1)} %copy-done.13), channel_id=1, source_target_pairs={{0,4},{1,5},{2,6},{3,7},{4,0},{5,1},{6,2},{7,3},{8,12},{9,13},{10,... | collective-permute-start | bytes 3145736 | tf_op jit(solution)/shard_map/ppermute | solution.py:276
  119.2 113.8 %collective-permute-start.18 = (bf16[128,32,128]{2,1,0:T(8,128)(2,1)}, bf16[128,32,128]{2,1,0:T(8,128)(2,1)}, u32[]{:S(2)}, u32[]{:S(2)}) collective-permute-start(bf16[128,32,128]{2,1,0:T(8,128)(2,1)} %get-tuple-element.79), channel_id=1, source_target_pairs={{0,5},{1,6},{2,7},{3,0},{4,1},{5,2},{6,3},{7,4},{8,13},{9,14},{10,... | collective-permute-start | bytes 3145736 | tf_op jit(solution)/shard_map/ppermute | solution.py:276
  121.9 123.8 %collective-permute-start.19 = (bf16[128,32,128]{2,1,0:T(8,128)(2,1)}, bf16[128,32,128]{2,1,0:T(8,128)(2,1)}, u32[]{:S(2)}, u32[]{:S(2)}) collective-permute-start(bf16[128,32,128]{2,1,0:T(8,128)(2,1)} %get-tuple-element.80), channel_id=1, source_target_pairs={{0,6},{1,7},{2,0},{3,1},{4,2},{5,3},{6,4},{7,5},{8,14},{9,15},{10,... | collective-permute-start | bytes 3145736 | tf_op jit(solution)/shard_map/ppermute | solution.py:276
  171.3 95.7 %collective-permute-start.20 = (bf16[128,32,128]{2,1,0:T(8,128)(2,1)}, bf16[128,32,128]{2,1,0:T(8,128)(2,1)}, u32[]{:S(2)}, u32[]{:S(2)}) collective-permute-start(bf16[128,32,128]{2,1,0:T(8,128)(2,1)} %get-tuple-element.81), channel_id=1, source_target_pairs={{0,7},{1,0},{2,1},{3,2},{4,3},{5,4},{6,5},{7,6},{8,15},{9,8},{10,9... | collective-permute-start | bytes 3145736 | tf_op jit(solution)/shard_map/ppermute | solution.py:276
  195.9 123.5 %collective-permute-start.2 = (bf16[32,32,128]{2,1,0:T(8,128)(2,1)S(1)}, bf16[32,32,128]{2,1,0:T(8,128)(2,1)S(1)}, u32[]{:S(2)}, u32[]{:S(2)}) collective-permute-start(bf16[32,32,128]{2,1,0:T(8,128)(2,1)S(1)} %copy-done.37), channel_id=1, source_target_pairs={{0,3},{1,4},{2,5},{3,6},{4,7},{5,0},{6,1},{7,2},{8,11},{9,12},{10,... | collective-permute-start | bytes 786440 | tf_op jit(solution)/shard_map/ppermute | solution.py:276
  230.7 88.8 %collective-permute-start.3 = (bf16[32,32,128]{2,1,0:T(8,128)(2,1)S(1)}, bf16[32,32,128]{2,1,0:T(8,128)(2,1)S(1)}, u32[]{:S(2)}, u32[]{:S(2)}) collective-permute-start(bf16[32,32,128]{2,1,0:T(8,128)(2,1)S(1)} %copy-done.35), channel_id=1, source_target_pairs={{0,4},{1,5},{2,6},{3,7},{4,0},{5,1},{6,2},{7,3},{8,12},{9,13},{10,... | collective-permute-start | bytes 786440 | tf_op jit(solution)/shard_map/ppermute | solution.py:276
  232.9 90.0 %collective-permute-start.4 = (bf16[32,32,128]{2,1,0:T(8,128)(2,1)S(1)}, bf16[32,32,128]{2,1,0:T(8,128)(2,1)S(1)}, u32[]{:S(2)}, u32[]{:S(2)}) collective-permute-start(bf16[32,32,128]{2,1,0:T(8,128)(2,1)S(1)} %copy-done.33), channel_id=1, source_target_pairs={{0,5},{1,6},{2,7},{3,0},{4,1},{5,2},{6,3},{7,4},{8,13},{9,14},{10,... | collective-permute-start | bytes 786440 | tf_op jit(solution)/shard_map/ppermute | solution.py:276
  245.7 77.2 %collective-permute-start.5 = (bf16[32,32,128]{2,1,0:T(8,128)(2,1)S(1)}, bf16[32,32,128]{2,1,0:T(8,128)(2,1)S(1)}, u32[]{:S(2)}, u32[]{:S(2)}) collective-permute-start(bf16[32,32,128]{2,1,0:T(8,128)(2,1)S(1)} %copy-done.31), channel_id=1, source_target_pairs={{0,6},{1,7},{2,0},{3,1},{4,2},{5,3},{6,4},{7,5},{8,14},{9,15},{10,... | collective-permute-start | bytes 786440 | tf_op jit(solution)/shard_map/ppermute | solution.py:276
  267.1 55.8 %collective-permute-start.6 = (bf16[32,32,128]{2,1,0:T(8,128)(2,1)S(1)}, bf16[32,32,128]{2,1,0:T(8,128)(2,1)S(1)}, u32[]{:S(2)}, u32[]{:S(2)}) collective-permute-start(bf16[32,32,128]{2,1,0:T(8,128)(2,1)S(1)} %copy-done.29), channel_id=1, source_target_pairs={{0,7},{1,0},{2,1},{3,2},{4,3},{5,4},{6,5},{7,6},{8,15},{9,8},{10,9... | collective-permute-start | bytes 786440 | tf_op jit(solution)/shard_map/ppermute | solution.py:276
  319.4 58.3 %collective-permute-start.28 = (bf16[80,32,128]{2,1,0:T(8,128)(2,1)S(1)}, bf16[80,32,128]{2,1,0:T(8,128)(2,1)S(1)}, u32[]{:S(2)}, u32[]{:S(2)}) collective-permute-start(bf16[80,32,128]{2,1,0:T(8,128)(2,1)S(1)} %get-tuple-element.101), channel_id=1, source_target_pairs={{0,7},{1,0},{2,1},{3,2},{4,3},{5,4},{6,5},{7,6},{8,15},{9,8},{10,9... | collective-permute-start | bytes 1966088 | tf_op jit(solution)/shard_map/ppermute | solution.py:276
  319.5 58.2 %collective-permute-start.29 = (bf16[80,32,128]{2,1,0:T(8,128)(2,1)S(1)}, bf16[80,32,128]{2,1,0:T(8,128)(2,1)S(1)}, u32[]{:S(2)}, u32[]{:S(2)}) collective-permute-start(bf16[80,32,128]{2,1,0:T(8,128)(2,1)S(1)} %get-tuple-element.102), channel_id=1, source_target_pairs={{0,6},{1,7},{2,0},{3,1},{4,2},{5,3},{6,4},{7,5},{8,14},{9,15},{10,... | collective-permute-start | bytes 1966088 | tf_op jit(solution)/shard_map/ppermute | solution.py:276
  329.8 46.3 %collective-permute-start.35 = (f32[928,128]{1,0:T(8,128)S(1)}, f32[928,128]{1,0:T(8,128)S(1)}, u32[]{:S(2)}, u32[]{:S(2)}) collective-permute-start(f32[928,128]{1,0:T(8,128)S(1)} %get-tuple-element.108), channel_id=1, source_target_pairs={{0,8},{8,0},{16,24},{24,16},{1,9},{9,1},{17,25},{25,17},{2,10},{10... | collective-permute-start | bytes 1425416 | tf_op jit(solution)/shard_map/ppermute | solution.py:318
  331.3 18.7 %collective-permute-start.21 = (bf16[16,32,128]{2,1,0:T(8,128)(2,1)S(1)}, bf16[16,32,128]{2,1,0:T(8,128)(2,1)S(1)}, u32[]{:S(2)}, u32[]{:S(2)}) collective-permute-start(bf16[16,32,128]{2,1,0:T(8,128)(2,1)S(1)} %get-tuple-element.93), channel_id=1, source_target_pairs={{0,7},{1,0},{2,1},{3,2},{4,3},{5,4},{6,5},{7,6},{8,15},{9,8},{10,9... | collective-permute-start | bytes 393224 | tf_op jit(solution)/shard_map/ppermute | solution.py:276
  331.3 49.5 %collective-permute-start.30 = (bf16[80,32,128]{2,1,0:T(8,128)(2,1)S(1)}, bf16[80,32,128]{2,1,0:T(8,128)(2,1)S(1)}, u32[]{:S(2)}, u32[]{:S(2)}) collective-permute-start(bf16[80,32,128]{2,1,0:T(8,128)(2,1)S(1)} %get-tuple-element.103), channel_id=1, source_target_pairs={{0,5},{1,6},{2,7},{3,0},{4,1},{5,2},{6,3},{7,4},{8,13},{9,14},{10,... | collective-permute-start | bytes 1966088 | tf_op jit(solution)/shard_map/ppermute | solution.py:276
  370.0 74.7 %collective-permute-start.31 = (bf16[80,32,128]{2,1,0:T(8,128)(2,1)S(1)}, bf16[80,32,128]{2,1,0:T(8,128)(2,1)S(1)}, u32[]{:S(2)}, u32[]{:S(2)}) collective-permute-start(bf16[80,32,128]{2,1,0:T(8,128)(2,1)S(1)} %copy-done.17), channel_id=1, source_target_pairs={{0,4},{1,5},{2,6},{3,7},{4,0},{5,1},{6,2},{7,3},{8,12},{9,13},{10,... | collective-permute-start | bytes 1966088 | tf_op jit(solution)/shard_map/ppermute | solution.py:276
  376.1 80.2 %collective-permute-start.32 = (bf16[80,32,128]{2,1,0:T(8,128)(2,1)S(1)}, bf16[80,32,128]{2,1,0:T(8,128)(2,1)S(1)}, u32[]{:S(2)}, u32[]{:S(2)}) collective-permute-start(bf16[80,32,128]{2,1,0:T(8,128)(2,1)S(1)} %copy-done.20), channel_id=1, source_target_pairs={{0,3},{1,4},{2,5},{3,6},{4,7},{5,0},{6,1},{7,2},{8,11},{9,12},{10,... | collective-permute-start | bytes 1966088 | tf_op jit(solution)/shard_map/ppermute | solution.py:276
  377.7 78.5 %collective-permute-start.33 = (bf16[80,32,128]{2,1,0:T(8,128)(2,1)S(1)}, bf16[80,32,128]{2,1,0:T(8,128)(2,1)S(1)}, u32[]{:S(2)}, u32[]{:S(2)}) collective-permute-start(bf16[80,32,128]{2,1,0:T(8,128)(2,1)S(1)} %copy-done.23), channel_id=1, source_target_pairs={{0,2},{1,3},{2,4},{3,5},{4,6},{5,7},{6,0},{7,1},{8,10},{9,11},{10,... | collective-permute-start | bytes 1966088 | tf_op jit(solution)/shard_map/ppermute | solution.py:276
  377.8 79.4 %collective-permute-start.34 = (bf16[80,32,128]{2,1,0:T(8,128)(2,1)S(1)}, bf16[80,32,128]{2,1,0:T(8,128)(2,1)S(1)}, u32[]{:S(2)}, u32[]{:S(2)}) collective-permute-start(bf16[80,32,128]{2,1,0:T(8,128)(2,1)S(1)} %copy-done.45), channel_id=1, source_target_pairs={{0,1},{1,2},{2,3},{3,4},{4,5},{5,6},{6,7},{7,0},{8,9},{9,10},{10,1... | collective-permute-start | bytes 1966088 | tf_op jit(solution)/shard_map/ppermute | solution.py:276
  380.7 90.2 %collective-permute-start.36 = (f32[928,128]{1,0:T(8,128)}, f32[928,128]{1,0:T(8,128)}, u32[]{:S(2)}, u32[]{:S(2)}) collective-permute-start(f32[928,128]{1,0:T(8,128)} %add.40), channel_id=1, source_target_pairs={{0,16},{8,24},{16,0},{24,8},{1,17},{9,25},{17,1},{25,9},{2,18},{10... | collective-permute-start | bytes 1425416 | tf_op jit(solution)/shard_map/ppermute | solution.py:318
  444.7 23.5 %collective-permute-start.24 = (bf16[16,32,128]{2,1,0:T(8,128)(2,1)}, bf16[16,32,128]{2,1,0:T(8,128)(2,1)}, u32[]{:S(2)}, u32[]{:S(2)}) collective-permute-start(bf16[16,32,128]{2,1,0:T(8,128)(2,1)} %get-tuple-element.96), channel_id=1, source_target_pairs={{0,4},{1,5},{2,6},{3,7},{4,0},{5,1},{6,2},{7,3},{8,12},{9,13},{10,... | collective-permute-start | bytes 393224 | tf_op jit(solution)/shard_map/ppermute | solution.py:276
  (51 other events, 1374.7 us)

commit v5 on v4

--- a/solution.py
+++ b/solution.py
@@ -20,27 +20,32 @@
     )
 
 
+def views(refs, rotated):
+    return list(refs) if rotated else [refs[0].at[i] for i in range(refs[0].shape[0])]
+
+
 def split_tile(first_channel, tok_ref, cot_ref, out_refs, swap_ref):
     rows = tok_ref.shape[0]
     share = LANES // len(out_refs)
     for which, ref in enumerate((tok_ref, cot_ref)):
         for row in range(rows):
             swap_ref[row * LANES : (row + 1) * LANES, :] = ref[row].astype(jnp.float32).T
-        for shift, out_ref in enumerate(out_refs):
-            start = (first_channel + shift * share) % LANES
+        for slot, out_ref in enumerate(out_refs):
+            start = (first_channel + slot * share) % LANES
             for channel in range(share):
                 out_ref[which * share + channel] = swap_ref[
                     pl.ds(start + channel, rows, stride=LANES), :
                 ].astype(jnp.bfloat16)
 
 
-def split_kernel(place_ref, tok_ref, cot_ref, *rest):
-    split_tile(place_ref[0], tok_ref, cot_ref, rest[:-1], rest[-1])
-
-
-def split_twiddle_kernel(place_ref, tok_ref, cot_ref, twiddle_ref, *rest):
-    out_refs = rest[:-1]
-    split_tile(place_ref[0], tok_ref, cot_ref, out_refs, rest[-1])
+def split_kernel(place_ref, tok_ref, cot_ref, *rest, rotated):
+    first_channel = place_ref[0] if rotated else 0
+    split_tile(first_channel, tok_ref, cot_ref, views(rest[:-1], rotated), rest[-1])
+
+
+def split_twiddle_kernel(place_ref, tok_ref, cot_ref, twiddle_ref, *rest, rotated):
+    split_kernel(place_ref, tok_ref, cot_ref, *rest, rotated=rotated)
+    out_refs = views(rest[:-1], rotated)
     share = LANES // len(out_refs)
     left = twiddle_ref[...]
     for plane in range(3):
@@ -50,10 +55,22 @@
             out_ref[2 * share + plane] = part
 
 
-def split_channels(place, tokens, cotangent, tile, tiles, ctx_size, twiddle=None):
+def part_specs(devices, rotated, block, index):
+    if rotated:
+        return [pl.BlockSpec(block, index)] * devices
+    return [pl.BlockSpec((devices, *block), lambda *at: (0, *index(*at)))]
+
+
+def part_shapes(devices, rotated, shape):
+    if rotated:
+        return [jax.ShapeDtypeStruct(shape, jnp.bfloat16)] * devices
+    return [jax.ShapeDtypeStruct((devices, *shape), jnp.bfloat16)]
+
+
+def split_channels(place, tokens, cotangent, tile, tiles, devices, rotated, twiddle=None):
     rows = tokens.shape[0]
     step = min(16, rows)
-    share = LANES // ctx_size
+    share = LANES // devices
     block = pl.BlockSpec((step, B, LANES), lambda t, i: (i, 0, tile + t))
     specs = [pl.BlockSpec(memory_space=pltpu.SMEM), block, block]
     if twiddle is None:
@@ -64,11 +81,11 @@
         specs.append(pl.BlockSpec((step, B), lambda t, i: (i, 0)))
         planes = 2 * share + 3
     return pl.pallas_call(
-        kernel,
+        functools.partial(kernel, rotated=rotated),
         grid=(tiles, rows // step),
         in_specs=specs,
-        out_specs=[pl.BlockSpec((planes, step, B), lambda t, i: (t, i, 0))] * ctx_size,
-        out_shape=[jax.ShapeDtypeStruct((tiles * planes, rows, B), jnp.bfloat16)] * ctx_size,
+        out_specs=part_specs(devices, rotated, (planes, step, B), lambda t, i: (t, i, 0)),
+        out_shape=part_shapes(devices, rotated, (tiles * planes, rows, B)),
         scratch_shapes=[pltpu.VMEM((step * LANES, B), jnp.float32)],
         compiler_params=pltpu.CompilerParams(vmem_limit_bytes=VMEM_BYTES),
         cost_estimate=pl.CostEstimate(
@@ -77,11 +94,11 @@
     )(*given)
 
 
-def merge_kernel(devices, place_ref, *rest):
-    part_refs, out_ref, swap_ref = rest[:devices], rest[-2], rest[-1]
+def merge_kernel(place_ref, *rest, parts, rotated):
+    part_refs, out_ref, swap_ref = views(rest[:parts], rotated), rest[-2], rest[-1]
     share, rows, _ = part_refs[0].shape
-    for shift, part_ref in enumerate(part_refs):
-        start = (place_ref[0] + shift * share) % LANES
+    for slot, part_ref in enumerate(part_refs):
+        start = (place_ref[0] + slot * share) % LANES if rotated else slot * share
         for channel in range(share):
             at = pl.multiple_of((start + channel) * rows, rows)
             swap_ref[pl.ds(at, rows), :] = part_ref[channel].astype(jnp.float32)
@@ -89,26 +106,25 @@
         out_ref[row] = swap_ref[pl.ds(row, LANES, stride=rows), :].T.astype(jnp.bfloat16)
 
 
-def merge_channels(place, parts, held, tile, width):
-    devices = len(parts)
-    channels, rows, _ = parts[0].shape
+def merge_channels(place, parts, held, tile, tiles, devices, rotated, width, after):
+    rows = parts[0].shape[-2]
     step = min(16, rows)
     share = LANES // devices
-    tiles = channels // share
     given = [place, *parts]
     specs = [pl.BlockSpec(memory_space=pltpu.SMEM)]
-    specs += [pl.BlockSpec((share, step, B), lambda t, i: (t, i, 0))] * devices
-    if held is not None:
-        given.append(held)
-        specs.append(pl.BlockSpec(memory_space=pl.ANY))
+    specs += part_specs(devices, rotated, (share, step, B), lambda t, i: (t, i, 0))
+    for array in (held, after):
+        if array is not None:
+            given.append(array)
+            specs.append(pl.BlockSpec(memory_space=pl.ANY))
     return pl.pallas_call(
-        functools.partial(merge_kernel, devices),
+        functools.partial(merge_kernel, parts=len(parts), rotated=rotated),
         grid=(tiles, rows // step),
         in_specs=specs,
         out_specs=pl.BlockSpec((step, B, LANES), lambda t, i: (i, 0, tile + t)),
         out_shape=jax.ShapeDtypeStruct((rows, B, width), jnp.bfloat16),
         scratch_shapes=[pltpu.VMEM((step * LANES, B), jnp.float32)],
-        input_output_aliases={} if held is None else {devices + 1: 0},
+        input_output_aliases={} if held is None else {len(parts) + 1: 0},
         compiler_params=pltpu.CompilerParams(vmem_limit_bytes=VMEM_BYTES),
         cost_estimate=pl.CostEstimate(
             flops=0, bytes_accessed=4 * rows * B * LANES * tiles, transcendentals=0
@@ -122,23 +138,28 @@
 
 
 def mix_kernel(
-    place_ref, gain_ref, bias_ref, skip_ref, *rest, devices, tile, tile_count, has_sums
+    place_ref, gain_ref, bias_ref, skip_ref, *rest, parts, tile, tile_count, rotated
 ):
-    tok_refs, cot_refs, rest = rest[:devices], rest[devices : 2 * devices], rest[2 * devices :]
-    first_ref, first_t_ref, second_ref, second_t_ref, twiddle_ref, *rest = rest
-    out_refs, (sums_ref, tok_all, cot_all) = rest[-3 - devices : -3], rest[-3:]
+    tok_refs = views(rest[:parts], rotated)
+    cot_refs = views(rest[parts : 2 * parts], rotated)
+    first_ref, first_t_ref, second_ref, second_t_ref, twiddle_ref = rest[2 * parts : 2 * parts + 5]
+    out_refs = views(rest[2 * parts + 5 : 3 * parts + 5], rotated)
+    sums_ref, tok_all, cot_all = rest[-3:]
     t, step = pl.program_id(0), pl.program_id(1)
 
     @pl.when((t == 0) & (step == 0))
     def _():
-        sums_ref[...] = rest[0][...] if has_sums else jnp.zeros(sums_ref.shape, jnp.float32)
-
+        sums_ref[...] = jnp.zeros(sums_ref.shape, jnp.float32)
+
+    devices = len(tok_refs)
     pair, rows, _ = tok_refs[0].shape
     share = LANES // devices
     lane_at = place_ref[0] + step * pair
     at = (tile + t) * LANES + lane_at
 
     def rows_from(shift):
+        if not rotated:
+            return slice(shift * rows, (shift + 1) * rows)
         source = (place_ref[0] // share - shift + devices) % devices
         return pl.ds(pl.multiple_of(source * rows, rows), rows)
 
@@ -193,9 +214,8 @@
             out_ref[c] = tok_all[rows_from(shift), c * B : (c + 1) * B].astype(jnp.bfloat16)
 
 
-def mix(parts, tile, tiles, planes, place, vectors, factors, sums, sum_rows, out_tiles, out_at, held):
-    devices = len(parts)
-    rows = parts[0].shape[1]
+def mix(parts, tile, tiles, planes, place, vectors, factors, sum_rows, devices, rotated):
+    rows = parts[0].shape[-2]
     share = LANES // devices
     pair = factors[2].shape[0] // B
     steps = share // pair
@@ -203,40 +223,28 @@
     tok_at = lambda t, i: (t * (planes // pair) + i, 0, 0)
     cot_at = lambda t, i: (t * (planes // pair) + steps + i, 0, 0)
     block = (pair, rows, B)
-    given = [place, *vectors, *parts, *parts, *factors]
-    specs = [pl.BlockSpec(memory_space=pltpu.SMEM)] * 4
-    specs += [pl.BlockSpec(block, tok_at)] * devices + [pl.BlockSpec(block, cot_at)] * devices
-    specs += [whole(f) for f in factors]
-    aliases = {}
-    if sums is not None:
-        given.append(sums)
-        specs.append(whole(sums))
-    if held is not None:
-        for shift, array in enumerate(held):
-            aliases[len(given)] = shift
-            given.append(array)
-            specs.append(pl.BlockSpec(memory_space=pl.ANY))
     tile_count = vectors[0].shape[0] // LANES
     *leaving, sums = pl.pallas_call(
         functools.partial(
-            mix_kernel, devices=devices, tile=tile, tile_count=tile_count,
-            has_sums=sums is not None,
+            mix_kernel, parts=len(parts), tile=tile, tile_count=tile_count, rotated=rotated
         ),
         grid=(tiles, steps),
-        in_specs=specs,
-        out_specs=[pl.BlockSpec(block, lambda t, i: ((out_at + t) * steps + i, 0, 0))] * devices
+        in_specs=[pl.BlockSpec(memory_space=pltpu.SMEM)] * 4
+        + part_specs(devices, rotated, block, tok_at)
+        + part_specs(devices, rotated, block, cot_at)
+        + [whole(f) for f in factors],
+        out_specs=part_specs(devices, rotated, block, lambda t, i: (t * steps + i, 0, 0))
         + [pl.BlockSpec((sum_rows, LANES), lambda t, i: (0, 0))],
-        out_shape=[jax.ShapeDtypeStruct((out_tiles * share, rows, B), jnp.bfloat16)] * devices
+        out_shape=part_shapes(devices, rotated, (tiles * share, rows, B))
         + [jax.ShapeDtypeStruct((sum_rows, LANES), jnp.float32)],
         scratch_shapes=[pltpu.VMEM((A, pair * B), jnp.float32)] * 2,
-        input_output_aliases=aliases,
         compiler_params=pltpu.CompilerParams(vmem_limit_bytes=VMEM_BYTES),
         cost_estimate=pl.CostEstimate(
-            flops=tiles * share * A * B * 2 * 2304,
+            flops=tiles * share * A * B * 2 * 7000,
             bytes_accessed=tiles * share * A * B * 6,
             transcendentals=tiles * share * A * B * 2,
         ),
-    )(*given)
+    )(place, *vectors, *parts, *parts, *factors)
     return leaving, sums
 
 
@@ -259,8 +267,9 @@
     local_rows = tok_rows // B
     tiles = width // LANES
     pair = 2
-    sent = [1, tiles - 2, 1]
-    returned = [tiles - 1, 1]
+    half = tiles // 2
+    groups = [(0, 1, False), (half, tiles - half, True), (1, half - 1, False)]
+    merge_order = [0, 1, 2]
 
     place = (lax.axis_index("ctx") * share).astype(jnp.int32).reshape(1)
     second = block_diagonal(second_factor, pair)
@@ -269,48 +278,36 @@
     used_rows = CHANNEL_AT + 3 * tiles
     sum_rows = -(-used_rows // (8 * dp_size)) * 8 * dp_size
 
-    def exchange(parts, sign):
+    def exchange(parts, sign, rotated):
+        if not rotated:
+            return [lax.all_to_all(parts[0], "ctx", split_axis=0, concat_axis=0, tiled=True)]
         moved = [parts[0]]
         for shift in range(1, ctx_size):
             pairs = [(i, (i + sign * shift) % ctx_size) for i in range(ctx_size)]
             moved.append(lax.ppermute(parts[shift], "ctx", pairs))
         return moved
 
-    sums = None
-    factors = None
-    grads = []
+    sums = jnp.zeros((sum_rows, LANES), jnp.float32)
+    leaving = []
     for seq in range(seq_count):
         tok_blocks = tokens[seq].reshape(local_rows, B, width)
         cot_blocks = cotangent[seq].reshape(local_rows, B, width)
         arrived = []
-        at = 0
-        for count in sent:
+        for at, count, rotated in groups:
             own = twiddle if at == 0 else None
-            parts = split_channels(place, tok_blocks, cot_blocks, at, count, ctx_size, own)
-            arrived.append((at, count, exchange(parts, 1)))
-            at += count
-        planes = jnp.stack([part[2 * share :] for part in arrived[0][2]]).astype(jnp.float32)
-        planes = (planes[:, 0] + planes[:, 1] + planes[:, 2]).reshape(A, B)
-        planes = planes.reshape(ctx_size, local_rows, B)[::-1]
-        planes = jnp.concatenate([planes, planes], axis=0)
-        turn = ctx_size - 1 - lax.axis_index("ctx")
-        twiddle_all = lax.dynamic_slice_in_dim(planes, turn, ctx_size, 0).reshape(A, B)
+            parts = split_channels(
+                place, tok_blocks, cot_blocks, at, count, ctx_size, rotated, own
+            )
+            arrived.append(exchange(parts, 1, rotated))
+        planes = arrived[0][0][:, 2 * share :].astype(jnp.float32)
+        twiddle_all = (planes[:, 0] + planes[:, 1] + planes[:, 2]).reshape(A, B)
         factors = [first_factor, first_factor.T, second, second_t, twiddle_all]
-        leaving = [None] * len(returned)
-        for at, count, parts in arrived:
-            back = 0 if at < returned[0] else 1
-            out_at = at - back * returned[0]
-            leaving[back], sums = mix(
-                parts, at, count, 2 * share, place, vectors, factors, sums, sum_rows,
-                returned[back], out_at, leaving[back],
+        for (at, count, rotated), parts in zip(groups, arrived):
+            parts, own_sums = mix(
+                parts, at, count, 2 * share, place, vectors, factors, sum_rows, ctx_size, rotated
             )
-        held = None
-        at = 0
-        for count, grad_parts in zip(returned, leaving):
-            held = merge_channels(place, exchange(grad_parts, -1), held, at, width)
-            at += count
-        grads.append(held.reshape(tok_rows, width))
-    grad_tokens = jnp.stack(grads)
+            leaving.append(parts)
+            sums = sums + own_sums
 
     own_rows = sum_rows // dp_size
     bit = 1
@@ -320,6 +317,20 @@
     sums = lax.dynamic_slice_in_dim(sums, lax.axis_index("dp") * own_rows, own_rows, 0)
     sums = jnp.sum(lax.all_gather(sums, "ctx"), axis=0)
     sums = lax.all_gather(sums, "dp", axis=0, tiled=True)
+
+    grads = []
+    for seq in range(seq_count):
+        held = None
+        for which in merge_order:
+            at, count, rotated = groups[which]
+            parts = exchange(leaving[seq * len(groups) + which], -1, rotated)
+            after = sums if which == merge_order[-1] else None
+            held = merge_channels(
+                place, parts, held, at, count, ctx_size, rotated, width, after
+            )
+        grads.append(held.reshape(tok_rows, width))
+    grad_tokens = jnp.stack(grads)
+
     total_seqs = seq_count * dp_size
     first_norm = math.sqrt(total_seqs * B * width)
     second_norm = math.sqrt(total_seqs * A * width)

time: 505 us -> 489 us (0.968)
  starting transfers between devices: 194 us -> 112 us
  waiting for transfers between devices: 174 us -> 236 us
  blocking collectives: 27.3 us -> 34.4 us
    all_to_all x0 -> x4, waiting for transfers between devices: none -> 176 us  [exchange(): lax.all_to_all(parts[0], 'ctx', split_axis=0, concat_axis=0, tiled=True)]
    ppermute x35 -> x14, waiting for transfers between devices: 174 us -> 60.4 us  [exchange(): moved.append(lax.ppermute(parts[shift], 'ctx', pairs))]
    ppermute x35 -> x14, starting transfers between devices: 191 us -> 90.4 us  [exchange(): moved.append(lax.ppermute(parts[shift], 'ctx', pairs))]
    all_to_all x0 -> x4, starting transfers between devices: none -> 18.1 us  [exchange(): lax.all_to_all(parts[0], 'ctx', split_axis=0, concat_axis=0, tiled=True)]
    all_gather x1, blocking collectives: 17.1 us -> 24.3 us  [body(): sums = jnp.sum(lax.all_gather(sums, 'ctx'), axis=0)]
    unnamed x101 -> x74, local copies, waits for them, and re-layouts: 24.6 us -> 22.3 us
    pallas_call x8 -> x9, Pallas kernels: 74.9 us -> 75.9 us  [the longest x3 40.4 us: mix(): pl.pallas_call(functools.partial(mix_kernel, parts=len(parts), tile=tile,...]
  transfers between devices with their start and end apart: 37 -> 20, of which waited for: 11 -> 9; matrix products, arithmetic and copies ran while one was open for 1% -> 1% of each run, Pallas kernels for 14% -> 14%
where the time goes in v5:
time: 489 us; the launch traced here: 486 us
  waiting for transfers between devices  236 us (48%)
  starting transfers between devices  112 us (23%)
  Pallas kernels  75.9 us (16%)
  blocking collectives  34.4 us (7%)
  local copies, waits for them, and re-layouts  22.3 us (5%)
    all_to_all x4, waiting for transfers between devices, exchange(): lax.all_to_all(parts[0], 'ctx', split_axis=0, concat_axis=0, tiled=True)  176 us
    ppermute x14, starting transfers between devices, exchange(): moved.append(lax.ppermute(parts[shift], 'ctx', pairs))  90.4 us
    ppermute x14, waiting for transfers between devices, exchange(): moved.append(lax.ppermute(parts[shift], 'ctx', pairs))  60.4 us
    pallas_call x3, Pallas kernels, mix(): pl.pallas_call(functools.partial(mix_kernel, parts=len(parts), tile=tile,...  40.4 us
    pallas_call x3, Pallas kernels, split_channels(): pl.pallas_call(functools.partial(kernel, rotated=rotated), grid=(tiles, r...  24.9 us
    all_gather x1, blocking collectives, body(): sums = jnp.sum(lax.all_gather(sums, 'ctx'), axis=0)  24.3 us
    unnamed x74, local copies, waits for them, and re-layouts  22.3 us
    all_to_all x4, starting transfers between devices, exchange(): lax.all_to_all(parts[0], 'ctx', split_axis=0, concat_axis=0, tiled=True)  18.1 us
  transfers between devices with their start and end apart: 20, of which 9 were waited for; matrix products, arithmetic and copies ran while one was open for 1% of the time, Pallas kernels for 14%

profile of v5, /device:TPU:0, one launch (start us, length us, event | category | flops | bytes accessed | tf_op | source)
XLA Modules:
  0.0 485.8 jit_solution(10574916832005360663)
XLA Ops:
  1.4 5.4 %shard_map.136 = bf16[8,35,32,128]{3,2,1,0:T(8,128)(2,1)} custom-call(s32[1]{0:T(128)} %bitcast.place_ref, bf16[32,128,768]{2,1,0:T(8,128)(2,1)} %bitcast.20, bf16[32,128,768]{2,1,0:T(8,128)(2,1)} %bitcast.23, f32[32,128]{1,0:T(8,128)S(1)} %copy-done.25), custom_call_target="tpu_custom_call" | custom-call | bytes 4194304 | tf_op jit(solution)/shard_map/pallas_call | solution.py:83
  6.7 6.3 %all-to-all-start.1 = ((bf16[8,35,32,128]{3,2,1,0:T(8,128)(2,1)}), bf16[8,35,32,128]{3,2,1,0:T(8,128)(2,1)S(1)}, u32[]{:S(2)}, u32[]{:S(2)}) async-start(bf16[8,35,32,128]{3,2,1,0:T(8,128)(2,1)} %shard_map.136), calls=%async_computation.1 | async-start | bytes 4587520 | tf_op jit(solution)/shard_map/all_to_all | solution.py:283
  13.1 7.8 %shard_map.135 = bf16[8,64,32,128]{3,2,1,0:T(8,128)(2,1)S(1)} custom-call(s32[1]{0:T(128)} %bitcast.place_ref, bf16[32,128,768]{2,1,0:T(8,128)(2,1)} %bitcast.21, bf16[32,128,768]{2,1,0:T(8,128)(2,1)} %bitcast.24), custom_call_target="tpu_custom_call" | custom-call | bytes 8388608 | tf_op jit(solution)/shard_map/pallas_call | solution.py:83
  20.9 2.0 copy-done
  22.9 43.4 %all-to-all-done.1.rest_0_.rest_1_ = bf16[8,35,32,128]{3,2,1,0:T(8,128)(2,1)S(1)} async-done(((bf16[8,35,32,128]{3,2,1,0:T(8,128)(2,1)}), bf16[8,35,32,128]{3,2,1,0:T(8,128)(2,1)S(1)}, u32[]{:S(2)}, u32[]{:S(2)}) %all-to-all-start.1) | async-done | bytes 2293792 | tf_op jit(solution)/shard_map/all_to_all | solution.py:283
  66.3 4.6 all-to-all-start
  71.0 11.7 %shard_map.138 = (bf16[96,32,128]{2,1,0:T(8,128)(2,1)S(1)}, bf16[96,32,128]{2,1,0:T(8,128)(2,1)}, bf16[96,32,128]{2,1,0:T(8,128)(2,1)}, bf16[96,32,128]{2,1,0:T(...) custom-call(s32[1]{0:T(128)} %bitcast.place_ref, ...), custom_call_target="tpu_custom_call" | custom-call | bytes 12582912 | tf_op jit(solution)/shard_map/pallas_call | solution.py:83
  87.5 1.7 collective-permute-start.1
  90.2 6.2 %shard_map.140 = (bf16[8,16,32,128]{3,2,1,0:T(8,128)(2,1)S(1)}, f32[928,128]{1,0:T(8,128)S(1)}) custom-call(s32[1]{0:T(128)} %bitcast.place_ref, f32[768]{0:T(1024)S(1)} %copy-done.32, f32[768]{0:T(1024)S(1)} %copy-done.33, f32[768]{0:T(1024)S(1)} %copy-done.34, bf16[8,35,32,128]{3,2,1,0:T(8,128)(2,1)S(1)} %all-to-all-done.1.rest_0_.rest_1_, ...), custom_call_target="tpu_custom_call" | custom-call | flops 7340032000 | bytes 3145728 | tf_op jit(solution)/shard_map/pallas_call | solution.py:227
  98.9 91.3 %all-to-all-done.rest_0_.rest_1_ = bf16[8,64,32,128]{3,2,1,0:T(8,128)(2,1)} async-done(((bf16[8,64,32,128]{3,2,1,0:T(8,128)(2,1)}), bf16[8,64,32,128]{3,2,1,0:T(8,128)(2,1)}, u32[]{:S(2)}, u32[]{:S(2)}) %all-to-all-start) | async-done | bytes 4194336 | tf_op jit(solution)/shard_map/all_to_all | solution.py:283
  190.2 3.6 all-to-all-start.3
  193.8 1.7 collective-permute-start.2
  195.5 2.4 collective-permute-start.3
  202.4 13.7 %shard_map.137 = (bf16[8,32,32,128]{3,2,1,0:T(8,128)(2,1)S(1)}, f32[928,128]{1,0:T(8,128)S(1)}) custom-call(s32[1]{0:T(128)} %bitcast.place_ref, f32[768]{0:T(1024)S(1)} %copy-done.32, f32[768]{0:T(1024)S(1)} %copy-done.33, f32[768]{0:T(1024)S(1)} %copy-done.34, bf16[8,64,32,128]{3,2,1,0:T(8,128)(2,1)} %all-to-all-done.rest_0_.rest_1_, ...), custom_call_target="tpu_custom_call" | custom-call | flops 14680064000 | bytes 6291456 | tf_op jit(solution)/shard_map/pallas_call | solution.py:227
  218.2 40.9 %all-to-all-done.3.rest_0_ = bf16[8,16,32,128]{3,2,1,0:T(8,128)(2,1)S(1)} async-done(((bf16[8,16,32,128]{3,2,1,0:T(8,128)(2,1)}), bf16[8,16,32,128]{3,2,1,0:T(8,128)(2,1)S(1)}, u32[]{:S(2)}, u32[]{:S(2)}) %all-to-all-start.3) | async-done | bytes 1048608 | tf_op jit(solution)/shard_map/all_to_all | solution.py:283
  259.1 3.6 all-to-all-start.2
  262.7 16.3 %collective-permute-done.2.rest_3_.rest_11_ = bf16[96,32,128]{2,1,0:T(8,128)(2,1)} collective-permute-done((bf16[96,32,128]{2,1,0:T(8,128)(2,1)}, bf16[96,32,128]{2,1,0:T(8,128)(2,1)}, u32[]{:S(2)}, u32[]{:S(2)}) %collective-permute-start.2) | collective-permute-done | bytes 786464 | tf_op jit(solution)/shard_map/ppermute | solution.py:287
  280.0 16.4 %collective-permute-done.6.rest_7_.rest_15_ = bf16[96,32,128]{2,1,0:T(8,128)(2,1)} collective-permute-done((bf16[96,32,128]{2,1,0:T(8,128)(2,1)}, bf16[96,32,128]{2,1,0:T(8,128)(2,1)}, u32[]{:S(2)}, u32[]{:S(2)}) %collective-permute-start.6) | collective-permute-done | bytes 786464 | tf_op jit(solution)/shard_map/ppermute | solution.py:287
  302.0 20.4 %shard_map.139 = (bf16[48,32,128]{2,1,0:T(8,128)(2,1)S(1)}, bf16[48,32,128]{2,1,0:T(8,128)(2,1)}, bf16[48,32,128]{2,1,0:T(8,128)(2,1)}, bf16[48,32,128]{2,1,0:T(...) custom-call(s32[1]{0:T(128)} %bitcast.place_ref, ...), custom_call_target="tpu_custom_call" | custom-call | flops 22020096000 | bytes 9437184 | tf_op jit(solution)/shard_map/pallas_call | solution.py:227
  322.5 1.6 collective-permute-start.14
  324.0 56.1 %collective-permute-start.10 = (bf16[48,32,128]{2,1,0:T(8,128)(2,1)S(1)}, bf16[48,32,128]{2,1,0:T(8,128)(2,1)S(1)}, u32[]{:S(2)}, u32[]{:S(2)}) collective-permute-start(bf16[48,32,128]{2,1,0:T(8,128)(2,1)S(1)} %get-tuple-element.41), channel_id=1, source_target_pairs={{0,4},{1,5},{2,6},{3,7},{4,0},{5,1},{6,2},{7,3},{8,12},{9,13},{10,... | collective-permute-start | bytes 1179656 | tf_op jit(solution)/shard_map/ppermute | solution.py:287
  380.2 9.2 %collective-permute-start.11 = (bf16[48,32,128]{2,1,0:T(8,128)(2,1)S(1)}, bf16[48,32,128]{2,1,0:T(8,128)(2,1)S(1)}, u32[]{:S(2)}, u32[]{:S(2)}) collective-permute-start(bf16[48,32,128]{2,1,0:T(8,128)(2,1)S(1)} %get-tuple-element.42), channel_id=1, source_target_pairs={{0,3},{1,4},{2,5},{3,6},{4,7},{5,0},{6,1},{7,2},{8,11},{9,12},{10,... | collective-permute-start | bytes 1179656 | tf_op jit(solution)/shard_map/ppermute | solution.py:287
  390.2 1.5 collective-permute-start.15
  392.7 12.3 %collective-permute-start.7 = (bf16[48,32,128]{2,1,0:T(8,128)(2,1)}, bf16[48,32,128]{2,1,0:T(8,128)(2,1)}, u32[]{:S(2)}, u32[]{:S(2)}) collective-permute-start(bf16[48,32,128]{2,1,0:T(8,128)(2,1)} %get-tuple-element.38), channel_id=1, source_target_pairs={{0,7},{1,0},{2,1},{3,2},{4,3},{5,4},{6,5},{7,6},{8,15},{9,8},{10,9... | collective-permute-start | bytes 1179656 | tf_op jit(solution)/shard_map/ppermute | solution.py:287
  405.0 19.2 %collective-permute-done.11.rest_5_ = bf16[48,32,128]{2,1,0:T(8,128)(2,1)S(1)} collective-permute-done((bf16[48,32,128]{2,1,0:T(8,128)(2,1)S(1)}, bf16[48,32,128]{2,1,0:T(8,128)(2,1)S(1)}, u32[]{:S(2)}, u32[]{:S(2)}) %collective-permute-start.11) | collective-permute-done | bytes 393248 | tf_op jit(solution)/shard_map/ppermute | solution.py:287
  425.7 3.8 collective-permute-start.9
  429.5 1.7 shard_map.141.rest_8_
  431.2 6.1 %collective-permute-done.8.rest_2_ = bf16[48,32,128]{2,1,0:T(8,128)(2,1)} collective-permute-done((bf16[48,32,128]{2,1,0:T(8,128)(2,1)}, bf16[48,32,128]{2,1,0:T(8,128)(2,1)}, u32[]{:S(2)}, u32[]{:S(2)}) %collective-permute-start.8) | collective-permute-done | bytes 393248 | tf_op jit(solution)/shard_map/ppermute | solution.py:287
  438.8 6.0 %shard_map.142.rest_1_ = bf16[32,128,768]{2,1,0:T(8,128)(2,1)} custom-call(s32[1]{0:T(128)} %bitcast.place_ref, bf16[48,32,128]{2,1,0:T(8,128)(2,1)S(1)} %get-tuple-element.37.rest_0_, bf16[48,32,128]{2,1,0:T(8,128)(2,1)} %collective-permute-done.7.rest_1_, bf16[48,32,128]{2,1,0:T(8,128)(2,1)} %collective-permute-done.8.rest_2_, ...), custom_call_target="tpu_custom_call", output_to_operand_aliasing={{}: (9, {})} | custom-call | bytes 6291456 | tf_op jit(solution)/shard_map/pallas_call | solution.py:120
  445.7 24.3 %all-gather = f32[1856,128]{1,0:T(8,128)S(1)} all-gather(f32[232,128]{1,0:T(8,128)S(1)} %dynamic-slice_add_fusion), channel_id=2, replica_groups=mesh['dp'=4,'ctx'=8] {'ctx'}, dimensions={0}, use_global_device_ids=true | all-gather | bytes 1069056 | tf_op jit(solution)/shard_map/all_gather | solution.py:318
  470.1 10.1 %all_gather.11.rest_2_ = f32[928,128]{1,0:T(8,128)S(1)} all-gather(f32[232,128]{1,0:T(8,128)S(1)} %reduce_sum.9), channel_id=1, replica_groups=mesh['dp'=4,'ctx'=8] {'dp'}, dimensions={0}, use_global_device_ids=true | all-gather | bytes 593920 | tf_op jit(solution)/shard_map/all_gather | solution.py:319
  482.8 3.0 shard_map.143
  (105 shorter events, 30.6 us)
Async XLA Ops:
  6.7 59.6 %all-to-all-start.1 = ((bf16[8,35,32,128]{3,2,1,0:T(8,128)(2,1)}), bf16[8,35,32,128]{3,2,1,0:T(8,128)(2,1)S(1)}, u32[]{:S(2)}, u32[]{:S(2)}) async-start(bf16[8,35,32,128]{3,2,1,0:T(8,128)(2,1)} %shard_map.136), calls=%async_computation.1 | async-start | bytes 4587520 | tf_op jit(solution)/shard_map/all_to_all | solution.py:283
  66.3 123.9 %all-to-all-start = ((bf16[8,64,32,128]{3,2,1,0:T(8,128)(2,1)}), bf16[8,64,32,128]{3,2,1,0:T(8,128)(2,1)}, u32[]{:S(2)}, u32[]{:S(2)}) async-start(bf16[8,64,32,128]{3,2,1,0:T(8,128)(2,1)} %copy-done), calls=%async_computation | async-start | bytes 8388608 | tf_op jit(solution)/shard_map/all_to_all | solution.py:283
  70.9 18.3 %copy-start.35 = (bf16[128,128]{1,0:T(8,128)(2,1)S(1)}, bf16[128,128]{1,0:T(8,128)(2,1)}, u32[]{:S(2)}) copy-start(bf16[128,128]{1,0:T(8,128)(2,1)} %param.11) | copy-start | bytes 98308
  70.9 18.4 %copy-start.13 = (bf16[256,256]{1,0:T(8,128)(2,1)S(1)}, bf16[256,256]{1,0:T(8,128)(2,1)}, u32[]{:S(2)}) copy-start(bf16[256,256]{1,0:T(8,128)(2,1)} %rest_2_.3) | copy-start | bytes 393220
  70.9 19.2 %copy-start.32 = (f32[768]{0:T(1024)S(1)}, f32[768]{0:T(1024)}, u32[]{:S(2)}) copy-start(f32[768]{0:T(1024)} %gain_ref.5) | copy-start | bytes 9220
  71.0 19.2 %copy-start.33 = (f32[768]{0:T(1024)S(1)}, f32[768]{0:T(1024)}, u32[]{:S(2)}) copy-start(f32[768]{0:T(1024)} %bias_ref.5) | copy-start | bytes 9220
  71.0 19.2 %copy-start.34 = (f32[768]{0:T(1024)S(1)}, f32[768]{0:T(1024)}, u32[]{:S(2)}) copy-start(f32[768]{0:T(1024)} %skip_ref.5) | copy-start | bytes 9220
  87.2 111.8 %collective-permute-start = (bf16[96,32,128]{2,1,0:T(8,128)(2,1)}, bf16[96,32,128]{2,1,0:T(8,128)(2,1)}, u32[]{:S(2)}, u32[]{:S(2)}) collective-permute-start(bf16[96,32,128]{2,1,0:T(8,128)(2,1)} %get-tuple-element.30), channel_id=1, source_target_pairs={{0,1},{1,2},{2,3},{3,4},{4,5},{5,6},{6,7},{7,0},{8,9},{9,10},{10,1... | collective-permute-start | bytes 2359304 | tf_op jit(solution)/shard_map/ppermute | solution.py:287
  87.5 112.9 %collective-permute-start.1 = (bf16[96,32,128]{2,1,0:T(8,128)(2,1)}, bf16[96,32,128]{2,1,0:T(8,128)(2,1)}, u32[]{:S(2)}, u32[]{:S(2)}) collective-permute-start(bf16[96,32,128]{2,1,0:T(8,128)(2,1)} %get-tuple-element.31), channel_id=1, source_target_pairs={{0,2},{1,3},{2,4},{3,5},{4,6},{5,7},{6,0},{7,1},{8,10},{9,11},{10,... | collective-permute-start | bytes 2359304 | tf_op jit(solution)/shard_map/ppermute | solution.py:287
  89.4 111.1 %copy-start.15 = (bf16[256,256]{0,1:T(8,128)(2,1)}, bf16[256,256]{0,1:T(8,128)(2,1)S(1)}, u32[]{:S(2)}) copy-start(bf16[256,256]{0,1:T(8,128)(2,1)S(1)} %copy.17) | copy-start | bytes 393220
  89.5 111.1 %copy-start.17 = (bf16[256,256]{1,0:T(8,128)(2,1)}, bf16[256,256]{1,0:T(8,128)(2,1)S(1)}, u32[]{:S(2)}) copy-start(bf16[256,256]{1,0:T(8,128)(2,1)S(1)} %get-tuple-element.54.rest_4_.rest_18_) | copy-start | bytes 393220
  190.2 68.9 %all-to-all-start.3 = ((bf16[8,16,32,128]{3,2,1,0:T(8,128)(2,1)}), bf16[8,16,32,128]{3,2,1,0:T(8,128)(2,1)S(1)}, u32[]{:S(2)}, u32[]{:S(2)}) async-start(bf16[8,16,32,128]{3,2,1,0:T(8,128)(2,1)} %copy-done.2), calls=%async_computation.3 | async-start | bytes 2097152 | tf_op jit(solution)/shard_map/all_to_all | solution.py:283
  193.8 85.2 %collective-permute-start.2 = (bf16[96,32,128]{2,1,0:T(8,128)(2,1)}, bf16[96,32,128]{2,1,0:T(8,128)(2,1)}, u32[]{:S(2)}, u32[]{:S(2)}) collective-permute-start(bf16[96,32,128]{2,1,0:T(8,128)(2,1)} %copy-done.31), channel_id=1, source_target_pairs={{0,3},{1,4},{2,5},{3,6},{4,7},{5,0},{6,1},{7,2},{8,11},{9,12},{10,... | collective-permute-start | bytes 2359304 | tf_op jit(solution)/shard_map/ppermute | solution.py:287
  195.5 84.5 %collective-permute-start.3 = (bf16[96,32,128]{2,1,0:T(8,128)(2,1)}, bf16[96,32,128]{2,1,0:T(8,128)(2,1)}, u32[]{:S(2)}, u32[]{:S(2)}) collective-permute-start(bf16[96,32,128]{2,1,0:T(8,128)(2,1)} %copy-done.30), channel_id=1, source_target_pairs={{0,4},{1,5},{2,6},{3,7},{4,0},{5,1},{6,2},{7,3},{8,12},{9,13},{10,... | collective-permute-start | bytes 2359304 | tf_op jit(solution)/shard_map/ppermute | solution.py:287
  197.8 82.1 %collective-permute-start.4 = (bf16[96,32,128]{2,1,0:T(8,128)(2,1)}, bf16[96,32,128]{2,1,0:T(8,128)(2,1)}, u32[]{:S(2)}, u32[]{:S(2)}) collective-permute-start(bf16[96,32,128]{2,1,0:T(8,128)(2,1)} %copy-done.29), channel_id=1, source_target_pairs={{0,5},{1,6},{2,7},{3,0},{4,1},{5,2},{6,3},{7,4},{8,13},{9,14},{10,... | collective-permute-start | bytes 2359304 | tf_op jit(solution)/shard_map/ppermute | solution.py:287
  199.0 81.0 %collective-permute-start.5 = (bf16[96,32,128]{2,1,0:T(8,128)(2,1)}, bf16[96,32,128]{2,1,0:T(8,128)(2,1)}, u32[]{:S(2)}, u32[]{:S(2)}) collective-permute-start(bf16[96,32,128]{2,1,0:T(8,128)(2,1)} %copy-done.28), channel_id=1, source_target_pairs={{0,6},{1,7},{2,0},{3,1},{4,2},{5,3},{6,4},{7,5},{8,14},{9,15},{10,... | collective-permute-start | bytes 2359304 | tf_op jit(solution)/shard_map/ppermute | solution.py:287
  200.4 95.9 %collective-permute-start.6 = (bf16[96,32,128]{2,1,0:T(8,128)(2,1)}, bf16[96,32,128]{2,1,0:T(8,128)(2,1)}, u32[]{:S(2)}, u32[]{:S(2)}) collective-permute-start(bf16[96,32,128]{2,1,0:T(8,128)(2,1)} %get-tuple-element.36), channel_id=1, source_target_pairs={{0,7},{1,0},{2,1},{3,2},{4,3},{5,4},{6,5},{7,6},{8,15},{9,8},{10,9... | collective-permute-start | bytes 2359304 | tf_op jit(solution)/shard_map/ppermute | solution.py:287
  259.1 223.7 %all-to-all-start.2 = ((bf16[8,32,32,128]{3,2,1,0:T(8,128)(2,1)}), bf16[8,32,32,128]{3,2,1,0:T(8,128)(2,1)S(1)}, u32[]{:S(2)}, u32[]{:S(2)}) async-start(bf16[8,32,32,128]{3,2,1,0:T(8,128)(2,1)} %copy-done.1), calls=%async_computation.2 | async-start | bytes 4194304 | tf_op jit(solution)/shard_map/all_to_all | solution.py:283
  302.0 20.4 %copy-start.4 = (f32[928,128]{1,0:T(8,128)S(1)}, f32[928,128]{1,0:T(8,128)}, u32[]{:S(2)}) copy-start(f32[928,128]{1,0:T(8,128)} %copy-done.3) | copy-start | bytes 1425412
  302.0 20.4 %copy-start.6 = (f32[928,128]{1,0:T(8,128)S(1)}, f32[928,128]{1,0:T(8,128)}, u32[]{:S(2)}) copy-start(f32[928,128]{1,0:T(8,128)} %copy-done.5) | copy-start | bytes 1425412
  322.5 66.9 %collective-permute-start.14 = (f32[928,128]{1,0:T(8,128)S(1)}, f32[928,128]{1,0:T(8,128)S(1)}, u32[]{:S(2)}, u32[]{:S(2)}) collective-permute-start(f32[928,128]{1,0:T(8,128)S(1)} %add_add_fusion), channel_id=1, source_target_pairs={{0,8},{8,0},{16,24},{24,16},{1,9},{9,1},{17,25},{25,17},{2,10},{10... | collective-permute-start | bytes 1425416 | tf_op jit(solution)/shard_map/ppermute | solution.py:315
  324.0 67.9 %collective-permute-start.10 = (bf16[48,32,128]{2,1,0:T(8,128)(2,1)S(1)}, bf16[48,32,128]{2,1,0:T(8,128)(2,1)S(1)}, u32[]{:S(2)}, u32[]{:S(2)}) collective-permute-start(bf16[48,32,128]{2,1,0:T(8,128)(2,1)S(1)} %get-tuple-element.41), channel_id=1, source_target_pairs={{0,4},{1,5},{2,6},{3,7},{4,0},{5,1},{6,2},{7,3},{8,12},{9,13},{10,... | collective-permute-start | bytes 1179656 | tf_op jit(solution)/shard_map/ppermute | solution.py:287
  380.2 44.0 %collective-permute-start.11 = (bf16[48,32,128]{2,1,0:T(8,128)(2,1)S(1)}, bf16[48,32,128]{2,1,0:T(8,128)(2,1)S(1)}, u32[]{:S(2)}, u32[]{:S(2)}) collective-permute-start(bf16[48,32,128]{2,1,0:T(8,128)(2,1)S(1)} %get-tuple-element.42), channel_id=1, source_target_pairs={{0,3},{1,4},{2,5},{3,6},{4,7},{5,0},{6,1},{7,2},{8,11},{9,12},{10,... | collective-permute-start | bytes 1179656 | tf_op jit(solution)/shard_map/ppermute | solution.py:287
  389.3 35.6 %collective-permute-start.12 = (bf16[48,32,128]{2,1,0:T(8,128)(2,1)S(1)}, bf16[48,32,128]{2,1,0:T(8,128)(2,1)S(1)}, u32[]{:S(2)}, u32[]{:S(2)}) collective-permute-start(bf16[48,32,128]{2,1,0:T(8,128)(2,1)S(1)} %get-tuple-element.43), channel_id=1, source_target_pairs={{0,2},{1,3},{2,4},{3,5},{4,6},{5,7},{6,0},{7,1},{8,10},{9,11},{10,... | collective-permute-start | bytes 1179656 | tf_op jit(solution)/shard_map/ppermute | solution.py:287
  390.2 54.6 %collective-permute-start.15 = (f32[928,128]{1,0:T(8,128)}, f32[928,128]{1,0:T(8,128)}, u32[]{:S(2)}, u32[]{:S(2)}) collective-permute-start(f32[928,128]{1,0:T(8,128)} %add.45), channel_id=1, source_target_pairs={{0,16},{8,24},{16,0},{24,8},{1,17},{9,25},{17,1},{25,9},{2,18},{10... | collective-permute-start | bytes 1425416 | tf_op jit(solution)/shard_map/ppermute | solution.py:315
  391.7 39.6 %collective-permute-start.13 = (bf16[48,32,128]{2,1,0:T(8,128)(2,1)}, bf16[48,32,128]{2,1,0:T(8,128)(2,1)}, u32[]{:S(2)}, u32[]{:S(2)}) collective-permute-start(bf16[48,32,128]{2,1,0:T(8,128)(2,1)} %get-tuple-element.44), channel_id=1, source_target_pairs={{0,1},{1,2},{2,3},{3,4},{4,5},{5,6},{6,7},{7,0},{8,9},{9,10},{10,1... | collective-permute-start | bytes 1179656 | tf_op jit(solution)/shard_map/ppermute | solution.py:287
  392.7 38.6 %collective-permute-start.7 = (bf16[48,32,128]{2,1,0:T(8,128)(2,1)}, bf16[48,32,128]{2,1,0:T(8,128)(2,1)}, u32[]{:S(2)}, u32[]{:S(2)}) collective-permute-start(bf16[48,32,128]{2,1,0:T(8,128)(2,1)} %get-tuple-element.38), channel_id=1, source_target_pairs={{0,7},{1,0},{2,1},{3,2},{4,3},{5,4},{6,5},{7,6},{8,15},{9,8},{10,9... | collective-permute-start | bytes 1179656 | tf_op jit(solution)/shard_map/ppermute | solution.py:287
  424.9 12.4 %collective-permute-start.8 = (bf16[48,32,128]{2,1,0:T(8,128)(2,1)}, bf16[48,32,128]{2,1,0:T(8,128)(2,1)}, u32[]{:S(2)}, u32[]{:S(2)}) collective-permute-start(bf16[48,32,128]{2,1,0:T(8,128)(2,1)} %get-tuple-element.39), channel_id=1, source_target_pairs={{0,6},{1,7},{2,0},{3,1},{4,2},{5,3},{6,4},{7,5},{8,14},{9,15},{10,... | collective-permute-start | bytes 1179656 | tf_op jit(solution)/shard_map/ppermute | solution.py:287
  425.7 13.1 %collective-permute-start.9 = (bf16[48,32,128]{2,1,0:T(8,128)(2,1)}, bf16[48,32,128]{2,1,0:T(8,128)(2,1)}, u32[]{:S(2)}, u32[]{:S(2)}) collective-permute-start(bf16[48,32,128]{2,1,0:T(8,128)(2,1)} %get-tuple-element.40), channel_id=1, source_target_pairs={{0,5},{1,6},{2,7},{3,0},{4,1},{5,2},{6,3},{7,4},{8,13},{9,14},{10,... | collective-permute-start | bytes 1179656 | tf_op jit(solution)/shard_map/ppermute | solution.py:287
  429.5 9.2 %copy-start.8 = (bf16[48,32,128]{2,1,0:T(8,128)(2,1)S(1)}, bf16[48,32,128]{2,1,0:T(8,128)(2,1)}, u32[]{:S(2)}) copy-start(bf16[48,32,128]{2,1,0:T(8,128)(2,1)} %copy-done.7) | copy-start | bytes 1179652
  429.5 9.2 %copy-start.10 = (bf16[48,32,128]{2,1,0:T(8,128)(2,1)S(1)}, bf16[48,32,128]{2,1,0:T(8,128)(2,1)}, u32[]{:S(2)}) copy-start(bf16[48,32,128]{2,1,0:T(8,128)(2,1)} %copy-done.9) | copy-start | bytes 1179652
  429.5 9.2 %copy-start.12 = (bf16[48,32,128]{2,1,0:T(8,128)(2,1)S(1)}, bf16[48,32,128]{2,1,0:T(8,128)(2,1)}, u32[]{:S(2)}) copy-start(bf16[48,32,128]{2,1,0:T(8,128)(2,1)} %copy-done.11) | copy-start | bytes 1179652
  (24 other events, 22.2 us)

commit v6 on v5

--- a/solution.py
+++ b/solution.py
@@ -88,9 +88,7 @@
         out_shape=part_shapes(devices, rotated, (tiles * planes, rows, B)),
         scratch_shapes=[pltpu.VMEM((step * LANES, B), jnp.float32)],
         compiler_params=pltpu.CompilerParams(vmem_limit_bytes=VMEM_BYTES),
-        cost_estimate=pl.CostEstimate(
-            flops=0, bytes_accessed=8 * rows * B * LANES * tiles, transcendentals=0
-        ),
+        cost_estimate=pl.CostEstimate(flops=1, bytes_accessed=16 * rows * B * LANES * tiles, transcendentals=0),
     )(*given)
 
 
@@ -113,10 +111,9 @@
     given = [place, *parts]
     specs = [pl.BlockSpec(memory_space=pltpu.SMEM)]
     specs += part_specs(devices, rotated, (share, step, B), lambda t, i: (t, i, 0))
-    for array in (held, after):
-        if array is not None:
-            given.append(array)
-            specs.append(pl.BlockSpec(memory_space=pl.ANY))
+    for array in after if held is None else [held, *after]:
+        given.append(array)
+        specs.append(pl.BlockSpec(memory_space=pl.ANY))
     return pl.pallas_call(
         functools.partial(merge_kernel, parts=len(parts), rotated=rotated),
         grid=(tiles, rows // step),
@@ -126,9 +123,7 @@
         scratch_shapes=[pltpu.VMEM((step * LANES, B), jnp.float32)],
         input_output_aliases={} if held is None else {len(parts) + 1: 0},
         compiler_params=pltpu.CompilerParams(vmem_limit_bytes=VMEM_BYTES),
-        cost_estimate=pl.CostEstimate(
-            flops=0, bytes_accessed=4 * rows * B * LANES * tiles, transcendentals=0
-        ),
+        cost_estimate=pl.CostEstimate(flops=1, bytes_accessed=8 * rows * B * LANES * tiles, transcendentals=0),
     )(*given)
 
 
@@ -143,7 +138,7 @@
     tok_refs = views(rest[:parts], rotated)
     cot_refs = views(rest[parts : 2 * parts], rotated)
     first_ref, first_t_ref, second_ref, second_t_ref, twiddle_ref = rest[2 * parts : 2 * parts + 5]
-    out_refs = views(rest[2 * parts + 5 : 3 * parts + 5], rotated)
+    out_refs = views(rest[-3 - parts : -3], rotated)
     sums_ref, tok_all, cot_all = rest[-3:]
     t, step = pl.program_id(0), pl.program_id(1)
 
@@ -214,7 +209,7 @@
             out_ref[c] = tok_all[rows_from(shift), c * B : (c + 1) * B].astype(jnp.bfloat16)
 
 
-def mix(parts, tile, tiles, planes, place, vectors, factors, sum_rows, devices, rotated):
+def mix(parts, tile, tiles, planes, place, vectors, factors, sum_rows, devices, rotated, after):
     rows = parts[0].shape[-2]
     share = LANES // devices
     pair = factors[2].shape[0] // B
@@ -232,20 +227,47 @@
         in_specs=[pl.BlockSpec(memory_space=pltpu.SMEM)] * 4
         + part_specs(devices, rotated, block, tok_at)
         + part_specs(devices, rotated, block, cot_at)
-        + [whole(f) for f in factors],
+        + [whole(f) for f in factors]
+        + [pl.BlockSpec(memory_space=pl.ANY)] * len(after),
         out_specs=part_specs(devices, rotated, block, lambda t, i: (t * steps + i, 0, 0))
         + [pl.BlockSpec((sum_rows, LANES), lambda t, i: (0, 0))],
         out_shape=part_shapes(devices, rotated, (tiles * share, rows, B))
         + [jax.ShapeDtypeStruct((sum_rows, LANES), jnp.float32)],
         scratch_shapes=[pltpu.VMEM((A, pair * B), jnp.float32)] * 2,
         compiler_params=pltpu.CompilerParams(vmem_limit_bytes=VMEM_BYTES),
-        cost_estimate=pl.CostEstimate(
-            flops=tiles * share * A * B * 2 * 7000,
-            bytes_accessed=tiles * share * A * B * 6,
-            transcendentals=tiles * share * A * B * 2,
-        ),
-    )(place, *vectors, *parts, *parts, *factors)
+        cost_estimate=pl.CostEstimate(flops=tiles * share * A * B * 16000, bytes_accessed=1024, transcendentals=0),
+    )(place, *vectors, *parts, *parts, *factors, *after)
     return leaving, sums
+
+
+def add_kernel(*refs):
+    total = refs[0][...]
+    for ref in refs[1:-1]:
+        total += ref[...]
+    refs[-1][...] = total
+
+
+def add(terms):
+    vmem = pl.BlockSpec(memory_space=pltpu.VMEM)
+    return pl.pallas_call(
+        add_kernel,
+        in_specs=[vmem] * len(terms),
+        out_specs=vmem,
+        out_shape=jax.ShapeDtypeStruct(terms[0].shape, terms[0].dtype),
+        cost_estimate=pl.CostEstimate(flops=1, bytes_accessed=1024, transcendentals=0),
+    )(*terms)
+
+
+def hold(arrays, after):
+    anywhere = pl.BlockSpec(memory_space=pl.ANY)
+    return pl.pallas_call(
+        lambda *refs: None,
+        in_specs=[anywhere] * (len(arrays) + 1),
+        out_specs=[anywhere] * len(arrays),
+        out_shape=[jax.ShapeDtypeStruct(a.shape, a.dtype) for a in arrays],
+        input_output_aliases={i: i for i in range(len(arrays))},
+        cost_estimate=pl.CostEstimate(flops=1, bytes_accessed=1024, transcendentals=0),
+    )(*arrays, after)
 
 
 def block_diagonal(square, count):
@@ -259,6 +281,34 @@
     )
 
 
+def sum_over_mesh(sums, beside):
+    beside = list(beside)
+
+    def exchange_with(array, axis, bit):
+        if beside:
+            (array,) = hold([array], beside.pop(0))
+        size = lax.axis_size(axis)
+        return array, lax.ppermute(array, axis, [(i, i ^ bit) for i in range(size)])
+
+    dp = lax.axis_index("dp")
+    bits = [1 << k for k in range(lax.axis_size("dp").bit_length() - 1)]
+    for bit in reversed(bits):
+        halves = sums.reshape(2, -1, LANES)
+        high = (dp & bit) != 0
+        _, other = exchange_with(jnp.where(high, halves[0], halves[1]), "dp", bit)
+        sums = jnp.where(high, halves[1], halves[0]) + other
+    bit = 1
+    while bit < lax.axis_size("ctx"):
+        sums, other = exchange_with(sums, "ctx", bit)
+        sums = sums + other
+        bit *= 2
+    for bit in bits:
+        sums, other = exchange_with(sums, "dp", bit)
+        high = (dp & bit) != 0
+        sums = jnp.concatenate([jnp.where(high, other, sums), jnp.where(high, sums, other)])
+    return sums
+
+
 def body(tokens, cotangent, first_factor, second_factor, twiddle, gate_gain, gate_bias, skip_gain):
     seq_count, tok_rows, width = tokens.shape
     ctx_size = lax.axis_size("ctx")
@@ -267,9 +317,7 @@
     local_rows = tok_rows // B
     tiles = width // LANES
     pair = 2
-    half = tiles // 2
-    groups = [(0, 1, False), (half, tiles - half, True), (1, half - 1, False)]
-    merge_order = [0, 1, 2]
+    groups = [(0, 1, True), (1, tiles - 2, True), (tiles - 1, 1, True)]
 
     place = (lax.axis_index("ctx") * share).astype(jnp.int32).reshape(1)
     second = block_diagonal(second_factor, pair)
@@ -287,7 +335,7 @@
             moved.append(lax.ppermute(parts[shift], "ctx", pairs))
         return moved
 
-    sums = jnp.zeros((sum_rows, LANES), jnp.float32)
+    terms = []
     leaving = []
     for seq in range(seq_count):
         tok_blocks = tokens[seq].reshape(local_rows, B, width)
@@ -298,33 +346,37 @@
             parts = split_channels(
                 place, tok_blocks, cot_blocks, at, count, ctx_size, rotated, own
             )
+            if arrived:
+                parts = hold(parts, arrived[-1][1])
             arrived.append(exchange(parts, 1, rotated))
-        planes = arrived[0][0][:, 2 * share :].astype(jnp.float32)
-        twiddle_all = (planes[:, 0] + planes[:, 1] + planes[:, 2]).reshape(A, B)
+        planes = [part[..., 2 * share :, :, :].astype(jnp.float32) for part in arrived[0]]
+        planes = jnp.stack(planes).reshape(ctx_size, 3, local_rows, B)
+        twiddle_all = planes[:, 0] + planes[:, 1] + planes[:, 2]
+        if groups[0][2]:
+            twice = jnp.concatenate([twiddle_all[::-1]] * 2, axis=0)
+            turn = ctx_size - 1 - lax.axis_index("ctx")
+            twiddle_all = lax.dynamic_slice_in_dim(twice, turn, ctx_size, 0)
+        twiddle_all = twiddle_all.reshape(A, B)
         factors = [first_factor, first_factor.T, second, second_t, twiddle_all]
-        for (at, count, rotated), parts in zip(groups, arrived):
+        returned = []
+        for which, ((at, count, rotated), parts) in enumerate(zip(groups, arrived)):
+            last = which == len(groups) - 1
             parts, own_sums = mix(
-                parts, at, count, 2 * share, place, vectors, factors, sum_rows, ctx_size, rotated
+                parts, at, count, 2 * share, place, vectors, factors, sum_rows, ctx_size, rotated,
+                [*returned[0], returned[1][1]] if last else [],
             )
-            leaving.append(parts)
-            sums = sums + own_sums
-
-    own_rows = sum_rows // dp_size
-    bit = 1
-    while bit < dp_size:
-        sums = sums + lax.ppermute(sums, "dp", [(i, i ^ bit) for i in range(dp_size)])
-        bit *= 2
-    sums = lax.dynamic_slice_in_dim(sums, lax.axis_index("dp") * own_rows, own_rows, 0)
-    sums = jnp.sum(lax.all_gather(sums, "ctx"), axis=0)
-    sums = lax.all_gather(sums, "dp", axis=0, tiled=True)
+            returned.append(parts if last else exchange(parts, -1, rotated))
+            terms.append(own_sums)
+        leaving.append(returned)
+
+    sums = sum_over_mesh(add(terms), leaving[-1][1][2:])
 
     grads = []
-    for seq in range(seq_count):
+    for returned in leaving:
+        returned[-1] = exchange(returned[-1], -1, True)
         held = None
-        for which in merge_order:
-            at, count, rotated = groups[which]
-            parts = exchange(leaving[seq * len(groups) + which], -1, rotated)
-            after = sums if which == merge_order[-1] else None
+        for which, ((at, count, rotated), parts) in enumerate(zip(groups, returned)):
+            after = [returned[-1][1]] if which == len(groups) - 2 else []
             held = merge_channels(
                 place, parts, held, at, count, ctx_size, rotated, width, after
             )

time: 489 us -> 518 us (1.059)
  starting transfers between devices: 112 us -> 200 us
  waiting for transfers between devices: 236 us -> 167 us
  blocking collectives: 34.4 us -> 0 us
  local copies, waits for them, and re-layouts: 22.3 us -> 54.2 us
  other arithmetic: 4.58 us -> 14.3 us
    all_to_all x4 -> x0, waiting for transfers between devices: 176 us -> none  [exchange(): lax.all_to_all(parts[0], 'ctx', split_axis=0, concat_axis=0, tiled=True)]
    ppermute x14 -> x42, starting transfers between devices: 90.4 us -> 195 us  [exchange(): moved.append(lax.ppermute(parts[shift], 'ctx', pairs))]
    ppermute x14 -> x42, waiting for transfers between devices: 60.4 us -> 145 us  [exchange(): moved.append(lax.ppermute(parts[shift], 'ctx', pairs))]
    all_gather x2 -> x0, blocking collectives: 34.4 us -> none  [the longest x1 24.3 us: body(): sums = jnp.sum(lax.all_gather(sums, 'ctx'), axis=0)]
    unnamed x74 -> x223, local copies, waits for them, and re-layouts: 22.3 us -> 54.2 us
    ppermute x2 -> x7, waiting for transfers between devices: 0.01 us -> 22.5 us  [exchange_with(): lax.ppermute(array, axis, [(i, i ^ bit) for i in range(size)])]
    all_to_all x4 -> x0, starting transfers between devices: 18.1 us -> none  [exchange(): lax.all_to_all(parts[0], 'ctx', split_axis=0, concat_axis=0, tiled=True)]
  transfers between devices with their start and end apart: 20 -> 49, of which waited for: 9 -> 17; matrix products, arithmetic and copies ran while one was open for 1% -> 2% of each run, Pallas kernels for 14% -> 14%
where the time goes in v6:
time: 518 us; the launch traced here: 514 us
  starting transfers between devices  200 us (39%)
  waiting for transfers between devices  167 us (32%)
  Pallas kernels  77 us (15%)
  local copies, waits for them, and re-layouts  54.2 us (10%)
  other arithmetic  14.3 us (3%)
    ppermute x42, starting transfers between devices, exchange(): moved.append(lax.ppermute(parts[shift], 'ctx', pairs))  195 us
    ppermute x42, waiting for transfers between devices, exchange(): moved.append(lax.ppermute(parts[shift], 'ctx', pairs))  145 us
    unnamed x223, local copies, waits for them, and re-layouts  54.2 us
    pallas_call x3, Pallas kernels, mix(): pl.pallas_call(functools.partial(mix_kernel, parts=len(parts), tile=tile,...  40 us
    pallas_call x3, Pallas kernels, split_channels(): pl.pallas_call(functools.partial(kernel, rotated=rotated), grid=(tiles, r...  24.6 us
    ppermute x7, waiting for transfers between devices, exchange_with(): lax.ppermute(array, axis, [(i, i ^ bit) for i in range(size)])  22.5 us
  transfers between devices with their start and end apart: 49, of which 17 were waited for; matrix products, arithmetic and copies ran while one was open for 2% of the time, Pallas kernels for 14%

profile of v6, /device:TPU:0, one launch (start us, length us, event | category | flops | bytes accessed | tf_op | source)
XLA Modules:
  0.0 514.0 jit_solution(13905589187276590609)
XLA Ops:
  1.4 5.2 %shard_map.137 = (bf16[35,32,128]{2,1,0:T(8,128)(2,1)S(1)}, bf16[35,32,128]{2,1,0:T(8,128)(2,1)S(1)}, bf16[35,32,128]{2,1,0:T(8,128)(2,1)S(1)}, bf16[35,32,128]{...) custom-call(s32[1]{0:T(128)} %bitcast.place_ref, ...), custom_call_target="tpu_custom_call" | custom-call | flops 1 | bytes 8388608 | tf_op jit(solution)/shard_map/pallas_call | solution.py:83
  7.1 2.6 collective-permute-start.9
  14.6 14.9 %shard_map.136 = (bf16[128,32,128]{2,1,0:T(8,128)(2,1)S(1)}, bf16[128,32,128]{2,1,0:T(8,128)(2,1)S(1)}, bf16[128,32,128]{2,1,0:T(8,128)(2,1)S(1)}, bf16[128,32,1...) custom-call(s32[1]{0:T(128)} %bitcast.place_ref, ...), custom_call_target="tpu_custom_call" | custom-call | flops 1 | bytes 33554432 | tf_op jit(solution)/shard_map/pallas_call | solution.py:83
  37.9 5.3 %collective-permute-done.10.rest_3_.rest_11_ = bf16[35,32,128]{2,1,0:T(8,128)(2,1)S(1)} collective-permute-done((bf16[35,32,128]{2,1,0:T(8,128)(2,1)}, bf16[35,32,128]{2,1,0:T(8,128)(2,1)S(1)}, u32[]{:S(2)}, u32[]{:S(2)}) %collective-permute-start.10) | collective-permute-done | bytes 286752 | tf_op jit(solution)/shard_map/ppermute | solution.py:335
  43.3 12.1 %collective-permute-start.22 = (bf16[128,32,128]{2,1,0:T(8,128)(2,1)}, bf16[128,32,128]{2,1,0:T(8,128)(2,1)}, u32[]{:S(2)}, u32[]{:S(2)}) collective-permute-start(bf16[128,32,128]{2,1,0:T(8,128)(2,1)} %get-tuple-element.116), channel_id=1, source_target_pairs={{0,2},{1,3},{2,4},{3,5},{4,6},{5,7},{6,0},{7,1},{8,10},{9,11},{10,... | collective-permute-start | bytes 3145736 | tf_op jit(solution)/shard_map/ppermute | solution.py:335
  55.4 33.7 %collective-permute-done.13.rest_6_.rest_14_ = bf16[35,32,128]{2,1,0:T(8,128)(2,1)S(1)} collective-permute-done((bf16[35,32,128]{2,1,0:T(8,128)(2,1)}, bf16[35,32,128]{2,1,0:T(8,128)(2,1)S(1)}, u32[]{:S(2)}, u32[]{:S(2)}) %collective-permute-start.13) | collective-permute-done | bytes 286752 | tf_op jit(solution)/shard_map/ppermute | solution.py:335
  95.7 6.1 %shard_map.140 = (bf16[16,32,128]{2,1,0:T(8,128)(2,1)S(1)}, bf16[16,32,128]{2,1,0:T(8,128)(2,1)S(1)}, bf16[16,32,128]{2,1,0:T(8,128)(2,1)S(1)}, bf16[16,32,128]{...) custom-call(s32[1]{0:T(128)} %bitcast.place_ref, ...), custom_call_target="tpu_custom_call" | custom-call | flops 8388608000 | bytes 1024 | tf_op jit(solution)/shard_map/pallas_call | solution.py:222
  101.9 6.9 %collective-permute-start.16 = (bf16[16,32,128]{2,1,0:T(8,128)(2,1)S(1)}, bf16[16,32,128]{2,1,0:T(8,128)(2,1)S(1)}, u32[]{:S(2)}, u32[]{:S(2)}) collective-permute-start(bf16[16,32,128]{2,1,0:T(8,128)(2,1)S(1)} %get-tuple-element.109), channel_id=1, source_target_pairs={{0,6},{1,7},{2,0},{3,1},{4,2},{5,3},{6,4},{7,5},{8,14},{9,15},{10,... | collective-permute-start | bytes 393224 | tf_op jit(solution)/shard_map/ppermute | solution.py:335
  109.2 4.0 collective-permute-start.18
  114.0 20.2 %collective-permute-start.24 = (bf16[128,32,128]{2,1,0:T(8,128)(2,1)S(1)}, bf16[128,32,128]{2,1,0:T(8,128)(2,1)}, u32[]{:S(2)}, u32[]{:S(2)}) collective-permute-start(bf16[128,32,128]{2,1,0:T(8,128)(2,1)S(1)} %copy-done.18), channel_id=1, source_target_pairs={{0,4},{1,5},{2,6},{3,7},{4,0},{5,1},{6,2},{7,3},{8,12},{9,13},{10,... | collective-permute-start | bytes 3145736 | tf_op jit(solution)/shard_map/ppermute | solution.py:335
  134.3 48.2 %collective-permute-done.18.rest_25_.rest_4_ = bf16[16,32,128]{2,1,0:T(8,128)(2,1)S(1)} collective-permute-done((bf16[16,32,128]{2,1,0:T(8,128)(2,1)S(1)}, bf16[16,32,128]{2,1,0:T(8,128)(2,1)S(1)}, u32[]{:S(2)}, u32[]{:S(2)}) %collective-permute-start.18) | collective-permute-done | bytes 131104 | tf_op jit(solution)/shard_map/ppermute | solution.py:335
  183.3 4.5 shard_map.135
  193.4 8.1 %collective-permute-done.23.rest_3_.rest_11_ = bf16[128,32,128]{2,1,0:T(8,128)(2,1)} collective-permute-done((bf16[128,32,128]{2,1,0:T(8,128)(2,1)S(1)}, bf16[128,32,128]{2,1,0:T(8,128)(2,1)}, u32[]{:S(2)}, u32[]{:S(2)}) %collective-permute-start.23) | collective-permute-done | bytes 1048608 | tf_op jit(solution)/shard_map/ppermute | solution.py:335
  201.5 3.7 collective-permute-done.24.rest_4_.rest_12_
  205.2 56.0 %collective-permute-start.20 = (bf16[16,32,128]{2,1,0:T(8,128)(2,1)}, bf16[16,32,128]{2,1,0:T(8,128)(2,1)S(1)}, u32[]{:S(2)}, u32[]{:S(2)}) collective-permute-start(bf16[16,32,128]{2,1,0:T(8,128)(2,1)} %copy-done.97), channel_id=1, source_target_pairs={{0,2},{1,3},{2,4},{3,5},{4,6},{5,7},{6,0},{7,1},{8,10},{9,11},{10,... | collective-permute-start | bytes 393224 | tf_op jit(solution)/shard_map/ppermute | solution.py:335
  261.2 14.2 %collective-permute-start.3 = (bf16[32,32,128]{2,1,0:T(8,128)(2,1)}, bf16[32,32,128]{2,1,0:T(8,128)(2,1)S(1)}, u32[]{:S(2)}, u32[]{:S(2)}) collective-permute-start(bf16[32,32,128]{2,1,0:T(8,128)(2,1)} %get-tuple-element.94), channel_id=1, source_target_pairs={{0,2},{1,3},{2,4},{3,5},{4,6},{5,7},{6,0},{7,1},{8,10},{9,11},{10,... | collective-permute-start | bytes 786440 | tf_op jit(solution)/shard_map/ppermute | solution.py:335
  277.7 26.8 %shard_map.141 = (bf16[64,32,128]{2,1,0:T(8,128)(2,1)S(1)}, bf16[64,32,128]{2,1,0:T(8,128)(2,1)}, bf16[64,32,128]{2,1,0:T(8,128)(2,1)S(1)}, bf16[64,32,128]{2,1,...) custom-call(s32[1]{0:T(128)} %bitcast.place_ref, ...), custom_call_target="tpu_custom_call" | custom-call | flops 33554432000 | bytes 1024 | tf_op jit(solution)/shard_map/pallas_call | solution.py:222
  313.2 7.6 %collective-permute-done.21.rest_28_.rest_7_ = bf16[16,32,128]{2,1,0:T(8,128)(2,1)S(1)} collective-permute-done((bf16[16,32,128]{2,1,0:T(8,128)(2,1)S(1)}, bf16[16,32,128]{2,1,0:T(8,128)(2,1)S(1)}, u32[]{:S(2)}, u32[]{:S(2)}) %collective-permute-start.21) | collective-permute-done | bytes 131104 | tf_op jit(solution)/shard_map/ppermute | solution.py:335
  327.7 9.7 %collective-permute-done.5.rest_4_.rest_12_ = bf16[32,32,128]{2,1,0:T(8,128)(2,1)S(1)} collective-permute-done((bf16[32,32,128]{2,1,0:T(8,128)(2,1)S(1)}, bf16[32,32,128]{2,1,0:T(8,128)(2,1)S(1)}, u32[]{:S(2)}, u32[]{:S(2)}) %collective-permute-start.5) | collective-permute-done | bytes 262176 | tf_op jit(solution)/shard_map/ppermute | solution.py:335
  338.1 12.9 %collective-permute-start.36 = (bf16[64,32,128]{2,1,0:T(8,128)(2,1)}, bf16[64,32,128]{2,1,0:T(8,128)(2,1)S(1)}, u32[]{:S(2)}, u32[]{:S(2)}) collective-permute-start(bf16[64,32,128]{2,1,0:T(8,128)(2,1)} %copy-done.80), channel_id=1, source_target_pairs={{0,6},{1,7},{2,0},{3,1},{4,2},{5,3},{6,4},{7,5},{8,14},{9,15},{10,... | collective-permute-start | bytes 1572872 | tf_op jit(solution)/shard_map/ppermute | solution.py:335
  358.7 7.2 %shard_map.142 = (bf16[16,32,128]{2,1,0:T(8,128)(2,1)S(1)}, bf16[16,32,128]{2,1,0:T(8,128)(2,1)}, bf16[16,32,128]{2,1,0:T(8,128)(2,1)S(1)}, bf16[16,32,128]{2,1,...) custom-call(s32[1]{0:T(128)} %bitcast.place_ref, ...), custom_call_target="tpu_custom_call" | custom-call | flops 8388608000 | bytes 1024 | tf_op jit(solution)/shard_map/pallas_call | solution.py:222
  379.4 3.9 collective-permute-done.42
  385.0 4.9 collective-permute-done.37.rest_3_.refs_1_
  392.2 33.1 %collective-permute-start.40 = (bf16[64,32,128]{2,1,0:T(8,128)(2,1)}, bf16[64,32,128]{2,1,0:T(8,128)(2,1)S(1)}, u32[]{:S(2)}, u32[]{:S(2)}) collective-permute-start(bf16[64,32,128]{2,1,0:T(8,128)(2,1)} %copy-done.76), channel_id=1, source_target_pairs={{0,2},{1,3},{2,4},{3,5},{4,6},{5,7},{6,0},{7,1},{8,10},{9,11},{10,... | collective-permute-start | bytes 1572872 | tf_op jit(solution)/shard_map/ppermute | solution.py:335
  428.4 20.0 %collective-permute-done.38.rest_4_.refs_1_ = bf16[64,32,128]{2,1,0:T(8,128)(2,1)S(1)} collective-permute-done((bf16[64,32,128]{2,1,0:T(8,128)(2,1)}, bf16[64,32,128]{2,1,0:T(8,128)(2,1)S(1)}, u32[]{:S(2)}, u32[]{:S(2)}) %collective-permute-start.38) | collective-permute-done | bytes 524320 | tf_op jit(solution)/shard_map/ppermute | solution.py:335
  453.1 5.5 %collective-permute-done.45 = f32[232,128]{1,0:T(8,128)S(1)} collective-permute-done((f32[232,128]{1,0:T(8,128)}, f32[232,128]{1,0:T(8,128)S(1)}, u32[]{:S(2)}, u32[]{:S(2)}) %collective-permute-start.45) | collective-permute-done | bytes 118816 | tf_op jit(solution)/shard_map/ppermute | solution.py:291
  461.0 8.1 %collective-permute-done.46 = f32[232,128]{1,0:T(8,128)S(1)} collective-permute-done((f32[232,128]{1,0:T(8,128)}, f32[232,128]{1,0:T(8,128)S(1)}, u32[]{:S(2)}, u32[]{:S(2)}) %collective-permute-start.46) | collective-permute-done | bytes 118816 | tf_op jit(solution)/shard_map/ppermute | solution.py:291
  473.3 3.4 collective-permute-done.47
  479.1 2.8 collective-permute-done.30.rest_2_
  483.5 9.4 %collective-permute-start.35 = (bf16[16,32,128]{2,1,0:T(8,128)(2,1)}, bf16[16,32,128]{2,1,0:T(8,128)(2,1)}, u32[]{:S(2)}, u32[]{:S(2)}) collective-permute-start(bf16[16,32,128]{2,1,0:T(8,128)(2,1)} %copy-done.89), channel_id=1, source_target_pairs={{0,1},{1,2},{2,3},{3,4},{4,5},{5,6},{6,7},{7,0},{8,9},{9,10},{10,1... | collective-permute-start | bytes 393224 | tf_op jit(solution)/shard_map/ppermute | solution.py:335
  501.9 5.7 %shard_map.144.rest_8_ = bf16[32,128,768]{2,1,0:T(8,128)(2,1)} custom-call(s32[1]{0:T(128)} %bitcast.place_ref, bf16[64,32,128]{2,1,0:T(8,128)(2,1)S(1)} %copy-done.20, bf16[64,32,128]{2,1,0:T(8,128)(2,1)S(1)} %copy-done.22, bf16[64,32,128]{2,1,0:T(8,128)(2,1)S(1)} %copy-done.1, bf16[64,32,128]{2,1,0:T(8,128)(2,1)S(1)} %copy-done.3, ...), custom_call_target="tpu_custom_call", output_to_operand_aliasing={{}: (9, {})} | custom-call | flops 1 | bytes 16777216 | tf_op jit(solution)/shard_map/pallas_call | solution.py:117
  507.7 2.7 shard_map.145
  (328 shorter events, 103.4 us)
Async XLA Ops:
  6.6 28.4 %collective-permute-start = (bf16[35,32,128]{2,1,0:T(8,128)(2,1)S(1)}, bf16[35,32,128]{2,1,0:T(8,128)(2,1)S(1)}, u32[]{:S(2)}, u32[]{:S(2)}) collective-permute-start(bf16[35,32,128]{2,1,0:T(8,128)(2,1)S(1)} %get-tuple-element.90), channel_id=1, source_target_pairs={{0,1},{1,2},{2,3},{3,4},{4,5},{5,6},{6,7},{7,0},{8,9},{9,10},{10,1... | collective-permute-start | bytes 860168 | tf_op jit(solution)/shard_map/ppermute | solution.py:335
  7.1 29.3 %collective-permute-start.9 = (bf16[35,32,128]{2,1,0:T(8,128)(2,1)S(1)}, bf16[35,32,128]{2,1,0:T(8,128)(2,1)S(1)}, u32[]{:S(2)}, u32[]{:S(2)}) collective-permute-start(bf16[35,32,128]{2,1,0:T(8,128)(2,1)S(1)} %get-tuple-element.101), channel_id=1, source_target_pairs={{0,2},{1,3},{2,4},{3,5},{4,6},{5,7},{6,0},{7,1},{8,10},{9,11},{10,... | collective-permute-start | bytes 860168 | tf_op jit(solution)/shard_map/ppermute | solution.py:335
  9.7 33.4 %collective-permute-start.10 = (bf16[35,32,128]{2,1,0:T(8,128)(2,1)}, bf16[35,32,128]{2,1,0:T(8,128)(2,1)S(1)}, u32[]{:S(2)}, u32[]{:S(2)}) collective-permute-start(bf16[35,32,128]{2,1,0:T(8,128)(2,1)} %get-tuple-element.102), channel_id=1, source_target_pairs={{0,3},{1,4},{2,5},{3,6},{4,7},{5,0},{6,1},{7,2},{8,11},{9,12},{10,... | collective-permute-start | bytes 860168 | tf_op jit(solution)/shard_map/ppermute | solution.py:335
  12.2 31.1 %collective-permute-start.11 = (bf16[35,32,128]{2,1,0:T(8,128)(2,1)}, bf16[35,32,128]{2,1,0:T(8,128)(2,1)S(1)}, u32[]{:S(2)}, u32[]{:S(2)}) collective-permute-start(bf16[35,32,128]{2,1,0:T(8,128)(2,1)} %get-tuple-element.103), channel_id=1, source_target_pairs={{0,4},{1,5},{2,6},{3,7},{4,0},{5,1},{6,2},{7,3},{8,12},{9,13},{10,... | collective-permute-start | bytes 860168 | tf_op jit(solution)/shard_map/ppermute | solution.py:335
  13.5 42.0 %collective-permute-start.12 = (bf16[35,32,128]{2,1,0:T(8,128)(2,1)}, bf16[35,32,128]{2,1,0:T(8,128)(2,1)S(1)}, u32[]{:S(2)}, u32[]{:S(2)}) collective-permute-start(bf16[35,32,128]{2,1,0:T(8,128)(2,1)} %get-tuple-element.104), channel_id=1, source_target_pairs={{0,5},{1,6},{2,7},{3,0},{4,1},{5,2},{6,3},{7,4},{8,13},{9,14},{10,... | collective-permute-start | bytes 860168 | tf_op jit(solution)/shard_map/ppermute | solution.py:335
  35.0 54.1 %collective-permute-start.13 = (bf16[35,32,128]{2,1,0:T(8,128)(2,1)}, bf16[35,32,128]{2,1,0:T(8,128)(2,1)S(1)}, u32[]{:S(2)}, u32[]{:S(2)}) collective-permute-start(bf16[35,32,128]{2,1,0:T(8,128)(2,1)} %get-tuple-element.105), channel_id=1, source_target_pairs={{0,6},{1,7},{2,0},{3,1},{4,2},{5,3},{6,4},{7,5},{8,14},{9,15},{10,... | collective-permute-start | bytes 860168 | tf_op jit(solution)/shard_map/ppermute | solution.py:335
  36.4 52.7 %collective-permute-start.14 = (bf16[35,32,128]{2,1,0:T(8,128)(2,1)S(1)}, bf16[35,32,128]{2,1,0:T(8,128)(2,1)S(1)}, u32[]{:S(2)}, u32[]{:S(2)}) collective-permute-start(bf16[35,32,128]{2,1,0:T(8,128)(2,1)S(1)} %get-tuple-element.106), channel_id=1, source_target_pairs={{0,7},{1,0},{2,1},{3,2},{4,3},{5,4},{6,5},{7,6},{8,15},{9,8},{10,9... | collective-permute-start | bytes 860168 | tf_op jit(solution)/shard_map/ppermute | solution.py:335
  43.1 139.4 %collective-permute-start.1 = (bf16[128,32,128]{2,1,0:T(8,128)(2,1)}, bf16[128,32,128]{2,1,0:T(8,128)(2,1)}, u32[]{:S(2)}, u32[]{:S(2)}) collective-permute-start(bf16[128,32,128]{2,1,0:T(8,128)(2,1)} %get-tuple-element.91), channel_id=1, source_target_pairs={{0,1},{1,2},{2,3},{3,4},{4,5},{5,6},{6,7},{7,0},{8,9},{9,10},{10,1... | collective-permute-start | bytes 3145736 | tf_op jit(solution)/shard_map/ppermute | solution.py:335
  43.3 139.3 %collective-permute-start.22 = (bf16[128,32,128]{2,1,0:T(8,128)(2,1)}, bf16[128,32,128]{2,1,0:T(8,128)(2,1)}, u32[]{:S(2)}, u32[]{:S(2)}) collective-permute-start(bf16[128,32,128]{2,1,0:T(8,128)(2,1)} %get-tuple-element.116), channel_id=1, source_target_pairs={{0,2},{1,3},{2,4},{3,5},{4,6},{5,7},{6,0},{7,1},{8,10},{9,11},{10,... | collective-permute-start | bytes 3145736 | tf_op jit(solution)/shard_map/ppermute | solution.py:335
  109.2 73.3 %collective-permute-start.18 = (bf16[16,32,128]{2,1,0:T(8,128)(2,1)S(1)}, bf16[16,32,128]{2,1,0:T(8,128)(2,1)S(1)}, u32[]{:S(2)}, u32[]{:S(2)}) collective-permute-start(bf16[16,32,128]{2,1,0:T(8,128)(2,1)S(1)} %get-tuple-element.111), channel_id=1, source_target_pairs={{0,4},{1,5},{2,6},{3,7},{4,0},{5,1},{6,2},{7,3},{8,12},{9,13},{10,... | collective-permute-start | bytes 393224 | tf_op jit(solution)/shard_map/ppermute | solution.py:335
  113.2 88.3 %collective-permute-start.23 = (bf16[128,32,128]{2,1,0:T(8,128)(2,1)S(1)}, bf16[128,32,128]{2,1,0:T(8,128)(2,1)}, u32[]{:S(2)}, u32[]{:S(2)}) collective-permute-start(bf16[128,32,128]{2,1,0:T(8,128)(2,1)S(1)} %copy-done.16), channel_id=1, source_target_pairs={{0,3},{1,4},{2,5},{3,6},{4,7},{5,0},{6,1},{7,2},{8,11},{9,12},{10,... | collective-permute-start | bytes 3145736 | tf_op jit(solution)/shard_map/ppermute | solution.py:335
  114.0 91.1 %collective-permute-start.24 = (bf16[128,32,128]{2,1,0:T(8,128)(2,1)S(1)}, bf16[128,32,128]{2,1,0:T(8,128)(2,1)}, u32[]{:S(2)}, u32[]{:S(2)}) collective-permute-start(bf16[128,32,128]{2,1,0:T(8,128)(2,1)S(1)} %copy-done.18), channel_id=1, source_target_pairs={{0,4},{1,5},{2,6},{3,7},{4,0},{5,1},{6,2},{7,3},{8,12},{9,13},{10,... | collective-permute-start | bytes 3145736 | tf_op jit(solution)/shard_map/ppermute | solution.py:335
  182.5 78.7 %collective-permute-start.25 = (bf16[128,32,128]{2,1,0:T(8,128)(2,1)}, bf16[128,32,128]{2,1,0:T(8,128)(2,1)}, u32[]{:S(2)}, u32[]{:S(2)}) collective-permute-start(bf16[128,32,128]{2,1,0:T(8,128)(2,1)} %get-tuple-element.119), channel_id=1, source_target_pairs={{0,5},{1,6},{2,7},{3,0},{4,1},{5,2},{6,3},{7,4},{8,13},{9,14},{10,... | collective-permute-start | bytes 3145736 | tf_op jit(solution)/shard_map/ppermute | solution.py:335
  182.5 78.7 %collective-permute-start.26 = (bf16[128,32,128]{2,1,0:T(8,128)(2,1)}, bf16[128,32,128]{2,1,0:T(8,128)(2,1)}, u32[]{:S(2)}, u32[]{:S(2)}) collective-permute-start(bf16[128,32,128]{2,1,0:T(8,128)(2,1)} %get-tuple-element.120), channel_id=1, source_target_pairs={{0,6},{1,7},{2,0},{3,1},{4,2},{5,3},{6,4},{7,5},{8,14},{9,15},{10,... | collective-permute-start | bytes 3145736 | tf_op jit(solution)/shard_map/ppermute | solution.py:335
  182.6 92.8 %collective-permute-start.27 = (bf16[128,32,128]{2,1,0:T(8,128)(2,1)}, bf16[128,32,128]{2,1,0:T(8,128)(2,1)}, u32[]{:S(2)}, u32[]{:S(2)}) collective-permute-start(bf16[128,32,128]{2,1,0:T(8,128)(2,1)} %get-tuple-element.121), channel_id=1, source_target_pairs={{0,7},{1,0},{2,1},{3,2},{4,3},{5,4},{6,5},{7,6},{8,15},{9,8},{10,9... | collective-permute-start | bytes 3145736 | tf_op jit(solution)/shard_map/ppermute | solution.py:335
  201.5 109.4 %collective-permute-start.19 = (bf16[16,32,128]{2,1,0:T(8,128)(2,1)}, bf16[16,32,128]{2,1,0:T(8,128)(2,1)S(1)}, u32[]{:S(2)}, u32[]{:S(2)}) collective-permute-start(bf16[16,32,128]{2,1,0:T(8,128)(2,1)} %copy-done.98), channel_id=1, source_target_pairs={{0,3},{1,4},{2,5},{3,6},{4,7},{5,0},{6,1},{7,2},{8,11},{9,12},{10,... | collective-permute-start | bytes 393224 | tf_op jit(solution)/shard_map/ppermute | solution.py:335
  205.2 107.3 %collective-permute-start.20 = (bf16[16,32,128]{2,1,0:T(8,128)(2,1)}, bf16[16,32,128]{2,1,0:T(8,128)(2,1)S(1)}, u32[]{:S(2)}, u32[]{:S(2)}) collective-permute-start(bf16[16,32,128]{2,1,0:T(8,128)(2,1)} %copy-done.97), channel_id=1, source_target_pairs={{0,2},{1,3},{2,4},{3,5},{4,6},{5,7},{6,0},{7,1},{8,10},{9,11},{10,... | collective-permute-start | bytes 393224 | tf_op jit(solution)/shard_map/ppermute | solution.py:335
  261.1 61.1 %collective-permute-start.2 = (bf16[32,32,128]{2,1,0:T(8,128)(2,1)}, bf16[32,32,128]{2,1,0:T(8,128)(2,1)S(1)}, u32[]{:S(2)}, u32[]{:S(2)}) collective-permute-start(bf16[32,32,128]{2,1,0:T(8,128)(2,1)} %get-tuple-element.93), channel_id=1, source_target_pairs={{0,1},{1,2},{2,3},{3,4},{4,5},{5,6},{6,7},{7,0},{8,9},{9,10},{10,1... | collective-permute-start | bytes 786440 | tf_op jit(solution)/shard_map/ppermute | solution.py:335
  261.2 61.8 %collective-permute-start.3 = (bf16[32,32,128]{2,1,0:T(8,128)(2,1)}, bf16[32,32,128]{2,1,0:T(8,128)(2,1)S(1)}, u32[]{:S(2)}, u32[]{:S(2)}) collective-permute-start(bf16[32,32,128]{2,1,0:T(8,128)(2,1)} %get-tuple-element.94), channel_id=1, source_target_pairs={{0,2},{1,3},{2,4},{3,5},{4,6},{5,7},{6,0},{7,1},{8,10},{9,11},{10,... | collective-permute-start | bytes 786440 | tf_op jit(solution)/shard_map/ppermute | solution.py:335
  275.3 49.8 %collective-permute-start.4 = (bf16[32,32,128]{2,1,0:T(8,128)(2,1)}, bf16[32,32,128]{2,1,0:T(8,128)(2,1)S(1)}, u32[]{:S(2)}, u32[]{:S(2)}) collective-permute-start(bf16[32,32,128]{2,1,0:T(8,128)(2,1)} %get-tuple-element.95), channel_id=1, source_target_pairs={{0,3},{1,4},{2,5},{3,6},{4,7},{5,0},{6,1},{7,2},{8,11},{9,12},{10,... | collective-permute-start | bytes 786440 | tf_op jit(solution)/shard_map/ppermute | solution.py:335
  311.5 39.5 %collective-permute-start.28 = (bf16[64,32,128]{2,1,0:T(8,128)(2,1)}, bf16[64,32,128]{2,1,0:T(8,128)(2,1)S(1)}, u32[]{:S(2)}, u32[]{:S(2)}) collective-permute-start(bf16[64,32,128]{2,1,0:T(8,128)(2,1)} %get-tuple-element.122), channel_id=1, source_target_pairs={{0,7},{1,0},{2,1},{3,2},{4,3},{5,4},{6,5},{7,6},{8,15},{9,8},{10,9... | collective-permute-start | bytes 1572872 | tf_op jit(solution)/shard_map/ppermute | solution.py:335
  323.0 28.1 %collective-permute-start.6 = (bf16[32,32,128]{2,1,0:T(8,128)(2,1)S(1)}, bf16[32,32,128]{2,1,0:T(8,128)(2,1)}, u32[]{:S(2)}, u32[]{:S(2)}) collective-permute-start(bf16[32,32,128]{2,1,0:T(8,128)(2,1)S(1)} %copy-done.36), channel_id=1, source_target_pairs={{0,5},{1,6},{2,7},{3,0},{4,1},{5,2},{6,3},{7,4},{8,13},{9,14},{10,... | collective-permute-start | bytes 786440 | tf_op jit(solution)/shard_map/ppermute | solution.py:335
  323.7 27.4 %collective-permute-start.7 = (bf16[32,32,128]{2,1,0:T(8,128)(2,1)S(1)}, bf16[32,32,128]{2,1,0:T(8,128)(2,1)}, u32[]{:S(2)}, u32[]{:S(2)}) collective-permute-start(bf16[32,32,128]{2,1,0:T(8,128)(2,1)S(1)} %copy-done.38), channel_id=1, source_target_pairs={{0,6},{1,7},{2,0},{3,1},{4,2},{5,3},{6,4},{7,5},{8,14},{9,15},{10,... | collective-permute-start | bytes 786440 | tf_op jit(solution)/shard_map/ppermute | solution.py:335
  338.1 36.3 %collective-permute-start.36 = (bf16[64,32,128]{2,1,0:T(8,128)(2,1)}, bf16[64,32,128]{2,1,0:T(8,128)(2,1)S(1)}, u32[]{:S(2)}, u32[]{:S(2)}) collective-permute-start(bf16[64,32,128]{2,1,0:T(8,128)(2,1)} %copy-done.80), channel_id=1, source_target_pairs={{0,6},{1,7},{2,0},{3,1},{4,2},{5,3},{6,4},{7,5},{8,14},{9,15},{10,... | collective-permute-start | bytes 1572872 | tf_op jit(solution)/shard_map/ppermute | solution.py:335
  377.3 71.1 %collective-permute-start.38 = (bf16[64,32,128]{2,1,0:T(8,128)(2,1)}, bf16[64,32,128]{2,1,0:T(8,128)(2,1)S(1)}, u32[]{:S(2)}, u32[]{:S(2)}) collective-permute-start(bf16[64,32,128]{2,1,0:T(8,128)(2,1)} %copy-done.78), channel_id=1, source_target_pairs={{0,4},{1,5},{2,6},{3,7},{4,0},{5,1},{6,2},{7,3},{8,12},{9,13},{10,... | collective-permute-start | bytes 1572872 | tf_op jit(solution)/shard_map/ppermute | solution.py:335
  379.4 72.9 %collective-permute-start.39 = (bf16[64,32,128]{2,1,0:T(8,128)(2,1)}, bf16[64,32,128]{2,1,0:T(8,128)(2,1)S(1)}, u32[]{:S(2)}, u32[]{:S(2)}) collective-permute-start(bf16[64,32,128]{2,1,0:T(8,128)(2,1)} %copy-done.77), channel_id=1, source_target_pairs={{0,3},{1,4},{2,5},{3,6},{4,7},{5,0},{6,1},{7,2},{8,11},{9,12},{10,... | collective-permute-start | bytes 1572872 | tf_op jit(solution)/shard_map/ppermute | solution.py:335
  390.7 37.0 %collective-permute-start.43 = (f32[232,128]{1,0:T(8,128)}, f32[232,128]{1,0:T(8,128)S(1)}, u32[]{:S(2)}, u32[]{:S(2)}) collective-permute-start(f32[232,128]{1,0:T(8,128)} %shard_map.148), channel_id=1, source_target_pairs={{0,8},{8,0},{16,24},{24,16},{1,9},{9,1},{17,25},{25,17},{2,10},{10... | collective-permute-start | bytes 356360 | tf_op jit(solution)/shard_map/ppermute | solution.py:291
  392.2 68.0 %collective-permute-start.40 = (bf16[64,32,128]{2,1,0:T(8,128)(2,1)}, bf16[64,32,128]{2,1,0:T(8,128)(2,1)S(1)}, u32[]{:S(2)}, u32[]{:S(2)}) collective-permute-start(bf16[64,32,128]{2,1,0:T(8,128)(2,1)} %copy-done.76), channel_id=1, source_target_pairs={{0,2},{1,3},{2,4},{3,5},{4,6},{5,7},{6,0},{7,1},{8,10},{9,11},{10,... | collective-permute-start | bytes 1572872 | tf_op jit(solution)/shard_map/ppermute | solution.py:335
  425.3 45.4 %collective-permute-start.41 = (bf16[64,32,128]{2,1,0:T(8,128)(2,1)}, bf16[64,32,128]{2,1,0:T(8,128)(2,1)S(1)}, u32[]{:S(2)}, u32[]{:S(2)}) collective-permute-start(bf16[64,32,128]{2,1,0:T(8,128)(2,1)} %copy-done.75), channel_id=1, source_target_pairs={{0,1},{1,2},{2,3},{3,4},{4,5},{5,6},{6,7},{7,0},{8,9},{9,10},{10,1... | collective-permute-start | bytes 1572872 | tf_op jit(solution)/shard_map/ppermute | solution.py:335
  478.5 31.9 %collective-permute-start.48 = (f32[464,128]{1,0:T(8,128)}, f32[464,128]{1,0:T(8,128)}, u32[]{:S(2)}, u32[]{:S(2)}) collective-permute-start(f32[464,128]{1,0:T(8,128)} %pad_maximum_fusion), channel_id=1, source_target_pairs={{0,16},{8,24},{16,0},{24,8},{1,17},{9,25},{17,1},{25,9},{2,18},{10... | collective-permute-start | bytes 712712 | tf_op jit(solution)/shard_map/ppermute | solution.py:291
  478.7 28.9 %collective-permute-start.32 = (bf16[16,32,128]{2,1,0:T(8,128)(2,1)}, bf16[16,32,128]{2,1,0:T(8,128)(2,1)}, u32[]{:S(2)}, u32[]{:S(2)}) collective-permute-start(bf16[16,32,128]{2,1,0:T(8,128)(2,1)} %copy-done.92), channel_id=1, source_target_pairs={{0,4},{1,5},{2,6},{3,7},{4,0},{5,1},{6,2},{7,3},{8,12},{9,13},{10,... | collective-permute-start | bytes 393224 | tf_op jit(solution)/shard_map/ppermute | solution.py:335
  478.7 28.9 %collective-permute-start.33 = (bf16[16,32,128]{2,1,0:T(8,128)(2,1)}, bf16[16,32,128]{2,1,0:T(8,128)(2,1)}, u32[]{:S(2)}, u32[]{:S(2)}) collective-permute-start(bf16[16,32,128]{2,1,0:T(8,128)(2,1)} %copy-done.91), channel_id=1, source_target_pairs={{0,3},{1,4},{2,5},{3,6},{4,7},{5,0},{6,1},{7,2},{8,11},{9,12},{10,... | collective-permute-start | bytes 393224 | tf_op jit(solution)/shard_map/ppermute | solution.py:335
  (124 other events, 2584.0 us)

commit v7 on v6

--- a/solution.py
+++ b/solution.py
@@ -262,12 +262,12 @@
     anywhere = pl.BlockSpec(memory_space=pl.ANY)
     return pl.pallas_call(
         lambda *refs: None,
-        in_specs=[anywhere] * (len(arrays) + 1),
+        in_specs=[anywhere] * (len(arrays) + len(after)),
         out_specs=[anywhere] * len(arrays),
         out_shape=[jax.ShapeDtypeStruct(a.shape, a.dtype) for a in arrays],
         input_output_aliases={i: i for i in range(len(arrays))},
         cost_estimate=pl.CostEstimate(flops=1, bytes_accessed=1024, transcendentals=0),
-    )(*arrays, after)
+    )(*arrays, *after)
 
 
 def block_diagonal(square, count):
@@ -281,32 +281,17 @@
     )
 
 
-def sum_over_mesh(sums, beside):
-    beside = list(beside)
-
-    def exchange_with(array, axis, bit):
-        if beside:
-            (array,) = hold([array], beside.pop(0))
-        size = lax.axis_size(axis)
-        return array, lax.ppermute(array, axis, [(i, i ^ bit) for i in range(size)])
-
+def sum_over_mesh(sums):
     dp = lax.axis_index("dp")
-    bits = [1 << k for k in range(lax.axis_size("dp").bit_length() - 1)]
-    for bit in reversed(bits):
+    size = lax.axis_size("dp")
+    for bit in reversed([1 << k for k in range(size.bit_length() - 1)]):
         halves = sums.reshape(2, -1, LANES)
         high = (dp & bit) != 0
-        _, other = exchange_with(jnp.where(high, halves[0], halves[1]), "dp", bit)
-        sums = jnp.where(high, halves[1], halves[0]) + other
-    bit = 1
-    while bit < lax.axis_size("ctx"):
-        sums, other = exchange_with(sums, "ctx", bit)
-        sums = sums + other
-        bit *= 2
-    for bit in bits:
-        sums, other = exchange_with(sums, "dp", bit)
-        high = (dp & bit) != 0
-        sums = jnp.concatenate([jnp.where(high, other, sums), jnp.where(high, sums, other)])
-    return sums
+        sent = jnp.where(high, halves[0], halves[1])
+        kept = jnp.where(high, halves[1], halves[0])
+        sums = kept + lax.ppermute(sent, "dp", [(i, i ^ bit) for i in range(size)])
+    sums = jnp.sum(lax.all_gather(sums, "ctx"), axis=0)
+    return lax.all_gather(sums, "dp", axis=0, tiled=True)
 
 
 def body(tokens, cotangent, first_factor, second_factor, twiddle, gate_gain, gate_bias, skip_gain):
@@ -317,7 +302,9 @@
     local_rows = tok_rows // B
     tiles = width // LANES
     pair = 2
-    groups = [(0, 1, True), (1, tiles - 2, True), (tiles - 1, 1, True)]
+    half = tiles // 2
+    groups = [(0, 1, False), (half, tiles - half, True), (1, half - 1, False)]
+    merge_order = [0, 1, 2]
 
     place = (lax.axis_index("ctx") * share).astype(jnp.int32).reshape(1)
     second = block_diagonal(second_factor, pair)
@@ -346,8 +333,8 @@
             parts = split_channels(
                 place, tok_blocks, cot_blocks, at, count, ctx_size, rotated, own
             )
-            if arrived:
-                parts = hold(parts, arrived[-1][1])
+            if len(arrived) == 2:
+                parts = hold(parts, arrived[1][1:6])
             arrived.append(exchange(parts, 1, rotated))
         planes = [part[..., 2 * share :, :, :].astype(jnp.float32) for part in arrived[0]]
         planes = jnp.stack(planes).reshape(ctx_size, 3, local_rows, B)
@@ -360,25 +347,24 @@
         factors = [first_factor, first_factor.T, second, second_t, twiddle_all]
         returned = []
         for which, ((at, count, rotated), parts) in enumerate(zip(groups, arrived)):
-            last = which == len(groups) - 1
+            after = returned[1][1:] if which == 2 else []
             parts, own_sums = mix(
                 parts, at, count, 2 * share, place, vectors, factors, sum_rows, ctx_size, rotated,
-                [*returned[0], returned[1][1]] if last else [],
+                after,
             )
-            returned.append(parts if last else exchange(parts, -1, rotated))
+            returned.append(exchange(parts, -1, rotated))
             terms.append(own_sums)
         leaving.append(returned)
 
-    sums = sum_over_mesh(add(terms), leaving[-1][1][2:])
-
+    sums = sum_over_mesh(add(terms))
     grads = []
     for returned in leaving:
-        returned[-1] = exchange(returned[-1], -1, True)
         held = None
-        for which, ((at, count, rotated), parts) in enumerate(zip(groups, returned)):
-            after = [returned[-1][1]] if which == len(groups) - 2 else []
+        for which in merge_order:
+            at, count, rotated = groups[which]
+            after = [sums] if which == merge_order[-1] else []
             held = merge_channels(
-                place, parts, held, at, count, ctx_size, rotated, width, after
+                place, returned[which], held, at, count, ctx_size, rotated, width, after
             )
         grads.append(held.reshape(tok_rows, width))
     grad_tokens = jnp.stack(grads)

time: 518 us -> 500 us (0.965)
  starting transfers between devices: 200 us -> 97 us
  waiting for transfers between devices: 167 us -> 246 us
  blocking collectives: 0 us -> 45.2 us
  local copies, waits for them, and re-layouts: 54.2 us -> 22.9 us
  other arithmetic: 14.3 us -> 7.27 us
    ppermute x42 -> x14, starting transfers between devices: 195 us -> 39.8 us  [exchange(): moved.append(lax.ppermute(parts[shift], 'ctx', pairs))]
    ppermute x42 -> x14, waiting for transfers between devices: 145 us -> 229 us  [exchange(): moved.append(lax.ppermute(parts[shift], 'ctx', pairs))]
    all_to_all x0 -> x4, starting transfers between devices: none -> 54.2 us  [exchange(): lax.all_to_all(parts[0], 'ctx', split_axis=0, concat_axis=0, tiled=True)]
    all_gather x0 -> x2, blocking collectives: none -> 45.2 us  [the longest x1 35 us: sum_over_mesh(): sums = jnp.sum(lax.all_gather(sums, 'ctx'), axis=0)]
    unnamed x223 -> x76, local copies, waits for them, and re-layouts: 54.2 us -> 22.9 us
    ppermute x7 -> x2, waiting for transfers between devices: 22.5 us -> 6.08 us  [sum_over_mesh(): sums = kept + lax.ppermute(sent, 'dp', [(i, i ^ bit) for i in range(size)])]
    all_to_all x0 -> x4, waiting for transfers between devices: none -> 10.6 us  [exchange(): lax.all_to_all(parts[0], 'ctx', split_axis=0, concat_axis=0, tiled=True)]
  transfers between devices with their start and end apart: 49 -> 20, of which waited for: 17 -> 10; matrix products, arithmetic and copies ran while one was open for 2% -> 2% of each run, Pallas kernels for 14% -> 14%
where the time goes in v7:
time: 500 us; the launch traced here: 497 us
  waiting for transfers between devices  246 us (49%)
  starting transfers between devices  97 us (19%)
  Pallas kernels  78 us (16%)
  blocking collectives  45.2 us (9%)
  local copies, waits for them, and re-layouts  22.9 us (5%)
  other arithmetic  7.27 us (1%)
    ppermute x14, waiting for transfers between devices, exchange(): moved.append(lax.ppermute(parts[shift], 'ctx', pairs))  229 us
    all_to_all x4, starting transfers between devices, exchange(): lax.all_to_all(parts[0], 'ctx', split_axis=0, concat_axis=0, tiled=True)  54.2 us
    pallas_call x3, Pallas kernels, mix(): pl.pallas_call(functools.partial(mix_kernel, parts=len(parts), tile=tile,...  40.2 us
    ppermute x14, starting transfers between devices, exchange(): moved.append(lax.ppermute(parts[shift], 'ctx', pairs))  39.8 us
    all_gather x1, blocking collectives, sum_over_mesh(): sums = jnp.sum(lax.all_gather(sums, 'ctx'), axis=0)  35 us
    pallas_call x3, Pallas kernels, split_channels(): pl.pallas_call(functools.partial(kernel, rotated=rotated), grid=(tiles, r...  24.9 us
    unnamed x76, local copies, waits for them, and re-layouts  22.9 us
    pallas_call x3, Pallas kernels, merge_channels(): pl.pallas_call(functools.partial(merge_kernel, parts=len(parts), rotated=...  10.8 us
  transfers between devices with their start and end apart: 20, of which 10 were waited for; matrix products, arithmetic and copies ran while one was open for 2% of the time, Pallas kernels for 14%

profile of v7, /device:TPU:0, one launch (start us, length us, event | category | flops | bytes accessed | tf_op | source)
XLA Modules:
  0.0 496.8 jit_solution(15446858739974093251)
XLA Ops:
  1.4 5.4 %shard_map.138 = bf16[8,35,32,128]{3,2,1,0:T(8,128)(2,1)} custom-call(s32[1]{0:T(128)} %bitcast.place_ref, bf16[32,128,768]{2,1,0:T(8,128)(2,1)} %bitcast.20, bf16[32,128,768]{2,1,0:T(8,128)(2,1)} %bitcast.23, f32[32,128]{1,0:T(8,128)S(1)} %copy-done.25), custom_call_target="tpu_custom_call" | custom-call | flops 1 | bytes 8388608 | tf_op jit(solution)/shard_map/pallas_call | solution.py:83
  6.7 6.3 %all-to-all-start.1 = ((bf16[8,35,32,128]{3,2,1,0:T(8,128)(2,1)}), bf16[8,35,32,128]{3,2,1,0:T(8,128)(2,1)S(1)}, u32[]{:S(2)}, u32[]{:S(2)}) async-start(bf16[8,35,32,128]{3,2,1,0:T(8,128)(2,1)} %shard_map.138), calls=%async_computation.1 | async-start | bytes 4587520 | tf_op jit(solution)/shard_map/all_to_all | solution.py:318
  13.1 11.7 %shard_map.136 = (bf16[96,32,128]{2,1,0:T(8,128)(2,1)S(1)}, bf16[96,32,128]{2,1,0:T(8,128)(2,1)S(1)}, bf16[96,32,128]{2,1,0:T(8,128)(2,1)S(1)}, bf16[96,32,128]{...) custom-call(s32[1]{0:T(128)} %bitcast.place_ref, ...), custom_call_target="tpu_custom_call" | custom-call | flops 1 | bytes 25165824 | tf_op jit(solution)/shard_map/pallas_call | solution.py:83
  26.1 1.7 collective-permute-start.1
  27.8 2.2 collective-permute-start.2
  32.5 7.8 %shard_map.135.refs_0_ = bf16[8,64,32,128]{3,2,1,0:T(8,128)(2,1)S(1)} custom-call(s32[1]{0:T(128)} %bitcast.place_ref, bf16[32,128,768]{2,1,0:T(8,128)(2,1)} %bitcast.22, bf16[32,128,768]{2,1,0:T(8,128)(2,1)} %bitcast.25), custom_call_target="tpu_custom_call" | custom-call | flops 1 | bytes 16777216 | tf_op jit(solution)/shard_map/pallas_call | solution.py:83
  40.4 2.0 copy-done
  42.4 29.1 %collective-permute-done.refs_1_.rest_1_.rest_9_ = bf16[96,32,128]{2,1,0:T(8,128)(2,1)S(1)} collective-permute-done((bf16[96,32,128]{2,1,0:T(8,128)(2,1)S(1)}, bf16[96,32,128]{2,1,0:T(8,128)(2,1)S(1)}, u32[]{:S(2)}, u32[]{:S(2)}) %collective-permute-start) | collective-permute-done | bytes 786464 | tf_op jit(solution)/shard_map/ppermute | solution.py:322
  72.4 77.7 %collective-permute-done.2.refs_3_.rest_3_.rest_11_ = bf16[96,32,128]{2,1,0:T(8,128)(2,1)S(1)} collective-permute-done((bf16[96,32,128]{2,1,0:T(8,128)(2,1)S(1)}, bf16[96,32,128]{2,1,0:T(8,128)(2,1)S(1)}, u32[]{:S(2)}, u32[]{:S(2)}) %collective-permute-start.2) | collective-permute-done | bytes 786464 | tf_op jit(solution)/shard_map/ppermute | solution.py:322
  152.1 26.9 %all-to-all-start = ((bf16[8,64,32,128]{3,2,1,0:T(8,128)(2,1)}), bf16[8,64,32,128]{3,2,1,0:T(8,128)(2,1)}, u32[]{:S(2)}, u32[]{:S(2)}) async-start(bf16[8,64,32,128]{3,2,1,0:T(8,128)(2,1)} %shard_map.137), calls=%async_computation | async-start | bytes 8388608 | tf_op jit(solution)/shard_map/all_to_all | solution.py:318
  179.0 3.8 collective-permute-start.5
  183.9 80.6 %collective-permute-done.5.rest_6_.rest_14_ = bf16[96,32,128]{2,1,0:T(8,128)(2,1)} collective-permute-done((bf16[96,32,128]{2,1,0:T(8,128)(2,1)}, bf16[96,32,128]{2,1,0:T(8,128)(2,1)}, u32[]{:S(2)}, u32[]{:S(2)}) %collective-permute-start.5) | collective-permute-done | bytes 786464 | tf_op jit(solution)/shard_map/ppermute | solution.py:322
  264.5 8.4 %collective-permute-done.6.rest_7_.rest_15_ = bf16[96,32,128]{2,1,0:T(8,128)(2,1)} collective-permute-done((bf16[96,32,128]{2,1,0:T(8,128)(2,1)}, bf16[96,32,128]{2,1,0:T(8,128)(2,1)}, u32[]{:S(2)}, u32[]{:S(2)}) %collective-permute-start.6) | collective-permute-done | bytes 786464 | tf_op jit(solution)/shard_map/ppermute | solution.py:322
  277.0 20.2 %shard_map.139 = (bf16[48,32,128]{2,1,0:T(8,128)(2,1)S(1)}, bf16[48,32,128]{2,1,0:T(8,128)(2,1)}, bf16[48,32,128]{2,1,0:T(8,128)(2,1)}, bf16[48,32,128]{2,1,0:T(...) custom-call(s32[1]{0:T(128)} %bitcast.place_ref, ...), custom_call_target="tpu_custom_call" | custom-call | flops 25165824000 | bytes 1024 | tf_op jit(solution)/shard_map/pallas_call | solution.py:222
  298.0 25.0 %collective-permute-start.10 = (bf16[48,32,128]{2,1,0:T(8,128)(2,1)S(1)}, bf16[48,32,128]{2,1,0:T(8,128)(2,1)S(1)}, u32[]{:S(2)}, u32[]{:S(2)}) collective-permute-start(bf16[48,32,128]{2,1,0:T(8,128)(2,1)S(1)} %get-tuple-element.39), channel_id=1, source_target_pairs={{0,4},{1,5},{2,6},{3,7},{4,0},{5,1},{6,2},{7,3},{8,12},{9,13},{10,... | collective-permute-start | bytes 1179656 | tf_op jit(solution)/shard_map/ppermute | solution.py:322
  323.6 3.4 collective-permute-start.7
  327.1 30.4 %collective-permute-done.10.rest_10_.rest_4_ = bf16[48,32,128]{2,1,0:T(8,128)(2,1)S(1)} collective-permute-done((bf16[48,32,128]{2,1,0:T(8,128)(2,1)S(1)}, bf16[48,32,128]{2,1,0:T(8,128)(2,1)S(1)}, u32[]{:S(2)}, u32[]{:S(2)}) %collective-permute-start.10) | collective-permute-done | bytes 393248 | tf_op jit(solution)/shard_map/ppermute | solution.py:322
  359.0 6.2 %shard_map.141 = (bf16[8,16,32,128]{3,2,1,0:T(8,128)(2,1)S(1)}, f32[928,128]{1,0:T(8,128)S(1)}) custom-call(s32[1]{0:T(128)} %bitcast.place_ref, f32[768]{0:T(1024)S(1)} %copy-done.28, f32[768]{0:T(1024)S(1)} %copy-done.29, f32[768]{0:T(1024)S(1)} %copy-done.30, bf16[8,35,32,128]{3,2,1,0:T(8,128)(2,1)S(1)} %all-to-all-done.1.rest_0_.rest_1_, ...), custom_call_target="tpu_custom_call" | custom-call | flops 8388608000 | bytes 1024 | tf_op jit(solution)/shard_map/pallas_call | solution.py:222
  367.1 4.5 all-to-all-start.3
  378.8 13.7 %shard_map.140 = (bf16[8,32,32,128]{3,2,1,0:T(8,128)(2,1)S(1)}, f32[928,128]{1,0:T(8,128)S(1)}) custom-call(s32[1]{0:T(128)} %bitcast.place_ref, f32[768]{0:T(1024)S(1)} %copy-done.28, f32[768]{0:T(1024)S(1)} %copy-done.29, f32[768]{0:T(1024)S(1)} %copy-done.30, bf16[8,64,32,128]{3,2,1,0:T(8,128)(2,1)} %all-to-all-done.rest_0_.rest_1_, ...), custom_call_target="tpu_custom_call" | custom-call | flops 16777216000 | bytes 1024 | tf_op jit(solution)/shard_map/pallas_call | solution.py:222
  394.7 10.6 %all-to-all-done.3.rest_0_ = bf16[8,16,32,128]{3,2,1,0:T(8,128)(2,1)S(1)} async-done(((bf16[8,16,32,128]{3,2,1,0:T(8,128)(2,1)}), bf16[8,16,32,128]{3,2,1,0:T(8,128)(2,1)S(1)}, u32[]{:S(2)}, u32[]{:S(2)}) %all-to-all-start.3) | async-done | bytes 1048608 | tf_op jit(solution)/shard_map/all_to_all | solution.py:318
  405.3 16.5 %all-to-all-start.2 = ((bf16[8,32,32,128]{3,2,1,0:T(8,128)(2,1)}), bf16[8,32,32,128]{3,2,1,0:T(8,128)(2,1)S(1)}, u32[]{:S(2)}, u32[]{:S(2)}) async-start(bf16[8,32,32,128]{3,2,1,0:T(8,128)(2,1)} %copy-done.1), calls=%async_computation.2 | async-start | bytes 4194304 | tf_op jit(solution)/shard_map/all_to_all | solution.py:318
  421.7 2.1 shard_map.144
  423.9 1.8 slice_select_fusion
  425.6 1.5 collective-permute-start.14
  427.2 6.1 %collective-permute-done.14 = f32[464,128]{1,0:T(8,128)} collective-permute-done((f32[464,128]{1,0:T(8,128)}, f32[464,128]{1,0:T(8,128)}, u32[]{:S(2)}, u32[]{:S(2)}) %collective-permute-start.14) | collective-permute-done | bytes 237600 | tf_op jit(solution)/shard_map/ppermute | solution.py:292
  435.8 1.5 collective-permute-start.15
  437.3 1.7 shard_map.142.rest_8_
  439.0 6.1 %shard_map.143.rest_1_ = bf16[32,128,768]{2,1,0:T(8,128)(2,1)} custom-call(s32[1]{0:T(128)} %bitcast.place_ref, bf16[48,32,128]{2,1,0:T(8,128)(2,1)S(1)} %get-tuple-element.44.rest_0_, bf16[48,32,128]{2,1,0:T(8,128)(2,1)} %collective-permute-done.7.rest_7_.rest_1_, ...), custom_call_target="tpu_custom_call", output_to_operand_aliasing={{}: (9, {})} | custom-call | flops 1 | bytes 12582912 | tf_op jit(solution)/shard_map/pallas_call | solution.py:117
  446.1 35.0 %all-gather = f32[1856,128]{1,0:T(8,128)S(1)} all-gather(f32[232,128]{1,0:T(8,128)S(1)} %select_add_fusion.1), channel_id=2, replica_groups=mesh['dp'=4,'ctx'=8] {'ctx'}, dimensions={0}, use_global_device_ids=true | all-gather | bytes 1069056 | tf_op jit(solution)/shard_map/all_gather | solution.py:293
  481.1 10.1 %all_gather.11.rest_2_ = f32[928,128]{1,0:T(8,128)S(1)} all-gather(f32[232,128]{1,0:T(8,128)S(1)} %reduce_sum.9), channel_id=1, replica_groups=mesh['dp'=4,'ctx'=8] {'dp'}, dimensions={0}, use_global_device_ids=true | all-gather | bytes 593920 | tf_op jit(solution)/shard_map/all_gather | solution.py:294
  493.9 3.0 shard_map.145
  (110 shorter events, 32.8 us)
Async XLA Ops:
  6.7 145.3 %all-to-all-start.1 = ((bf16[8,35,32,128]{3,2,1,0:T(8,128)(2,1)}), bf16[8,35,32,128]{3,2,1,0:T(8,128)(2,1)S(1)}, u32[]{:S(2)}, u32[]{:S(2)}) async-start(bf16[8,35,32,128]{3,2,1,0:T(8,128)(2,1)} %shard_map.138), calls=%async_computation.1 | async-start | bytes 4587520 | tf_op jit(solution)/shard_map/all_to_all | solution.py:318
  25.6 45.8 %collective-permute-start = (bf16[96,32,128]{2,1,0:T(8,128)(2,1)S(1)}, bf16[96,32,128]{2,1,0:T(8,128)(2,1)S(1)}, u32[]{:S(2)}, u32[]{:S(2)}) collective-permute-start(bf16[96,32,128]{2,1,0:T(8,128)(2,1)S(1)} %get-tuple-element.28), channel_id=1, source_target_pairs={{0,1},{1,2},{2,3},{3,4},{4,5},{5,6},{6,7},{7,0},{8,9},{9,10},{10,1... | collective-permute-start | bytes 2359304 | tf_op jit(solution)/shard_map/ppermute | solution.py:322
  26.1 46.3 %collective-permute-start.1 = (bf16[96,32,128]{2,1,0:T(8,128)(2,1)S(1)}, bf16[96,32,128]{2,1,0:T(8,128)(2,1)S(1)}, u32[]{:S(2)}, u32[]{:S(2)}) collective-permute-start(bf16[96,32,128]{2,1,0:T(8,128)(2,1)S(1)} %get-tuple-element.29), channel_id=1, source_target_pairs={{0,2},{1,3},{2,4},{3,5},{4,6},{5,7},{6,0},{7,1},{8,10},{9,11},{10,... | collective-permute-start | bytes 2359304 | tf_op jit(solution)/shard_map/ppermute | solution.py:322
  27.8 122.4 %collective-permute-start.2 = (bf16[96,32,128]{2,1,0:T(8,128)(2,1)S(1)}, bf16[96,32,128]{2,1,0:T(8,128)(2,1)S(1)}, u32[]{:S(2)}, u32[]{:S(2)}) collective-permute-start(bf16[96,32,128]{2,1,0:T(8,128)(2,1)S(1)} %get-tuple-element.30), channel_id=1, source_target_pairs={{0,3},{1,4},{2,5},{3,6},{4,7},{5,0},{6,1},{7,2},{8,11},{9,12},{10,... | collective-permute-start | bytes 2359304 | tf_op jit(solution)/shard_map/ppermute | solution.py:322
  30.0 121.1 %collective-permute-start.3 = (bf16[96,32,128]{2,1,0:T(8,128)(2,1)S(1)}, bf16[96,32,128]{2,1,0:T(8,128)(2,1)S(1)}, u32[]{:S(2)}, u32[]{:S(2)}) collective-permute-start(bf16[96,32,128]{2,1,0:T(8,128)(2,1)S(1)} %get-tuple-element.31), channel_id=1, source_target_pairs={{0,4},{1,5},{2,6},{3,7},{4,0},{5,1},{6,2},{7,3},{8,12},{9,13},{10,... | collective-permute-start | bytes 2359304 | tf_op jit(solution)/shard_map/ppermute | solution.py:322
  31.5 120.5 %collective-permute-start.4 = (bf16[96,32,128]{2,1,0:T(8,128)(2,1)S(1)}, bf16[96,32,128]{2,1,0:T(8,128)(2,1)}, u32[]{:S(2)}, u32[]{:S(2)}) collective-permute-start(bf16[96,32,128]{2,1,0:T(8,128)(2,1)S(1)} %get-tuple-element.32), channel_id=1, source_target_pairs={{0,5},{1,6},{2,7},{3,0},{4,1},{5,2},{6,3},{7,4},{8,13},{9,14},{10,... | collective-permute-start | bytes 2359304 | tf_op jit(solution)/shard_map/ppermute | solution.py:322
  40.3 2.0 copy-start
  71.5 80.5 %copy-start.3 = (bf16[96,32,128]{2,1,0:T(8,128)(2,1)}, bf16[96,32,128]{2,1,0:T(8,128)(2,1)S(1)}, u32[]{:S(2)}) copy-start(bf16[96,32,128]{2,1,0:T(8,128)(2,1)S(1)} %collective-permute-done.refs_1_.rest_1_.rest_9_) | copy-start | bytes 2359300
  72.4 78.7 %copy-start.33 = (bf16[96,32,128]{2,1,0:T(8,128)(2,1)}, bf16[96,32,128]{2,1,0:T(8,128)(2,1)S(1)}, u32[]{:S(2)}) copy-start(bf16[96,32,128]{2,1,0:T(8,128)(2,1)S(1)} %collective-permute-done.1.refs_2_.rest_2_.rest_10_) | copy-start | bytes 2359300
  152.0 30.8 %copy-start.36 = (bf16[128,128]{1,0:T(8,128)(2,1)S(1)}, bf16[128,128]{1,0:T(8,128)(2,1)}, u32[]{:S(2)}) copy-start(bf16[128,128]{1,0:T(8,128)(2,1)} %param.11) | copy-start | bytes 98308
  152.0 31.0 %copy-start.14 = (bf16[256,256]{1,0:T(8,128)(2,1)S(1)}, bf16[256,256]{1,0:T(8,128)(2,1)}, u32[]{:S(2)}) copy-start(bf16[256,256]{1,0:T(8,128)(2,1)} %rest_2_.3) | copy-start | bytes 393220
  152.0 120.9 %copy-start.28 = (f32[768]{0:T(1024)S(1)}, f32[768]{0:T(1024)}, u32[]{:S(2)}) copy-start(f32[768]{0:T(1024)} %gain_ref.5) | copy-start | bytes 9220
  152.0 120.9 %copy-start.29 = (f32[768]{0:T(1024)S(1)}, f32[768]{0:T(1024)}, u32[]{:S(2)}) copy-start(f32[768]{0:T(1024)} %bias_ref.5) | copy-start | bytes 9220
  152.0 120.9 %copy-start.30 = (f32[768]{0:T(1024)S(1)}, f32[768]{0:T(1024)}, u32[]{:S(2)}) copy-start(f32[768]{0:T(1024)} %skip_ref.5) | copy-start | bytes 9220
  152.1 215.0 %all-to-all-start = ((bf16[8,64,32,128]{3,2,1,0:T(8,128)(2,1)}), bf16[8,64,32,128]{3,2,1,0:T(8,128)(2,1)}, u32[]{:S(2)}, u32[]{:S(2)}) async-start(bf16[8,64,32,128]{3,2,1,0:T(8,128)(2,1)} %shard_map.137), calls=%async_computation | async-start | bytes 8388608 | tf_op jit(solution)/shard_map/all_to_all | solution.py:318
  179.0 85.5 %collective-permute-start.5 = (bf16[96,32,128]{2,1,0:T(8,128)(2,1)}, bf16[96,32,128]{2,1,0:T(8,128)(2,1)}, u32[]{:S(2)}, u32[]{:S(2)}) collective-permute-start(bf16[96,32,128]{2,1,0:T(8,128)(2,1)} %get-tuple-element.34), channel_id=1, source_target_pairs={{0,6},{1,7},{2,0},{3,1},{4,2},{5,3},{6,4},{7,5},{8,14},{9,15},{10,... | collective-permute-start | bytes 2359304 | tf_op jit(solution)/shard_map/ppermute | solution.py:322
  182.8 90.1 %collective-permute-start.6 = (bf16[96,32,128]{2,1,0:T(8,128)(2,1)}, bf16[96,32,128]{2,1,0:T(8,128)(2,1)}, u32[]{:S(2)}, u32[]{:S(2)}) collective-permute-start(bf16[96,32,128]{2,1,0:T(8,128)(2,1)} %get-tuple-element.35), channel_id=1, source_target_pairs={{0,7},{1,0},{2,1},{3,2},{4,3},{5,4},{6,5},{7,6},{8,15},{9,8},{10,9... | collective-permute-start | bytes 2359304 | tf_op jit(solution)/shard_map/ppermute | solution.py:322
  183.8 175.2 %copy-start.19 = (bf16[256,256]{1,0:T(8,128)(2,1)}, bf16[256,256]{1,0:T(8,128)(2,1)S(1)}, u32[]{:S(2)}) copy-start(bf16[256,256]{1,0:T(8,128)(2,1)S(1)} %get-tuple-element.54.rest_18_.rest_4_) | copy-start | bytes 393220
  183.8 175.2 %copy-start.21 = (bf16[256,256]{1,0:T(8,128)(2,1)}, bf16[256,256]{1,0:T(8,128)(2,1)S(1)}, u32[]{:S(2)}) copy-start(bf16[256,256]{1,0:T(8,128)(2,1)S(1)} %get-tuple-element.55.rest_19_.rest_5_) | copy-start | bytes 393220
  183.8 175.2 %copy-start.23 = (f32[8,1,32,128]{3,2,1,0:T(8,128)}, f32[8,1,32,128]{3,2,1,0:T(8,128)S(1)}, u32[]{:S(2)}) copy-start(f32[8,1,32,128]{3,2,1,0:T(8,128)S(1)} %slice_add_fusion) | copy-start | bytes 393220
  298.0 59.5 %collective-permute-start.10 = (bf16[48,32,128]{2,1,0:T(8,128)(2,1)S(1)}, bf16[48,32,128]{2,1,0:T(8,128)(2,1)S(1)}, u32[]{:S(2)}, u32[]{:S(2)}) collective-permute-start(bf16[48,32,128]{2,1,0:T(8,128)(2,1)S(1)} %get-tuple-element.39), channel_id=1, source_target_pairs={{0,4},{1,5},{2,6},{3,7},{4,0},{5,1},{6,2},{7,3},{8,12},{9,13},{10,... | collective-permute-start | bytes 1179656 | tf_op jit(solution)/shard_map/ppermute | solution.py:322
  323.0 35.2 %collective-permute-start.11 = (bf16[48,32,128]{2,1,0:T(8,128)(2,1)S(1)}, bf16[48,32,128]{2,1,0:T(8,128)(2,1)S(1)}, u32[]{:S(2)}, u32[]{:S(2)}) collective-permute-start(bf16[48,32,128]{2,1,0:T(8,128)(2,1)S(1)} %get-tuple-element.40), channel_id=1, source_target_pairs={{0,3},{1,4},{2,5},{3,6},{4,7},{5,0},{6,1},{7,2},{8,11},{9,12},{10,... | collective-permute-start | bytes 1179656 | tf_op jit(solution)/shard_map/ppermute | solution.py:322
  323.5 48.1 %collective-permute-start.12 = (bf16[48,32,128]{2,1,0:T(8,128)(2,1)}, bf16[48,32,128]{2,1,0:T(8,128)(2,1)}, u32[]{:S(2)}, u32[]{:S(2)}) collective-permute-start(bf16[48,32,128]{2,1,0:T(8,128)(2,1)} %get-tuple-element.41), channel_id=1, source_target_pairs={{0,2},{1,3},{2,4},{3,5},{4,6},{5,7},{6,0},{7,1},{8,10},{9,11},{10,... | collective-permute-start | bytes 1179656 | tf_op jit(solution)/shard_map/ppermute | solution.py:322
  323.5 48.1 %collective-permute-start.13 = (bf16[48,32,128]{2,1,0:T(8,128)(2,1)}, bf16[48,32,128]{2,1,0:T(8,128)(2,1)}, u32[]{:S(2)}, u32[]{:S(2)}) collective-permute-start(bf16[48,32,128]{2,1,0:T(8,128)(2,1)} %get-tuple-element.42), channel_id=1, source_target_pairs={{0,1},{1,2},{2,3},{3,4},{4,5},{5,6},{6,7},{7,0},{8,9},{9,10},{10,1... | collective-permute-start | bytes 1179656 | tf_op jit(solution)/shard_map/ppermute | solution.py:322
  323.6 47.9 %collective-permute-start.7 = (bf16[48,32,128]{2,1,0:T(8,128)(2,1)}, bf16[48,32,128]{2,1,0:T(8,128)(2,1)}, u32[]{:S(2)}, u32[]{:S(2)}) collective-permute-start(bf16[48,32,128]{2,1,0:T(8,128)(2,1)} %get-tuple-element.36), channel_id=1, source_target_pairs={{0,7},{1,0},{2,1},{3,2},{4,3},{5,4},{6,5},{7,6},{8,15},{9,8},{10,9... | collective-permute-start | bytes 1179656 | tf_op jit(solution)/shard_map/ppermute | solution.py:322
  358.2 13.3 %collective-permute-start.8 = (bf16[48,32,128]{2,1,0:T(8,128)(2,1)}, bf16[48,32,128]{2,1,0:T(8,128)(2,1)}, u32[]{:S(2)}, u32[]{:S(2)}) collective-permute-start(bf16[48,32,128]{2,1,0:T(8,128)(2,1)} %get-tuple-element.37), channel_id=1, source_target_pairs={{0,6},{1,7},{2,0},{3,1},{4,2},{5,3},{6,4},{7,5},{8,14},{9,15},{10,... | collective-permute-start | bytes 1179656 | tf_op jit(solution)/shard_map/ppermute | solution.py:322
  359.0 13.3 %collective-permute-start.9 = (bf16[48,32,128]{2,1,0:T(8,128)(2,1)}, bf16[48,32,128]{2,1,0:T(8,128)(2,1)}, u32[]{:S(2)}, u32[]{:S(2)}) collective-permute-start(bf16[48,32,128]{2,1,0:T(8,128)(2,1)} %get-tuple-element.38), channel_id=1, source_target_pairs={{0,5},{1,6},{2,7},{3,0},{4,1},{5,2},{6,3},{7,4},{8,13},{9,14},{10,... | collective-permute-start | bytes 1179656 | tf_op jit(solution)/shard_map/ppermute | solution.py:322
  367.1 38.2 %all-to-all-start.3 = ((bf16[8,16,32,128]{3,2,1,0:T(8,128)(2,1)}), bf16[8,16,32,128]{3,2,1,0:T(8,128)(2,1)S(1)}, u32[]{:S(2)}, u32[]{:S(2)}) async-start(bf16[8,16,32,128]{3,2,1,0:T(8,128)(2,1)} %copy-done.2), calls=%async_computation.3 | async-start | bytes 2097152 | tf_op jit(solution)/shard_map/all_to_all | solution.py:318
  405.3 88.6 %all-to-all-start.2 = ((bf16[8,32,32,128]{3,2,1,0:T(8,128)(2,1)}), bf16[8,32,32,128]{3,2,1,0:T(8,128)(2,1)S(1)}, u32[]{:S(2)}, u32[]{:S(2)}) async-start(bf16[8,32,32,128]{3,2,1,0:T(8,128)(2,1)} %copy-done.1), calls=%async_computation.2 | async-start | bytes 4194304 | tf_op jit(solution)/shard_map/all_to_all | solution.py:318
  425.6 7.6 %collective-permute-start.14 = (f32[464,128]{1,0:T(8,128)}, f32[464,128]{1,0:T(8,128)}, u32[]{:S(2)}, u32[]{:S(2)}) collective-permute-start(f32[464,128]{1,0:T(8,128)} %slice_select_fusion), channel_id=1, source_target_pairs={{0,16},{8,24},{16,0},{24,8},{1,17},{9,25},{17,1},{25,9},{2,18},{10... | collective-permute-start | bytes 712712 | tf_op jit(solution)/shard_map/ppermute | solution.py:292
  435.8 9.3 %collective-permute-start.15 = (f32[232,128]{1,0:T(8,128)}, f32[232,128]{1,0:T(8,128)}, u32[]{:S(2)}, u32[]{:S(2)}) collective-permute-start(f32[232,128]{1,0:T(8,128)} %slice_select_fusion.1), channel_id=1, source_target_pairs={{0,8},{8,0},{16,24},{24,16},{1,9},{9,1},{17,25},{25,17},{2,10},{10... | collective-permute-start | bytes 356360 | tf_op jit(solution)/shard_map/ppermute | solution.py:292
  439.0 6.1 %copy-start.32 = (f32[464,128]{1,0:T(8,128)S(1)}, f32[464,128]{1,0:T(8,128)}, u32[]{:S(2)}) copy-start(f32[464,128]{1,0:T(8,128)} %copy-done.31) | copy-start | bytes 712708
  (25 other events, 24.4 us)

commit v8 on v7

--- a/solution.py
+++ b/solution.py
@@ -11,6 +11,7 @@
 A = 256
 B = 128
 LANES = 128
+RETURN_FIRST = 4
 VMEM_BYTES = 48 * 1024 * 1024
 
 
@@ -240,22 +241,22 @@
     return leaving, sums
 
 
-def add_kernel(*refs):
+def add_kernel(*refs, count):
     total = refs[0][...]
-    for ref in refs[1:-1]:
+    for ref in refs[1:count]:
         total += ref[...]
     refs[-1][...] = total
 
 
-def add(terms):
+def add(terms, after):
     vmem = pl.BlockSpec(memory_space=pltpu.VMEM)
     return pl.pallas_call(
-        add_kernel,
-        in_specs=[vmem] * len(terms),
+        functools.partial(add_kernel, count=len(terms)),
+        in_specs=[vmem] * len(terms) + [pl.BlockSpec(memory_space=pl.ANY)] * len(after),
         out_specs=vmem,
         out_shape=jax.ShapeDtypeStruct(terms[0].shape, terms[0].dtype),
         cost_estimate=pl.CostEstimate(flops=1, bytes_accessed=1024, transcendentals=0),
-    )(*terms)
+    )(*terms, *after)
 
 
 def hold(arrays, after):
@@ -302,9 +303,7 @@
     local_rows = tok_rows // B
     tiles = width // LANES
     pair = 2
-    half = tiles // 2
-    groups = [(0, 1, False), (half, tiles - half, True), (1, half - 1, False)]
-    merge_order = [0, 1, 2]
+    groups = [(0, 1, False), (1, tiles - 2, True), (tiles - 1, 1, False)]
 
     place = (lax.axis_index("ctx") * share).astype(jnp.int32).reshape(1)
     second = block_diagonal(second_factor, pair)
@@ -327,42 +326,36 @@
     for seq in range(seq_count):
         tok_blocks = tokens[seq].reshape(local_rows, B, width)
         cot_blocks = cotangent[seq].reshape(local_rows, B, width)
-        arrived = []
+        split = []
         for at, count, rotated in groups:
             own = twiddle if at == 0 else None
-            parts = split_channels(
-                place, tok_blocks, cot_blocks, at, count, ctx_size, rotated, own
+            split.append(
+                split_channels(place, tok_blocks, cot_blocks, at, count, ctx_size, rotated, own)
             )
-            if len(arrived) == 2:
-                parts = hold(parts, arrived[1][1:6])
-            arrived.append(exchange(parts, 1, rotated))
-        planes = [part[..., 2 * share :, :, :].astype(jnp.float32) for part in arrived[0]]
-        planes = jnp.stack(planes).reshape(ctx_size, 3, local_rows, B)
-        twiddle_all = planes[:, 0] + planes[:, 1] + planes[:, 2]
-        if groups[0][2]:
-            twice = jnp.concatenate([twiddle_all[::-1]] * 2, axis=0)
-            turn = ctx_size - 1 - lax.axis_index("ctx")
-            twiddle_all = lax.dynamic_slice_in_dim(twice, turn, ctx_size, 0)
-        twiddle_all = twiddle_all.reshape(A, B)
+        arrived = [exchange(split[0], 1, False), exchange(split[1], 1, True)]
+        planes = arrived[0][0][:, 2 * share :].astype(jnp.float32)
+        twiddle_all = (planes[:, 0] + planes[:, 1] + planes[:, 2]).reshape(A, B)
         factors = [first_factor, first_factor.T, second, second_t, twiddle_all]
         returned = []
-        for which, ((at, count, rotated), parts) in enumerate(zip(groups, arrived)):
-            after = returned[1][1:] if which == 2 else []
+        for which, (at, count, rotated) in enumerate(groups):
+            if which == 2:
+                parts = hold(split[2], returned[0] + arrived[1][1:])
+                arrived.append(exchange(parts, 1, rotated))
             parts, own_sums = mix(
-                parts, at, count, 2 * share, place, vectors, factors, sum_rows, ctx_size, rotated,
-                after,
+                arrived[which], at, count, 2 * share, place, vectors, factors, sum_rows, ctx_size,
+                rotated, [],
             )
             returned.append(exchange(parts, -1, rotated))
             terms.append(own_sums)
         leaving.append(returned)
 
-    sums = sum_over_mesh(add(terms))
+    begun = [part for returned in leaving for part in returned[1][1:RETURN_FIRST]]
+    sums = sum_over_mesh(add(terms, begun))
     grads = []
     for returned in leaving:
         held = None
-        for which in merge_order:
-            at, count, rotated = groups[which]
-            after = [sums] if which == merge_order[-1] else []
+        for which, (at, count, rotated) in enumerate(groups):
+            after = [sums] if which == 2 else []
             held = merge_channels(
                 place, returned[which], held, at, count, ctx_size, rotated, width, after
             )

time: 500 us -> 493 us (0.986)
  blocking collectives: 45.2 us -> 26.4 us
  starting transfers between devices: 97 us -> 114 us
  local copies, waits for them, and re-layouts: 22.9 us -> 14 us
  waiting for transfers between devices: 246 us -> 251 us
    all_to_all x4, waiting for transfers between devices: 10.6 us -> 83.5 us  [exchange(): lax.all_to_all(parts[0], 'ctx', split_axis=0, concat_axis=0, tiled=True)]
    ppermute x14, waiting for transfers between devices: 229 us -> 168 us  [exchange(): moved.append(lax.ppermute(parts[shift], 'ctx', pairs))]
    all_gather x1, blocking collectives: 35 us -> 16.3 us  [sum_over_mesh(): sums = jnp.sum(lax.all_gather(sums, 'ctx'), axis=0)]
    all_to_all x4, starting transfers between devices: 54.2 us -> 72.1 us  [exchange(): lax.all_to_all(parts[0], 'ctx', split_axis=0, concat_axis=0, tiled=True)]
    unnamed x76 -> x62, local copies, waits for them, and re-layouts: 22.9 us -> 14 us
    ppermute x2, waiting for transfers between devices: 6.08 us -> 0.01 us  [sum_over_mesh(): sums = kept + lax.ppermute(sent, 'dp', [(i, i ^ bit) for i in range(size)])]
  transfers between devices with their start and end apart: 20 -> 20, of which waited for: 10 -> 9; matrix products, arithmetic and copies ran while one was open for 2% -> 1% of each run, Pallas kernels for 14% -> 14%
where the time goes in v8:
time: 493 us; the launch traced here: 489 us
  waiting for transfers between devices  251 us (51%)
  starting transfers between devices  114 us (23%)
  Pallas kernels  77.6 us (16%)
  blocking collectives  26.4 us (5%)
  local copies, waits for them, and re-layouts  14 us (3%)
  other arithmetic  5.77 us (1%)
    ppermute x14, waiting for transfers between devices, exchange(): moved.append(lax.ppermute(parts[shift], 'ctx', pairs))  168 us
    all_to_all x4, waiting for transfers between devices, exchange(): lax.all_to_all(parts[0], 'ctx', split_axis=0, concat_axis=0, tiled=True)  83.5 us
    all_to_all x4, starting transfers between devices, exchange(): lax.all_to_all(parts[0], 'ctx', split_axis=0, concat_axis=0, tiled=True)  72.1 us
    pallas_call x3, Pallas kernels, mix(): pl.pallas_call(functools.partial(mix_kernel, parts=len(parts), tile=tile,...  39.7 us
    ppermute x14, starting transfers between devices, exchange(): moved.append(lax.ppermute(parts[shift], 'ctx', pairs))  38.5 us
    pallas_call x3, Pallas kernels, split_channels(): pl.pallas_call(functools.partial(kernel, rotated=rotated), grid=(tiles, r...  24.8 us
    all_gather x1, blocking collectives, sum_over_mesh(): sums = jnp.sum(lax.all_gather(sums, 'ctx'), axis=0)  16.3 us
    unnamed x62, local copies, waits for them, and re-layouts  14 us
  transfers between devices with their start and end apart: 20, of which 9 were waited for; matrix products, arithmetic and copies ran while one was open for 1% of the time, Pallas kernels for 14%

profile of v8, /device:TPU:0, one launch (start us, length us, event | category | flops | bytes accessed | tf_op | source)
XLA Modules:
  0.0 489.5 jit_solution(9172560607234632877)
XLA Ops:
  1.4 5.3 %shard_map.136 = bf16[8,35,32,128]{3,2,1,0:T(8,128)(2,1)} custom-call(s32[1]{0:T(128)} %bitcast.place_ref, bf16[32,128,768]{2,1,0:T(8,128)(2,1)} %bitcast.21, bf16[32,128,768]{2,1,0:T(8,128)(2,1)} %bitcast.24, f32[32,128]{1,0:T(8,128)S(1)} %copy-done.18), custom_call_target="tpu_custom_call" | custom-call | flops 1 | bytes 8388608 | tf_op jit(solution)/shard_map/pallas_call | solution.py:84
  6.7 6.3 %all-to-all-start = ((bf16[8,35,32,128]{3,2,1,0:T(8,128)(2,1)}), bf16[8,35,32,128]{3,2,1,0:T(8,128)(2,1)S(1)}, u32[]{:S(2)}, u32[]{:S(2)}) async-start(bf16[8,35,32,128]{3,2,1,0:T(8,128)(2,1)} %shard_map.136), calls=%async_computation | async-start | bytes 4587520 | tf_op jit(solution)/shard_map/all_to_all | solution.py:317
  13.1 14.9 %shard_map.138 = (bf16[128,32,128]{2,1,0:T(8,128)(2,1)S(1)}, bf16[128,32,128]{2,1,0:T(8,128)(2,1)}, bf16[128,32,128]{2,1,0:T(8,128)(2,1)}, bf16[128,32,128]{2,1,...) custom-call(s32[1]{0:T(128)} %bitcast.place_ref, ...), custom_call_target="tpu_custom_call" | custom-call | flops 1 | bytes 33554432 | tf_op jit(solution)/shard_map/pallas_call | solution.py:84
  31.4 1.7 collective-permute-start.1
  33.4 66.6 %all-to-all-done.rest_0_.rest_1_ = bf16[8,35,32,128]{3,2,1,0:T(8,128)(2,1)S(1)} async-done(((bf16[8,35,32,128]{3,2,1,0:T(8,128)(2,1)}), bf16[8,35,32,128]{3,2,1,0:T(8,128)(2,1)S(1)}, u32[]{:S(2)}, u32[]{:S(2)}) %all-to-all-start) | async-done | bytes 2293792 | tf_op jit(solution)/shard_map/all_to_all | solution.py:317
  100.1 6.9 %shard_map.137 = (bf16[8,16,32,128]{3,2,1,0:T(8,128)(2,1)}, f32[928,128]{1,0:T(8,128)S(1)}) custom-call(s32[1]{0:T(128)} %bitcast.place_ref, f32[768]{0:T(1024)S(1)} %copy-done.22, f32[768]{0:T(1024)S(1)} %copy-done.23, f32[768]{0:T(1024)S(1)} %copy-done.24, bf16[8,35,32,128]{3,2,1,0:T(8,128)(2,1)S(1)} %all-to-all-done.rest_0_.rest_1_, ...), custom_call_target="tpu_custom_call" | custom-call | flops 8388608000 | bytes 1024 | tf_op jit(solution)/shard_map/pallas_call | solution.py:223
  107.8 3.6 all-to-all-start.1
  111.4 1.7 collective-permute-start.2
  113.1 2.4 collective-permute-start.3
  118.2 4.5 shard_map.135.refs_0_
  124.0 92.1 %collective-permute-done.2.refs_4_.rest_3_.rest_11_ = bf16[128,32,128]{2,1,0:T(8,128)(2,1)S(1)} collective-permute-done((bf16[128,32,128]{2,1,0:T(8,128)(2,1)}, bf16[128,32,128]{2,1,0:T(8,128)(2,1)S(1)}, u32[]{:S(2)}, u32[]{:S(2)}) %collective-permute-start.2) | collective-permute-done | bytes 1048608 | tf_op jit(solution)/shard_map/ppermute | solution.py:321
  217.0 2.3 collective-permute-done.5.refs_7_.rest_6_.rest_14_
  220.4 10.2 %collective-permute-done.6.refs_8_.rest_7_.rest_15_ = bf16[128,32,128]{2,1,0:T(8,128)(2,1)} collective-permute-done((bf16[128,32,128]{2,1,0:T(8,128)(2,1)}, bf16[128,32,128]{2,1,0:T(8,128)(2,1)}, u32[]{:S(2)}, u32[]{:S(2)}) %collective-permute-start.6) | collective-permute-done | bytes 1048608 | tf_op jit(solution)/shard_map/ppermute | solution.py:321
  231.6 57.4 %all-to-all-start.2 = ((bf16[8,32,32,128]{3,2,1,0:T(8,128)(2,1)}), bf16[8,32,32,128]{3,2,1,0:T(8,128)(2,1)S(1)}, u32[]{:S(2)}, u32[]{:S(2)}) async-start(bf16[8,32,32,128]{3,2,1,0:T(8,128)(2,1)} %shard_map.139), calls=%async_computation.2 | async-start | bytes 4194304 | tf_op jit(solution)/shard_map/all_to_all | solution.py:317
  289.0 27.0 %shard_map.141 = (bf16[64,32,128]{2,1,0:T(8,128)(2,1)S(1)}, bf16[64,32,128]{2,1,0:T(8,128)(2,1)}, bf16[64,32,128]{2,1,0:T(8,128)(2,1)}, bf16[64,32,128]{2,1,0:T(...) custom-call(s32[1]{0:T(128)} %bitcast.place_ref, ...), custom_call_target="tpu_custom_call" | custom-call | flops 33554432000 | bytes 1024 | tf_op jit(solution)/shard_map/pallas_call | solution.py:223
  317.6 3.6 collective-permute-start.7
  321.7 16.8 %all-to-all-done.2.rest_0_.rest_1_ = bf16[8,32,32,128]{3,2,1,0:T(8,128)(2,1)S(1)} async-done(((bf16[8,32,32,128]{3,2,1,0:T(8,128)(2,1)}), bf16[8,32,32,128]{3,2,1,0:T(8,128)(2,1)S(1)}, u32[]{:S(2)}, u32[]{:S(2)}) %all-to-all-start.2) | async-done | bytes 2097184 | tf_op jit(solution)/shard_map/all_to_all | solution.py:317
  340.4 5.8 %shard_map.140 = (bf16[8,16,32,128]{3,2,1,0:T(8,128)(2,1)S(1)}, f32[928,128]{1,0:T(8,128)S(1)}) custom-call(s32[1]{0:T(128)} %bitcast.place_ref, f32[768]{0:T(1024)S(1)} %copy-done.22, f32[768]{0:T(1024)S(1)} %copy-done.23, f32[768]{0:T(1024)S(1)} %copy-done.24, bf16[8,32,32,128]{3,2,1,0:T(8,128)(2,1)S(1)} %all-to-all-done.2.rest_0_.rest_1_, ...), custom_call_target="tpu_custom_call" | custom-call | flops 8388608000 | bytes 1024 | tf_op jit(solution)/shard_map/pallas_call | solution.py:223
  347.9 4.2 collective-permute-done.8.rest_2_.refs_4_
  352.9 2.2 shard_map.144
  356.2 1.6 collective-permute-start.14
  357.8 18.6 %collective-permute-start.10 = (bf16[64,32,128]{2,1,0:T(8,128)(2,1)}, bf16[64,32,128]{2,1,0:T(8,128)(2,1)S(1)}, u32[]{:S(2)}, u32[]{:S(2)}) collective-permute-start(bf16[64,32,128]{2,1,0:T(8,128)(2,1)} %get-tuple-element.42), channel_id=1, source_target_pairs={{0,4},{1,5},{2,6},{3,7},{4,0},{5,1},{6,2},{7,3},{8,12},{9,13},{10,... | collective-permute-start | bytes 1572872 | tf_op jit(solution)/shard_map/ppermute | solution.py:321
  376.4 5.9 %collective-permute-start.11 = (bf16[64,32,128]{2,1,0:T(8,128)(2,1)}, bf16[64,32,128]{2,1,0:T(8,128)(2,1)S(1)}, u32[]{:S(2)}, u32[]{:S(2)}) collective-permute-start(bf16[64,32,128]{2,1,0:T(8,128)(2,1)} %get-tuple-element.43), channel_id=1, source_target_pairs={{0,3},{1,4},{2,5},{3,6},{4,7},{5,0},{6,1},{7,2},{8,11},{9,12},{10,... | collective-permute-start | bytes 1572872 | tf_op jit(solution)/shard_map/ppermute | solution.py:321
  383.2 4.8 all-to-all-start.3
  389.9 1.5 collective-permute-start.15
  391.4 1.7 shard_map.142.rest_8_
  393.2 39.2 %collective-permute-done.10.rest_4_ = bf16[64,32,128]{2,1,0:T(8,128)(2,1)S(1)} collective-permute-done((bf16[64,32,128]{2,1,0:T(8,128)(2,1)}, bf16[64,32,128]{2,1,0:T(8,128)(2,1)S(1)}, u32[]{:S(2)}, u32[]{:S(2)}) %collective-permute-start.10) | collective-permute-done | bytes 524320 | tf_op jit(solution)/shard_map/ppermute | solution.py:321
  432.4 18.8 %collective-permute-done.11.rest_5_ = bf16[64,32,128]{2,1,0:T(8,128)(2,1)S(1)} collective-permute-done((bf16[64,32,128]{2,1,0:T(8,128)(2,1)}, bf16[64,32,128]{2,1,0:T(8,128)(2,1)S(1)}, u32[]{:S(2)}, u32[]{:S(2)}) %collective-permute-start.11) | collective-permute-done | bytes 524320 | tf_op jit(solution)/shard_map/ppermute | solution.py:321
  451.2 7.5 %shard_map.143.rest_1_ = bf16[32,128,768]{2,1,0:T(8,128)(2,1)} custom-call(s32[1]{0:T(128)} %bitcast.place_ref, bf16[64,32,128]{2,1,0:T(8,128)(2,1)S(1)} %copy-done.9, bf16[64,32,128]{2,1,0:T(8,128)(2,1)S(1)} %copy-done.4, bf16[64,32,128]{2,1,0:T(8,128)(2,1)S(1)} %copy-done.6, ...), custom_call_target="tpu_custom_call", output_to_operand_aliasing={{}: (9, {})} | custom-call | flops 1 | bytes 16777216 | tf_op jit(solution)/shard_map/pallas_call | solution.py:118
  458.7 16.3 %all-gather = f32[1856,128]{1,0:T(8,128)S(1)} all-gather(f32[232,128]{1,0:T(8,128)S(1)} %select_add_fusion.1), channel_id=2, replica_groups=mesh['dp'=4,'ctx'=8] {'ctx'}, dimensions={0}, use_global_device_ids=true | all-gather | bytes 1069056 | tf_op jit(solution)/shard_map/all_gather | solution.py:294
  475.1 10.1 %all_gather.11.rest_2_ = f32[928,128]{1,0:T(8,128)S(1)} all-gather(f32[232,128]{1,0:T(8,128)S(1)} %reduce_sum.9), channel_id=1, replica_groups=mesh['dp'=4,'ctx'=8] {'dp'}, dimensions={0}, use_global_device_ids=true | all-gather | bytes 593920 | tf_op jit(solution)/shard_map/all_gather | solution.py:295
  487.8 1.7 shard_map.145
  (96 shorter events, 25.4 us)
Async XLA Ops:
  6.7 93.3 %all-to-all-start = ((bf16[8,35,32,128]{3,2,1,0:T(8,128)(2,1)}), bf16[8,35,32,128]{3,2,1,0:T(8,128)(2,1)S(1)}, u32[]{:S(2)}, u32[]{:S(2)}) async-start(bf16[8,35,32,128]{3,2,1,0:T(8,128)(2,1)} %shard_map.136), calls=%async_computation | async-start | bytes 4587520 | tf_op jit(solution)/shard_map/all_to_all | solution.py:317
  13.0 20.1 %copy-start.29 = (bf16[128,128]{1,0:T(8,128)(2,1)S(1)}, bf16[128,128]{1,0:T(8,128)(2,1)}, u32[]{:S(2)}) copy-start(bf16[128,128]{1,0:T(8,128)(2,1)} %param.11) | copy-start | bytes 98308
  13.0 20.2 %copy-start.13 = (bf16[256,256]{1,0:T(8,128)(2,1)S(1)}, bf16[256,256]{1,0:T(8,128)(2,1)}, u32[]{:S(2)}) copy-start(bf16[256,256]{1,0:T(8,128)(2,1)} %rest_16_.1) | copy-start | bytes 393220
  13.0 87.1 %copy-start.22 = (f32[768]{0:T(1024)S(1)}, f32[768]{0:T(1024)}, u32[]{:S(2)}) copy-start(f32[768]{0:T(1024)} %gain_ref.5) | copy-start | bytes 9220
  13.0 87.1 %copy-start.23 = (f32[768]{0:T(1024)S(1)}, f32[768]{0:T(1024)}, u32[]{:S(2)}) copy-start(f32[768]{0:T(1024)} %bias_ref.5) | copy-start | bytes 9220
  13.1 87.1 %copy-start.24 = (f32[768]{0:T(1024)S(1)}, f32[768]{0:T(1024)}, u32[]{:S(2)}) copy-start(f32[768]{0:T(1024)} %skip_ref.5) | copy-start | bytes 9220
  30.9 85.7 %collective-permute-start = (bf16[128,32,128]{2,1,0:T(8,128)(2,1)}, bf16[128,32,128]{2,1,0:T(8,128)(2,1)}, u32[]{:S(2)}, u32[]{:S(2)}) collective-permute-start(bf16[128,32,128]{2,1,0:T(8,128)(2,1)} %get-tuple-element.29), channel_id=1, source_target_pairs={{0,1},{1,2},{2,3},{3,4},{4,5},{5,6},{6,7},{7,0},{8,9},{9,10},{10,1... | collective-permute-start | bytes 3145736 | tf_op jit(solution)/shard_map/ppermute | solution.py:321
  31.4 86.6 %collective-permute-start.1 = (bf16[128,32,128]{2,1,0:T(8,128)(2,1)}, bf16[128,32,128]{2,1,0:T(8,128)(2,1)}, u32[]{:S(2)}, u32[]{:S(2)}) collective-permute-start(bf16[128,32,128]{2,1,0:T(8,128)(2,1)} %get-tuple-element.30), channel_id=1, source_target_pairs={{0,2},{1,3},{2,4},{3,5},{4,6},{5,7},{6,0},{7,1},{8,10},{9,11},{10,... | collective-permute-start | bytes 3145736 | tf_op jit(solution)/shard_map/ppermute | solution.py:321
  33.4 255.6 %copy-start.14 = (bf16[256,256]{1,0:T(8,128)(2,1)}, bf16[256,256]{1,0:T(8,128)(2,1)S(1)}, u32[]{:S(2)}) copy-start(bf16[256,256]{1,0:T(8,128)(2,1)S(1)} %get-tuple-element.55.rest_5_.rest_19_) | copy-start | bytes 393220
  100.1 188.9 %copy-start.16 = (f32[8,1,32,128]{3,2,1,0:T(8,128)}, f32[8,1,32,128]{3,2,1,0:T(8,128)S(1)}, u32[]{:S(2)}) copy-start(f32[8,1,32,128]{3,2,1,0:T(8,128)S(1)} %slice_add_fusion) | copy-start | bytes 393220
  107.8 122.7 %all-to-all-start.1 = ((bf16[8,16,32,128]{3,2,1,0:T(8,128)(2,1)}), bf16[8,16,32,128]{3,2,1,0:T(8,128)(2,1)S(1)}, u32[]{:S(2)}, u32[]{:S(2)}) async-start(bf16[8,16,32,128]{3,2,1,0:T(8,128)(2,1)} %get-tuple-element.28), calls=%async_computation.1 | async-start | bytes 2097152 | tf_op jit(solution)/shard_map/all_to_all | solution.py:317
  111.4 104.7 %collective-permute-start.2 = (bf16[128,32,128]{2,1,0:T(8,128)(2,1)}, bf16[128,32,128]{2,1,0:T(8,128)(2,1)S(1)}, u32[]{:S(2)}, u32[]{:S(2)}) collective-permute-start(bf16[128,32,128]{2,1,0:T(8,128)(2,1)} %copy-done.21), channel_id=1, source_target_pairs={{0,3},{1,4},{2,5},{3,6},{4,7},{5,0},{6,1},{7,2},{8,11},{9,12},{10,... | collective-permute-start | bytes 3145736 | tf_op jit(solution)/shard_map/ppermute | solution.py:321
  113.1 104.0 %collective-permute-start.3 = (bf16[128,32,128]{2,1,0:T(8,128)(2,1)}, bf16[128,32,128]{2,1,0:T(8,128)(2,1)S(1)}, u32[]{:S(2)}, u32[]{:S(2)}) collective-permute-start(bf16[128,32,128]{2,1,0:T(8,128)(2,1)} %copy-done.20), channel_id=1, source_target_pairs={{0,4},{1,5},{2,6},{3,7},{4,0},{5,1},{6,2},{7,3},{8,12},{9,13},{10,... | collective-permute-start | bytes 3145736 | tf_op jit(solution)/shard_map/ppermute | solution.py:321
  115.5 101.6 %collective-permute-start.4 = (bf16[128,32,128]{2,1,0:T(8,128)(2,1)}, bf16[128,32,128]{2,1,0:T(8,128)(2,1)S(1)}, u32[]{:S(2)}, u32[]{:S(2)}) collective-permute-start(bf16[128,32,128]{2,1,0:T(8,128)(2,1)} %get-tuple-element.33), channel_id=1, source_target_pairs={{0,5},{1,6},{2,7},{3,0},{4,1},{5,2},{6,3},{7,4},{8,13},{9,14},{10,... | collective-permute-start | bytes 3145736 | tf_op jit(solution)/shard_map/ppermute | solution.py:321
  116.6 102.7 %collective-permute-start.5 = (bf16[128,32,128]{2,1,0:T(8,128)(2,1)}, bf16[128,32,128]{2,1,0:T(8,128)(2,1)S(1)}, u32[]{:S(2)}, u32[]{:S(2)}) collective-permute-start(bf16[128,32,128]{2,1,0:T(8,128)(2,1)} %get-tuple-element.34), channel_id=1, source_target_pairs={{0,6},{1,7},{2,0},{3,1},{4,2},{5,3},{6,4},{7,5},{8,14},{9,15},{10,... | collective-permute-start | bytes 3145736 | tf_op jit(solution)/shard_map/ppermute | solution.py:321
  118.1 112.5 %collective-permute-start.6 = (bf16[128,32,128]{2,1,0:T(8,128)(2,1)}, bf16[128,32,128]{2,1,0:T(8,128)(2,1)}, u32[]{:S(2)}, u32[]{:S(2)}) collective-permute-start(bf16[128,32,128]{2,1,0:T(8,128)(2,1)} %get-tuple-element.35), channel_id=1, source_target_pairs={{0,7},{1,0},{2,1},{3,2},{4,3},{5,4},{6,5},{7,6},{8,15},{9,8},{10,9... | collective-permute-start | bytes 3145736 | tf_op jit(solution)/shard_map/ppermute | solution.py:321
  216.1 14.5 %copy-start.25 = (bf16[128,32,128]{2,1,0:T(8,128)(2,1)}, bf16[128,32,128]{2,1,0:T(8,128)(2,1)S(1)}, u32[]{:S(2)}) copy-start(bf16[128,32,128]{2,1,0:T(8,128)(2,1)S(1)} %collective-permute-done.2.refs_4_.rest_3_.rest_11_) | copy-start | bytes 3145732
  231.6 107.0 %all-to-all-start.2 = ((bf16[8,32,32,128]{3,2,1,0:T(8,128)(2,1)}), bf16[8,32,32,128]{3,2,1,0:T(8,128)(2,1)S(1)}, u32[]{:S(2)}, u32[]{:S(2)}) async-start(bf16[8,32,32,128]{3,2,1,0:T(8,128)(2,1)} %shard_map.139), calls=%async_computation.2 | async-start | bytes 4194304 | tf_op jit(solution)/shard_map/all_to_all | solution.py:317
  317.6 30.3 %collective-permute-start.7 = (bf16[64,32,128]{2,1,0:T(8,128)(2,1)}, bf16[64,32,128]{2,1,0:T(8,128)(2,1)S(1)}, u32[]{:S(2)}, u32[]{:S(2)}) collective-permute-start(bf16[64,32,128]{2,1,0:T(8,128)(2,1)} %get-tuple-element.39), channel_id=1, source_target_pairs={{0,7},{1,0},{2,1},{3,2},{4,3},{5,4},{6,5},{7,6},{8,15},{9,8},{10,9... | collective-permute-start | bytes 1572872 | tf_op jit(solution)/shard_map/ppermute | solution.py:321
  321.2 30.9 %collective-permute-start.8 = (bf16[64,32,128]{2,1,0:T(8,128)(2,1)}, bf16[64,32,128]{2,1,0:T(8,128)(2,1)S(1)}, u32[]{:S(2)}, u32[]{:S(2)}) collective-permute-start(bf16[64,32,128]{2,1,0:T(8,128)(2,1)} %get-tuple-element.40), channel_id=1, source_target_pairs={{0,6},{1,7},{2,0},{3,1},{4,2},{5,3},{6,4},{7,5},{8,14},{9,15},{10,... | collective-permute-start | bytes 1572872 | tf_op jit(solution)/shard_map/ppermute | solution.py:321
  321.7 30.4 %collective-permute-start.9 = (bf16[64,32,128]{2,1,0:T(8,128)(2,1)}, bf16[64,32,128]{2,1,0:T(8,128)(2,1)}, u32[]{:S(2)}, u32[]{:S(2)}) collective-permute-start(bf16[64,32,128]{2,1,0:T(8,128)(2,1)} %get-tuple-element.41), channel_id=1, source_target_pairs={{0,5},{1,6},{2,7},{3,0},{4,1},{5,2},{6,3},{7,4},{8,13},{9,14},{10,... | collective-permute-start | bytes 1572872 | tf_op jit(solution)/shard_map/ppermute | solution.py:321
  355.1 36.4 %copy-start.2 = (bf16[8,16,32,128]{3,2,1,0:T(8,128)(2,1)S(1)}, bf16[8,16,32,128]{3,2,1,0:T(8,128)(2,1)}, u32[]{:S(2)}) copy-start(bf16[8,16,32,128]{3,2,1,0:T(8,128)(2,1)} %copy-done.1) | copy-start | bytes 3145732
  356.2 31.8 %collective-permute-start.14 = (f32[464,128]{1,0:T(8,128)S(1)}, f32[464,128]{1,0:T(8,128)}, u32[]{:S(2)}, u32[]{:S(2)}) collective-permute-start(f32[464,128]{1,0:T(8,128)S(1)} %slice_select_fusion), channel_id=1, source_target_pairs={{0,16},{8,24},{16,0},{24,8},{1,17},{9,25},{17,1},{25,9},{2,18},{10... | collective-permute-start | bytes 712712 | tf_op jit(solution)/shard_map/ppermute | solution.py:293
  357.8 74.6 %collective-permute-start.10 = (bf16[64,32,128]{2,1,0:T(8,128)(2,1)}, bf16[64,32,128]{2,1,0:T(8,128)(2,1)S(1)}, u32[]{:S(2)}, u32[]{:S(2)}) collective-permute-start(bf16[64,32,128]{2,1,0:T(8,128)(2,1)} %get-tuple-element.42), channel_id=1, source_target_pairs={{0,4},{1,5},{2,6},{3,7},{4,0},{5,1},{6,2},{7,3},{8,12},{9,13},{10,... | collective-permute-start | bytes 1572872 | tf_op jit(solution)/shard_map/ppermute | solution.py:321
  376.4 74.8 %collective-permute-start.11 = (bf16[64,32,128]{2,1,0:T(8,128)(2,1)}, bf16[64,32,128]{2,1,0:T(8,128)(2,1)S(1)}, u32[]{:S(2)}, u32[]{:S(2)}) collective-permute-start(bf16[64,32,128]{2,1,0:T(8,128)(2,1)} %get-tuple-element.43), channel_id=1, source_target_pairs={{0,3},{1,4},{2,5},{3,6},{4,7},{5,0},{6,1},{7,2},{8,11},{9,12},{10,... | collective-permute-start | bytes 1572872 | tf_op jit(solution)/shard_map/ppermute | solution.py:321
  382.3 68.8 %collective-permute-start.12 = (bf16[64,32,128]{2,1,0:T(8,128)(2,1)}, bf16[64,32,128]{2,1,0:T(8,128)(2,1)}, u32[]{:S(2)}, u32[]{:S(2)}) collective-permute-start(bf16[64,32,128]{2,1,0:T(8,128)(2,1)} %get-tuple-element.44), channel_id=1, source_target_pairs={{0,2},{1,3},{2,4},{3,5},{4,6},{5,7},{6,0},{7,1},{8,10},{9,11},{10,... | collective-permute-start | bytes 1572872 | tf_op jit(solution)/shard_map/ppermute | solution.py:321
  383.2 68.0 %collective-permute-start.13 = (bf16[64,32,128]{2,1,0:T(8,128)(2,1)}, bf16[64,32,128]{2,1,0:T(8,128)(2,1)}, u32[]{:S(2)}, u32[]{:S(2)}) collective-permute-start(bf16[64,32,128]{2,1,0:T(8,128)(2,1)} %get-tuple-element.45), channel_id=1, source_target_pairs={{0,1},{1,2},{2,3},{3,4},{4,5},{5,6},{6,7},{7,0},{8,9},{9,10},{10,1... | collective-permute-start | bytes 1572872 | tf_op jit(solution)/shard_map/ppermute | solution.py:321
  383.2 104.5 %all-to-all-start.3 = ((bf16[8,16,32,128]{3,2,1,0:T(8,128)(2,1)}), bf16[8,16,32,128]{3,2,1,0:T(8,128)(2,1)S(1)}, u32[]{:S(2)}, u32[]{:S(2)}) async-start(bf16[8,16,32,128]{3,2,1,0:T(8,128)(2,1)} %copy-done.7), calls=%async_computation.3 | async-start | bytes 2097152 | tf_op jit(solution)/shard_map/all_to_all | solution.py:317
  389.9 68.7 %collective-permute-start.15 = (f32[232,128]{1,0:T(8,128)}, f32[232,128]{1,0:T(8,128)S(1)}, u32[]{:S(2)}, u32[]{:S(2)}) collective-permute-start(f32[232,128]{1,0:T(8,128)} %slice_select_fusion.1), channel_id=1, source_target_pairs={{0,8},{8,0},{16,24},{24,16},{1,9},{9,1},{17,25},{25,17},{2,10},{10... | collective-permute-start | bytes 356360 | tf_op jit(solution)/shard_map/ppermute | solution.py:293
  391.4 59.8 %copy-start.4 = (bf16[64,32,128]{2,1,0:T(8,128)(2,1)S(1)}, bf16[64,32,128]{2,1,0:T(8,128)(2,1)}, u32[]{:S(2)}) copy-start(bf16[64,32,128]{2,1,0:T(8,128)(2,1)} %copy-done.3) | copy-start | bytes 1572868
  391.4 59.8 %copy-start.6 = (bf16[64,32,128]{2,1,0:T(8,128)(2,1)S(1)}, bf16[64,32,128]{2,1,0:T(8,128)(2,1)}, u32[]{:S(2)}) copy-start(bf16[64,32,128]{2,1,0:T(8,128)(2,1)} %copy-done.5) | copy-start | bytes 1572868
  391.4 59.8 %copy-start.9 = (bf16[64,32,128]{2,1,0:T(8,128)(2,1)S(1)}, bf16[64,32,128]{2,1,0:T(8,128)(2,1)}, u32[]{:S(2)}) copy-start(bf16[64,32,128]{2,1,0:T(8,128)(2,1)} %copy-done.8) | copy-start | bytes 1572868
  (18 other events, 22.5 us)

commit v9 on v8

--- a/solution.py
+++ b/solution.py
@@ -11,7 +11,6 @@
 A = 256
 B = 128
 LANES = 128
-RETURN_FIRST = 4
 VMEM_BYTES = 48 * 1024 * 1024
 
 
@@ -282,7 +281,7 @@
     )
 
 
-def sum_over_mesh(sums):
+def sum_over_mesh(sums, after):
     dp = lax.axis_index("dp")
     size = lax.axis_size("dp")
     for bit in reversed([1 << k for k in range(size.bit_length() - 1)]):
@@ -291,6 +290,7 @@
         sent = jnp.where(high, halves[0], halves[1])
         kept = jnp.where(high, halves[1], halves[0])
         sums = kept + lax.ppermute(sent, "dp", [(i, i ^ bit) for i in range(size)])
+    (sums,) = hold([sums], after)
     sums = jnp.sum(lax.all_gather(sums, "ctx"), axis=0)
     return lax.all_gather(sums, "dp", axis=0, tiled=True)
 
@@ -303,7 +303,8 @@
     local_rows = tok_rows // B
     tiles = width // LANES
     pair = 2
-    groups = [(0, 1, False), (1, tiles - 2, True), (tiles - 1, 1, False)]
+    half = tiles // 2
+    groups = [(0, 1, False), (half, tiles - half, True), (1, half - 1, False)]
 
     place = (lax.axis_index("ctx") * share).astype(jnp.int32).reshape(1)
     second = block_diagonal(second_factor, pair)
@@ -332,30 +333,29 @@
             split.append(
                 split_channels(place, tok_blocks, cot_blocks, at, count, ctx_size, rotated, own)
             )
-        arrived = [exchange(split[0], 1, False), exchange(split[1], 1, True)]
+        arrived = [exchange(p, 1, group[2]) for p, group in zip(split, groups)]
         planes = arrived[0][0][:, 2 * share :].astype(jnp.float32)
         twiddle_all = (planes[:, 0] + planes[:, 1] + planes[:, 2]).reshape(A, B)
         factors = [first_factor, first_factor.T, second, second_t, twiddle_all]
         returned = []
         for which, (at, count, rotated) in enumerate(groups):
-            if which == 2:
-                parts = hold(split[2], returned[0] + arrived[1][1:])
-                arrived.append(exchange(parts, 1, rotated))
             parts, own_sums = mix(
                 arrived[which], at, count, 2 * share, place, vectors, factors, sum_rows, ctx_size,
                 rotated, [],
             )
+            if which == 2:
+                parts = hold(parts, arrived[1][1:])
             returned.append(exchange(parts, -1, rotated))
             terms.append(own_sums)
         leaving.append(returned)
 
-    begun = [part for returned in leaving for part in returned[1][1:RETURN_FIRST]]
-    sums = sum_over_mesh(add(terms, begun))
+    sums = sum_over_mesh(add(terms, []), [part for r in leaving for part in r[1][-2:]])
     grads = []
     for returned in leaving:
         held = None
-        for which, (at, count, rotated) in enumerate(groups):
-            after = [sums] if which == 2 else []
+        for which in (0, 2, 1):
+            at, count, rotated = groups[which]
+            after = [sums] if which else []
             held = merge_channels(
                 place, returned[which], held, at, count, ctx_size, rotated, width, after
             )

time: 493 us -> 484 us (0.982)
  waiting for transfers between devices: 251 us -> 210 us
  blocking collectives: 26.4 us -> 53.9 us
  local copies, waits for them, and re-layouts: 14 us -> 22.6 us
  starting transfers between devices: 114 us -> 107 us
    ppermute x14, waiting for transfers between devices: 168 us -> 69.5 us  [exchange(): moved.append(lax.ppermute(parts[shift], 'ctx', pairs))]
    all_to_all x4, waiting for transfers between devices: 83.5 us -> 135 us  [exchange(): lax.all_to_all(parts[0], 'ctx', split_axis=0, concat_axis=0, tiled=True)]
    all_gather x1, blocking collectives: 16.3 us -> 43.7 us  [sum_over_mesh(): sums = jnp.sum(lax.all_gather(sums, 'ctx'), axis=0)]
    all_to_all x4, starting transfers between devices: 72.1 us -> 58.7 us  [exchange(): lax.all_to_all(parts[0], 'ctx', split_axis=0, concat_axis=0, tiled=True)]
    unnamed x62 -> x74, local copies, waits for them, and re-layouts: 14 us -> 22.6 us
    ppermute x14, starting transfers between devices: 38.5 us -> 45.2 us  [exchange(): moved.append(lax.ppermute(parts[shift], 'ctx', pairs))]
    ppermute x2, waiting for transfers between devices: 0.01 us -> 4.96 us  [sum_over_mesh(): sums = kept + lax.ppermute(sent, 'dp', [(i, i ^ bit) for i in range(size)])]
  transfers between devices with their start and end apart: 20 -> 20, of which waited for: 9 -> 6; matrix products, arithmetic and copies ran while one was open for 1% -> 2% of each run, Pallas kernels for 14% -> 14%
where the time goes in v9:
time: 484 us; the launch traced here: 481 us
  waiting for transfers between devices  210 us (43%)
  starting transfers between devices  107 us (22%)
  Pallas kernels  78.6 us (16%)
  blocking collectives  53.9 us (11%)
  local copies, waits for them, and re-layouts  22.6 us (5%)
  other arithmetic  7.92 us (2%)
    all_to_all x4, waiting for transfers between devices, exchange(): lax.all_to_all(parts[0], 'ctx', split_axis=0, concat_axis=0, tiled=True)  135 us
    ppermute x14, waiting for transfers between devices, exchange(): moved.append(lax.ppermute(parts[shift], 'ctx', pairs))  69.5 us
    all_to_all x4, starting transfers between devices, exchange(): lax.all_to_all(parts[0], 'ctx', split_axis=0, concat_axis=0, tiled=True)  58.7 us
    ppermute x14, starting transfers between devices, exchange(): moved.append(lax.ppermute(parts[shift], 'ctx', pairs))  45.2 us
    all_gather x1, blocking collectives, sum_over_mesh(): sums = jnp.sum(lax.all_gather(sums, 'ctx'), axis=0)  43.7 us
    pallas_call x3, Pallas kernels, mix(): pl.pallas_call(functools.partial(mix_kernel, parts=len(parts), tile=tile,...  40.8 us
    pallas_call x3, Pallas kernels, split_channels(): pl.pallas_call(functools.partial(kernel, rotated=rotated), grid=(tiles, r...  24.9 us
    unnamed x74, local copies, waits for them, and re-layouts  22.6 us
  transfers between devices with their start and end apart: 20, of which 6 were waited for; matrix products, arithmetic and copies ran while one was open for 2% of the time, Pallas kernels for 14%

profile of v9, /device:TPU:0, one launch (start us, length us, event | category | flops | bytes accessed | tf_op | source)
XLA Modules:
  0.0 480.5 jit_solution(12446612583796651891)
XLA Ops:
  1.4 5.4 %shard_map.136 = bf16[8,35,32,128]{3,2,1,0:T(8,128)(2,1)} custom-call(s32[1]{0:T(128)} %bitcast.place_ref, bf16[32,128,768]{2,1,0:T(8,128)(2,1)} %bitcast.20, bf16[32,128,768]{2,1,0:T(8,128)(2,1)} %bitcast.23, f32[32,128]{1,0:T(8,128)S(1)} %copy-done.18), custom_call_target="tpu_custom_call" | custom-call | flops 1 | bytes 8388608 | tf_op jit(solution)/shard_map/pallas_call | solution.py:83
  6.7 6.3 %all-to-all-start = ((bf16[8,35,32,128]{3,2,1,0:T(8,128)(2,1)}), bf16[8,35,32,128]{3,2,1,0:T(8,128)(2,1)S(1)}, u32[]{:S(2)}, u32[]{:S(2)}) async-start(bf16[8,35,32,128]{3,2,1,0:T(8,128)(2,1)} %shard_map.136), calls=%async_computation | async-start | bytes 4587520 | tf_op jit(solution)/shard_map/all_to_all | solution.py:318
  13.1 7.8 %shard_map.138 = bf16[8,64,32,128]{3,2,1,0:T(8,128)(2,1)S(1)} custom-call(s32[1]{0:T(128)} %bitcast.place_ref, bf16[32,128,768]{2,1,0:T(8,128)(2,1)} %bitcast.21, bf16[32,128,768]{2,1,0:T(8,128)(2,1)} %bitcast.24), custom_call_target="tpu_custom_call" | custom-call | flops 1 | bytes 16777216 | tf_op jit(solution)/shard_map/pallas_call | solution.py:83
  20.9 2.0 copy-done
  22.9 43.4 %all-to-all-done.rest_0_.rest_1_ = bf16[8,35,32,128]{3,2,1,0:T(8,128)(2,1)S(1)} async-done(((bf16[8,35,32,128]{3,2,1,0:T(8,128)(2,1)}), bf16[8,35,32,128]{3,2,1,0:T(8,128)(2,1)S(1)}, u32[]{:S(2)}, u32[]{:S(2)}) %all-to-all-start) | async-done | bytes 2293792 | tf_op jit(solution)/shard_map/all_to_all | solution.py:318
  66.3 4.6 all-to-all-start.1
  71.0 11.7 %shard_map.135 = (bf16[96,32,128]{2,1,0:T(8,128)(2,1)S(1)}, bf16[96,32,128]{2,1,0:T(8,128)(2,1)}, bf16[96,32,128]{2,1,0:T(8,128)(2,1)}, bf16[96,32,128]{2,1,0:T(...) custom-call(s32[1]{0:T(128)} %bitcast.place_ref, ...), custom_call_target="tpu_custom_call" | custom-call | flops 1 | bytes 25165824 | tf_op jit(solution)/shard_map/pallas_call | solution.py:83
  87.5 1.7 collective-permute-start.1
  90.1 6.9 %shard_map.141 = (bf16[8,16,32,128]{3,2,1,0:T(8,128)(2,1)}, f32[928,128]{1,0:T(8,128)S(1)}) custom-call(s32[1]{0:T(128)} %bitcast.place_ref, f32[768]{0:T(1024)S(1)} %copy-done.29, f32[768]{0:T(1024)S(1)} %copy-done.30, f32[768]{0:T(1024)S(1)} %copy-done.31, bf16[8,35,32,128]{3,2,1,0:T(8,128)(2,1)S(1)} %all-to-all-done.rest_0_.rest_1_, ...), custom_call_target="tpu_custom_call" | custom-call | flops 8388608000 | bytes 1024 | tf_op jit(solution)/shard_map/pallas_call | solution.py:222
  98.4 91.8 %all-to-all-done.1.rest_0_.rest_1_ = bf16[8,64,32,128]{3,2,1,0:T(8,128)(2,1)} async-done(((bf16[8,64,32,128]{3,2,1,0:T(8,128)(2,1)}), bf16[8,64,32,128]{3,2,1,0:T(8,128)(2,1)}, u32[]{:S(2)}, u32[]{:S(2)}) %all-to-all-start.1) | async-done | bytes 4194336 | tf_op jit(solution)/shard_map/all_to_all | solution.py:318
  190.2 3.6 all-to-all-start.3
  193.8 1.7 collective-permute-start.2
  195.5 2.4 collective-permute-start.3
  202.4 13.7 %shard_map.139 = (bf16[8,32,32,128]{3,2,1,0:T(8,128)(2,1)S(1)}, f32[928,128]{1,0:T(8,128)S(1)}) custom-call(s32[1]{0:T(128)} %bitcast.place_ref, f32[768]{0:T(1024)S(1)} %copy-done.29, f32[768]{0:T(1024)S(1)} %copy-done.30, f32[768]{0:T(1024)S(1)} %copy-done.31, bf16[8,64,32,128]{3,2,1,0:T(8,128)(2,1)} %all-to-all-done.1.rest_0_.rest_1_, ...), custom_call_target="tpu_custom_call" | custom-call | flops 16777216000 | bytes 1024 | tf_op jit(solution)/shard_map/pallas_call | solution.py:222
  218.2 60.6 %collective-permute-done.2.rest_3_.rest_11_.refs_3_ = bf16[96,32,128]{2,1,0:T(8,128)(2,1)S(1)} collective-permute-done((bf16[96,32,128]{2,1,0:T(8,128)(2,1)}, bf16[96,32,128]{2,1,0:T(8,128)(2,1)S(1)}, u32[]{:S(2)}, u32[]{:S(2)}) %collective-permute-start.2) | collective-permute-done | bytes 786464 | tf_op jit(solution)/shard_map/ppermute | solution.py:322
  279.9 7.8 %collective-permute-done.6.rest_7_.rest_15_.refs_7_ = bf16[96,32,128]{2,1,0:T(8,128)(2,1)} collective-permute-done((bf16[96,32,128]{2,1,0:T(8,128)(2,1)}, bf16[96,32,128]{2,1,0:T(8,128)(2,1)}, u32[]{:S(2)}, u32[]{:S(2)}) %collective-permute-start.6) | collective-permute-done | bytes 786464 | tf_op jit(solution)/shard_map/ppermute | solution.py:322
  287.7 44.3 %all-to-all-start.2 = ((bf16[8,32,32,128]{3,2,1,0:T(8,128)(2,1)}), bf16[8,32,32,128]{3,2,1,0:T(8,128)(2,1)S(1)}, u32[]{:S(2)}, u32[]{:S(2)}) async-start(bf16[8,32,32,128]{3,2,1,0:T(8,128)(2,1)} %shard_map.140), calls=%async_computation.2 | async-start | bytes 4194304 | tf_op jit(solution)/shard_map/all_to_all | solution.py:318
  336.0 20.1 %shard_map.137 = (bf16[48,32,128]{2,1,0:T(8,128)(2,1)S(1)}, bf16[48,32,128]{2,1,0:T(8,128)(2,1)}, bf16[48,32,128]{2,1,0:T(8,128)(2,1)}, bf16[48,32,128]{2,1,0:T(...) custom-call(s32[1]{0:T(128)} %bitcast.place_ref, ...), custom_call_target="tpu_custom_call" | custom-call | flops 25165824000 | bytes 1024 | tf_op jit(solution)/shard_map/pallas_call | solution.py:222
  360.7 2.2 shard_map.143
  362.8 1.8 slice_select_fusion
  366.1 2.0 collective-permute-start.12
  368.1 5.0 %collective-permute-done.14 = f32[464,128]{1,0:T(8,128)} collective-permute-done((f32[464,128]{1,0:T(8,128)}, f32[464,128]{1,0:T(8,128)}, u32[]{:S(2)}, u32[]{:S(2)}) %collective-permute-start.14) | collective-permute-done | bytes 237600 | tf_op jit(solution)/shard_map/ppermute | solution.py:292
  377.1 2.6 collective-permute-start.10
  379.7 1.7 shard_map.142.rest_1_
  381.4 3.6 collective-permute-start.7
  385.0 1.6 select_add_fusion.1.refs_0_
  386.6 2.6 collective-permute-start.8
  389.2 25.6 %collective-permute-start.9 = (bf16[48,32,128]{2,1,0:T(8,128)(2,1)}, bf16[48,32,128]{2,1,0:T(8,128)(2,1)}, u32[]{:S(2)}, u32[]{:S(2)}) collective-permute-start(bf16[48,32,128]{2,1,0:T(8,128)(2,1)} %get-tuple-element.39), channel_id=1, source_target_pairs={{0,5},{1,6},{2,7},{3,0},{4,1},{5,2},{6,3},{7,4},{8,13},{9,14},{10,... | collective-permute-start | bytes 1179656 | tf_op jit(solution)/shard_map/ppermute | solution.py:322
  414.8 43.7 %all-gather = f32[1856,128]{1,0:T(8,128)S(1)} all-gather(f32[232,128]{1,0:T(8,128)} %shard_map.144), channel_id=2, replica_groups=mesh['dp'=4,'ctx'=8] {'ctx'}, dimensions={0}, use_global_device_ids=true | all-gather | bytes 1069056 | tf_op jit(solution)/shard_map/all_gather | solution.py:294
  458.6 10.1 %all_gather.11.rest_2_.rest_9_ = f32[928,128]{1,0:T(8,128)S(1)} all-gather(f32[232,128]{1,0:T(8,128)S(1)} %reduce_sum.9), channel_id=1, replica_groups=mesh['dp'=4,'ctx'=8] {'dp'}, dimensions={0}, use_global_device_ids=true | all-gather | bytes 593920 | tf_op jit(solution)/shard_map/all_gather | solution.py:295
  471.4 3.0 shard_map.145.rest_8_
  474.4 6.1 %shard_map.146 = bf16[32,128,768]{2,1,0:T(8,128)(2,1)} custom-call(s32[1]{0:T(128)} %bitcast.place_ref, bf16[48,32,128]{2,1,0:T(8,128)(2,1)S(1)} %copy-done.10, bf16[48,32,128]{2,1,0:T(8,128)(2,1)} %collective-permute-done.7.rest_1_, bf16[48,32,128]{2,1,0:T(8,128)(2,1)} %collective-permute-done.8.rest_2_, ...), custom_call_target="tpu_custom_call", output_to_operand_aliasing={{}: (9, {})} | custom-call | flops 1 | bytes 12582912 | tf_op jit(solution)/shard_map/pallas_call | solution.py:117
  (109 shorter events, 32.4 us)
Async XLA Ops:
  6.7 59.6 %all-to-all-start = ((bf16[8,35,32,128]{3,2,1,0:T(8,128)(2,1)}), bf16[8,35,32,128]{3,2,1,0:T(8,128)(2,1)S(1)}, u32[]{:S(2)}, u32[]{:S(2)}) async-start(bf16[8,35,32,128]{3,2,1,0:T(8,128)(2,1)} %shard_map.136), calls=%async_computation | async-start | bytes 4587520 | tf_op jit(solution)/shard_map/all_to_all | solution.py:318
  20.9 2.0 copy-start
  66.3 123.9 %all-to-all-start.1 = ((bf16[8,64,32,128]{3,2,1,0:T(8,128)(2,1)}), bf16[8,64,32,128]{3,2,1,0:T(8,128)(2,1)}, u32[]{:S(2)}, u32[]{:S(2)}) async-start(bf16[8,64,32,128]{3,2,1,0:T(8,128)(2,1)} %copy-done), calls=%async_computation.1 | async-start | bytes 8388608 | tf_op jit(solution)/shard_map/all_to_all | solution.py:318
  70.9 18.3 %copy-start.35 = (bf16[128,128]{1,0:T(8,128)(2,1)S(1)}, bf16[128,128]{1,0:T(8,128)(2,1)}, u32[]{:S(2)}) copy-start(bf16[128,128]{1,0:T(8,128)(2,1)} %param.11) | copy-start | bytes 98308
  70.9 18.4 %copy-start.11 = (bf16[256,256]{1,0:T(8,128)(2,1)S(1)}, bf16[256,256]{1,0:T(8,128)(2,1)}, u32[]{:S(2)}) copy-start(bf16[256,256]{1,0:T(8,128)(2,1)} %rest_2_.3) | copy-start | bytes 393220
  70.9 19.2 %copy-start.29 = (f32[768]{0:T(1024)S(1)}, f32[768]{0:T(1024)}, u32[]{:S(2)}) copy-start(f32[768]{0:T(1024)} %gain_ref.5) | copy-start | bytes 9220
  71.0 19.1 %copy-start.30 = (f32[768]{0:T(1024)S(1)}, f32[768]{0:T(1024)}, u32[]{:S(2)}) copy-start(f32[768]{0:T(1024)} %bias_ref.5) | copy-start | bytes 9220
  71.0 19.1 %copy-start.31 = (f32[768]{0:T(1024)S(1)}, f32[768]{0:T(1024)}, u32[]{:S(2)}) copy-start(f32[768]{0:T(1024)} %skip_ref.5) | copy-start | bytes 9220
  87.1 111.8 %collective-permute-start = (bf16[96,32,128]{2,1,0:T(8,128)(2,1)}, bf16[96,32,128]{2,1,0:T(8,128)(2,1)S(1)}, u32[]{:S(2)}, u32[]{:S(2)}) collective-permute-start(bf16[96,32,128]{2,1,0:T(8,128)(2,1)} %get-tuple-element.29), channel_id=1, source_target_pairs={{0,1},{1,2},{2,3},{3,4},{4,5},{5,6},{6,7},{7,0},{8,9},{9,10},{10,1... | collective-permute-start | bytes 2359304 | tf_op jit(solution)/shard_map/ppermute | solution.py:322
  87.5 112.9 %collective-permute-start.1 = (bf16[96,32,128]{2,1,0:T(8,128)(2,1)}, bf16[96,32,128]{2,1,0:T(8,128)(2,1)}, u32[]{:S(2)}, u32[]{:S(2)}) collective-permute-start(bf16[96,32,128]{2,1,0:T(8,128)(2,1)} %get-tuple-element.30), channel_id=1, source_target_pairs={{0,2},{1,3},{2,4},{3,5},{4,6},{5,7},{6,0},{7,1},{8,10},{9,11},{10,... | collective-permute-start | bytes 2359304 | tf_op jit(solution)/shard_map/ppermute | solution.py:322
  190.2 97.5 %all-to-all-start.3 = ((bf16[8,16,32,128]{3,2,1,0:T(8,128)(2,1)}), bf16[8,16,32,128]{3,2,1,0:T(8,128)(2,1)S(1)}, u32[]{:S(2)}, u32[]{:S(2)}) async-start(bf16[8,16,32,128]{3,2,1,0:T(8,128)(2,1)} %get-tuple-element.45), calls=%async_computation.3 | async-start | bytes 2097152 | tf_op jit(solution)/shard_map/all_to_all | solution.py:318
  193.8 85.0 %collective-permute-start.2 = (bf16[96,32,128]{2,1,0:T(8,128)(2,1)}, bf16[96,32,128]{2,1,0:T(8,128)(2,1)S(1)}, u32[]{:S(2)}, u32[]{:S(2)}) collective-permute-start(bf16[96,32,128]{2,1,0:T(8,128)(2,1)} %copy-done.24), channel_id=1, source_target_pairs={{0,3},{1,4},{2,5},{3,6},{4,7},{5,0},{6,1},{7,2},{8,11},{9,12},{10,... | collective-permute-start | bytes 2359304 | tf_op jit(solution)/shard_map/ppermute | solution.py:322
  195.5 84.4 %collective-permute-start.3 = (bf16[96,32,128]{2,1,0:T(8,128)(2,1)}, bf16[96,32,128]{2,1,0:T(8,128)(2,1)}, u32[]{:S(2)}, u32[]{:S(2)}) collective-permute-start(bf16[96,32,128]{2,1,0:T(8,128)(2,1)} %copy-done.23), channel_id=1, source_target_pairs={{0,4},{1,5},{2,6},{3,7},{4,0},{5,1},{6,2},{7,3},{8,12},{9,13},{10,... | collective-permute-start | bytes 2359304 | tf_op jit(solution)/shard_map/ppermute | solution.py:322
  197.8 82.0 %collective-permute-start.4 = (bf16[96,32,128]{2,1,0:T(8,128)(2,1)}, bf16[96,32,128]{2,1,0:T(8,128)(2,1)}, u32[]{:S(2)}, u32[]{:S(2)}) collective-permute-start(bf16[96,32,128]{2,1,0:T(8,128)(2,1)} %copy-done.22), channel_id=1, source_target_pairs={{0,5},{1,6},{2,7},{3,0},{4,1},{5,2},{6,3},{7,4},{8,13},{9,14},{10,... | collective-permute-start | bytes 2359304 | tf_op jit(solution)/shard_map/ppermute | solution.py:322
  199.0 17.1 %copy-start.4 = (bf16[96,32,128]{2,1,0:T(8,128)(2,1)}, bf16[96,32,128]{2,1,0:T(8,128)(2,1)S(1)}, u32[]{:S(2)}) copy-start(bf16[96,32,128]{2,1,0:T(8,128)(2,1)S(1)} %collective-permute-done.rest_1_.rest_9_.refs_1_) | copy-start | bytes 2359300
  199.0 80.9 %collective-permute-start.5 = (bf16[96,32,128]{2,1,0:T(8,128)(2,1)}, bf16[96,32,128]{2,1,0:T(8,128)(2,1)}, u32[]{:S(2)}, u32[]{:S(2)}) collective-permute-start(bf16[96,32,128]{2,1,0:T(8,128)(2,1)} %copy-done.21), channel_id=1, source_target_pairs={{0,6},{1,7},{2,0},{3,1},{4,2},{5,3},{6,4},{7,5},{8,14},{9,15},{10,... | collective-permute-start | bytes 2359304 | tf_op jit(solution)/shard_map/ppermute | solution.py:322
  200.4 87.2 %collective-permute-start.6 = (bf16[96,32,128]{2,1,0:T(8,128)(2,1)}, bf16[96,32,128]{2,1,0:T(8,128)(2,1)}, u32[]{:S(2)}, u32[]{:S(2)}) collective-permute-start(bf16[96,32,128]{2,1,0:T(8,128)(2,1)} %get-tuple-element.35), channel_id=1, source_target_pairs={{0,7},{1,0},{2,1},{3,2},{4,3},{5,4},{6,5},{7,6},{8,15},{9,8},{10,9... | collective-permute-start | bytes 2359304 | tf_op jit(solution)/shard_map/ppermute | solution.py:322
  278.8 8.9 %copy-start.34 = (bf16[96,32,128]{2,1,0:T(8,128)(2,1)}, bf16[96,32,128]{2,1,0:T(8,128)(2,1)S(1)}, u32[]{:S(2)}) copy-start(bf16[96,32,128]{2,1,0:T(8,128)(2,1)S(1)} %collective-permute-done.2.rest_3_.rest_11_.refs_3_) | copy-start | bytes 2359300
  287.7 183.7 %all-to-all-start.2 = ((bf16[8,32,32,128]{3,2,1,0:T(8,128)(2,1)}), bf16[8,32,32,128]{3,2,1,0:T(8,128)(2,1)S(1)}, u32[]{:S(2)}, u32[]{:S(2)}) async-start(bf16[8,32,32,128]{3,2,1,0:T(8,128)(2,1)} %shard_map.140), calls=%async_computation.2 | async-start | bytes 4194304 | tf_op jit(solution)/shard_map/all_to_all | solution.py:318
  364.6 8.5 %collective-permute-start.14 = (f32[464,128]{1,0:T(8,128)}, f32[464,128]{1,0:T(8,128)}, u32[]{:S(2)}, u32[]{:S(2)}) collective-permute-start(f32[464,128]{1,0:T(8,128)} %slice_select_fusion), channel_id=1, source_target_pairs={{0,16},{8,24},{16,0},{24,8},{1,17},{9,25},{17,1},{25,9},{2,18},{10... | collective-permute-start | bytes 712712 | tf_op jit(solution)/shard_map/ppermute | solution.py:292
  366.1 20.5 %collective-permute-start.12 = (bf16[48,32,128]{2,1,0:T(8,128)(2,1)}, bf16[48,32,128]{2,1,0:T(8,128)(2,1)S(1)}, u32[]{:S(2)}, u32[]{:S(2)}) collective-permute-start(bf16[48,32,128]{2,1,0:T(8,128)(2,1)} %copy-done.28), channel_id=1, source_target_pairs={{0,2},{1,3},{2,4},{3,5},{4,6},{5,7},{6,0},{7,1},{8,10},{9,11},{10,... | collective-permute-start | bytes 1179656 | tf_op jit(solution)/shard_map/ppermute | solution.py:322
  368.1 21.1 %collective-permute-start.13 = (bf16[48,32,128]{2,1,0:T(8,128)(2,1)}, bf16[48,32,128]{2,1,0:T(8,128)(2,1)}, u32[]{:S(2)}, u32[]{:S(2)}) collective-permute-start(bf16[48,32,128]{2,1,0:T(8,128)(2,1)} %copy-done.27), channel_id=1, source_target_pairs={{0,1},{1,2},{2,3},{3,4},{4,5},{5,6},{6,7},{7,0},{8,9},{9,10},{10,1... | collective-permute-start | bytes 1179656 | tf_op jit(solution)/shard_map/ppermute | solution.py:322
  375.7 5.8 %collective-permute-start.15 = (f32[232,128]{1,0:T(8,128)}, f32[232,128]{1,0:T(8,128)}, u32[]{:S(2)}, u32[]{:S(2)}) collective-permute-start(f32[232,128]{1,0:T(8,128)} %slice_select_fusion.1), channel_id=1, source_target_pairs={{0,8},{8,0},{16,24},{24,16},{1,9},{9,1},{17,25},{25,17},{2,10},{10... | collective-permute-start | bytes 356360 | tf_op jit(solution)/shard_map/ppermute | solution.py:292
  377.1 7.9 %copy-start.33 = (f32[464,128]{1,0:T(8,128)S(1)}, f32[464,128]{1,0:T(8,128)}, u32[]{:S(2)}) copy-start(f32[464,128]{1,0:T(8,128)} %copy-done.32) | copy-start | bytes 712708
  377.1 97.2 %collective-permute-start.10 = (bf16[48,32,128]{2,1,0:T(8,128)(2,1)}, bf16[48,32,128]{2,1,0:T(8,128)(2,1)}, u32[]{:S(2)}, u32[]{:S(2)}) collective-permute-start(bf16[48,32,128]{2,1,0:T(8,128)(2,1)} %copy-done.26), channel_id=1, source_target_pairs={{0,4},{1,5},{2,6},{3,7},{4,0},{5,1},{6,2},{7,3},{8,12},{9,13},{10,... | collective-permute-start | bytes 1179656 | tf_op jit(solution)/shard_map/ppermute | solution.py:322
  379.7 94.6 %collective-permute-start.11 = (bf16[48,32,128]{2,1,0:T(8,128)(2,1)}, bf16[48,32,128]{2,1,0:T(8,128)(2,1)}, u32[]{:S(2)}, u32[]{:S(2)}) collective-permute-start(bf16[48,32,128]{2,1,0:T(8,128)(2,1)} %copy-done.25), channel_id=1, source_target_pairs={{0,3},{1,4},{2,5},{3,6},{4,7},{5,0},{6,1},{7,2},{8,11},{9,12},{10,... | collective-permute-start | bytes 1179656 | tf_op jit(solution)/shard_map/ppermute | solution.py:322
  381.4 92.9 %collective-permute-start.7 = (bf16[48,32,128]{2,1,0:T(8,128)(2,1)}, bf16[48,32,128]{2,1,0:T(8,128)(2,1)}, u32[]{:S(2)}, u32[]{:S(2)}) collective-permute-start(bf16[48,32,128]{2,1,0:T(8,128)(2,1)} %get-tuple-element.37), channel_id=1, source_target_pairs={{0,7},{1,0},{2,1},{3,2},{4,3},{5,4},{6,5},{7,6},{8,15},{9,8},{10,9... | collective-permute-start | bytes 1179656 | tf_op jit(solution)/shard_map/ppermute | solution.py:322
  386.6 28.2 %copy-start.2 = (bf16[48,32,128]{2,1,0:T(8,128)(2,1)}, bf16[48,32,128]{2,1,0:T(8,128)(2,1)S(1)}, u32[]{:S(2)}) copy-start(bf16[48,32,128]{2,1,0:T(8,128)(2,1)S(1)} %collective-permute-done.12.refs_1_.rest_6_) | copy-start | bytes 1179652
  386.6 87.8 %collective-permute-start.8 = (bf16[48,32,128]{2,1,0:T(8,128)(2,1)}, bf16[48,32,128]{2,1,0:T(8,128)(2,1)}, u32[]{:S(2)}, u32[]{:S(2)}) collective-permute-start(bf16[48,32,128]{2,1,0:T(8,128)(2,1)} %get-tuple-element.38), channel_id=1, source_target_pairs={{0,6},{1,7},{2,0},{3,1},{4,2},{5,3},{6,4},{7,5},{8,14},{9,15},{10,... | collective-permute-start | bytes 1179656 | tf_op jit(solution)/shard_map/ppermute | solution.py:322
  389.2 85.1 %collective-permute-start.9 = (bf16[48,32,128]{2,1,0:T(8,128)(2,1)}, bf16[48,32,128]{2,1,0:T(8,128)(2,1)}, u32[]{:S(2)}, u32[]{:S(2)}) collective-permute-start(bf16[48,32,128]{2,1,0:T(8,128)(2,1)} %get-tuple-element.39), channel_id=1, source_target_pairs={{0,5},{1,6},{2,7},{3,0},{4,1},{5,2},{6,3},{7,4},{8,13},{9,14},{10,... | collective-permute-start | bytes 1179656 | tf_op jit(solution)/shard_map/ppermute | solution.py:322
  471.4 3.0 copy-start.3
  471.4 3.0 copy-start.10
  (24 other events, 20.5 us)

commit v10 on v9

--- a/solution.py
+++ b/solution.py
@@ -282,17 +282,25 @@
 
 
 def sum_over_mesh(sums, after):
+    size = lax.axis_size("dp")
     dp = lax.axis_index("dp")
-    size = lax.axis_size("dp")
-    for bit in reversed([1 << k for k in range(size.bit_length() - 1)]):
+    bits = [1 << k for k in range(size.bit_length() - 1)]
+
+    def exchange_with(array, bit):
+        return lax.ppermute(array, "dp", [(i, i ^ bit) for i in range(size)])
+
+    for bit in reversed(bits):
         halves = sums.reshape(2, -1, LANES)
         high = (dp & bit) != 0
-        sent = jnp.where(high, halves[0], halves[1])
-        kept = jnp.where(high, halves[1], halves[0])
-        sums = kept + lax.ppermute(sent, "dp", [(i, i ^ bit) for i in range(size)])
+        other = exchange_with(jnp.where(high, halves[0], halves[1]), bit)
+        sums = jnp.where(high, halves[1], halves[0]) + other
     (sums,) = hold([sums], after)
-    sums = jnp.sum(lax.all_gather(sums, "ctx"), axis=0)
-    return lax.all_gather(sums, "dp", axis=0, tiled=True)
+    sums = own = jnp.sum(lax.all_gather(sums, "ctx"), axis=0)
+    for bit in bits:
+        other = exchange_with(sums, bit)
+        high = (dp & bit) != 0
+        sums = jnp.concatenate([jnp.where(high, other, sums), jnp.where(high, sums, other)])
+    return sums, own
 
 
 def body(tokens, cotangent, first_factor, second_factor, twiddle, gate_gain, gate_bias, skip_gain):
@@ -304,7 +312,7 @@
     tiles = width // LANES
     pair = 2
     half = tiles // 2
-    groups = [(0, 1, False), (half, tiles - half, True), (1, half - 1, False)]
+    groups = [(0, 1, True), (1, half - 1, False), (half, tiles - half, True)]
 
     place = (lax.axis_index("ctx") * share).astype(jnp.int32).reshape(1)
     second = block_diagonal(second_factor, pair)
@@ -334,8 +342,11 @@
                 split_channels(place, tok_blocks, cot_blocks, at, count, ctx_size, rotated, own)
             )
         arrived = [exchange(p, 1, group[2]) for p, group in zip(split, groups)]
-        planes = arrived[0][0][:, 2 * share :].astype(jnp.float32)
-        twiddle_all = (planes[:, 0] + planes[:, 1] + planes[:, 2]).reshape(A, B)
+        planes = jnp.stack([part[2 * share :] for part in arrived[0]]).astype(jnp.float32)
+        planes = planes[:, 0] + planes[:, 1] + planes[:, 2]
+        twice = jnp.concatenate([planes[::-1]] * 2, axis=0)
+        turn = ctx_size - 1 - lax.axis_index("ctx")
+        twiddle_all = lax.dynamic_slice_in_dim(twice, turn, ctx_size, 0).reshape(A, B)
         factors = [first_factor, first_factor.T, second, second_t, twiddle_all]
         returned = []
         for which, (at, count, rotated) in enumerate(groups):
@@ -343,19 +354,19 @@
                 arrived[which], at, count, 2 * share, place, vectors, factors, sum_rows, ctx_size,
                 rotated, [],
             )
-            if which == 2:
-                parts = hold(parts, arrived[1][1:])
+            if which == 1:
+                parts = hold(parts, arrived[2][1:])
             returned.append(exchange(parts, -1, rotated))
             terms.append(own_sums)
         leaving.append(returned)
 
-    sums = sum_over_mesh(add(terms, []), [part for r in leaving for part in r[1][-2:]])
+    sums, own_sums = sum_over_mesh(add(terms, []), [part for r in leaving for part in r[2][-2:]])
     grads = []
     for returned in leaving:
         held = None
-        for which in (0, 2, 1):
+        for which in (0, 1, 2):
             at, count, rotated = groups[which]
-            after = [sums] if which else []
+            after = [own_sums] if which else []
             held = merge_channels(
                 place, returned[which], held, at, count, ctx_size, rotated, width, after
             )

time: 484 us -> 475 us (0.981)
  blocking collectives: 53.9 us -> 25.5 us
  starting transfers between devices: 107 us -> 134 us
  waiting for transfers between devices: 210 us -> 196 us
    all_to_all x4 -> x2, waiting for transfers between devices: 135 us -> 0.01 us  [exchange(): lax.all_to_all(parts[0], 'ctx', split_axis=0, concat_axis=0, tiled=True)]
    ppermute x14 -> x28, waiting for transfers between devices: 69.5 us -> 185 us  [exchange(): moved.append(lax.ppermute(parts[shift], 'ctx', pairs))]
    ppermute x14 -> x28, starting transfers between devices: 45.2 us -> 99.7 us  [exchange(): moved.append(lax.ppermute(parts[shift], 'ctx', pairs))]
    all_to_all x4 -> x2, starting transfers between devices: 58.7 us -> 28.6 us  [exchange(): lax.all_to_all(parts[0], 'ctx', split_axis=0, concat_axis=0, tiled=True)]
    all_gather x2 -> x1, blocking collectives: 53.9 us -> 25.5 us  [sum_over_mesh(): sums = own = jnp.sum(lax.all_gather(sums, 'ctx'), axis=0)]
    ppermute x2 -> x4, waiting for transfers between devices: 4.96 us -> 10.5 us  [exchange_with(): return lax.ppermute(array, 'dp', [(i, i ^ bit) for i in range(size)])]
    unnamed x74 -> x113, local copies, waits for them, and re-layouts: 22.6 us -> 27.2 us
  transfers between devices with their start and end apart: 20 -> 34, of which waited for: 6 -> 19; matrix products, arithmetic and copies ran while one was open for 2% -> 2% of each run, Pallas kernels for 14% -> 14%
where the time goes in v10:
time: 475 us; the launch traced here: 472 us
  waiting for transfers between devices  196 us (41%)
  starting transfers between devices  134 us (28%)
  Pallas kernels  78.7 us (17%)
  local copies, waits for them, and re-layouts  27.2 us (6%)
  blocking collectives  25.5 us (5%)
  other arithmetic  9.4 us (2%)
    ppermute x28, waiting for transfers between devices, exchange(): moved.append(lax.ppermute(parts[shift], 'ctx', pairs))  185 us
    ppermute x28, starting transfers between devices, exchange(): moved.append(lax.ppermute(parts[shift], 'ctx', pairs))  99.7 us
    pallas_call x3, Pallas kernels, mix(): pl.pallas_call(functools.partial(mix_kernel, parts=len(parts), tile=tile,...  40.1 us
    all_to_all x2, starting transfers between devices, exchange(): lax.all_to_all(parts[0], 'ctx', split_axis=0, concat_axis=0, tiled=True)  28.6 us
    unnamed x113, local copies, waits for them, and re-layouts  27.2 us
    all_gather x1, blocking collectives, sum_over_mesh(): sums = own = jnp.sum(lax.all_gather(sums, 'ctx'), axis=0)  25.5 us
    pallas_call x3, Pallas kernels, split_channels(): pl.pallas_call(functools.partial(kernel, rotated=rotated), grid=(tiles, r...  24.8 us
    pallas_call x3, Pallas kernels, merge_channels(): pl.pallas_call(functools.partial(merge_kernel, parts=len(parts), rotated=...  11.6 us
  transfers between devices with their start and end apart: 34, of which 19 were waited for; matrix products, arithmetic and copies ran while one was open for 2% of the time, Pallas kernels for 14%

profile of v10, /device:TPU:0, one launch (start us, length us, event | category | flops | bytes accessed | tf_op | source)
XLA Modules:
  0.0 472.0 jit_solution(13539822623026216368)
XLA Ops:
  0.6 7.8 %shard_map.138 = bf16[8,64,32,128]{3,2,1,0:T(8,128)(2,1)S(1)} custom-call(s32[1]{0:T(128)} %bitcast.place_ref, bf16[32,128,768]{2,1,0:T(8,128)(2,1)} %bitcast.52, bf16[32,128,768]{2,1,0:T(8,128)(2,1)} %bitcast.55), custom_call_target="tpu_custom_call" | custom-call | flops 1 | bytes 16777216 | tf_op jit(solution)/shard_map/pallas_call | solution.py:83
  10.5 6.5 %all-to-all-start = ((bf16[8,64,32,128]{3,2,1,0:T(8,128)(2,1)}), bf16[8,64,32,128]{3,2,1,0:T(8,128)(2,1)}, u32[]{:S(2)}, u32[]{:S(2)}) async-start(bf16[8,64,32,128]{3,2,1,0:T(8,128)(2,1)} %copy-done), calls=%async_computation | async-start | bytes 8388608 | tf_op jit(solution)/shard_map/all_to_all | solution.py:326
  17.0 5.3 %shard_map.136 = (bf16[35,32,128]{2,1,0:T(8,128)(2,1)S(1)}, bf16[35,32,128]{2,1,0:T(8,128)(2,1)S(1)}, bf16[35,32,128]{2,1,0:T(8,128)(2,1)S(1)}, bf16[35,32,128]{...) custom-call(s32[1]{0:T(128)} %bitcast.place_ref, ...), custom_call_target="tpu_custom_call" | custom-call | flops 1 | bytes 8388608 | tf_op jit(solution)/shard_map/pallas_call | solution.py:83
  24.4 2.2 collective-permute-start.9
  29.2 11.7 %shard_map.135 = (bf16[96,32,128]{2,1,0:T(8,128)(2,1)S(1)}, bf16[96,32,128]{2,1,0:T(8,128)(2,1)S(1)}, bf16[96,32,128]{2,1,0:T(8,128)(2,1)S(1)}, bf16[96,32,128]{...) custom-call(s32[1]{0:T(128)} %bitcast.place_ref, ...), custom_call_target="tpu_custom_call" | custom-call | flops 1 | bytes 25165824 | tf_op jit(solution)/shard_map/pallas_call | solution.py:83
  46.6 48.6 %collective-permute-done.7.rest_1_.rest_9_ = bf16[35,32,128]{2,1,0:T(8,128)(2,1)S(1)} collective-permute-done((bf16[35,32,128]{2,1,0:T(8,128)(2,1)S(1)}, bf16[35,32,128]{2,1,0:T(8,128)(2,1)S(1)}, u32[]{:S(2)}, u32[]{:S(2)}) %collective-permute-start.7) | collective-permute-done | bytes 286752 | tf_op jit(solution)/shard_map/ppermute | solution.py:330
  96.1 4.4 collective-permute-start.13
  100.6 40.7 %collective-permute-done.9.rest_3_.rest_11_ = bf16[35,32,128]{2,1,0:T(8,128)(2,1)S(1)} collective-permute-done((bf16[35,32,128]{2,1,0:T(8,128)(2,1)S(1)}, bf16[35,32,128]{2,1,0:T(8,128)(2,1)S(1)}, u32[]{:S(2)}, u32[]{:S(2)}) %collective-permute-start.9) | collective-permute-done | bytes 286752 | tf_op jit(solution)/shard_map/ppermute | solution.py:330
  142.3 10.3 %collective-permute-start.1 = (bf16[96,32,128]{2,1,0:T(8,128)(2,1)}, bf16[96,32,128]{2,1,0:T(8,128)(2,1)}, u32[]{:S(2)}, u32[]{:S(2)}) collective-permute-start(bf16[96,32,128]{2,1,0:T(8,128)(2,1)} %copy-done.32), channel_id=1, source_target_pairs={{0,2},{1,3},{2,4},{3,5},{4,6},{5,7},{6,0},{7,1},{8,10},{9,11},{10,... | collective-permute-start | bytes 2359304 | tf_op jit(solution)/shard_map/ppermute | solution.py:330
  152.6 5.9 %collective-permute-start.2 = (bf16[96,32,128]{2,1,0:T(8,128)(2,1)}, bf16[96,32,128]{2,1,0:T(8,128)(2,1)}, u32[]{:S(2)}, u32[]{:S(2)}) collective-permute-start(bf16[96,32,128]{2,1,0:T(8,128)(2,1)} %copy-done.31), channel_id=1, source_target_pairs={{0,3},{1,4},{2,5},{3,6},{4,7},{5,0},{6,1},{7,2},{8,11},{9,12},{10,... | collective-permute-start | bytes 2359304 | tf_op jit(solution)/shard_map/ppermute | solution.py:330
  158.5 29.4 %collective-permute-start.3 = (bf16[96,32,128]{2,1,0:T(8,128)(2,1)}, bf16[96,32,128]{2,1,0:T(8,128)(2,1)}, u32[]{:S(2)}, u32[]{:S(2)}) collective-permute-start(bf16[96,32,128]{2,1,0:T(8,128)(2,1)} %copy-done.30), channel_id=1, source_target_pairs={{0,4},{1,5},{2,6},{3,7},{4,0},{5,1},{6,2},{7,3},{8,12},{9,13},{10,... | collective-permute-start | bytes 2359304 | tf_op jit(solution)/shard_map/ppermute | solution.py:330
  188.6 21.8 %collective-permute-start.4 = (bf16[96,32,128]{2,1,0:T(8,128)(2,1)}, bf16[96,32,128]{2,1,0:T(8,128)(2,1)}, u32[]{:S(2)}, u32[]{:S(2)}) collective-permute-start(bf16[96,32,128]{2,1,0:T(8,128)(2,1)} %copy-done.29), channel_id=1, source_target_pairs={{0,5},{1,6},{2,7},{3,0},{4,1},{5,2},{6,3},{7,4},{8,13},{9,14},{10,... | collective-permute-start | bytes 2359304 | tf_op jit(solution)/shard_map/ppermute | solution.py:330
  213.3 6.1 %shard_map.141 = (bf16[16,32,128]{2,1,0:T(8,128)(2,1)S(1)}, bf16[16,32,128]{2,1,0:T(8,128)(2,1)S(1)}, bf16[16,32,128]{2,1,0:T(8,128)(2,1)S(1)}, bf16[16,32,128]{...) custom-call(s32[1]{0:T(128)} %bitcast.place_ref, ...), custom_call_target="tpu_custom_call" | custom-call | flops 8388608000 | bytes 1024 | tf_op jit(solution)/shard_map/pallas_call | solution.py:222
  224.7 3.2 collective-permute-start.5
  227.9 13.8 %shard_map.139 = (bf16[8,32,32,128]{3,2,1,0:T(8,128)(2,1)S(1)}, f32[928,128]{1,0:T(8,128)S(1)}) custom-call(s32[1]{0:T(128)} %bitcast.place_ref, f32[768]{0:T(1024)S(1)} %copy-done.43, f32[768]{0:T(1024)S(1)} %copy-done.44, f32[768]{0:T(1024)S(1)} %copy-done.45, bf16[8,64,32,128]{3,2,1,0:T(8,128)(2,1)} %all-to-all-done.rest_0_.rest_1_, ...), custom_call_target="tpu_custom_call" | custom-call | flops 16777216000 | bytes 1024 | tf_op jit(solution)/shard_map/pallas_call | solution.py:222
  245.1 29.9 %collective-permute-done.5.rest_6_.rest_14_.refs_6_ = bf16[96,32,128]{2,1,0:T(8,128)(2,1)S(1)} collective-permute-done((bf16[96,32,128]{2,1,0:T(8,128)(2,1)}, bf16[96,32,128]{2,1,0:T(8,128)(2,1)S(1)}, u32[]{:S(2)}, u32[]{:S(2)}) %collective-permute-start.5) | collective-permute-done | bytes 786464 | tf_op jit(solution)/shard_map/ppermute | solution.py:330
  275.9 22.2 %all-to-all-start.1 = ((bf16[8,32,32,128]{3,2,1,0:T(8,128)(2,1)}), bf16[8,32,32,128]{3,2,1,0:T(8,128)(2,1)S(1)}, u32[]{:S(2)}, u32[]{:S(2)}) async-start(bf16[8,32,32,128]{3,2,1,0:T(8,128)(2,1)} %shard_map.140), calls=%async_computation.1 | async-start | bytes 4194304 | tf_op jit(solution)/shard_map/all_to_all | solution.py:326
  302.8 20.2 %shard_map.137 = (bf16[48,32,128]{2,1,0:T(8,128)(2,1)S(1)}, bf16[48,32,128]{2,1,0:T(8,128)(2,1)}, bf16[48,32,128]{2,1,0:T(8,128)(2,1)}, bf16[48,32,128]{2,1,0:T(...) custom-call(s32[1]{0:T(128)} %bitcast.place_ref, ...), custom_call_target="tpu_custom_call" | custom-call | flops 25165824000 | bytes 1024 | tf_op jit(solution)/shard_map/pallas_call | solution.py:222
  325.3 2.2 shard_map.143
  332.8 5.0 %collective-permute-done.28 = f32[464,128]{1,0:T(8,128)} collective-permute-done((f32[464,128]{1,0:T(8,128)}, f32[464,128]{1,0:T(8,128)}, u32[]{:S(2)}, u32[]{:S(2)}) %collective-permute-start.28) | collective-permute-done | bytes 237600 | tf_op jit(solution)/shard_map/ppermute | solution.py:290
  340.6 3.4 collective-permute-done.29
  345.8 3.7 collective-permute-done.20.refs_2_.rest_7_
  350.3 25.5 %all-gather = f32[1856,128]{1,0:T(8,128)} all-gather(f32[232,128]{1,0:T(8,128)} %shard_map.144), channel_id=2, replica_groups=mesh['dp'=4,'ctx'=8] {'ctx'}, dimensions={0}, use_global_device_ids=true | all-gather | bytes 1069056 | tf_op jit(solution)/shard_map/all_gather | solution.py:298
  385.7 3.2 collective-permute-done.22.rest_2_
  389.6 8.1 %collective-permute-start.27 = (bf16[16,32,128]{2,1,0:T(8,128)(2,1)}, bf16[16,32,128]{2,1,0:T(8,128)(2,1)}, u32[]{:S(2)}, u32[]{:S(2)}) collective-permute-start(bf16[16,32,128]{2,1,0:T(8,128)(2,1)} %copy-done.36), channel_id=1, source_target_pairs={{0,1},{1,2},{2,3},{3,4},{4,5},{5,6},{6,7},{7,0},{8,9},{9,10},{10,1... | collective-permute-start | bytes 393224 | tf_op jit(solution)/shard_map/ppermute | solution.py:330
  397.7 4.3 collective-permute-done.24.rest_4_
  403.4 2.6 shard_map.142.rest_1_
  414.7 3.0 shard_map.145.rest_8_
  417.7 8.4 %collective-permute-done.15.rest_2_ = bf16[48,32,128]{2,1,0:T(8,128)(2,1)} collective-permute-done((bf16[48,32,128]{2,1,0:T(8,128)(2,1)}, bf16[48,32,128]{2,1,0:T(8,128)(2,1)}, u32[]{:S(2)}, u32[]{:S(2)}) %collective-permute-start.15) | collective-permute-done | bytes 393248 | tf_op jit(solution)/shard_map/ppermute | solution.py:330
  426.0 6.7 %collective-permute-done.16.rest_3_ = bf16[48,32,128]{2,1,0:T(8,128)(2,1)} collective-permute-done((bf16[48,32,128]{2,1,0:T(8,128)(2,1)}, bf16[48,32,128]{2,1,0:T(8,128)(2,1)}, u32[]{:S(2)}, u32[]{:S(2)}) %collective-permute-start.16) | collective-permute-done | bytes 393248 | tf_op jit(solution)/shard_map/ppermute | solution.py:330
  432.7 33.2 %collective-permute-done.17.rest_4_ = bf16[48,32,128]{2,1,0:T(8,128)(2,1)} collective-permute-done((bf16[48,32,128]{2,1,0:T(8,128)(2,1)}, bf16[48,32,128]{2,1,0:T(8,128)(2,1)}, u32[]{:S(2)}, u32[]{:S(2)}) %collective-permute-start.17) | collective-permute-done | bytes 393248 | tf_op jit(solution)/shard_map/ppermute | solution.py:330
  465.9 6.1 %shard_map.146 = bf16[32,128,768]{2,1,0:T(8,128)(2,1)} custom-call(s32[1]{0:T(128)} %bitcast.place_ref, bf16[48,32,128]{2,1,0:T(8,128)(2,1)S(1)} %get-tuple-element.59.rest_0_, bf16[48,32,128]{2,1,0:T(8,128)(2,1)} %collective-permute-done.14.rest_1_, bf16[48,32,128]{2,1,0:T(8,128)(2,1)} %collective-permute-done.15.rest_2_, ...), custom_call_target="tpu_custom_call", output_to_operand_aliasing={{}: (9, {})} | custom-call | flops 1 | bytes 12582912 | tf_op jit(solution)/shard_map/pallas_call | solution.py:117
  (181 shorter events, 66.0 us)
Async XLA Ops:
  10.5 217.4 %all-to-all-start = ((bf16[8,64,32,128]{3,2,1,0:T(8,128)(2,1)}), bf16[8,64,32,128]{3,2,1,0:T(8,128)(2,1)}, u32[]{:S(2)}, u32[]{:S(2)}) async-start(bf16[8,64,32,128]{3,2,1,0:T(8,128)(2,1)} %copy-done), calls=%async_computation | async-start | bytes 8388608 | tf_op jit(solution)/shard_map/all_to_all | solution.py:326
  22.2 73.0 %collective-permute-start.7 = (bf16[35,32,128]{2,1,0:T(8,128)(2,1)S(1)}, bf16[35,32,128]{2,1,0:T(8,128)(2,1)S(1)}, u32[]{:S(2)}, u32[]{:S(2)}) collective-permute-start(bf16[35,32,128]{2,1,0:T(8,128)(2,1)S(1)} %get-tuple-element.52), channel_id=1, source_target_pairs={{0,1},{1,2},{2,3},{3,4},{4,5},{5,6},{6,7},{7,0},{8,9},{9,10},{10,1... | collective-permute-start | bytes 860168 | tf_op jit(solution)/shard_map/ppermute | solution.py:330
  22.7 73.4 %collective-permute-start.8 = (bf16[35,32,128]{2,1,0:T(8,128)(2,1)S(1)}, bf16[35,32,128]{2,1,0:T(8,128)(2,1)S(1)}, u32[]{:S(2)}, u32[]{:S(2)}) collective-permute-start(bf16[35,32,128]{2,1,0:T(8,128)(2,1)S(1)} %get-tuple-element.53), channel_id=1, source_target_pairs={{0,2},{1,3},{2,4},{3,5},{4,6},{5,7},{6,0},{7,1},{8,10},{9,11},{10,... | collective-permute-start | bytes 860168 | tf_op jit(solution)/shard_map/ppermute | solution.py:330
  24.4 116.9 %collective-permute-start.9 = (bf16[35,32,128]{2,1,0:T(8,128)(2,1)S(1)}, bf16[35,32,128]{2,1,0:T(8,128)(2,1)S(1)}, u32[]{:S(2)}, u32[]{:S(2)}) collective-permute-start(bf16[35,32,128]{2,1,0:T(8,128)(2,1)S(1)} %get-tuple-element.54), channel_id=1, source_target_pairs={{0,3},{1,4},{2,5},{3,6},{4,7},{5,0},{6,1},{7,2},{8,11},{9,12},{10,... | collective-permute-start | bytes 860168 | tf_op jit(solution)/shard_map/ppermute | solution.py:330
  26.6 115.7 %collective-permute-start.10 = (bf16[35,32,128]{2,1,0:T(8,128)(2,1)}, bf16[35,32,128]{2,1,0:T(8,128)(2,1)S(1)}, u32[]{:S(2)}, u32[]{:S(2)}) collective-permute-start(bf16[35,32,128]{2,1,0:T(8,128)(2,1)} %get-tuple-element.55), channel_id=1, source_target_pairs={{0,4},{1,5},{2,6},{3,7},{4,0},{5,1},{6,2},{7,3},{8,12},{9,13},{10,... | collective-permute-start | bytes 860168 | tf_op jit(solution)/shard_map/ppermute | solution.py:330
  28.1 124.5 %collective-permute-start.11 = (bf16[35,32,128]{2,1,0:T(8,128)(2,1)}, bf16[35,32,128]{2,1,0:T(8,128)(2,1)S(1)}, u32[]{:S(2)}, u32[]{:S(2)}) collective-permute-start(bf16[35,32,128]{2,1,0:T(8,128)(2,1)} %get-tuple-element.56), channel_id=1, source_target_pairs={{0,5},{1,6},{2,7},{3,0},{4,1},{5,2},{6,3},{7,4},{8,13},{9,14},{10,... | collective-permute-start | bytes 860168 | tf_op jit(solution)/shard_map/ppermute | solution.py:330
  95.2 63.3 %collective-permute-start.12 = (bf16[35,32,128]{2,1,0:T(8,128)(2,1)}, bf16[35,32,128]{2,1,0:T(8,128)(2,1)S(1)}, u32[]{:S(2)}, u32[]{:S(2)}) collective-permute-start(bf16[35,32,128]{2,1,0:T(8,128)(2,1)} %get-tuple-element.57), channel_id=1, source_target_pairs={{0,6},{1,7},{2,0},{3,1},{4,2},{5,3},{6,4},{7,5},{8,14},{9,15},{10,... | collective-permute-start | bytes 860168 | tf_op jit(solution)/shard_map/ppermute | solution.py:330
  96.1 92.5 %collective-permute-start.13 = (bf16[35,32,128]{2,1,0:T(8,128)(2,1)}, bf16[35,32,128]{2,1,0:T(8,128)(2,1)S(1)}, u32[]{:S(2)}, u32[]{:S(2)}) collective-permute-start(bf16[35,32,128]{2,1,0:T(8,128)(2,1)} %get-tuple-element.58), channel_id=1, source_target_pairs={{0,7},{1,0},{2,1},{3,2},{4,3},{5,4},{6,5},{7,6},{8,15},{9,8},{10,9... | collective-permute-start | bytes 860168 | tf_op jit(solution)/shard_map/ppermute | solution.py:330
  141.2 83.4 %collective-permute-start = (bf16[96,32,128]{2,1,0:T(8,128)(2,1)}, bf16[96,32,128]{2,1,0:T(8,128)(2,1)S(1)}, u32[]{:S(2)}, u32[]{:S(2)}) collective-permute-start(bf16[96,32,128]{2,1,0:T(8,128)(2,1)} %copy-done.33), channel_id=1, source_target_pairs={{0,1},{1,2},{2,3},{3,4},{4,5},{5,6},{6,7},{7,0},{8,9},{9,10},{10,1... | collective-permute-start | bytes 2359304 | tf_op jit(solution)/shard_map/ppermute | solution.py:330
  142.3 85.6 %collective-permute-start.1 = (bf16[96,32,128]{2,1,0:T(8,128)(2,1)}, bf16[96,32,128]{2,1,0:T(8,128)(2,1)}, u32[]{:S(2)}, u32[]{:S(2)}) collective-permute-start(bf16[96,32,128]{2,1,0:T(8,128)(2,1)} %copy-done.32), channel_id=1, source_target_pairs={{0,2},{1,3},{2,4},{3,5},{4,6},{5,7},{6,0},{7,1},{8,10},{9,11},{10,... | collective-permute-start | bytes 2359304 | tf_op jit(solution)/shard_map/ppermute | solution.py:330
  152.6 91.6 %collective-permute-start.2 = (bf16[96,32,128]{2,1,0:T(8,128)(2,1)}, bf16[96,32,128]{2,1,0:T(8,128)(2,1)}, u32[]{:S(2)}, u32[]{:S(2)}) collective-permute-start(bf16[96,32,128]{2,1,0:T(8,128)(2,1)} %copy-done.31), channel_id=1, source_target_pairs={{0,3},{1,4},{2,5},{3,6},{4,7},{5,0},{6,1},{7,2},{8,11},{9,12},{10,... | collective-permute-start | bytes 2359304 | tf_op jit(solution)/shard_map/ppermute | solution.py:330
  158.5 86.7 %collective-permute-start.3 = (bf16[96,32,128]{2,1,0:T(8,128)(2,1)}, bf16[96,32,128]{2,1,0:T(8,128)(2,1)}, u32[]{:S(2)}, u32[]{:S(2)}) collective-permute-start(bf16[96,32,128]{2,1,0:T(8,128)(2,1)} %copy-done.30), channel_id=1, source_target_pairs={{0,4},{1,5},{2,6},{3,7},{4,0},{5,1},{6,2},{7,3},{8,12},{9,13},{10,... | collective-permute-start | bytes 2359304 | tf_op jit(solution)/shard_map/ppermute | solution.py:330
  188.6 56.5 %collective-permute-start.4 = (bf16[96,32,128]{2,1,0:T(8,128)(2,1)}, bf16[96,32,128]{2,1,0:T(8,128)(2,1)}, u32[]{:S(2)}, u32[]{:S(2)}) collective-permute-start(bf16[96,32,128]{2,1,0:T(8,128)(2,1)} %copy-done.29), channel_id=1, source_target_pairs={{0,5},{1,6},{2,7},{3,0},{4,1},{5,2},{6,3},{7,4},{8,13},{9,14},{10,... | collective-permute-start | bytes 2359304 | tf_op jit(solution)/shard_map/ppermute | solution.py:330
  224.7 50.3 %collective-permute-start.5 = (bf16[96,32,128]{2,1,0:T(8,128)(2,1)}, bf16[96,32,128]{2,1,0:T(8,128)(2,1)S(1)}, u32[]{:S(2)}, u32[]{:S(2)}) collective-permute-start(bf16[96,32,128]{2,1,0:T(8,128)(2,1)} %get-tuple-element.49), channel_id=1, source_target_pairs={{0,6},{1,7},{2,0},{3,1},{4,2},{5,3},{6,4},{7,5},{8,14},{9,15},{10,... | collective-permute-start | bytes 2359304 | tf_op jit(solution)/shard_map/ppermute | solution.py:330
  227.9 47.2 %collective-permute-start.6 = (bf16[96,32,128]{2,1,0:T(8,128)(2,1)}, bf16[96,32,128]{2,1,0:T(8,128)(2,1)}, u32[]{:S(2)}, u32[]{:S(2)}) collective-permute-start(bf16[96,32,128]{2,1,0:T(8,128)(2,1)} %get-tuple-element.50), channel_id=1, source_target_pairs={{0,7},{1,0},{2,1},{3,2},{4,3},{5,4},{6,5},{7,6},{8,15},{9,8},{10,9... | collective-permute-start | bytes 2359304 | tf_op jit(solution)/shard_map/ppermute | solution.py:330
  275.9 138.8 %all-to-all-start.1 = ((bf16[8,32,32,128]{3,2,1,0:T(8,128)(2,1)}), bf16[8,32,32,128]{3,2,1,0:T(8,128)(2,1)S(1)}, u32[]{:S(2)}, u32[]{:S(2)}) async-start(bf16[8,32,32,128]{3,2,1,0:T(8,128)(2,1)} %shard_map.140), calls=%async_computation.1 | async-start | bytes 4194304 | tf_op jit(solution)/shard_map/all_to_all | solution.py:326
  329.3 8.5 %collective-permute-start.28 = (f32[464,128]{1,0:T(8,128)}, f32[464,128]{1,0:T(8,128)}, u32[]{:S(2)}, u32[]{:S(2)}) collective-permute-start(f32[464,128]{1,0:T(8,128)} %slice_select_fusion), channel_id=1, source_target_pairs={{0,16},{8,24},{16,0},{24,8},{1,17},{9,25},{17,1},{25,9},{2,18},{10... | collective-permute-start | bytes 712712 | tf_op jit(solution)/shard_map/ppermute | solution.py:290
  330.8 15.0 %collective-permute-start.19 = (bf16[48,32,128]{2,1,0:T(8,128)(2,1)}, bf16[48,32,128]{2,1,0:T(8,128)(2,1)S(1)}, u32[]{:S(2)}, u32[]{:S(2)}) collective-permute-start(bf16[48,32,128]{2,1,0:T(8,128)(2,1)} %copy-done.35), channel_id=1, source_target_pairs={{0,2},{1,3},{2,4},{3,5},{4,6},{5,7},{6,0},{7,1},{8,10},{9,11},{10,... | collective-permute-start | bytes 1179656 | tf_op jit(solution)/shard_map/ppermute | solution.py:330
  332.8 16.8 %collective-permute-start.20 = (bf16[48,32,128]{2,1,0:T(8,128)(2,1)}, bf16[48,32,128]{2,1,0:T(8,128)(2,1)S(1)}, u32[]{:S(2)}, u32[]{:S(2)}) collective-permute-start(bf16[48,32,128]{2,1,0:T(8,128)(2,1)} %copy-done.34), channel_id=1, source_target_pairs={{0,1},{1,2},{2,3},{3,4},{4,5},{5,6},{6,7},{7,0},{8,9},{9,10},{10,1... | collective-permute-start | bytes 1179656 | tf_op jit(solution)/shard_map/ppermute | solution.py:330
  378.6 7.0 %collective-permute-start.21 = (bf16[16,32,128]{2,1,0:T(8,128)(2,1)}, bf16[16,32,128]{2,1,0:T(8,128)(2,1)S(1)}, u32[]{:S(2)}, u32[]{:S(2)}) collective-permute-start(bf16[16,32,128]{2,1,0:T(8,128)(2,1)} %copy-done.42), channel_id=1, source_target_pairs={{0,7},{1,0},{2,1},{3,2},{4,3},{5,4},{6,5},{7,6},{8,15},{9,8},{10,9... | collective-permute-start | bytes 393224 | tf_op jit(solution)/shard_map/ppermute | solution.py:330
  379.7 9.1 %collective-permute-start.22 = (bf16[16,32,128]{2,1,0:T(8,128)(2,1)}, bf16[16,32,128]{2,1,0:T(8,128)(2,1)S(1)}, u32[]{:S(2)}, u32[]{:S(2)}) collective-permute-start(bf16[16,32,128]{2,1,0:T(8,128)(2,1)} %copy-done.41), channel_id=1, source_target_pairs={{0,6},{1,7},{2,0},{3,1},{4,2},{5,3},{6,4},{7,5},{8,14},{9,15},{10,... | collective-permute-start | bytes 393224 | tf_op jit(solution)/shard_map/ppermute | solution.py:330
  380.5 9.1 %collective-permute-start.23 = (bf16[16,32,128]{2,1,0:T(8,128)(2,1)}, bf16[16,32,128]{2,1,0:T(8,128)(2,1)S(1)}, u32[]{:S(2)}, u32[]{:S(2)}) collective-permute-start(bf16[16,32,128]{2,1,0:T(8,128)(2,1)} %copy-done.40), channel_id=1, source_target_pairs={{0,5},{1,6},{2,7},{3,0},{4,1},{5,2},{6,3},{7,4},{8,13},{9,14},{10,... | collective-permute-start | bytes 393224 | tf_op jit(solution)/shard_map/ppermute | solution.py:330
  383.4 26.2 %collective-permute-start.31 = (f32[464,128]{1,0:T(8,128)}, f32[464,128]{1,0:T(8,128)}, u32[]{:S(2)}, u32[]{:S(2)}) collective-permute-start(f32[464,128]{1,0:T(8,128)} %pad_maximum_fusion), channel_id=1, source_target_pairs={{0,16},{8,24},{16,0},{24,8},{1,17},{9,25},{17,1},{25,9},{2,18},{10... | collective-permute-start | bytes 712712 | tf_op jit(solution)/shard_map/ppermute | solution.py:290
  384.9 17.1 %collective-permute-start.24 = (bf16[16,32,128]{2,1,0:T(8,128)(2,1)}, bf16[16,32,128]{2,1,0:T(8,128)(2,1)S(1)}, u32[]{:S(2)}, u32[]{:S(2)}) collective-permute-start(bf16[16,32,128]{2,1,0:T(8,128)(2,1)} %copy-done.39), channel_id=1, source_target_pairs={{0,4},{1,5},{2,6},{3,7},{4,0},{5,1},{6,2},{7,3},{8,12},{9,13},{10,... | collective-permute-start | bytes 393224 | tf_op jit(solution)/shard_map/ppermute | solution.py:330
  385.7 17.7 %collective-permute-start.25 = (bf16[16,32,128]{2,1,0:T(8,128)(2,1)}, bf16[16,32,128]{2,1,0:T(8,128)(2,1)S(1)}, u32[]{:S(2)}, u32[]{:S(2)}) collective-permute-start(bf16[16,32,128]{2,1,0:T(8,128)(2,1)} %copy-done.38), channel_id=1, source_target_pairs={{0,3},{1,4},{2,5},{3,6},{4,7},{5,0},{6,1},{7,2},{8,11},{9,12},{10,... | collective-permute-start | bytes 393224 | tf_op jit(solution)/shard_map/ppermute | solution.py:330
  388.8 14.6 %collective-permute-start.26 = (bf16[16,32,128]{2,1,0:T(8,128)(2,1)}, bf16[16,32,128]{2,1,0:T(8,128)(2,1)S(1)}, u32[]{:S(2)}, u32[]{:S(2)}) collective-permute-start(bf16[16,32,128]{2,1,0:T(8,128)(2,1)} %copy-done.37), channel_id=1, source_target_pairs={{0,2},{1,3},{2,4},{3,5},{4,6},{5,7},{6,0},{7,1},{8,10},{9,11},{10,... | collective-permute-start | bytes 393224 | tf_op jit(solution)/shard_map/ppermute | solution.py:330
  389.6 13.8 %collective-permute-start.27 = (bf16[16,32,128]{2,1,0:T(8,128)(2,1)}, bf16[16,32,128]{2,1,0:T(8,128)(2,1)}, u32[]{:S(2)}, u32[]{:S(2)}) collective-permute-start(bf16[16,32,128]{2,1,0:T(8,128)(2,1)} %copy-done.36), channel_id=1, source_target_pairs={{0,1},{1,2},{2,3},{3,4},{4,5},{5,6},{6,7},{7,0},{8,9},{9,10},{10,1... | collective-permute-start | bytes 393224 | tf_op jit(solution)/shard_map/ppermute | solution.py:330
  406.0 11.7 %collective-permute-start.14 = (bf16[48,32,128]{2,1,0:T(8,128)(2,1)}, bf16[48,32,128]{2,1,0:T(8,128)(2,1)}, u32[]{:S(2)}, u32[]{:S(2)}) collective-permute-start(bf16[48,32,128]{2,1,0:T(8,128)(2,1)} %get-tuple-element.60), channel_id=1, source_target_pairs={{0,7},{1,0},{2,1},{3,2},{4,3},{5,4},{6,5},{7,6},{8,15},{9,8},{10,9... | collective-permute-start | bytes 1179656 | tf_op jit(solution)/shard_map/ppermute | solution.py:330
  406.0 20.1 %collective-permute-start.15 = (bf16[48,32,128]{2,1,0:T(8,128)(2,1)}, bf16[48,32,128]{2,1,0:T(8,128)(2,1)}, u32[]{:S(2)}, u32[]{:S(2)}) collective-permute-start(bf16[48,32,128]{2,1,0:T(8,128)(2,1)} %get-tuple-element.61), channel_id=1, source_target_pairs={{0,6},{1,7},{2,0},{3,1},{4,2},{5,3},{6,4},{7,5},{8,14},{9,15},{10,... | collective-permute-start | bytes 1179656 | tf_op jit(solution)/shard_map/ppermute | solution.py:330
  407.8 24.9 %collective-permute-start.16 = (bf16[48,32,128]{2,1,0:T(8,128)(2,1)}, bf16[48,32,128]{2,1,0:T(8,128)(2,1)}, u32[]{:S(2)}, u32[]{:S(2)}) collective-permute-start(bf16[48,32,128]{2,1,0:T(8,128)(2,1)} %get-tuple-element.62), channel_id=1, source_target_pairs={{0,5},{1,6},{2,7},{3,0},{4,1},{5,2},{6,3},{7,4},{8,13},{9,14},{10,... | collective-permute-start | bytes 1179656 | tf_op jit(solution)/shard_map/ppermute | solution.py:330
  409.6 56.3 %collective-permute-start.17 = (bf16[48,32,128]{2,1,0:T(8,128)(2,1)}, bf16[48,32,128]{2,1,0:T(8,128)(2,1)}, u32[]{:S(2)}, u32[]{:S(2)}) collective-permute-start(bf16[48,32,128]{2,1,0:T(8,128)(2,1)} %get-tuple-element.63), channel_id=1, source_target_pairs={{0,4},{1,5},{2,6},{3,7},{4,0},{5,1},{6,2},{7,3},{8,12},{9,13},{10,... | collective-permute-start | bytes 1179656 | tf_op jit(solution)/shard_map/ppermute | solution.py:330
  409.6 56.3 %collective-permute-start.18 = (bf16[48,32,128]{2,1,0:T(8,128)(2,1)}, bf16[48,32,128]{2,1,0:T(8,128)(2,1)}, u32[]{:S(2)}, u32[]{:S(2)}) collective-permute-start(bf16[48,32,128]{2,1,0:T(8,128)(2,1)} %get-tuple-element.64), channel_id=1, source_target_pairs={{0,3},{1,4},{2,5},{3,6},{4,7},{5,0},{6,1},{7,2},{8,11},{9,12},{10,... | collective-permute-start | bytes 1179656 | tf_op jit(solution)/shard_map/ppermute | solution.py:330
  (54 other events, 1471.8 us)

commit v11 on v10

--- a/solution.py
+++ b/solution.py
@@ -281,26 +281,33 @@
     )
 
 
-def sum_over_mesh(sums, after):
-    size = lax.axis_size("dp")
+def sum_over_mesh(sums, beside):
+    beside = [None, *beside]
+
+    def exchange_with(array, axis, bit):
+        after = beside.pop(0) if beside else None
+        if after is not None:
+            (array,) = hold([array], after)
+        size = lax.axis_size(axis)
+        return array, lax.ppermute(array, axis, [(i, i ^ bit) for i in range(size)])
+
     dp = lax.axis_index("dp")
-    bits = [1 << k for k in range(size.bit_length() - 1)]
-
-    def exchange_with(array, bit):
-        return lax.ppermute(array, "dp", [(i, i ^ bit) for i in range(size)])
-
+    bits = [1 << k for k in range(lax.axis_size("dp").bit_length() - 1)]
     for bit in reversed(bits):
         halves = sums.reshape(2, -1, LANES)
         high = (dp & bit) != 0
-        other = exchange_with(jnp.where(high, halves[0], halves[1]), bit)
+        _, other = exchange_with(jnp.where(high, halves[0], halves[1]), "dp", bit)
         sums = jnp.where(high, halves[1], halves[0]) + other
-    (sums,) = hold([sums], after)
-    sums = own = jnp.sum(lax.all_gather(sums, "ctx"), axis=0)
+    bit = 1
+    while bit < lax.axis_size("ctx"):
+        sums, other = exchange_with(sums, "ctx", bit)
+        sums = sums + other
+        bit *= 2
     for bit in bits:
-        other = exchange_with(sums, bit)
+        sums, other = exchange_with(sums, "dp", bit)
         high = (dp & bit) != 0
         sums = jnp.concatenate([jnp.where(high, other, sums), jnp.where(high, sums, other)])
-    return sums, own
+    return sums
 
 
 def body(tokens, cotangent, first_factor, second_factor, twiddle, gate_gain, gate_bias, skip_gain):
@@ -360,13 +367,14 @@
             terms.append(own_sums)
         leaving.append(returned)
 
-    sums, own_sums = sum_over_mesh(add(terms, []), [part for r in leaving for part in r[2][-2:]])
+    back = leaving[-1][2]
+    sums = sum_over_mesh(add(terms, []), [None, back[-2:], back[1:2], back[2:3], back[3:5], back[5:-2]])
     grads = []
     for returned in leaving:
         held = None
-        for which in (0, 1, 2):
+        for which in (1, 2, 0):
             at, count, rotated = groups[which]
-            after = [own_sums] if which else []
+            after = []
             held = merge_channels(
                 place, returned[which], held, at, count, ctx_size, rotated, width, after
             )

time: 475 us -> 465 us (0.979)
  starting transfers between devices: 134 us -> 170 us
  waiting for transfers between devices: 196 us -> 170 us
  blocking collectives: 25.5 us -> 0 us
    ppermute x28, waiting for transfers between devices: 185 us -> 140 us  [exchange(): moved.append(lax.ppermute(parts[shift], 'ctx', pairs))]
    all_gather x1 -> x0, blocking collectives: 25.5 us -> none  [sum_over_mesh(): sums = own = jnp.sum(lax.all_gather(sums, 'ctx'), axis=0)]
    ppermute x4 -> x7, starting transfers between devices: 6.16 us -> 27.2 us  [exchange_with(): lax.ppermute(array, axis, [(i, i ^ bit) for i in range(size)])]
    ppermute x4 -> x7, waiting for transfers between devices: 10.5 us -> 29.7 us  [exchange_with(): lax.ppermute(array, axis, [(i, i ^ bit) for i in range(size)])]
    ppermute x28, starting transfers between devices: 99.7 us -> 114 us  [exchange(): moved.append(lax.ppermute(parts[shift], 'ctx', pairs))]
    unnamed x113 -> x117, local copies, waits for them, and re-layouts: 27.2 us -> 30.8 us
  transfers between devices with their start and end apart: 34 -> 37, of which waited for: 19 -> 18; matrix products, arithmetic and copies ran while one was open for 2% -> 3% of each run, Pallas kernels for 14% -> 15%
where the time goes in v11:
time: 465 us; the launch traced here: 462 us
  starting transfers between devices  170 us (37%)
  waiting for transfers between devices  170 us (37%)
  Pallas kernels  77.8 us (17%)
  local copies, waits for them, and re-layouts  30.9 us (7%)
  other arithmetic  13 us (3%)
    ppermute x28, waiting for transfers between devices, exchange(): moved.append(lax.ppermute(parts[shift], 'ctx', pairs))  140 us
    ppermute x28, starting transfers between devices, exchange(): moved.append(lax.ppermute(parts[shift], 'ctx', pairs))  114 us
    pallas_call x3, Pallas kernels, mix(): pl.pallas_call(functools.partial(mix_kernel, parts=len(parts), tile=tile,...  39.3 us
    unnamed x117, local copies, waits for them, and re-layouts  30.8 us
    ppermute x7, waiting for transfers between devices, exchange_with(): lax.ppermute(array, axis, [(i, i ^ bit) for i in range(size)])  29.7 us
    all_to_all x2, starting transfers between devices, exchange(): lax.all_to_all(parts[0], 'ctx', split_axis=0, concat_axis=0, tiled=True)  28.7 us
    ppermute x7, starting transfers between devices, exchange_with(): lax.ppermute(array, axis, [(i, i ^ bit) for i in range(size)])  27.2 us
    pallas_call x3, Pallas kernels, split_channels(): pl.pallas_call(functools.partial(kernel, rotated=rotated), grid=(tiles, r...  24.8 us
  transfers between devices with their start and end apart: 37, of which 18 were waited for; matrix products, arithmetic and copies ran while one was open for 3% of the time, Pallas kernels for 15%

profile of v11, /device:TPU:0, one launch (start us, length us, event | category | flops | bytes accessed | tf_op | source)
XLA Modules:
  0.0 461.9 jit_solution(10924195311108748779)
XLA Ops:
  0.6 7.8 %shard_map.139 = bf16[8,64,32,128]{3,2,1,0:T(8,128)(2,1)S(1)} custom-call(s32[1]{0:T(128)} %bitcast.place_ref, bf16[32,128,768]{2,1,0:T(8,128)(2,1)} %bitcast.51, bf16[32,128,768]{2,1,0:T(8,128)(2,1)} %bitcast.54), custom_call_target="tpu_custom_call" | custom-call | flops 1 | bytes 16777216 | tf_op jit(solution)/shard_map/pallas_call | solution.py:83
  10.5 6.5 %all-to-all-start = ((bf16[8,64,32,128]{3,2,1,0:T(8,128)(2,1)}), bf16[8,64,32,128]{3,2,1,0:T(8,128)(2,1)}, u32[]{:S(2)}, u32[]{:S(2)}) async-start(bf16[8,64,32,128]{3,2,1,0:T(8,128)(2,1)} %copy-done), calls=%async_computation | async-start | bytes 8388608 | tf_op jit(solution)/shard_map/all_to_all | solution.py:333
  17.0 5.3 %shard_map.135 = (bf16[35,32,128]{2,1,0:T(8,128)(2,1)S(1)}, bf16[35,32,128]{2,1,0:T(8,128)(2,1)S(1)}, bf16[35,32,128]{2,1,0:T(8,128)(2,1)S(1)}, bf16[35,32,128]{...) custom-call(s32[1]{0:T(128)} %bitcast.place_ref, ...), custom_call_target="tpu_custom_call" | custom-call | flops 1 | bytes 8388608 | tf_op jit(solution)/shard_map/pallas_call | solution.py:83
  24.4 2.2 collective-permute-start.2
  29.2 11.7 %shard_map.137 = (bf16[96,32,128]{2,1,0:T(8,128)(2,1)S(1)}, bf16[96,32,128]{2,1,0:T(8,128)(2,1)S(1)}, bf16[96,32,128]{2,1,0:T(8,128)(2,1)S(1)}, bf16[96,32,128]{...) custom-call(s32[1]{0:T(128)} %bitcast.place_ref, ...), custom_call_target="tpu_custom_call" | custom-call | flops 1 | bytes 25165824 | tf_op jit(solution)/shard_map/pallas_call | solution.py:83
  46.5 48.7 %collective-permute-done.rest_1_.rest_9_ = bf16[35,32,128]{2,1,0:T(8,128)(2,1)S(1)} collective-permute-done((bf16[35,32,128]{2,1,0:T(8,128)(2,1)S(1)}, bf16[35,32,128]{2,1,0:T(8,128)(2,1)S(1)}, u32[]{:S(2)}, u32[]{:S(2)}) %collective-permute-start) | collective-permute-done | bytes 286752 | tf_op jit(solution)/shard_map/ppermute | solution.py:337
  96.1 4.4 collective-permute-start.6
  100.6 40.7 %collective-permute-done.2.rest_3_.rest_11_ = bf16[35,32,128]{2,1,0:T(8,128)(2,1)S(1)} collective-permute-done((bf16[35,32,128]{2,1,0:T(8,128)(2,1)S(1)}, bf16[35,32,128]{2,1,0:T(8,128)(2,1)S(1)}, u32[]{:S(2)}, u32[]{:S(2)}) %collective-permute-start.2) | collective-permute-done | bytes 286752 | tf_op jit(solution)/shard_map/ppermute | solution.py:337
  142.3 10.3 %collective-permute-start.15 = (bf16[96,32,128]{2,1,0:T(8,128)(2,1)}, bf16[96,32,128]{2,1,0:T(8,128)(2,1)}, u32[]{:S(2)}, u32[]{:S(2)}) collective-permute-start(bf16[96,32,128]{2,1,0:T(8,128)(2,1)} %copy-done.32), channel_id=1, source_target_pairs={{0,2},{1,3},{2,4},{3,5},{4,6},{5,7},{6,0},{7,1},{8,10},{9,11},{10,... | collective-permute-start | bytes 2359304 | tf_op jit(solution)/shard_map/ppermute | solution.py:337
  152.6 5.9 %collective-permute-start.16 = (bf16[96,32,128]{2,1,0:T(8,128)(2,1)}, bf16[96,32,128]{2,1,0:T(8,128)(2,1)}, u32[]{:S(2)}, u32[]{:S(2)}) collective-permute-start(bf16[96,32,128]{2,1,0:T(8,128)(2,1)} %copy-done.31), channel_id=1, source_target_pairs={{0,3},{1,4},{2,5},{3,6},{4,7},{5,0},{6,1},{7,2},{8,11},{9,12},{10,... | collective-permute-start | bytes 2359304 | tf_op jit(solution)/shard_map/ppermute | solution.py:337
  158.5 29.4 %collective-permute-start.17 = (bf16[96,32,128]{2,1,0:T(8,128)(2,1)}, bf16[96,32,128]{2,1,0:T(8,128)(2,1)}, u32[]{:S(2)}, u32[]{:S(2)}) collective-permute-start(bf16[96,32,128]{2,1,0:T(8,128)(2,1)} %copy-done.30), channel_id=1, source_target_pairs={{0,4},{1,5},{2,6},{3,7},{4,0},{5,1},{6,2},{7,3},{8,12},{9,13},{10,... | collective-permute-start | bytes 2359304 | tf_op jit(solution)/shard_map/ppermute | solution.py:337
  188.6 21.8 %collective-permute-start.18 = (bf16[96,32,128]{2,1,0:T(8,128)(2,1)}, bf16[96,32,128]{2,1,0:T(8,128)(2,1)}, u32[]{:S(2)}, u32[]{:S(2)}) collective-permute-start(bf16[96,32,128]{2,1,0:T(8,128)(2,1)} %copy-done.29), channel_id=1, source_target_pairs={{0,5},{1,6},{2,7},{3,0},{4,1},{5,2},{6,3},{7,4},{8,13},{9,14},{10,... | collective-permute-start | bytes 2359304 | tf_op jit(solution)/shard_map/ppermute | solution.py:337
  213.2 6.1 %shard_map.136 = (bf16[16,32,128]{2,1,0:T(8,128)(2,1)S(1)}, bf16[16,32,128]{2,1,0:T(8,128)(2,1)S(1)}, bf16[16,32,128]{2,1,0:T(8,128)(2,1)S(1)}, bf16[16,32,128]{...) custom-call(s32[1]{0:T(128)} %bitcast.place_ref, ...), custom_call_target="tpu_custom_call" | custom-call | flops 8388608000 | bytes 1024 | tf_op jit(solution)/shard_map/pallas_call | solution.py:222
  224.7 3.2 collective-permute-start.19
  227.9 13.8 %shard_map.140 = (bf16[8,32,32,128]{3,2,1,0:T(8,128)(2,1)S(1)}, f32[928,128]{1,0:T(8,128)S(1)}) custom-call(s32[1]{0:T(128)} %bitcast.place_ref, f32[768]{0:T(1024)S(1)} %copy-done.48, f32[768]{0:T(1024)S(1)} %copy-done.49, f32[768]{0:T(1024)S(1)} %copy-done.50, bf16[8,64,32,128]{3,2,1,0:T(8,128)(2,1)} %all-to-all-done.rest_0_.rest_1_, ...), custom_call_target="tpu_custom_call" | custom-call | flops 16777216000 | bytes 1024 | tf_op jit(solution)/shard_map/pallas_call | solution.py:222
  245.1 29.8 %collective-permute-done.19.rest_6_.rest_14_.refs_6_ = bf16[96,32,128]{2,1,0:T(8,128)(2,1)S(1)} collective-permute-done((bf16[96,32,128]{2,1,0:T(8,128)(2,1)}, bf16[96,32,128]{2,1,0:T(8,128)(2,1)S(1)}, u32[]{:S(2)}, u32[]{:S(2)}) %collective-permute-start.19) | collective-permute-done | bytes 786464 | tf_op jit(solution)/shard_map/ppermute | solution.py:337
  276.2 22.2 %all-to-all-start.1 = ((bf16[8,32,32,128]{3,2,1,0:T(8,128)(2,1)}), bf16[8,32,32,128]{3,2,1,0:T(8,128)(2,1)S(1)}, u32[]{:S(2)}, u32[]{:S(2)}) async-start(bf16[8,32,32,128]{3,2,1,0:T(8,128)(2,1)} %shard_map.141), calls=%async_computation.1 | async-start | bytes 4194304 | tf_op jit(solution)/shard_map/all_to_all | solution.py:333
  300.4 19.4 %shard_map.138 = (bf16[48,32,128]{2,1,0:T(8,128)(2,1)S(1)}, bf16[48,32,128]{2,1,0:T(8,128)(2,1)S(1)}, bf16[48,32,128]{2,1,0:T(8,128)(2,1)S(1)}, bf16[48,32,128]{...) custom-call(s32[1]{0:T(128)} %bitcast.place_ref, ...), custom_call_target="tpu_custom_call" | custom-call | flops 25165824000 | bytes 1024 | tf_op jit(solution)/shard_map/pallas_call | solution.py:222
  326.7 2.2 shard_map.145
  333.6 4.6 %collective-permute-done.28 = f32[464,128]{1,0:T(8,128)S(1)} collective-permute-done((f32[464,128]{1,0:T(8,128)S(1)}, f32[464,128]{1,0:T(8,128)S(1)}, u32[]{:S(2)}, u32[]{:S(2)}) %collective-permute-start.28) | collective-permute-done | bytes 237600 | tf_op jit(solution)/shard_map/ppermute | solution.py:292
  340.9 2.2 collective-permute-start.21
  346.2 22.3 %collective-permute-start.23 = (bf16[48,32,128]{2,1,0:T(8,128)(2,1)}, bf16[48,32,128]{2,1,0:T(8,128)(2,1)}, u32[]{:S(2)}, u32[]{:S(2)}) collective-permute-start(bf16[48,32,128]{2,1,0:T(8,128)(2,1)} %copy-done.36), channel_id=1, source_target_pairs={{0,5},{1,6},{2,7},{3,0},{4,1},{5,2},{6,3},{7,4},{8,13},{9,14},{10,... | collective-permute-start | bytes 1179656 | tf_op jit(solution)/shard_map/ppermute | solution.py:337
  373.6 20.9 %collective-permute-start.31 = (f32[232,128]{1,0:T(8,128)}, f32[232,128]{1,0:T(8,128)S(1)}, u32[]{:S(2)}, u32[]{:S(2)}) collective-permute-start(f32[232,128]{1,0:T(8,128)} %shard_map.147), channel_id=1, source_target_pairs={{0,2},{1,3},{2,0},{3,1},{4,6},{5,7},{6,4},{7,5},{8,10},{9,11},{10,... | collective-permute-start | bytes 356360 | tf_op jit(solution)/shard_map/ppermute | solution.py:292
  394.5 10.3 %collective-permute-done.31 = f32[232,128]{1,0:T(8,128)S(1)} collective-permute-done((f32[232,128]{1,0:T(8,128)}, f32[232,128]{1,0:T(8,128)S(1)}, u32[]{:S(2)}, u32[]{:S(2)}) %collective-permute-start.31) | collective-permute-done | bytes 118816 | tf_op jit(solution)/shard_map/ppermute | solution.py:292
  407.1 8.0 %collective-permute-done.32 = f32[232,128]{1,0:T(8,128)S(1)} collective-permute-done((f32[232,128]{1,0:T(8,128)}, f32[232,128]{1,0:T(8,128)S(1)}, u32[]{:S(2)}, u32[]{:S(2)}) %collective-permute-start.32) | collective-permute-done | bytes 118816 | tf_op jit(solution)/shard_map/ppermute | solution.py:292
  418.2 3.9 collective-permute-done.33
  423.7 10.0 %collective-permute-done.25.rest_5_.refs_1_ = bf16[48,32,128]{2,1,0:T(8,128)(2,1)S(1)} collective-permute-done((bf16[48,32,128]{2,1,0:T(8,128)(2,1)}, bf16[48,32,128]{2,1,0:T(8,128)(2,1)S(1)}, u32[]{:S(2)}, u32[]{:S(2)}) %collective-permute-start.25) | collective-permute-done | bytes 393248 | tf_op jit(solution)/shard_map/ppermute | solution.py:337
  436.8 2.8 collective-permute-start.10
  445.9 3.0 shard_map.142.rest_8_
  448.9 5.9 %shard_map.143.rest_8_ = bf16[32,128,768]{2,1,0:T(8,128)(2,1)} custom-call(s32[1]{0:T(128)} %bitcast.place_ref, bf16[48,32,128]{2,1,0:T(8,128)(2,1)S(1)} %copy-done.16, bf16[48,32,128]{2,1,0:T(8,128)(2,1)S(1)} %copy-done.3, bf16[48,32,128]{2,1,0:T(8,128)(2,1)S(1)} %copy-done.5, ...), custom_call_target="tpu_custom_call", output_to_operand_aliasing={{}: (9, {})} | custom-call | flops 1 | bytes 12582912 | tf_op jit(solution)/shard_map/pallas_call | solution.py:117
  454.8 3.4 collective-permute-done.10.rest_4_
  459.2 2.7 shard_map.144
  (196 shorter events, 69.6 us)
Async XLA Ops:
  10.5 217.4 %all-to-all-start = ((bf16[8,64,32,128]{3,2,1,0:T(8,128)(2,1)}), bf16[8,64,32,128]{3,2,1,0:T(8,128)(2,1)}, u32[]{:S(2)}, u32[]{:S(2)}) async-start(bf16[8,64,32,128]{3,2,1,0:T(8,128)(2,1)} %copy-done), calls=%async_computation | async-start | bytes 8388608 | tf_op jit(solution)/shard_map/all_to_all | solution.py:333
  22.2 73.0 %collective-permute-start = (bf16[35,32,128]{2,1,0:T(8,128)(2,1)S(1)}, bf16[35,32,128]{2,1,0:T(8,128)(2,1)S(1)}, u32[]{:S(2)}, u32[]{:S(2)}) collective-permute-start(bf16[35,32,128]{2,1,0:T(8,128)(2,1)S(1)} %get-tuple-element.44), channel_id=1, source_target_pairs={{0,1},{1,2},{2,3},{3,4},{4,5},{5,6},{6,7},{7,0},{8,9},{9,10},{10,1... | collective-permute-start | bytes 860168 | tf_op jit(solution)/shard_map/ppermute | solution.py:337
  22.7 73.4 %collective-permute-start.1 = (bf16[35,32,128]{2,1,0:T(8,128)(2,1)S(1)}, bf16[35,32,128]{2,1,0:T(8,128)(2,1)S(1)}, u32[]{:S(2)}, u32[]{:S(2)}) collective-permute-start(bf16[35,32,128]{2,1,0:T(8,128)(2,1)S(1)} %get-tuple-element.45), channel_id=1, source_target_pairs={{0,2},{1,3},{2,4},{3,5},{4,6},{5,7},{6,0},{7,1},{8,10},{9,11},{10,... | collective-permute-start | bytes 860168 | tf_op jit(solution)/shard_map/ppermute | solution.py:337
  24.4 116.9 %collective-permute-start.2 = (bf16[35,32,128]{2,1,0:T(8,128)(2,1)S(1)}, bf16[35,32,128]{2,1,0:T(8,128)(2,1)S(1)}, u32[]{:S(2)}, u32[]{:S(2)}) collective-permute-start(bf16[35,32,128]{2,1,0:T(8,128)(2,1)S(1)} %get-tuple-element.46), channel_id=1, source_target_pairs={{0,3},{1,4},{2,5},{3,6},{4,7},{5,0},{6,1},{7,2},{8,11},{9,12},{10,... | collective-permute-start | bytes 860168 | tf_op jit(solution)/shard_map/ppermute | solution.py:337
  26.6 115.7 %collective-permute-start.3 = (bf16[35,32,128]{2,1,0:T(8,128)(2,1)}, bf16[35,32,128]{2,1,0:T(8,128)(2,1)S(1)}, u32[]{:S(2)}, u32[]{:S(2)}) collective-permute-start(bf16[35,32,128]{2,1,0:T(8,128)(2,1)} %get-tuple-element.47), channel_id=1, source_target_pairs={{0,4},{1,5},{2,6},{3,7},{4,0},{5,1},{6,2},{7,3},{8,12},{9,13},{10,... | collective-permute-start | bytes 860168 | tf_op jit(solution)/shard_map/ppermute | solution.py:337
  28.1 124.5 %collective-permute-start.4 = (bf16[35,32,128]{2,1,0:T(8,128)(2,1)}, bf16[35,32,128]{2,1,0:T(8,128)(2,1)S(1)}, u32[]{:S(2)}, u32[]{:S(2)}) collective-permute-start(bf16[35,32,128]{2,1,0:T(8,128)(2,1)} %get-tuple-element.48), channel_id=1, source_target_pairs={{0,5},{1,6},{2,7},{3,0},{4,1},{5,2},{6,3},{7,4},{8,13},{9,14},{10,... | collective-permute-start | bytes 860168 | tf_op jit(solution)/shard_map/ppermute | solution.py:337
  95.2 63.3 %collective-permute-start.5 = (bf16[35,32,128]{2,1,0:T(8,128)(2,1)}, bf16[35,32,128]{2,1,0:T(8,128)(2,1)S(1)}, u32[]{:S(2)}, u32[]{:S(2)}) collective-permute-start(bf16[35,32,128]{2,1,0:T(8,128)(2,1)} %get-tuple-element.49), channel_id=1, source_target_pairs={{0,6},{1,7},{2,0},{3,1},{4,2},{5,3},{6,4},{7,5},{8,14},{9,15},{10,... | collective-permute-start | bytes 860168 | tf_op jit(solution)/shard_map/ppermute | solution.py:337
  96.1 92.5 %collective-permute-start.6 = (bf16[35,32,128]{2,1,0:T(8,128)(2,1)}, bf16[35,32,128]{2,1,0:T(8,128)(2,1)S(1)}, u32[]{:S(2)}, u32[]{:S(2)}) collective-permute-start(bf16[35,32,128]{2,1,0:T(8,128)(2,1)} %get-tuple-element.50), channel_id=1, source_target_pairs={{0,7},{1,0},{2,1},{3,2},{4,3},{5,4},{6,5},{7,6},{8,15},{9,8},{10,9... | collective-permute-start | bytes 860168 | tf_op jit(solution)/shard_map/ppermute | solution.py:337
  141.2 83.4 %collective-permute-start.14 = (bf16[96,32,128]{2,1,0:T(8,128)(2,1)}, bf16[96,32,128]{2,1,0:T(8,128)(2,1)S(1)}, u32[]{:S(2)}, u32[]{:S(2)}) collective-permute-start(bf16[96,32,128]{2,1,0:T(8,128)(2,1)} %copy-done.33), channel_id=1, source_target_pairs={{0,1},{1,2},{2,3},{3,4},{4,5},{5,6},{6,7},{7,0},{8,9},{9,10},{10,1... | collective-permute-start | bytes 2359304 | tf_op jit(solution)/shard_map/ppermute | solution.py:337
  142.3 85.6 %collective-permute-start.15 = (bf16[96,32,128]{2,1,0:T(8,128)(2,1)}, bf16[96,32,128]{2,1,0:T(8,128)(2,1)}, u32[]{:S(2)}, u32[]{:S(2)}) collective-permute-start(bf16[96,32,128]{2,1,0:T(8,128)(2,1)} %copy-done.32), channel_id=1, source_target_pairs={{0,2},{1,3},{2,4},{3,5},{4,6},{5,7},{6,0},{7,1},{8,10},{9,11},{10,... | collective-permute-start | bytes 2359304 | tf_op jit(solution)/shard_map/ppermute | solution.py:337
  152.6 91.6 %collective-permute-start.16 = (bf16[96,32,128]{2,1,0:T(8,128)(2,1)}, bf16[96,32,128]{2,1,0:T(8,128)(2,1)}, u32[]{:S(2)}, u32[]{:S(2)}) collective-permute-start(bf16[96,32,128]{2,1,0:T(8,128)(2,1)} %copy-done.31), channel_id=1, source_target_pairs={{0,3},{1,4},{2,5},{3,6},{4,7},{5,0},{6,1},{7,2},{8,11},{9,12},{10,... | collective-permute-start | bytes 2359304 | tf_op jit(solution)/shard_map/ppermute | solution.py:337
  158.5 86.7 %collective-permute-start.17 = (bf16[96,32,128]{2,1,0:T(8,128)(2,1)}, bf16[96,32,128]{2,1,0:T(8,128)(2,1)}, u32[]{:S(2)}, u32[]{:S(2)}) collective-permute-start(bf16[96,32,128]{2,1,0:T(8,128)(2,1)} %copy-done.30), channel_id=1, source_target_pairs={{0,4},{1,5},{2,6},{3,7},{4,0},{5,1},{6,2},{7,3},{8,12},{9,13},{10,... | collective-permute-start | bytes 2359304 | tf_op jit(solution)/shard_map/ppermute | solution.py:337
  188.6 56.5 %collective-permute-start.18 = (bf16[96,32,128]{2,1,0:T(8,128)(2,1)}, bf16[96,32,128]{2,1,0:T(8,128)(2,1)}, u32[]{:S(2)}, u32[]{:S(2)}) collective-permute-start(bf16[96,32,128]{2,1,0:T(8,128)(2,1)} %copy-done.29), channel_id=1, source_target_pairs={{0,5},{1,6},{2,7},{3,0},{4,1},{5,2},{6,3},{7,4},{8,13},{9,14},{10,... | collective-permute-start | bytes 2359304 | tf_op jit(solution)/shard_map/ppermute | solution.py:337
  224.7 50.3 %collective-permute-start.19 = (bf16[96,32,128]{2,1,0:T(8,128)(2,1)}, bf16[96,32,128]{2,1,0:T(8,128)(2,1)S(1)}, u32[]{:S(2)}, u32[]{:S(2)}) collective-permute-start(bf16[96,32,128]{2,1,0:T(8,128)(2,1)} %get-tuple-element.65), channel_id=1, source_target_pairs={{0,6},{1,7},{2,0},{3,1},{4,2},{5,3},{6,4},{7,5},{8,14},{9,15},{10,... | collective-permute-start | bytes 2359304 | tf_op jit(solution)/shard_map/ppermute | solution.py:337
  227.8 47.1 %collective-permute-start.20 = (bf16[96,32,128]{2,1,0:T(8,128)(2,1)}, bf16[96,32,128]{2,1,0:T(8,128)(2,1)S(1)}, u32[]{:S(2)}, u32[]{:S(2)}) collective-permute-start(bf16[96,32,128]{2,1,0:T(8,128)(2,1)} %get-tuple-element.66), channel_id=1, source_target_pairs={{0,7},{1,0},{2,1},{3,2},{4,3},{5,4},{6,5},{7,6},{8,15},{9,8},{10,9... | collective-permute-start | bytes 2359304 | tf_op jit(solution)/shard_map/ppermute | solution.py:337
  276.2 169.7 %all-to-all-start.1 = ((bf16[8,32,32,128]{3,2,1,0:T(8,128)(2,1)}), bf16[8,32,32,128]{3,2,1,0:T(8,128)(2,1)S(1)}, u32[]{:S(2)}, u32[]{:S(2)}) async-start(bf16[8,32,32,128]{3,2,1,0:T(8,128)(2,1)} %shard_map.141), calls=%async_computation.1 | async-start | bytes 4194304 | tf_op jit(solution)/shard_map/all_to_all | solution.py:333
  330.0 8.2 %collective-permute-start.28 = (f32[464,128]{1,0:T(8,128)S(1)}, f32[464,128]{1,0:T(8,128)S(1)}, u32[]{:S(2)}, u32[]{:S(2)}) collective-permute-start(f32[464,128]{1,0:T(8,128)S(1)} %slice_select_fusion), channel_id=1, source_target_pairs={{0,16},{8,24},{16,0},{24,8},{1,17},{9,25},{17,1},{25,9},{2,18},{10... | collective-permute-start | bytes 712712 | tf_op jit(solution)/shard_map/ppermute | solution.py:292
  331.6 14.7 %collective-permute-start.26 = (bf16[48,32,128]{2,1,0:T(8,128)(2,1)}, bf16[48,32,128]{2,1,0:T(8,128)(2,1)S(1)}, u32[]{:S(2)}, u32[]{:S(2)}) collective-permute-start(bf16[48,32,128]{2,1,0:T(8,128)(2,1)} %copy-done.40), channel_id=1, source_target_pairs={{0,2},{1,3},{2,4},{3,5},{4,6},{5,7},{6,0},{7,1},{8,10},{9,11},{10,... | collective-permute-start | bytes 1179656 | tf_op jit(solution)/shard_map/ppermute | solution.py:337
  333.6 36.1 %collective-permute-start.27 = (bf16[48,32,128]{2,1,0:T(8,128)(2,1)}, bf16[48,32,128]{2,1,0:T(8,128)(2,1)}, u32[]{:S(2)}, u32[]{:S(2)}) collective-permute-start(bf16[48,32,128]{2,1,0:T(8,128)(2,1)} %copy-done.39), channel_id=1, source_target_pairs={{0,1},{1,2},{2,3},{3,4},{4,5},{5,6},{6,7},{7,0},{8,9},{9,10},{10,1... | collective-permute-start | bytes 1179656 | tf_op jit(solution)/shard_map/ppermute | solution.py:337
  339.3 29.3 %collective-permute-start.29 = (f32[232,128]{1,0:T(8,128)S(1)}, f32[232,128]{1,0:T(8,128)S(1)}, u32[]{:S(2)}, u32[]{:S(2)}) collective-permute-start(f32[232,128]{1,0:T(8,128)S(1)} %slice_select_fusion.1), channel_id=1, source_target_pairs={{0,8},{8,0},{16,24},{24,16},{1,9},{9,1},{17,25},{25,17},{2,10},{10... | collective-permute-start | bytes 356360 | tf_op jit(solution)/shard_map/ppermute | solution.py:292
  340.9 31.9 %collective-permute-start.21 = (bf16[48,32,128]{2,1,0:T(8,128)(2,1)}, bf16[48,32,128]{2,1,0:T(8,128)(2,1)S(1)}, u32[]{:S(2)}, u32[]{:S(2)}) collective-permute-start(bf16[48,32,128]{2,1,0:T(8,128)(2,1)} %copy-done.38), channel_id=1, source_target_pairs={{0,7},{1,0},{2,1},{3,2},{4,3},{5,4},{6,5},{7,6},{8,15},{9,8},{10,9... | collective-permute-start | bytes 1179656 | tf_op jit(solution)/shard_map/ppermute | solution.py:337
  343.1 63.3 %collective-permute-start.22 = (bf16[48,32,128]{2,1,0:T(8,128)(2,1)}, bf16[48,32,128]{2,1,0:T(8,128)(2,1)S(1)}, u32[]{:S(2)}, u32[]{:S(2)}) collective-permute-start(bf16[48,32,128]{2,1,0:T(8,128)(2,1)} %copy-done.37), channel_id=1, source_target_pairs={{0,6},{1,7},{2,0},{3,1},{4,2},{5,3},{6,4},{7,5},{8,14},{9,15},{10,... | collective-permute-start | bytes 1179656 | tf_op jit(solution)/shard_map/ppermute | solution.py:337
  346.2 70.4 %collective-permute-start.23 = (bf16[48,32,128]{2,1,0:T(8,128)(2,1)}, bf16[48,32,128]{2,1,0:T(8,128)(2,1)}, u32[]{:S(2)}, u32[]{:S(2)}) collective-permute-start(bf16[48,32,128]{2,1,0:T(8,128)(2,1)} %copy-done.36), channel_id=1, source_target_pairs={{0,5},{1,6},{2,7},{3,0},{4,1},{5,2},{6,3},{7,4},{8,13},{9,14},{10,... | collective-permute-start | bytes 1179656 | tf_op jit(solution)/shard_map/ppermute | solution.py:337
  368.6 48.1 %collective-permute-start.24 = (bf16[48,32,128]{2,1,0:T(8,128)(2,1)}, bf16[48,32,128]{2,1,0:T(8,128)(2,1)}, u32[]{:S(2)}, u32[]{:S(2)}) collective-permute-start(bf16[48,32,128]{2,1,0:T(8,128)(2,1)} %copy-done.35), channel_id=1, source_target_pairs={{0,4},{1,5},{2,6},{3,7},{4,0},{5,1},{6,2},{7,3},{8,12},{9,13},{10,... | collective-permute-start | bytes 1179656 | tf_op jit(solution)/shard_map/ppermute | solution.py:337
  373.6 31.2 %collective-permute-start.31 = (f32[232,128]{1,0:T(8,128)}, f32[232,128]{1,0:T(8,128)S(1)}, u32[]{:S(2)}, u32[]{:S(2)}) collective-permute-start(f32[232,128]{1,0:T(8,128)} %shard_map.147), channel_id=1, source_target_pairs={{0,2},{1,3},{2,0},{3,1},{4,6},{5,7},{6,4},{7,5},{8,10},{9,11},{10,... | collective-permute-start | bytes 356360 | tf_op jit(solution)/shard_map/ppermute | solution.py:292
  418.2 15.6 %collective-permute-start.25 = (bf16[48,32,128]{2,1,0:T(8,128)(2,1)}, bf16[48,32,128]{2,1,0:T(8,128)(2,1)S(1)}, u32[]{:S(2)}, u32[]{:S(2)}) collective-permute-start(bf16[48,32,128]{2,1,0:T(8,128)(2,1)} %copy-done.34), channel_id=1, source_target_pairs={{0,3},{1,4},{2,5},{3,6},{4,7},{5,0},{6,1},{7,2},{8,11},{9,12},{10,... | collective-permute-start | bytes 1179656 | tf_op jit(solution)/shard_map/ppermute | solution.py:337
  436.1 8.4 %collective-permute-start.8 = (bf16[16,32,128]{2,1,0:T(8,128)(2,1)}, bf16[16,32,128]{2,1,0:T(8,128)(2,1)S(1)}, u32[]{:S(2)}, u32[]{:S(2)}) collective-permute-start(bf16[16,32,128]{2,1,0:T(8,128)(2,1)} %copy-done.46), channel_id=1, source_target_pairs={{0,6},{1,7},{2,0},{3,1},{4,2},{5,3},{6,4},{7,5},{8,14},{9,15},{10,... | collective-permute-start | bytes 393224 | tf_op jit(solution)/shard_map/ppermute | solution.py:337
  436.8 18.0 %collective-permute-start.9 = (bf16[16,32,128]{2,1,0:T(8,128)(2,1)}, bf16[16,32,128]{2,1,0:T(8,128)(2,1)}, u32[]{:S(2)}, u32[]{:S(2)}) collective-permute-start(bf16[16,32,128]{2,1,0:T(8,128)(2,1)} %copy-done.45), channel_id=1, source_target_pairs={{0,5},{1,6},{2,7},{3,0},{4,1},{5,2},{6,3},{7,4},{8,13},{9,14},{10,... | collective-permute-start | bytes 393224 | tf_op jit(solution)/shard_map/ppermute | solution.py:337
  436.8 21.4 %collective-permute-start.10 = (bf16[16,32,128]{2,1,0:T(8,128)(2,1)}, bf16[16,32,128]{2,1,0:T(8,128)(2,1)}, u32[]{:S(2)}, u32[]{:S(2)}) collective-permute-start(bf16[16,32,128]{2,1,0:T(8,128)(2,1)} %copy-done.44), channel_id=1, source_target_pairs={{0,4},{1,5},{2,6},{3,7},{4,0},{5,1},{6,2},{7,3},{8,12},{9,13},{10,... | collective-permute-start | bytes 393224 | tf_op jit(solution)/shard_map/ppermute | solution.py:337
  441.0 18.2 %collective-permute-start.11 = (bf16[16,32,128]{2,1,0:T(8,128)(2,1)}, bf16[16,32,128]{2,1,0:T(8,128)(2,1)}, u32[]{:S(2)}, u32[]{:S(2)}) collective-permute-start(bf16[16,32,128]{2,1,0:T(8,128)(2,1)} %copy-done.43), channel_id=1, source_target_pairs={{0,3},{1,4},{2,5},{3,6},{4,7},{5,0},{6,1},{7,2},{8,11},{9,12},{10,... | collective-permute-start | bytes 393224 | tf_op jit(solution)/shard_map/ppermute | solution.py:337
  443.3 15.9 %collective-permute-start.12 = (bf16[16,32,128]{2,1,0:T(8,128)(2,1)}, bf16[16,32,128]{2,1,0:T(8,128)(2,1)}, u32[]{:S(2)}, u32[]{:S(2)}) collective-permute-start(bf16[16,32,128]{2,1,0:T(8,128)(2,1)} %copy-done.42), channel_id=1, source_target_pairs={{0,2},{1,3},{2,4},{3,5},{4,6},{5,7},{6,0},{7,1},{8,10},{9,11},{10,... | collective-permute-start | bytes 393224 | tf_op jit(solution)/shard_map/ppermute | solution.py:337
  444.4 14.7 %collective-permute-start.13 = (bf16[16,32,128]{2,1,0:T(8,128)(2,1)}, bf16[16,32,128]{2,1,0:T(8,128)(2,1)}, u32[]{:S(2)}, u32[]{:S(2)}) collective-permute-start(bf16[16,32,128]{2,1,0:T(8,128)(2,1)} %copy-done.41), channel_id=1, source_target_pairs={{0,1},{1,2},{2,3},{3,4},{4,5},{5,6},{6,7},{7,0},{8,9},{9,10},{10,1... | collective-permute-start | bytes 393224 | tf_op jit(solution)/shard_map/ppermute | solution.py:337
  (59 other events, 814.9 us)

commit v12 on v11

--- a/solution.py
+++ b/solution.py
@@ -24,35 +24,37 @@
     return list(refs) if rotated else [refs[0].at[i] for i in range(refs[0].shape[0])]
 
 
-def split_tile(first_channel, tok_ref, cot_ref, out_refs, swap_ref):
-    rows = tok_ref.shape[0]
+def split_tile(first_channel, ref, out_refs, swap_ref, lanes, at):
+    rows = ref.shape[0]
     share = LANES // len(out_refs)
-    for which, ref in enumerate((tok_ref, cot_ref)):
-        for row in range(rows):
-            swap_ref[row * LANES : (row + 1) * LANES, :] = ref[row].astype(jnp.float32).T
-        for slot, out_ref in enumerate(out_refs):
-            start = (first_channel + slot * share) % LANES
-            for channel in range(share):
-                out_ref[which * share + channel] = swap_ref[
-                    pl.ds(start + channel, rows, stride=LANES), :
-                ].astype(jnp.bfloat16)
-
-
-def split_kernel(place_ref, tok_ref, cot_ref, *rest, rotated):
+    for row in range(rows):
+        swap_ref[row * LANES : (row + 1) * LANES, :] = ref[row, :, lanes].astype(jnp.float32).T
+    for slot, out_ref in enumerate(out_refs):
+        start = (first_channel + slot * share) % LANES
+        for channel in range(share):
+            out_ref[at + channel] = swap_ref[pl.ds(start + channel, rows, stride=LANES), :].astype(
+                jnp.bfloat16
+            )
+
+
+def split_kernel(place_ref, tok_ref, cot_ref, *rest, rotated, tiles):
     first_channel = place_ref[0] if rotated else 0
-    split_tile(first_channel, tok_ref, cot_ref, views(rest[:-1], rotated), rest[-1])
-
-
-def split_twiddle_kernel(place_ref, tok_ref, cot_ref, twiddle_ref, *rest, rotated):
-    split_kernel(place_ref, tok_ref, cot_ref, *rest, rotated=rotated)
-    out_refs = views(rest[:-1], rotated)
+    *rest, swap_ref = rest
+    twiddle_ref = rest.pop(0) if tiles else None
+    out_refs = views(rest, rotated)
     share = LANES // len(out_refs)
-    left = twiddle_ref[...]
-    for plane in range(3):
-        part = left.astype(jnp.bfloat16)
-        left = left - part.astype(jnp.float32)
-        for out_ref in out_refs:
-            out_ref[2 * share + plane] = part
+    for tile in range(max(tiles, 1)):
+        lanes = slice(tile * LANES, (tile + 1) * LANES)
+        for which, ref in enumerate((tok_ref, cot_ref)):
+            at = (2 * tile + which) * share
+            split_tile(first_channel, ref, out_refs, swap_ref, lanes, at)
+    if tiles:
+        left = twiddle_ref[...]
+        for plane in range(3):
+            part = left.astype(jnp.bfloat16)
+            left = left - part.astype(jnp.float32)
+            for out_ref in out_refs:
+                out_ref[2 * tiles * share + plane] = part
 
 
 def part_specs(devices, rotated, block, index):
@@ -68,27 +70,30 @@
 
 
 def split_channels(place, tokens, cotangent, tile, tiles, devices, rotated, twiddle=None):
-    rows = tokens.shape[0]
+    rows, _, width = tokens.shape
     step = min(16, rows)
     share = LANES // devices
-    block = pl.BlockSpec((step, B, LANES), lambda t, i: (i, 0, tile + t))
-    specs = [pl.BlockSpec(memory_space=pltpu.SMEM), block, block]
+    specs = [pl.BlockSpec(memory_space=pltpu.SMEM)]
     if twiddle is None:
-        kernel, given = split_kernel, [place, tokens, cotangent]
-        planes = 2 * share
+        given, inner, steps, planes = [place, tokens, cotangent], 0, tiles, 2 * share
+        specs += [pl.BlockSpec((step, B, LANES), lambda t, i: (i, 0, tile + t))] * 2
     else:
-        kernel, given = split_twiddle_kernel, [place, tokens, cotangent, twiddle]
+        given, inner, steps = [place, tokens, cotangent, twiddle], tiles, 1
+        planes = 2 * tiles * share + 3
+        block = (step, B, tiles * LANES)
+        specs += [pl.BlockSpec(block, lambda t, i: (i, 0, tile // tiles))] * 2
         specs.append(pl.BlockSpec((step, B), lambda t, i: (i, 0)))
-        planes = 2 * share + 3
     return pl.pallas_call(
-        functools.partial(kernel, rotated=rotated),
-        grid=(tiles, rows // step),
+        functools.partial(split_kernel, rotated=rotated, tiles=inner),
+        grid=(steps, rows // step),
         in_specs=specs,
         out_specs=part_specs(devices, rotated, (planes, step, B), lambda t, i: (t, i, 0)),
-        out_shape=part_shapes(devices, rotated, (tiles * planes, rows, B)),
+        out_shape=part_shapes(devices, rotated, (steps * planes, rows, B)),
         scratch_shapes=[pltpu.VMEM((step * LANES, B), jnp.float32)],
         compiler_params=pltpu.CompilerParams(vmem_limit_bytes=VMEM_BYTES),
-        cost_estimate=pl.CostEstimate(flops=1, bytes_accessed=16 * rows * B * LANES * tiles, transcendentals=0),
+        cost_estimate=pl.CostEstimate(
+            flops=1, bytes_accessed=16 * rows * B * LANES * tiles, transcendentals=0
+        ),
     )(*given)
 
 
@@ -319,7 +324,7 @@
     tiles = width // LANES
     pair = 2
     half = tiles // 2
-    groups = [(0, 1, True), (1, half - 1, False), (half, tiles - half, True)]
+    groups = [(0, half, True), (half, tiles - half - 1, False), (tiles - 1, 1, True)]
 
     place = (lax.axis_index("ctx") * share).astype(jnp.int32).reshape(1)
     second = block_diagonal(second_factor, pair)
@@ -349,7 +354,7 @@
                 split_channels(place, tok_blocks, cot_blocks, at, count, ctx_size, rotated, own)
             )
         arrived = [exchange(p, 1, group[2]) for p, group in zip(split, groups)]
-        planes = jnp.stack([part[2 * share :] for part in arrived[0]]).astype(jnp.float32)
+        planes = jnp.stack([part[2 * half * share :] for part in arrived[0]]).astype(jnp.float32)
         planes = planes[:, 0] + planes[:, 1] + planes[:, 2]
         twice = jnp.concatenate([planes[::-1]] * 2, axis=0)
         turn = ctx_size - 1 - lax.axis_index("ctx")
@@ -367,12 +372,12 @@
             terms.append(own_sums)
         leaving.append(returned)
 
-    back = leaving[-1][2]
+    back = leaving[-1][0]
     sums = sum_over_mesh(add(terms, []), [None, back[-2:], back[1:2], back[2:3], back[3:5], back[5:-2]])
     grads = []
     for returned in leaving:
         held = None
-        for which in (1, 2, 0):
+        for which in (1, 0, 2):
             at, count, rotated = groups[which]
             after = []
             held = merge_channels(

time: 465 us -> 478 us (1.028)
  starting transfers between devices: 170 us -> 203 us
  waiting for transfers between devices: 170 us -> 144 us
    ppermute x28, starting transfers between devices: 114 us -> 170 us  [exchange(): moved.append(lax.ppermute(parts[shift], 'ctx', pairs))]
    ppermute x28, waiting for transfers between devices: 140 us -> 114 us  [exchange(): moved.append(lax.ppermute(parts[shift], 'ctx', pairs))]
    all_to_all x2, starting transfers between devices: 28.7 us -> 10.1 us  [exchange(): lax.all_to_all(parts[0], 'ctx', split_axis=0, concat_axis=0, tiled=True)]
    unnamed x117 -> x147, local copies, waits for them, and re-layouts: 30.8 us -> 35.1 us
  transfers between devices with their start and end apart: 37 -> 37, of which waited for: 18 -> 13; matrix products, arithmetic and copies ran while one was open for 3% -> 3% of each run, Pallas kernels for 15% -> 15%
where the time goes in v12:
time: 478 us; the launch traced here: 476 us
  starting transfers between devices  203 us (42%)
  waiting for transfers between devices  144 us (30%)
  Pallas kernels  79.7 us (17%)
  local copies, waits for them, and re-layouts  35.1 us (7%)
  other arithmetic  13 us (3%)
    ppermute x28, starting transfers between devices, exchange(): moved.append(lax.ppermute(parts[shift], 'ctx', pairs))  170 us
    ppermute x28, waiting for transfers between devices, exchange(): moved.append(lax.ppermute(parts[shift], 'ctx', pairs))  114 us
    pallas_call x3, Pallas kernels, mix(): pl.pallas_call(functools.partial(mix_kernel, parts=len(parts), tile=tile,...  40.6 us
    unnamed x147, local copies, waits for them, and re-layouts  35.1 us
    ppermute x7, waiting for transfers between devices, exchange_with(): lax.ppermute(array, axis, [(i, i ^ bit) for i in range(size)])  30 us
    pallas_call x3, Pallas kernels, split_channels(): pl.pallas_call(functools.partial(split_kernel, rotated=rotated, tiles=inn...  25.3 us
    ppermute x7, starting transfers between devices, exchange_with(): lax.ppermute(array, axis, [(i, i ^ bit) for i in range(size)])  22.9 us
    pallas_call x3, Pallas kernels, merge_channels(): pl.pallas_call(functools.partial(merge_kernel, parts=len(parts), rotated=...  11.6 us
  transfers between devices with their start and end apart: 37, of which 13 were waited for; matrix products, arithmetic and copies ran while one was open for 3% of the time, Pallas kernels for 15%

profile of v12, /device:TPU:0, one launch (start us, length us, event | category | flops | bytes accessed | tf_op | source)
XLA Modules:
  0.0 475.9 jit_solution(13035032255962287232)
XLA Ops:
  0.6 7.8 %shard_map.139 = bf16[8,64,32,128]{3,2,1,0:T(8,128)(2,1)S(1)} custom-call(s32[1]{0:T(128)} %bitcast.place_ref, bf16[32,128,768]{2,1,0:T(8,128)(2,1)} %bitcast.51, bf16[32,128,768]{2,1,0:T(8,128)(2,1)} %bitcast.54), custom_call_target="tpu_custom_call" | custom-call | flops 1 | bytes 16777216 | tf_op jit(solution)/shard_map/pallas_call | solution.py:86
  10.5 6.5 %all-to-all-start = ((bf16[8,64,32,128]{3,2,1,0:T(8,128)(2,1)}), bf16[8,64,32,128]{3,2,1,0:T(8,128)(2,1)}, u32[]{:S(2)}, u32[]{:S(2)}) async-start(bf16[8,64,32,128]{3,2,1,0:T(8,128)(2,1)} %copy-done), calls=%async_computation | async-start | bytes 8388608 | tf_op jit(solution)/shard_map/all_to_all | solution.py:338
  17.0 12.4 %shard_map.136 = (bf16[99,32,128]{2,1,0:T(8,128)(2,1)S(1)}, bf16[99,32,128]{2,1,0:T(8,128)(2,1)}, bf16[99,32,128]{2,1,0:T(8,128)(2,1)}, bf16[99,32,128]{2,1,0:T(...) custom-call(s32[1]{0:T(128)} %bitcast.place_ref, ...), custom_call_target="tpu_custom_call" | custom-call | flops 1 | bytes 25165824 | tf_op jit(solution)/shard_map/pallas_call | solution.py:86
  31.5 2.3 collective-permute-start.9
  33.8 5.2 %shard_map.135 = (bf16[32,32,128]{2,1,0:T(8,128)(2,1)S(1)}, bf16[32,32,128]{2,1,0:T(8,128)(2,1)}, bf16[32,32,128]{2,1,0:T(8,128)(2,1)S(1)}, bf16[32,32,128]{2,1,...) custom-call(s32[1]{0:T(128)} %bitcast.place_ref, ...), custom_call_target="tpu_custom_call" | custom-call | flops 1 | bytes 8388608 | tf_op jit(solution)/shard_map/pallas_call | solution.py:86
  41.5 65.0 %collective-permute-done.7.rest_1_.rest_9_ = bf16[99,32,128]{2,1,0:T(8,128)(2,1)S(1)} collective-permute-done((bf16[99,32,128]{2,1,0:T(8,128)(2,1)}, bf16[99,32,128]{2,1,0:T(8,128)(2,1)S(1)}, u32[]{:S(2)}, u32[]{:S(2)}) %collective-permute-start.7) | collective-permute-done | bytes 811040 | tf_op jit(solution)/shard_map/ppermute | solution.py:342
  107.5 65.8 %collective-permute-start.12 = (bf16[99,32,128]{2,1,0:T(8,128)(2,1)}, bf16[99,32,128]{2,1,0:T(8,128)(2,1)S(1)}, u32[]{:S(2)}, u32[]{:S(2)}) collective-permute-start(bf16[99,32,128]{2,1,0:T(8,128)(2,1)} %copy-done.43), channel_id=1, source_target_pairs={{0,6},{1,7},{2,0},{3,1},{4,2},{5,3},{6,4},{7,5},{8,14},{9,15},{10,... | collective-permute-start | bytes 2433032 | tf_op jit(solution)/shard_map/ppermute | solution.py:342
  174.1 26.4 %collective-permute-done.9.rest_3_.rest_11_ = bf16[99,32,128]{2,1,0:T(8,128)(2,1)} collective-permute-done((bf16[99,32,128]{2,1,0:T(8,128)(2,1)}, bf16[99,32,128]{2,1,0:T(8,128)(2,1)}, u32[]{:S(2)}, u32[]{:S(2)}) %collective-permute-start.9) | collective-permute-done | bytes 811040 | tf_op jit(solution)/shard_map/ppermute | solution.py:342
  200.4 7.9 %collective-permute-start.13 = (bf16[99,32,128]{2,1,0:T(8,128)(2,1)}, bf16[99,32,128]{2,1,0:T(8,128)(2,1)S(1)}, u32[]{:S(2)}, u32[]{:S(2)}) collective-permute-start(bf16[99,32,128]{2,1,0:T(8,128)(2,1)} %get-tuple-element.58), channel_id=1, source_target_pairs={{0,7},{1,0},{2,1},{3,2},{4,3},{5,4},{6,5},{7,6},{8,15},{9,8},{10,9... | collective-permute-start | bytes 2433032 | tf_op jit(solution)/shard_map/ppermute | solution.py:342
  209.1 22.1 %collective-permute-start.1 = (bf16[32,32,128]{2,1,0:T(8,128)(2,1)}, bf16[32,32,128]{2,1,0:T(8,128)(2,1)S(1)}, u32[]{:S(2)}, u32[]{:S(2)}) collective-permute-start(bf16[32,32,128]{2,1,0:T(8,128)(2,1)} %copy-done.54), channel_id=1, source_target_pairs={{0,2},{1,3},{2,4},{3,5},{4,6},{5,7},{6,0},{7,1},{8,10},{9,11},{10,... | collective-permute-start | bytes 786440 | tf_op jit(solution)/shard_map/ppermute | solution.py:342
  232.0 22.7 %collective-permute-start.2 = (bf16[32,32,128]{2,1,0:T(8,128)(2,1)S(1)}, bf16[32,32,128]{2,1,0:T(8,128)(2,1)S(1)}, u32[]{:S(2)}, u32[]{:S(2)}) collective-permute-start(bf16[32,32,128]{2,1,0:T(8,128)(2,1)S(1)} %get-tuple-element.46), channel_id=1, source_target_pairs={{0,3},{1,4},{2,5},{3,6},{4,7},{5,0},{6,1},{7,2},{8,11},{9,12},{10,... | collective-permute-start | bytes 786440 | tf_op jit(solution)/shard_map/ppermute | solution.py:342
  254.8 3.1 collective-permute-start.3
  260.2 20.7 %shard_map.138 = (bf16[48,32,128]{2,1,0:T(8,128)(2,1)S(1)}, bf16[48,32,128]{2,1,0:T(8,128)(2,1)S(1)}, bf16[48,32,128]{2,1,0:T(8,128)(2,1)S(1)}, bf16[48,32,128]{...) custom-call(s32[1]{0:T(128)} %bitcast.place_ref, ...), custom_call_target="tpu_custom_call" | custom-call | flops 25165824000 | bytes 1024 | tf_op jit(solution)/shard_map/pallas_call | solution.py:227
  287.9 2.6 collective-permute-start.5
  290.6 13.9 %shard_map.140 = (bf16[8,32,32,128]{3,2,1,0:T(8,128)(2,1)S(1)}, f32[928,128]{1,0:T(8,128)S(1)}) custom-call(s32[1]{0:T(128)} %bitcast.place_ref, f32[768]{0:T(1024)S(1)} %copy-done.62, f32[768]{0:T(1024)S(1)} %copy-done.63, f32[768]{0:T(1024)S(1)} %copy-done.64, bf16[8,64,32,128]{3,2,1,0:T(8,128)(2,1)} %all-to-all-done.rest_0_.rest_1_, ...), custom_call_target="tpu_custom_call" | custom-call | flops 16777216000 | bytes 1024 | tf_op jit(solution)/shard_map/pallas_call | solution.py:227
  307.7 3.6 all-to-all-start.1
  320.7 6.0 %shard_map.137 = (bf16[16,32,128]{2,1,0:T(8,128)(2,1)S(1)}, bf16[16,32,128]{2,1,0:T(8,128)(2,1)S(1)}, bf16[16,32,128]{2,1,0:T(8,128)(2,1)S(1)}, bf16[16,32,128]{...) custom-call(s32[1]{0:T(128)} %bitcast.place_ref, ...), custom_call_target="tpu_custom_call" | custom-call | flops 8388608000 | bytes 1024 | tf_op jit(solution)/shard_map/pallas_call | solution.py:227
  332.1 2.2 shard_map.145
  338.8 4.7 collective-permute-done.28
  346.2 2.1 collective-permute-start.21
  349.7 9.5 %collective-permute-done.26.rest_6_.refs_1_ = bf16[48,32,128]{2,1,0:T(8,128)(2,1)S(1)} collective-permute-done((bf16[48,32,128]{2,1,0:T(8,128)(2,1)}, bf16[48,32,128]{2,1,0:T(8,128)(2,1)S(1)}, u32[]{:S(2)}, u32[]{:S(2)}) %collective-permute-start.26) | collective-permute-done | bytes 393248 | tf_op jit(solution)/shard_map/ppermute | solution.py:342
  359.1 26.5 %collective-permute-start.23 = (bf16[48,32,128]{2,1,0:T(8,128)(2,1)}, bf16[48,32,128]{2,1,0:T(8,128)(2,1)}, u32[]{:S(2)}, u32[]{:S(2)}) collective-permute-start(bf16[48,32,128]{2,1,0:T(8,128)(2,1)} %copy-done.47), channel_id=1, source_target_pairs={{0,5},{1,6},{2,7},{3,0},{4,1},{5,2},{6,3},{7,4},{8,13},{9,14},{10,... | collective-permute-start | bytes 1179656 | tf_op jit(solution)/shard_map/ppermute | solution.py:342
  390.6 16.7 %collective-permute-start.31 = (f32[232,128]{1,0:T(8,128)}, f32[232,128]{1,0:T(8,128)S(1)}, u32[]{:S(2)}, u32[]{:S(2)}) collective-permute-start(f32[232,128]{1,0:T(8,128)} %shard_map.147), channel_id=1, source_target_pairs={{0,2},{1,3},{2,0},{3,1},{4,6},{5,7},{6,4},{7,5},{8,10},{9,11},{10,... | collective-permute-start | bytes 356360 | tf_op jit(solution)/shard_map/ppermute | solution.py:297
  407.4 11.8 %collective-permute-done.31 = f32[232,128]{1,0:T(8,128)S(1)} collective-permute-done((f32[232,128]{1,0:T(8,128)}, f32[232,128]{1,0:T(8,128)S(1)}, u32[]{:S(2)}, u32[]{:S(2)}) %collective-permute-start.31) | collective-permute-done | bytes 118816 | tf_op jit(solution)/shard_map/ppermute | solution.py:297
  421.5 8.0 %collective-permute-done.32 = f32[232,128]{1,0:T(8,128)S(1)} collective-permute-done((f32[232,128]{1,0:T(8,128)}, f32[232,128]{1,0:T(8,128)S(1)}, u32[]{:S(2)}, u32[]{:S(2)}) %collective-permute-start.32) | collective-permute-done | bytes 118816 | tf_op jit(solution)/shard_map/ppermute | solution.py:297
  432.6 3.9 collective-permute-done.33
  438.1 8.8 %collective-permute-done.25.rest_5_.refs_1_ = bf16[48,32,128]{2,1,0:T(8,128)(2,1)S(1)} collective-permute-done((bf16[48,32,128]{2,1,0:T(8,128)(2,1)}, bf16[48,32,128]{2,1,0:T(8,128)(2,1)S(1)}, u32[]{:S(2)}, u32[]{:S(2)}) %collective-permute-start.25) | collective-permute-done | bytes 393248 | tf_op jit(solution)/shard_map/ppermute | solution.py:342
  451.2 2.8 collective-permute-start.17
  460.2 3.0 shard_map.142.rest_8_
  463.2 5.9 %shard_map.143.rest_8_ = bf16[32,128,768]{2,1,0:T(8,128)(2,1)} custom-call(s32[1]{0:T(128)} %bitcast.place_ref, bf16[48,32,128]{2,1,0:T(8,128)(2,1)S(1)} %copy-done.14, bf16[48,32,128]{2,1,0:T(8,128)(2,1)S(1)} %copy-done.3, bf16[48,32,128]{2,1,0:T(8,128)(2,1)S(1)} %copy-done.5, ...), custom_call_target="tpu_custom_call", output_to_operand_aliasing={{}: (9, {})} | custom-call | flops 1 | bytes 12582912 | tf_op jit(solution)/shard_map/pallas_call | solution.py:122
  469.1 3.6 collective-permute-done.17.rest_4_
  473.2 2.7 shard_map.144
  (226 shorter events, 68.6 us)
Async XLA Ops:
  10.5 280.0 %all-to-all-start = ((bf16[8,64,32,128]{3,2,1,0:T(8,128)(2,1)}), bf16[8,64,32,128]{3,2,1,0:T(8,128)(2,1)}, u32[]{:S(2)}, u32[]{:S(2)}) async-start(bf16[8,64,32,128]{3,2,1,0:T(8,128)(2,1)} %copy-done), calls=%async_computation | async-start | bytes 8388608 | tf_op jit(solution)/shard_map/all_to_all | solution.py:338
  29.3 77.1 %collective-permute-start.7 = (bf16[99,32,128]{2,1,0:T(8,128)(2,1)}, bf16[99,32,128]{2,1,0:T(8,128)(2,1)S(1)}, u32[]{:S(2)}, u32[]{:S(2)}) collective-permute-start(bf16[99,32,128]{2,1,0:T(8,128)(2,1)} %get-tuple-element.52), channel_id=1, source_target_pairs={{0,1},{1,2},{2,3},{3,4},{4,5},{5,6},{6,7},{7,0},{8,9},{9,10},{10,1... | collective-permute-start | bytes 2433032 | tf_op jit(solution)/shard_map/ppermute | solution.py:342
  29.9 77.6 %collective-permute-start.8 = (bf16[99,32,128]{2,1,0:T(8,128)(2,1)}, bf16[99,32,128]{2,1,0:T(8,128)(2,1)}, u32[]{:S(2)}, u32[]{:S(2)}) collective-permute-start(bf16[99,32,128]{2,1,0:T(8,128)(2,1)} %get-tuple-element.53), channel_id=1, source_target_pairs={{0,2},{1,3},{2,4},{3,5},{4,6},{5,7},{6,0},{7,1},{8,10},{9,11},{10,... | collective-permute-start | bytes 2433032 | tf_op jit(solution)/shard_map/ppermute | solution.py:342
  31.5 168.9 %collective-permute-start.9 = (bf16[99,32,128]{2,1,0:T(8,128)(2,1)}, bf16[99,32,128]{2,1,0:T(8,128)(2,1)}, u32[]{:S(2)}, u32[]{:S(2)}) collective-permute-start(bf16[99,32,128]{2,1,0:T(8,128)(2,1)} %get-tuple-element.54), channel_id=1, source_target_pairs={{0,3},{1,4},{2,5},{3,6},{4,7},{5,0},{6,1},{7,2},{8,11},{9,12},{10,... | collective-permute-start | bytes 2433032 | tf_op jit(solution)/shard_map/ppermute | solution.py:342
  39.7 248.2 %collective-permute-start = (bf16[32,32,128]{2,1,0:T(8,128)(2,1)}, bf16[32,32,128]{2,1,0:T(8,128)(2,1)S(1)}, u32[]{:S(2)}, u32[]{:S(2)}) collective-permute-start(bf16[32,32,128]{2,1,0:T(8,128)(2,1)} %get-tuple-element.44), channel_id=1, source_target_pairs={{0,1},{1,2},{2,3},{3,4},{4,5},{5,6},{6,7},{7,0},{8,9},{9,10},{10,1... | collective-permute-start | bytes 786440 | tf_op jit(solution)/shard_map/ppermute | solution.py:342
  40.0 169.1 %collective-permute-start.10 = (bf16[99,32,128]{2,1,0:T(8,128)(2,1)}, bf16[99,32,128]{2,1,0:T(8,128)(2,1)}, u32[]{:S(2)}, u32[]{:S(2)}) collective-permute-start(bf16[99,32,128]{2,1,0:T(8,128)(2,1)} %get-tuple-element.55), channel_id=1, source_target_pairs={{0,4},{1,5},{2,6},{3,7},{4,0},{5,1},{6,2},{7,3},{8,12},{9,13},{10,... | collective-permute-start | bytes 2433032 | tf_op jit(solution)/shard_map/ppermute | solution.py:342
  106.4 125.6 %collective-permute-start.11 = (bf16[99,32,128]{2,1,0:T(8,128)(2,1)}, bf16[99,32,128]{2,1,0:T(8,128)(2,1)S(1)}, u32[]{:S(2)}, u32[]{:S(2)}) collective-permute-start(bf16[99,32,128]{2,1,0:T(8,128)(2,1)} %copy-done.44), channel_id=1, source_target_pairs={{0,5},{1,6},{2,7},{3,0},{4,1},{5,2},{6,3},{7,4},{8,13},{9,14},{10,... | collective-permute-start | bytes 2433032 | tf_op jit(solution)/shard_map/ppermute | solution.py:342
  107.5 147.3 %collective-permute-start.12 = (bf16[99,32,128]{2,1,0:T(8,128)(2,1)}, bf16[99,32,128]{2,1,0:T(8,128)(2,1)S(1)}, u32[]{:S(2)}, u32[]{:S(2)}) collective-permute-start(bf16[99,32,128]{2,1,0:T(8,128)(2,1)} %copy-done.43), channel_id=1, source_target_pairs={{0,6},{1,7},{2,0},{3,1},{4,2},{5,3},{6,4},{7,5},{8,14},{9,15},{10,... | collective-permute-start | bytes 2433032 | tf_op jit(solution)/shard_map/ppermute | solution.py:342
  200.4 57.5 %collective-permute-start.13 = (bf16[99,32,128]{2,1,0:T(8,128)(2,1)}, bf16[99,32,128]{2,1,0:T(8,128)(2,1)S(1)}, u32[]{:S(2)}, u32[]{:S(2)}) collective-permute-start(bf16[99,32,128]{2,1,0:T(8,128)(2,1)} %get-tuple-element.58), channel_id=1, source_target_pairs={{0,7},{1,0},{2,1},{3,2},{4,3},{5,4},{6,5},{7,6},{8,15},{9,8},{10,9... | collective-permute-start | bytes 2433032 | tf_op jit(solution)/shard_map/ppermute | solution.py:342
  209.1 81.4 %collective-permute-start.1 = (bf16[32,32,128]{2,1,0:T(8,128)(2,1)}, bf16[32,32,128]{2,1,0:T(8,128)(2,1)S(1)}, u32[]{:S(2)}, u32[]{:S(2)}) collective-permute-start(bf16[32,32,128]{2,1,0:T(8,128)(2,1)} %copy-done.54), channel_id=1, source_target_pairs={{0,2},{1,3},{2,4},{3,5},{4,6},{5,7},{6,0},{7,1},{8,10},{9,11},{10,... | collective-permute-start | bytes 786440 | tf_op jit(solution)/shard_map/ppermute | solution.py:342
  232.0 74.6 %collective-permute-start.2 = (bf16[32,32,128]{2,1,0:T(8,128)(2,1)S(1)}, bf16[32,32,128]{2,1,0:T(8,128)(2,1)S(1)}, u32[]{:S(2)}, u32[]{:S(2)}) collective-permute-start(bf16[32,32,128]{2,1,0:T(8,128)(2,1)S(1)} %get-tuple-element.46), channel_id=1, source_target_pairs={{0,3},{1,4},{2,5},{3,6},{4,7},{5,0},{6,1},{7,2},{8,11},{9,12},{10,... | collective-permute-start | bytes 786440 | tf_op jit(solution)/shard_map/ppermute | solution.py:342
  254.8 51.9 %collective-permute-start.3 = (bf16[32,32,128]{2,1,0:T(8,128)(2,1)}, bf16[32,32,128]{2,1,0:T(8,128)(2,1)S(1)}, u32[]{:S(2)}, u32[]{:S(2)}) collective-permute-start(bf16[32,32,128]{2,1,0:T(8,128)(2,1)} %get-tuple-element.47), channel_id=1, source_target_pairs={{0,4},{1,5},{2,6},{3,7},{4,0},{5,1},{6,2},{7,3},{8,12},{9,13},{10,... | collective-permute-start | bytes 786440 | tf_op jit(solution)/shard_map/ppermute | solution.py:342
  257.9 48.7 %collective-permute-start.4 = (bf16[32,32,128]{2,1,0:T(8,128)(2,1)}, bf16[32,32,128]{2,1,0:T(8,128)(2,1)S(1)}, u32[]{:S(2)}, u32[]{:S(2)}) collective-permute-start(bf16[32,32,128]{2,1,0:T(8,128)(2,1)} %get-tuple-element.48), channel_id=1, source_target_pairs={{0,5},{1,6},{2,7},{3,0},{4,1},{5,2},{6,3},{7,4},{8,13},{9,14},{10,... | collective-permute-start | bytes 786440 | tf_op jit(solution)/shard_map/ppermute | solution.py:342
  287.9 18.8 %collective-permute-start.5 = (bf16[32,32,128]{2,1,0:T(8,128)(2,1)}, bf16[32,32,128]{2,1,0:T(8,128)(2,1)S(1)}, u32[]{:S(2)}, u32[]{:S(2)}) collective-permute-start(bf16[32,32,128]{2,1,0:T(8,128)(2,1)} %get-tuple-element.49), channel_id=1, source_target_pairs={{0,6},{1,7},{2,0},{3,1},{4,2},{5,3},{6,4},{7,5},{8,14},{9,15},{10,... | collective-permute-start | bytes 786440 | tf_op jit(solution)/shard_map/ppermute | solution.py:342
  290.5 16.2 %collective-permute-start.6 = (bf16[32,32,128]{2,1,0:T(8,128)(2,1)}, bf16[32,32,128]{2,1,0:T(8,128)(2,1)S(1)}, u32[]{:S(2)}, u32[]{:S(2)}) collective-permute-start(bf16[32,32,128]{2,1,0:T(8,128)(2,1)} %get-tuple-element.50), channel_id=1, source_target_pairs={{0,7},{1,0},{2,1},{3,2},{4,3},{5,4},{6,5},{7,6},{8,15},{9,8},{10,9... | collective-permute-start | bytes 786440 | tf_op jit(solution)/shard_map/ppermute | solution.py:342
  307.7 152.5 %all-to-all-start.1 = ((bf16[8,32,32,128]{3,2,1,0:T(8,128)(2,1)}), bf16[8,32,32,128]{3,2,1,0:T(8,128)(2,1)S(1)}, u32[]{:S(2)}, u32[]{:S(2)}) async-start(bf16[8,32,32,128]{3,2,1,0:T(8,128)(2,1)} %shard_map.141), calls=%async_computation.1 | async-start | bytes 4194304 | tf_op jit(solution)/shard_map/all_to_all | solution.py:338
  335.3 8.2 %collective-permute-start.28 = (f32[464,128]{1,0:T(8,128)S(1)}, f32[464,128]{1,0:T(8,128)S(1)}, u32[]{:S(2)}, u32[]{:S(2)}) collective-permute-start(f32[464,128]{1,0:T(8,128)S(1)} %slice_select_fusion), channel_id=1, source_target_pairs={{0,16},{8,24},{16,0},{24,8},{1,17},{9,25},{17,1},{25,9},{2,18},{10... | collective-permute-start | bytes 712712 | tf_op jit(solution)/shard_map/ppermute | solution.py:297
  336.9 22.2 %collective-permute-start.26 = (bf16[48,32,128]{2,1,0:T(8,128)(2,1)}, bf16[48,32,128]{2,1,0:T(8,128)(2,1)S(1)}, u32[]{:S(2)}, u32[]{:S(2)}) collective-permute-start(bf16[48,32,128]{2,1,0:T(8,128)(2,1)} %copy-done.51), channel_id=1, source_target_pairs={{0,2},{1,3},{2,4},{3,5},{4,6},{5,7},{6,0},{7,1},{8,10},{9,11},{10,... | collective-permute-start | bytes 1179656 | tf_op jit(solution)/shard_map/ppermute | solution.py:342
  338.8 48.0 %collective-permute-start.27 = (bf16[48,32,128]{2,1,0:T(8,128)(2,1)}, bf16[48,32,128]{2,1,0:T(8,128)(2,1)}, u32[]{:S(2)}, u32[]{:S(2)}) collective-permute-start(bf16[48,32,128]{2,1,0:T(8,128)(2,1)} %copy-done.50), channel_id=1, source_target_pairs={{0,1},{1,2},{2,3},{3,4},{4,5},{5,6},{6,7},{7,0},{8,9},{9,10},{10,1... | collective-permute-start | bytes 1179656 | tf_op jit(solution)/shard_map/ppermute | solution.py:342
  344.6 41.0 %collective-permute-start.29 = (f32[232,128]{1,0:T(8,128)S(1)}, f32[232,128]{1,0:T(8,128)S(1)}, u32[]{:S(2)}, u32[]{:S(2)}) collective-permute-start(f32[232,128]{1,0:T(8,128)S(1)} %slice_select_fusion.1), channel_id=1, source_target_pairs={{0,8},{8,0},{16,24},{24,16},{1,9},{9,1},{17,25},{25,17},{2,10},{10... | collective-permute-start | bytes 356360 | tf_op jit(solution)/shard_map/ppermute | solution.py:297
  346.2 43.7 %collective-permute-start.21 = (bf16[48,32,128]{2,1,0:T(8,128)(2,1)}, bf16[48,32,128]{2,1,0:T(8,128)(2,1)S(1)}, u32[]{:S(2)}, u32[]{:S(2)}) collective-permute-start(bf16[48,32,128]{2,1,0:T(8,128)(2,1)} %copy-done.49), channel_id=1, source_target_pairs={{0,7},{1,0},{2,1},{3,2},{4,3},{5,4},{6,5},{7,6},{8,15},{9,8},{10,9... | collective-permute-start | bytes 1179656 | tf_op jit(solution)/shard_map/ppermute | solution.py:342
  348.3 72.4 %collective-permute-start.22 = (bf16[48,32,128]{2,1,0:T(8,128)(2,1)}, bf16[48,32,128]{2,1,0:T(8,128)(2,1)S(1)}, u32[]{:S(2)}, u32[]{:S(2)}) collective-permute-start(bf16[48,32,128]{2,1,0:T(8,128)(2,1)} %copy-done.48), channel_id=1, source_target_pairs={{0,6},{1,7},{2,0},{3,1},{4,2},{5,3},{6,4},{7,5},{8,14},{9,15},{10,... | collective-permute-start | bytes 1179656 | tf_op jit(solution)/shard_map/ppermute | solution.py:342
  359.1 71.9 %collective-permute-start.23 = (bf16[48,32,128]{2,1,0:T(8,128)(2,1)}, bf16[48,32,128]{2,1,0:T(8,128)(2,1)}, u32[]{:S(2)}, u32[]{:S(2)}) collective-permute-start(bf16[48,32,128]{2,1,0:T(8,128)(2,1)} %copy-done.47), channel_id=1, source_target_pairs={{0,5},{1,6},{2,7},{3,0},{4,1},{5,2},{6,3},{7,4},{8,13},{9,14},{10,... | collective-permute-start | bytes 1179656 | tf_op jit(solution)/shard_map/ppermute | solution.py:342
  385.7 45.4 %collective-permute-start.24 = (bf16[48,32,128]{2,1,0:T(8,128)(2,1)}, bf16[48,32,128]{2,1,0:T(8,128)(2,1)}, u32[]{:S(2)}, u32[]{:S(2)}) collective-permute-start(bf16[48,32,128]{2,1,0:T(8,128)(2,1)} %copy-done.46), channel_id=1, source_target_pairs={{0,4},{1,5},{2,6},{3,7},{4,0},{5,1},{6,2},{7,3},{8,12},{9,13},{10,... | collective-permute-start | bytes 1179656 | tf_op jit(solution)/shard_map/ppermute | solution.py:342
  390.6 28.5 %collective-permute-start.31 = (f32[232,128]{1,0:T(8,128)}, f32[232,128]{1,0:T(8,128)S(1)}, u32[]{:S(2)}, u32[]{:S(2)}) collective-permute-start(f32[232,128]{1,0:T(8,128)} %shard_map.147), channel_id=1, source_target_pairs={{0,2},{1,3},{2,0},{3,1},{4,6},{5,7},{6,4},{7,5},{8,10},{9,11},{10,... | collective-permute-start | bytes 356360 | tf_op jit(solution)/shard_map/ppermute | solution.py:297
  421.5 8.0 %collective-permute-start.32 = (f32[232,128]{1,0:T(8,128)}, f32[232,128]{1,0:T(8,128)S(1)}, u32[]{:S(2)}, u32[]{:S(2)}) collective-permute-start(f32[232,128]{1,0:T(8,128)} %shard_map.148), channel_id=1, source_target_pairs={{0,4},{1,5},{2,6},{3,7},{4,0},{5,1},{6,2},{7,3},{8,12},{9,13},{10,... | collective-permute-start | bytes 356360 | tf_op jit(solution)/shard_map/ppermute | solution.py:297
  432.6 14.3 %collective-permute-start.25 = (bf16[48,32,128]{2,1,0:T(8,128)(2,1)}, bf16[48,32,128]{2,1,0:T(8,128)(2,1)S(1)}, u32[]{:S(2)}, u32[]{:S(2)}) collective-permute-start(bf16[48,32,128]{2,1,0:T(8,128)(2,1)} %copy-done.45), channel_id=1, source_target_pairs={{0,3},{1,4},{2,5},{3,6},{4,7},{5,0},{6,1},{7,2},{8,11},{9,12},{10,... | collective-permute-start | bytes 1179656 | tf_op jit(solution)/shard_map/ppermute | solution.py:342
  451.2 18.0 %collective-permute-start.16 = (bf16[16,32,128]{2,1,0:T(8,128)(2,1)}, bf16[16,32,128]{2,1,0:T(8,128)(2,1)}, u32[]{:S(2)}, u32[]{:S(2)}) collective-permute-start(bf16[16,32,128]{2,1,0:T(8,128)(2,1)} %copy-done.59), channel_id=1, source_target_pairs={{0,5},{1,6},{2,7},{3,0},{4,1},{5,2},{6,3},{7,4},{8,13},{9,14},{10,... | collective-permute-start | bytes 393224 | tf_op jit(solution)/shard_map/ppermute | solution.py:342
  451.2 21.5 %collective-permute-start.17 = (bf16[16,32,128]{2,1,0:T(8,128)(2,1)}, bf16[16,32,128]{2,1,0:T(8,128)(2,1)}, u32[]{:S(2)}, u32[]{:S(2)}) collective-permute-start(bf16[16,32,128]{2,1,0:T(8,128)(2,1)} %copy-done.58), channel_id=1, source_target_pairs={{0,4},{1,5},{2,6},{3,7},{4,0},{5,1},{6,2},{7,3},{8,12},{9,13},{10,... | collective-permute-start | bytes 393224 | tf_op jit(solution)/shard_map/ppermute | solution.py:342
  454.0 19.1 %collective-permute-start.18 = (bf16[16,32,128]{2,1,0:T(8,128)(2,1)}, bf16[16,32,128]{2,1,0:T(8,128)(2,1)}, u32[]{:S(2)}, u32[]{:S(2)}) collective-permute-start(bf16[16,32,128]{2,1,0:T(8,128)(2,1)} %copy-done.57), channel_id=1, source_target_pairs={{0,3},{1,4},{2,5},{3,6},{4,7},{5,0},{6,1},{7,2},{8,11},{9,12},{10,... | collective-permute-start | bytes 393224 | tf_op jit(solution)/shard_map/ppermute | solution.py:342
  456.9 16.3 %collective-permute-start.19 = (bf16[16,32,128]{2,1,0:T(8,128)(2,1)}, bf16[16,32,128]{2,1,0:T(8,128)(2,1)}, u32[]{:S(2)}, u32[]{:S(2)}) collective-permute-start(bf16[16,32,128]{2,1,0:T(8,128)(2,1)} %copy-done.56), channel_id=1, source_target_pairs={{0,2},{1,3},{2,4},{3,5},{4,6},{5,7},{6,0},{7,1},{8,10},{9,11},{10,... | collective-permute-start | bytes 393224 | tf_op jit(solution)/shard_map/ppermute | solution.py:342
  456.9 16.2 %collective-permute-start.20 = (bf16[16,32,128]{2,1,0:T(8,128)(2,1)}, bf16[16,32,128]{2,1,0:T(8,128)(2,1)}, u32[]{:S(2)}, u32[]{:S(2)}) collective-permute-start(bf16[16,32,128]{2,1,0:T(8,128)(2,1)} %copy-done.55), channel_id=1, source_target_pairs={{0,1},{1,2},{2,3},{3,4},{4,5},{5,6},{6,7},{7,0},{8,9},{9,10},{10,1... | collective-permute-start | bytes 393224 | tf_op jit(solution)/shard_map/ppermute | solution.py:342
  (74 other events, 1923.5 us)

commit v13 on v11

--- a/solution.py
+++ b/solution.py
@@ -367,8 +367,8 @@
             terms.append(own_sums)
         leaving.append(returned)
 
-    back = leaving[-1][2]
-    sums = sum_over_mesh(add(terms, []), [None, back[-2:], back[1:2], back[2:3], back[3:5], back[5:-2]])
+    back, first = leaving[-1][2], leaving[-1][0]
+    sums = sum_over_mesh(add(terms, []), [None, back[-2:], back[1:2], back[2:4], back[4:-2], first[1:4]])
     grads = []
     for returned in leaving:
         held = None

time: 465 us -> 503 us (1.082)
  waiting for transfers between devices: 170 us -> 203 us
  starting transfers between devices: 170 us -> 176 us
    ppermute x28, waiting for transfers between devices: 140 us -> 170 us  [exchange(): moved.append(lax.ppermute(parts[shift], 'ctx', pairs))]
    ppermute x7, starting transfers between devices: 27.2 us -> 9.14 us  [exchange_with(): lax.ppermute(array, axis, [(i, i ^ bit) for i in range(size)])]
    ppermute x28, starting transfers between devices: 114 us -> 128 us  [exchange(): moved.append(lax.ppermute(parts[shift], 'ctx', pairs))]
    all_to_all x2, starting transfers between devices: 28.7 us -> 38.8 us  [exchange(): lax.all_to_all(parts[0], 'ctx', split_axis=0, concat_axis=0, tiled=True)]
    unnamed x117 -> x115, local copies, waits for them, and re-layouts: 30.8 us -> 25.7 us
  transfers between devices with their start and end apart: 37 -> 37, of which waited for: 18 -> 16; matrix products, arithmetic and copies ran while one was open for 3% -> 3% of each run, Pallas kernels for 15% -> 11%
where the time goes in v13:
time: 503 us; the launch traced here: 500 us
  waiting for transfers between devices  203 us (40%)
  starting transfers between devices  176 us (35%)
  Pallas kernels  79.7 us (16%)
  local copies, waits for them, and re-layouts  26.3 us (5%)
  other arithmetic  13.9 us (3%)
    ppermute x28, waiting for transfers between devices, exchange(): moved.append(lax.ppermute(parts[shift], 'ctx', pairs))  170 us
    ppermute x28, starting transfers between devices, exchange(): moved.append(lax.ppermute(parts[shift], 'ctx', pairs))  128 us
    pallas_call x3, Pallas kernels, mix(): pl.pallas_call(functools.partial(mix_kernel, parts=len(parts), tile=tile,...  41.3 us
    all_to_all x2, starting transfers between devices, exchange(): lax.all_to_all(parts[0], 'ctx', split_axis=0, concat_axis=0, tiled=True)  38.8 us
    ppermute x7, waiting for transfers between devices, exchange_with(): lax.ppermute(array, axis, [(i, i ^ bit) for i in range(size)])  32.3 us
    unnamed x115, local copies, waits for them, and re-layouts  25.7 us
    pallas_call x3, Pallas kernels, split_channels(): pl.pallas_call(functools.partial(kernel, rotated=rotated), grid=(tiles, r...  24.8 us
    pallas_call x3, Pallas kernels, merge_channels(): pl.pallas_call(functools.partial(merge_kernel, parts=len(parts), rotated=...  11.5 us
  transfers between devices with their start and end apart: 37, of which 16 were waited for; matrix products, arithmetic and copies ran while one was open for 3% of the time, Pallas kernels for 11%

profile of v13, /device:TPU:0, one launch (start us, length us, event | category | flops | bytes accessed | tf_op | source)
XLA Modules:
  0.0 500.2 jit_solution(11229617089275708814)
XLA Ops:
  0.6 7.8 %shard_map.139 = bf16[8,64,32,128]{3,2,1,0:T(8,128)(2,1)S(1)} custom-call(s32[1]{0:T(128)} %bitcast.place_ref, bf16[32,128,768]{2,1,0:T(8,128)(2,1)} %bitcast.51, bf16[32,128,768]{2,1,0:T(8,128)(2,1)} %bitcast.54), custom_call_target="tpu_custom_call" | custom-call | flops 1 | bytes 16777216 | tf_op jit(solution)/shard_map/pallas_call | solution.py:83
  10.5 6.5 %all-to-all-start = ((bf16[8,64,32,128]{3,2,1,0:T(8,128)(2,1)}), bf16[8,64,32,128]{3,2,1,0:T(8,128)(2,1)}, u32[]{:S(2)}, u32[]{:S(2)}) async-start(bf16[8,64,32,128]{3,2,1,0:T(8,128)(2,1)} %copy-done), calls=%async_computation | async-start | bytes 8388608 | tf_op jit(solution)/shard_map/all_to_all | solution.py:333
  17.0 5.3 %shard_map.135 = (bf16[35,32,128]{2,1,0:T(8,128)(2,1)S(1)}, bf16[35,32,128]{2,1,0:T(8,128)(2,1)S(1)}, bf16[35,32,128]{2,1,0:T(8,128)(2,1)S(1)}, bf16[35,32,128]{...) custom-call(s32[1]{0:T(128)} %bitcast.place_ref, ...), custom_call_target="tpu_custom_call" | custom-call | flops 1 | bytes 8388608 | tf_op jit(solution)/shard_map/pallas_call | solution.py:83
  24.4 2.2 collective-permute-start.2
  29.2 11.7 %shard_map.137 = (bf16[96,32,128]{2,1,0:T(8,128)(2,1)S(1)}, bf16[96,32,128]{2,1,0:T(8,128)(2,1)S(1)}, bf16[96,32,128]{2,1,0:T(8,128)(2,1)S(1)}, bf16[96,32,128]{...) custom-call(s32[1]{0:T(128)} %bitcast.place_ref, ...), custom_call_target="tpu_custom_call" | custom-call | flops 1 | bytes 25165824 | tf_op jit(solution)/shard_map/pallas_call | solution.py:83
  47.4 47.8 %collective-permute-done.rest_1_.rest_9_ = bf16[35,32,128]{2,1,0:T(8,128)(2,1)S(1)} collective-permute-done((bf16[35,32,128]{2,1,0:T(8,128)(2,1)S(1)}, bf16[35,32,128]{2,1,0:T(8,128)(2,1)S(1)}, u32[]{:S(2)}, u32[]{:S(2)}) %collective-permute-start) | collective-permute-done | bytes 286752 | tf_op jit(solution)/shard_map/ppermute | solution.py:337
  96.1 4.4 collective-permute-start.6
  100.6 40.7 %collective-permute-done.2.rest_3_.rest_11_ = bf16[35,32,128]{2,1,0:T(8,128)(2,1)S(1)} collective-permute-done((bf16[35,32,128]{2,1,0:T(8,128)(2,1)S(1)}, bf16[35,32,128]{2,1,0:T(8,128)(2,1)S(1)}, u32[]{:S(2)}, u32[]{:S(2)}) %collective-permute-start.2) | collective-permute-done | bytes 286752 | tf_op jit(solution)/shard_map/ppermute | solution.py:337
  142.3 10.3 %collective-permute-start.15 = (bf16[96,32,128]{2,1,0:T(8,128)(2,1)}, bf16[96,32,128]{2,1,0:T(8,128)(2,1)}, u32[]{:S(2)}, u32[]{:S(2)}) collective-permute-start(bf16[96,32,128]{2,1,0:T(8,128)(2,1)} %copy-done.34), channel_id=1, source_target_pairs={{0,2},{1,3},{2,4},{3,5},{4,6},{5,7},{6,0},{7,1},{8,10},{9,11},{10,... | collective-permute-start | bytes 2359304 | tf_op jit(solution)/shard_map/ppermute | solution.py:337
  152.6 5.9 %collective-permute-start.16 = (bf16[96,32,128]{2,1,0:T(8,128)(2,1)}, bf16[96,32,128]{2,1,0:T(8,128)(2,1)}, u32[]{:S(2)}, u32[]{:S(2)}) collective-permute-start(bf16[96,32,128]{2,1,0:T(8,128)(2,1)} %copy-done.33), channel_id=1, source_target_pairs={{0,3},{1,4},{2,5},{3,6},{4,7},{5,0},{6,1},{7,2},{8,11},{9,12},{10,... | collective-permute-start | bytes 2359304 | tf_op jit(solution)/shard_map/ppermute | solution.py:337
  158.5 29.4 %collective-permute-start.17 = (bf16[96,32,128]{2,1,0:T(8,128)(2,1)}, bf16[96,32,128]{2,1,0:T(8,128)(2,1)}, u32[]{:S(2)}, u32[]{:S(2)}) collective-permute-start(bf16[96,32,128]{2,1,0:T(8,128)(2,1)} %copy-done.32), channel_id=1, source_target_pairs={{0,4},{1,5},{2,6},{3,7},{4,0},{5,1},{6,2},{7,3},{8,12},{9,13},{10,... | collective-permute-start | bytes 2359304 | tf_op jit(solution)/shard_map/ppermute | solution.py:337
  187.9 21.8 %collective-permute-start.18 = (bf16[96,32,128]{2,1,0:T(8,128)(2,1)}, bf16[96,32,128]{2,1,0:T(8,128)(2,1)}, u32[]{:S(2)}, u32[]{:S(2)}) collective-permute-start(bf16[96,32,128]{2,1,0:T(8,128)(2,1)} %copy-done.31), channel_id=1, source_target_pairs={{0,5},{1,6},{2,7},{3,0},{4,1},{5,2},{6,3},{7,4},{8,13},{9,14},{10,... | collective-permute-start | bytes 2359304 | tf_op jit(solution)/shard_map/ppermute | solution.py:337
  212.2 3.9 collective-permute-start.19
  217.1 6.8 %shard_map.136 = (bf16[16,32,128]{2,1,0:T(8,128)(2,1)S(1)}, bf16[16,32,128]{2,1,0:T(8,128)(2,1)}, bf16[16,32,128]{2,1,0:T(8,128)(2,1)S(1)}, bf16[16,32,128]{2,1,...) custom-call(s32[1]{0:T(128)} %bitcast.place_ref, ...), custom_call_target="tpu_custom_call" | custom-call | flops 8388608000 | bytes 1024 | tf_op jit(solution)/shard_map/pallas_call | solution.py:222
  229.2 15.0 %collective-permute-done.16.rest_3_.rest_11_.refs_3_ = bf16[96,32,128]{2,1,0:T(8,128)(2,1)} collective-permute-done((bf16[96,32,128]{2,1,0:T(8,128)(2,1)}, bf16[96,32,128]{2,1,0:T(8,128)(2,1)}, u32[]{:S(2)}, u32[]{:S(2)}) %collective-permute-start.16) | collective-permute-done | bytes 786464 | tf_op jit(solution)/shard_map/ppermute | solution.py:337
  245.1 19.6 %collective-permute-done.19.rest_6_.rest_14_.refs_6_ = bf16[96,32,128]{2,1,0:T(8,128)(2,1)S(1)} collective-permute-done((bf16[96,32,128]{2,1,0:T(8,128)(2,1)}, bf16[96,32,128]{2,1,0:T(8,128)(2,1)S(1)}, u32[]{:S(2)}, u32[]{:S(2)}) %collective-permute-start.19) | collective-permute-done | bytes 786464 | tf_op jit(solution)/shard_map/ppermute | solution.py:337
  265.9 20.4 %shard_map.138 = (bf16[48,32,128]{2,1,0:T(8,128)(2,1)S(1)}, bf16[48,32,128]{2,1,0:T(8,128)(2,1)S(1)}, bf16[48,32,128]{2,1,0:T(8,128)(2,1)S(1)}, bf16[48,32,128]{...) custom-call(s32[1]{0:T(128)} %bitcast.place_ref, ...), custom_call_target="tpu_custom_call" | custom-call | flops 25165824000 | bytes 1024 | tf_op jit(solution)/shard_map/pallas_call | solution.py:222
  290.1 14.2 %shard_map.140 = (bf16[8,32,32,128]{3,2,1,0:T(8,128)(2,1)S(1)}, f32[928,128]{1,0:T(8,128)S(1)}) custom-call(s32[1]{0:T(128)} %bitcast.place_ref, f32[768]{0:T(1024)S(1)} %copy-done.47, f32[768]{0:T(1024)S(1)} %copy-done.48, f32[768]{0:T(1024)S(1)} %copy-done.49, bf16[8,64,32,128]{3,2,1,0:T(8,128)(2,1)} %all-to-all-done.rest_0_.rest_1_, ...), custom_call_target="tpu_custom_call" | custom-call | flops 16777216000 | bytes 1024 | tf_op jit(solution)/shard_map/pallas_call | solution.py:222
  306.3 32.4 %all-to-all-start.1 = ((bf16[8,32,32,128]{3,2,1,0:T(8,128)(2,1)}), bf16[8,32,32,128]{3,2,1,0:T(8,128)(2,1)S(1)}, u32[]{:S(2)}, u32[]{:S(2)}) async-start(bf16[8,32,32,128]{3,2,1,0:T(8,128)(2,1)} %shard_map.141), calls=%async_computation.1 | async-start | bytes 4194304 | tf_op jit(solution)/shard_map/all_to_all | solution.py:333
  345.6 4.6 collective-permute-done.28
  357.5 29.0 %collective-permute-done.26.rest_6_.refs_1_ = bf16[48,32,128]{2,1,0:T(8,128)(2,1)S(1)} collective-permute-done((bf16[48,32,128]{2,1,0:T(8,128)(2,1)}, bf16[48,32,128]{2,1,0:T(8,128)(2,1)S(1)}, u32[]{:S(2)}, u32[]{:S(2)}) %collective-permute-start.26) | collective-permute-done | bytes 393248 | tf_op jit(solution)/shard_map/ppermute | solution.py:337
  386.6 7.4 %collective-permute-done.27.rest_7_.refs_2_ = bf16[48,32,128]{2,1,0:T(8,128)(2,1)S(1)} collective-permute-done((bf16[48,32,128]{2,1,0:T(8,128)(2,1)}, bf16[48,32,128]{2,1,0:T(8,128)(2,1)S(1)}, u32[]{:S(2)}, u32[]{:S(2)}) %collective-permute-start.27) | collective-permute-done | bytes 393248 | tf_op jit(solution)/shard_map/ppermute | solution.py:337
  394.7 32.1 %collective-permute-start.24 = (bf16[48,32,128]{2,1,0:T(8,128)(2,1)}, bf16[48,32,128]{2,1,0:T(8,128)(2,1)S(1)}, u32[]{:S(2)}, u32[]{:S(2)}) collective-permute-start(bf16[48,32,128]{2,1,0:T(8,128)(2,1)} %copy-done.37), channel_id=1, source_target_pairs={{0,4},{1,5},{2,6},{3,7},{4,0},{5,1},{6,2},{7,3},{8,12},{9,13},{10,... | collective-permute-start | bytes 1179656 | tf_op jit(solution)/shard_map/ppermute | solution.py:337
  431.0 16.2 %collective-permute-done.31 = f32[232,128]{1,0:T(8,128)S(1)} collective-permute-done((f32[232,128]{1,0:T(8,128)}, f32[232,128]{1,0:T(8,128)S(1)}, u32[]{:S(2)}, u32[]{:S(2)}) %collective-permute-start.31) | collective-permute-done | bytes 118816 | tf_op jit(solution)/shard_map/ppermute | solution.py:292
  449.9 8.7 %collective-permute-done.32 = f32[232,128]{1,0:T(8,128)S(1)} collective-permute-done((f32[232,128]{1,0:T(8,128)}, f32[232,128]{1,0:T(8,128)S(1)}, u32[]{:S(2)}, u32[]{:S(2)}) %collective-permute-start.32) | collective-permute-done | bytes 118816 | tf_op jit(solution)/shard_map/ppermute | solution.py:292
  463.8 2.7 collective-permute-start.7
  470.0 6.3 %collective-permute-done.8.rest_2_.refs_2_ = bf16[16,32,128]{2,1,0:T(8,128)(2,1)S(1)} collective-permute-done((bf16[16,32,128]{2,1,0:T(8,128)(2,1)}, bf16[16,32,128]{2,1,0:T(8,128)(2,1)S(1)}, u32[]{:S(2)}, u32[]{:S(2)}) %collective-permute-start.8) | collective-permute-done | bytes 131104 | tf_op jit(solution)/shard_map/ppermute | solution.py:337
  478.5 3.0 collective-permute-start.11
  482.1 2.7 collective-permute-done.34
  488.6 3.0 shard_map.142.rest_8_
  491.6 5.9 %shard_map.143.rest_8_ = bf16[32,128,768]{2,1,0:T(8,128)(2,1)} custom-call(s32[1]{0:T(128)} %bitcast.place_ref, bf16[48,32,128]{2,1,0:T(8,128)(2,1)S(1)} %copy-done.21, bf16[48,32,128]{2,1,0:T(8,128)(2,1)S(1)} %copy-done.3, bf16[48,32,128]{2,1,0:T(8,128)(2,1)} %collective-permute-done.22.rest_2_.refs_1_, ...), custom_call_target="tpu_custom_call", output_to_operand_aliasing={{}: (9, {})} | custom-call | flops 1 | bytes 12582912 | tf_op jit(solution)/shard_map/pallas_call | solution.py:117
  497.6 2.6 shard_map.144
  (194 shorter events, 68.9 us)
Async XLA Ops:
  10.5 279.6 %all-to-all-start = ((bf16[8,64,32,128]{3,2,1,0:T(8,128)(2,1)}), bf16[8,64,32,128]{3,2,1,0:T(8,128)(2,1)}, u32[]{:S(2)}, u32[]{:S(2)}) async-start(bf16[8,64,32,128]{3,2,1,0:T(8,128)(2,1)} %copy-done), calls=%async_computation | async-start | bytes 8388608 | tf_op jit(solution)/shard_map/all_to_all | solution.py:333
  22.2 73.0 %collective-permute-start = (bf16[35,32,128]{2,1,0:T(8,128)(2,1)S(1)}, bf16[35,32,128]{2,1,0:T(8,128)(2,1)S(1)}, u32[]{:S(2)}, u32[]{:S(2)}) collective-permute-start(bf16[35,32,128]{2,1,0:T(8,128)(2,1)S(1)} %get-tuple-element.44), channel_id=1, source_target_pairs={{0,1},{1,2},{2,3},{3,4},{4,5},{5,6},{6,7},{7,0},{8,9},{9,10},{10,1... | collective-permute-start | bytes 860168 | tf_op jit(solution)/shard_map/ppermute | solution.py:337
  22.7 73.4 %collective-permute-start.1 = (bf16[35,32,128]{2,1,0:T(8,128)(2,1)S(1)}, bf16[35,32,128]{2,1,0:T(8,128)(2,1)S(1)}, u32[]{:S(2)}, u32[]{:S(2)}) collective-permute-start(bf16[35,32,128]{2,1,0:T(8,128)(2,1)S(1)} %get-tuple-element.45), channel_id=1, source_target_pairs={{0,2},{1,3},{2,4},{3,5},{4,6},{5,7},{6,0},{7,1},{8,10},{9,11},{10,... | collective-permute-start | bytes 860168 | tf_op jit(solution)/shard_map/ppermute | solution.py:337
  24.4 116.9 %collective-permute-start.2 = (bf16[35,32,128]{2,1,0:T(8,128)(2,1)S(1)}, bf16[35,32,128]{2,1,0:T(8,128)(2,1)S(1)}, u32[]{:S(2)}, u32[]{:S(2)}) collective-permute-start(bf16[35,32,128]{2,1,0:T(8,128)(2,1)S(1)} %get-tuple-element.46), channel_id=1, source_target_pairs={{0,3},{1,4},{2,5},{3,6},{4,7},{5,0},{6,1},{7,2},{8,11},{9,12},{10,... | collective-permute-start | bytes 860168 | tf_op jit(solution)/shard_map/ppermute | solution.py:337
  26.6 115.7 %collective-permute-start.3 = (bf16[35,32,128]{2,1,0:T(8,128)(2,1)}, bf16[35,32,128]{2,1,0:T(8,128)(2,1)S(1)}, u32[]{:S(2)}, u32[]{:S(2)}) collective-permute-start(bf16[35,32,128]{2,1,0:T(8,128)(2,1)} %get-tuple-element.47), channel_id=1, source_target_pairs={{0,4},{1,5},{2,6},{3,7},{4,0},{5,1},{6,2},{7,3},{8,12},{9,13},{10,... | collective-permute-start | bytes 860168 | tf_op jit(solution)/shard_map/ppermute | solution.py:337
  28.1 124.5 %collective-permute-start.4 = (bf16[35,32,128]{2,1,0:T(8,128)(2,1)}, bf16[35,32,128]{2,1,0:T(8,128)(2,1)S(1)}, u32[]{:S(2)}, u32[]{:S(2)}) collective-permute-start(bf16[35,32,128]{2,1,0:T(8,128)(2,1)} %get-tuple-element.48), channel_id=1, source_target_pairs={{0,5},{1,6},{2,7},{3,0},{4,1},{5,2},{6,3},{7,4},{8,13},{9,14},{10,... | collective-permute-start | bytes 860168 | tf_op jit(solution)/shard_map/ppermute | solution.py:337
  95.2 63.3 %collective-permute-start.5 = (bf16[35,32,128]{2,1,0:T(8,128)(2,1)}, bf16[35,32,128]{2,1,0:T(8,128)(2,1)S(1)}, u32[]{:S(2)}, u32[]{:S(2)}) collective-permute-start(bf16[35,32,128]{2,1,0:T(8,128)(2,1)} %get-tuple-element.49), channel_id=1, source_target_pairs={{0,6},{1,7},{2,0},{3,1},{4,2},{5,3},{6,4},{7,5},{8,14},{9,15},{10,... | collective-permute-start | bytes 860168 | tf_op jit(solution)/shard_map/ppermute | solution.py:337
  96.1 91.8 %collective-permute-start.6 = (bf16[35,32,128]{2,1,0:T(8,128)(2,1)}, bf16[35,32,128]{2,1,0:T(8,128)(2,1)S(1)}, u32[]{:S(2)}, u32[]{:S(2)}) collective-permute-start(bf16[35,32,128]{2,1,0:T(8,128)(2,1)} %get-tuple-element.50), channel_id=1, source_target_pairs={{0,7},{1,0},{2,1},{3,2},{4,3},{5,4},{6,5},{7,6},{8,15},{9,8},{10,9... | collective-permute-start | bytes 860168 | tf_op jit(solution)/shard_map/ppermute | solution.py:337
  141.2 70.9 %collective-permute-start.14 = (bf16[96,32,128]{2,1,0:T(8,128)(2,1)}, bf16[96,32,128]{2,1,0:T(8,128)(2,1)S(1)}, u32[]{:S(2)}, u32[]{:S(2)}) collective-permute-start(bf16[96,32,128]{2,1,0:T(8,128)(2,1)} %copy-done.35), channel_id=1, source_target_pairs={{0,1},{1,2},{2,3},{3,4},{4,5},{5,6},{6,7},{7,0},{8,9},{9,10},{10,1... | collective-permute-start | bytes 2359304 | tf_op jit(solution)/shard_map/ppermute | solution.py:337
  142.3 73.8 %collective-permute-start.15 = (bf16[96,32,128]{2,1,0:T(8,128)(2,1)}, bf16[96,32,128]{2,1,0:T(8,128)(2,1)}, u32[]{:S(2)}, u32[]{:S(2)}) collective-permute-start(bf16[96,32,128]{2,1,0:T(8,128)(2,1)} %copy-done.34), channel_id=1, source_target_pairs={{0,2},{1,3},{2,4},{3,5},{4,6},{5,7},{6,0},{7,1},{8,10},{9,11},{10,... | collective-permute-start | bytes 2359304 | tf_op jit(solution)/shard_map/ppermute | solution.py:337
  152.6 91.6 %collective-permute-start.16 = (bf16[96,32,128]{2,1,0:T(8,128)(2,1)}, bf16[96,32,128]{2,1,0:T(8,128)(2,1)}, u32[]{:S(2)}, u32[]{:S(2)}) collective-permute-start(bf16[96,32,128]{2,1,0:T(8,128)(2,1)} %copy-done.33), channel_id=1, source_target_pairs={{0,3},{1,4},{2,5},{3,6},{4,7},{5,0},{6,1},{7,2},{8,11},{9,12},{10,... | collective-permute-start | bytes 2359304 | tf_op jit(solution)/shard_map/ppermute | solution.py:337
  158.5 86.7 %collective-permute-start.17 = (bf16[96,32,128]{2,1,0:T(8,128)(2,1)}, bf16[96,32,128]{2,1,0:T(8,128)(2,1)}, u32[]{:S(2)}, u32[]{:S(2)}) collective-permute-start(bf16[96,32,128]{2,1,0:T(8,128)(2,1)} %copy-done.32), channel_id=1, source_target_pairs={{0,4},{1,5},{2,6},{3,7},{4,0},{5,1},{6,2},{7,3},{8,12},{9,13},{10,... | collective-permute-start | bytes 2359304 | tf_op jit(solution)/shard_map/ppermute | solution.py:337
  187.9 57.2 %collective-permute-start.18 = (bf16[96,32,128]{2,1,0:T(8,128)(2,1)}, bf16[96,32,128]{2,1,0:T(8,128)(2,1)}, u32[]{:S(2)}, u32[]{:S(2)}) collective-permute-start(bf16[96,32,128]{2,1,0:T(8,128)(2,1)} %copy-done.31), channel_id=1, source_target_pairs={{0,5},{1,6},{2,7},{3,0},{4,1},{5,2},{6,3},{7,4},{8,13},{9,14},{10,... | collective-permute-start | bytes 2359304 | tf_op jit(solution)/shard_map/ppermute | solution.py:337
  212.2 52.5 %collective-permute-start.19 = (bf16[96,32,128]{2,1,0:T(8,128)(2,1)}, bf16[96,32,128]{2,1,0:T(8,128)(2,1)S(1)}, u32[]{:S(2)}, u32[]{:S(2)}) collective-permute-start(bf16[96,32,128]{2,1,0:T(8,128)(2,1)} %copy-done.30), channel_id=1, source_target_pairs={{0,6},{1,7},{2,0},{3,1},{4,2},{5,3},{6,4},{7,5},{8,14},{9,15},{10,... | collective-permute-start | bytes 2359304 | tf_op jit(solution)/shard_map/ppermute | solution.py:337
  216.1 48.6 %collective-permute-start.20 = (bf16[96,32,128]{2,1,0:T(8,128)(2,1)}, bf16[96,32,128]{2,1,0:T(8,128)(2,1)S(1)}, u32[]{:S(2)}, u32[]{:S(2)}) collective-permute-start(bf16[96,32,128]{2,1,0:T(8,128)(2,1)} %get-tuple-element.66), channel_id=1, source_target_pairs={{0,7},{1,0},{2,1},{3,2},{4,3},{5,4},{6,5},{7,6},{8,15},{9,8},{10,9... | collective-permute-start | bytes 2359304 | tf_op jit(solution)/shard_map/ppermute | solution.py:337
  306.3 182.2 %all-to-all-start.1 = ((bf16[8,32,32,128]{3,2,1,0:T(8,128)(2,1)}), bf16[8,32,32,128]{3,2,1,0:T(8,128)(2,1)S(1)}, u32[]{:S(2)}, u32[]{:S(2)}) async-start(bf16[8,32,32,128]{3,2,1,0:T(8,128)(2,1)} %shard_map.141), calls=%async_computation.1 | async-start | bytes 4194304 | tf_op jit(solution)/shard_map/all_to_all | solution.py:333
  343.5 43.0 %collective-permute-start.26 = (bf16[48,32,128]{2,1,0:T(8,128)(2,1)}, bf16[48,32,128]{2,1,0:T(8,128)(2,1)S(1)}, u32[]{:S(2)}, u32[]{:S(2)}) collective-permute-start(bf16[48,32,128]{2,1,0:T(8,128)(2,1)} %get-tuple-element.73), channel_id=1, source_target_pairs={{0,2},{1,3},{2,4},{3,5},{4,6},{5,7},{6,0},{7,1},{8,10},{9,11},{10,... | collective-permute-start | bytes 1179656 | tf_op jit(solution)/shard_map/ppermute | solution.py:337
  345.6 48.4 %collective-permute-start.27 = (bf16[48,32,128]{2,1,0:T(8,128)(2,1)}, bf16[48,32,128]{2,1,0:T(8,128)(2,1)S(1)}, u32[]{:S(2)}, u32[]{:S(2)}) collective-permute-start(bf16[48,32,128]{2,1,0:T(8,128)(2,1)} %get-tuple-element.74), channel_id=1, source_target_pairs={{0,1},{1,2},{2,3},{3,4},{4,5},{5,6},{6,7},{7,0},{8,9},{9,10},{10,1... | collective-permute-start | bytes 1179656 | tf_op jit(solution)/shard_map/ppermute | solution.py:337
  352.9 75.5 %collective-permute-start.21 = (bf16[48,32,128]{2,1,0:T(8,128)(2,1)}, bf16[48,32,128]{2,1,0:T(8,128)(2,1)S(1)}, u32[]{:S(2)}, u32[]{:S(2)}) collective-permute-start(bf16[48,32,128]{2,1,0:T(8,128)(2,1)} %copy-done.40), channel_id=1, source_target_pairs={{0,7},{1,0},{2,1},{3,2},{4,3},{5,4},{6,5},{7,6},{8,15},{9,8},{10,9... | collective-permute-start | bytes 1179656 | tf_op jit(solution)/shard_map/ppermute | solution.py:337
  355.0 93.8 %collective-permute-start.22 = (bf16[48,32,128]{2,1,0:T(8,128)(2,1)}, bf16[48,32,128]{2,1,0:T(8,128)(2,1)}, u32[]{:S(2)}, u32[]{:S(2)}) collective-permute-start(bf16[48,32,128]{2,1,0:T(8,128)(2,1)} %copy-done.39), channel_id=1, source_target_pairs={{0,6},{1,7},{2,0},{3,1},{4,2},{5,3},{6,4},{7,5},{8,14},{9,15},{10,... | collective-permute-start | bytes 1179656 | tf_op jit(solution)/shard_map/ppermute | solution.py:337
  356.4 92.4 %collective-permute-start.23 = (bf16[48,32,128]{2,1,0:T(8,128)(2,1)}, bf16[48,32,128]{2,1,0:T(8,128)(2,1)}, u32[]{:S(2)}, u32[]{:S(2)}) collective-permute-start(bf16[48,32,128]{2,1,0:T(8,128)(2,1)} %copy-done.38), channel_id=1, source_target_pairs={{0,5},{1,6},{2,7},{3,0},{4,1},{5,2},{6,3},{7,4},{8,13},{9,14},{10,... | collective-permute-start | bytes 1179656 | tf_op jit(solution)/shard_map/ppermute | solution.py:337
  394.7 32.1 %collective-permute-start.30 = (f32[232,128]{1,0:T(8,128)}, f32[232,128]{1,0:T(8,128)S(1)}, u32[]{:S(2)}, u32[]{:S(2)}) collective-permute-start(f32[232,128]{1,0:T(8,128)} %shard_map.146), channel_id=1, source_target_pairs={{0,1},{1,0},{2,3},{3,2},{4,5},{5,4},{6,7},{7,6},{8,9},{9,8},{10,11... | collective-permute-start | bytes 356360 | tf_op jit(solution)/shard_map/ppermute | solution.py:292
  394.7 65.5 %collective-permute-start.24 = (bf16[48,32,128]{2,1,0:T(8,128)(2,1)}, bf16[48,32,128]{2,1,0:T(8,128)(2,1)S(1)}, u32[]{:S(2)}, u32[]{:S(2)}) collective-permute-start(bf16[48,32,128]{2,1,0:T(8,128)(2,1)} %copy-done.37), channel_id=1, source_target_pairs={{0,4},{1,5},{2,6},{3,7},{4,0},{5,1},{6,2},{7,3},{8,12},{9,13},{10,... | collective-permute-start | bytes 1179656 | tf_op jit(solution)/shard_map/ppermute | solution.py:337
  426.8 34.8 %collective-permute-start.25 = (bf16[48,32,128]{2,1,0:T(8,128)(2,1)}, bf16[48,32,128]{2,1,0:T(8,128)(2,1)S(1)}, u32[]{:S(2)}, u32[]{:S(2)}) collective-permute-start(bf16[48,32,128]{2,1,0:T(8,128)(2,1)} %copy-done.36), channel_id=1, source_target_pairs={{0,3},{1,4},{2,5},{3,6},{4,7},{5,0},{6,1},{7,2},{8,11},{9,12},{10,... | collective-permute-start | bytes 1179656 | tf_op jit(solution)/shard_map/ppermute | solution.py:337
  429.1 18.0 %collective-permute-start.31 = (f32[232,128]{1,0:T(8,128)}, f32[232,128]{1,0:T(8,128)S(1)}, u32[]{:S(2)}, u32[]{:S(2)}) collective-permute-start(f32[232,128]{1,0:T(8,128)} %shard_map.147), channel_id=1, source_target_pairs={{0,2},{1,3},{2,0},{3,1},{4,6},{5,7},{6,4},{7,5},{8,10},{9,11},{10,... | collective-permute-start | bytes 356360 | tf_op jit(solution)/shard_map/ppermute | solution.py:292
  448.8 9.9 %collective-permute-start.32 = (f32[232,128]{1,0:T(8,128)}, f32[232,128]{1,0:T(8,128)S(1)}, u32[]{:S(2)}, u32[]{:S(2)}) collective-permute-start(f32[232,128]{1,0:T(8,128)} %shard_map.148), channel_id=1, source_target_pairs={{0,4},{1,5},{2,6},{3,7},{4,0},{5,1},{6,2},{7,3},{8,12},{9,13},{10,... | collective-permute-start | bytes 356360 | tf_op jit(solution)/shard_map/ppermute | solution.py:292
  466.5 9.8 %collective-permute-start.8 = (bf16[16,32,128]{2,1,0:T(8,128)(2,1)}, bf16[16,32,128]{2,1,0:T(8,128)(2,1)S(1)}, u32[]{:S(2)}, u32[]{:S(2)}) collective-permute-start(bf16[16,32,128]{2,1,0:T(8,128)(2,1)} %copy-done.46), channel_id=1, source_target_pairs={{0,6},{1,7},{2,0},{3,1},{4,2},{5,3},{6,4},{7,5},{8,14},{9,15},{10,... | collective-permute-start | bytes 393224 | tf_op jit(solution)/shard_map/ppermute | solution.py:337
  468.0 8.4 %collective-permute-start.9 = (bf16[16,32,128]{2,1,0:T(8,128)(2,1)}, bf16[16,32,128]{2,1,0:T(8,128)(2,1)}, u32[]{:S(2)}, u32[]{:S(2)}) collective-permute-start(bf16[16,32,128]{2,1,0:T(8,128)(2,1)} %copy-done.45), channel_id=1, source_target_pairs={{0,5},{1,6},{2,7},{3,0},{4,1},{5,2},{6,3},{7,4},{8,13},{9,14},{10,... | collective-permute-start | bytes 393224 | tf_op jit(solution)/shard_map/ppermute | solution.py:337
  478.5 19.0 %collective-permute-start.10 = (bf16[16,32,128]{2,1,0:T(8,128)(2,1)}, bf16[16,32,128]{2,1,0:T(8,128)(2,1)S(1)}, u32[]{:S(2)}, u32[]{:S(2)}) collective-permute-start(bf16[16,32,128]{2,1,0:T(8,128)(2,1)} %copy-done.44), channel_id=1, source_target_pairs={{0,4},{1,5},{2,6},{3,7},{4,0},{5,1},{6,2},{7,3},{8,12},{9,13},{10,... | collective-permute-start | bytes 393224 | tf_op jit(solution)/shard_map/ppermute | solution.py:337
  478.5 19.0 %collective-permute-start.11 = (bf16[16,32,128]{2,1,0:T(8,128)(2,1)}, bf16[16,32,128]{2,1,0:T(8,128)(2,1)S(1)}, u32[]{:S(2)}, u32[]{:S(2)}) collective-permute-start(bf16[16,32,128]{2,1,0:T(8,128)(2,1)} %copy-done.43), channel_id=1, source_target_pairs={{0,3},{1,4},{2,5},{3,6},{4,7},{5,0},{6,1},{7,2},{8,11},{9,12},{10,... | collective-permute-start | bytes 393224 | tf_op jit(solution)/shard_map/ppermute | solution.py:337
  481.6 15.9 %collective-permute-start.12 = (bf16[16,32,128]{2,1,0:T(8,128)(2,1)}, bf16[16,32,128]{2,1,0:T(8,128)(2,1)}, u32[]{:S(2)}, u32[]{:S(2)}) collective-permute-start(bf16[16,32,128]{2,1,0:T(8,128)(2,1)} %copy-done.42), channel_id=1, source_target_pairs={{0,2},{1,3},{2,4},{3,5},{4,6},{5,7},{6,0},{7,1},{8,10},{9,11},{10,... | collective-permute-start | bytes 393224 | tf_op jit(solution)/shard_map/ppermute | solution.py:337
  481.6 15.9 %collective-permute-start.13 = (bf16[16,32,128]{2,1,0:T(8,128)(2,1)}, bf16[16,32,128]{2,1,0:T(8,128)(2,1)}, u32[]{:S(2)}, u32[]{:S(2)}) collective-permute-start(bf16[16,32,128]{2,1,0:T(8,128)(2,1)} %copy-done.41), channel_id=1, source_target_pairs={{0,1},{1,2},{2,3},{3,4},{4,5},{5,6},{6,7},{7,0},{8,9},{9,10},{10,1... | collective-permute-start | bytes 393224 | tf_op jit(solution)/shard_map/ppermute | solution.py:337
  (58 other events, 907.4 us)

commit v14 on v13

--- a/solution.py
+++ b/solution.py
@@ -356,19 +356,20 @@
         twiddle_all = lax.dynamic_slice_in_dim(twice, turn, ctx_size, 0).reshape(A, B)
         factors = [first_factor, first_factor.T, second, second_t, twiddle_all]
         returned = []
+        released = []
         for which, (at, count, rotated) in enumerate(groups):
             parts, own_sums = mix(
                 arrived[which], at, count, 2 * share, place, vectors, factors, sum_rows, ctx_size,
-                rotated, [],
+                rotated, released if which == 2 else [],
             )
             if which == 1:
-                parts = hold(parts, arrived[2][1:])
+                parts = released = hold(parts, arrived[2][1:])
             returned.append(exchange(parts, -1, rotated))
             terms.append(own_sums)
         leaving.append(returned)
 
     back, first = leaving[-1][2], leaving[-1][0]
-    sums = sum_over_mesh(add(terms, []), [None, back[-2:], back[1:2], back[2:4], back[4:-2], first[1:4]])
+    sums = sum_over_mesh(add(terms, []), [None, back[-2:], back[1:2], back[2:3], back[3:-2], first[1:3]])
     grads = []
     for returned in leaving:
         held = None

time: 503 us -> 461 us (0.917)
  waiting for transfers between devices: 203 us -> 180 us
  starting transfers between devices: 176 us -> 156 us
    ppermute x28, waiting for transfers between devices: 170 us -> 139 us  [exchange(): moved.append(lax.ppermute(parts[shift], 'ctx', pairs))]
    all_to_all x2, starting transfers between devices: 38.8 us -> 28.1 us  [exchange(): lax.all_to_all(parts[0], 'ctx', split_axis=0, concat_axis=0, tiled=True)]
    ppermute x28, starting transfers between devices: 128 us -> 118 us  [exchange(): moved.append(lax.ppermute(parts[shift], 'ctx', pairs))]
    ppermute x7, waiting for transfers between devices: 32.3 us -> 40.8 us  [exchange_with(): lax.ppermute(array, axis, [(i, i ^ bit) for i in range(size)])]
  transfers between devices with their start and end apart: 37 -> 37, of which waited for: 16 -> 16; matrix products, arithmetic and copies ran while one was open for 3% -> 3% of each run, Pallas kernels for 11% -> 15%
where the time goes in v14:
time: 461 us; the launch traced here: 458 us
  waiting for transfers between devices  180 us (39%)
  starting transfers between devices  156 us (34%)
  Pallas kernels  78.5 us (17%)
  local copies, waits for them, and re-layouts  28.7 us (6%)
  other arithmetic  13.9 us (3%)
    ppermute x28, waiting for transfers between devices, exchange(): moved.append(lax.ppermute(parts[shift], 'ctx', pairs))  139 us
    ppermute x28, starting transfers between devices, exchange(): moved.append(lax.ppermute(parts[shift], 'ctx', pairs))  118 us
    ppermute x7, waiting for transfers between devices, exchange_with(): lax.ppermute(array, axis, [(i, i ^ bit) for i in range(size)])  40.8 us
    pallas_call x3, Pallas kernels, mix(): pl.pallas_call(functools.partial(mix_kernel, parts=len(parts), tile=tile,...  39.9 us
    all_to_all x2, starting transfers between devices, exchange(): lax.all_to_all(parts[0], 'ctx', split_axis=0, concat_axis=0, tiled=True)  28.1 us
    unnamed x115, local copies, waits for them, and re-layouts  28 us
    pallas_call x3, Pallas kernels, split_channels(): pl.pallas_call(functools.partial(kernel, rotated=rotated), grid=(tiles, r...  24.8 us
    pallas_call x3, Pallas kernels, merge_channels(): pl.pallas_call(functools.partial(merge_kernel, parts=len(parts), rotated=...  11.6 us
  transfers between devices with their start and end apart: 37, of which 16 were waited for; matrix products, arithmetic and copies ran while one was open for 3% of the time, Pallas kernels for 15%

profile of v14, /device:TPU:0, one launch (start us, length us, event | category | flops | bytes accessed | tf_op | source)
XLA Modules:
  0.0 458.0 jit_solution(7880295666528793341)
XLA Ops:
  0.6 7.8 %shard_map.138 = bf16[8,64,32,128]{3,2,1,0:T(8,128)(2,1)S(1)} custom-call(s32[1]{0:T(128)} %bitcast.place_ref, bf16[32,128,768]{2,1,0:T(8,128)(2,1)} %bitcast.51, bf16[32,128,768]{2,1,0:T(8,128)(2,1)} %bitcast.54), custom_call_target="tpu_custom_call" | custom-call | flops 1 | bytes 16777216 | tf_op jit(solution)/shard_map/pallas_call | solution.py:83
  10.5 6.5 %all-to-all-start = ((bf16[8,64,32,128]{3,2,1,0:T(8,128)(2,1)}), bf16[8,64,32,128]{3,2,1,0:T(8,128)(2,1)}, u32[]{:S(2)}, u32[]{:S(2)}) async-start(bf16[8,64,32,128]{3,2,1,0:T(8,128)(2,1)} %copy-done), calls=%async_computation | async-start | bytes 8388608 | tf_op jit(solution)/shard_map/all_to_all | solution.py:333
  17.0 5.3 %shard_map.135 = (bf16[35,32,128]{2,1,0:T(8,128)(2,1)S(1)}, bf16[35,32,128]{2,1,0:T(8,128)(2,1)S(1)}, bf16[35,32,128]{2,1,0:T(8,128)(2,1)S(1)}, bf16[35,32,128]{...) custom-call(s32[1]{0:T(128)} %bitcast.place_ref, ...), custom_call_target="tpu_custom_call" | custom-call | flops 1 | bytes 8388608 | tf_op jit(solution)/shard_map/pallas_call | solution.py:83
  24.4 2.2 collective-permute-start.2
  29.2 11.7 %shard_map.137 = (bf16[96,32,128]{2,1,0:T(8,128)(2,1)S(1)}, bf16[96,32,128]{2,1,0:T(8,128)(2,1)S(1)}, bf16[96,32,128]{2,1,0:T(8,128)(2,1)S(1)}, bf16[96,32,128]{...) custom-call(s32[1]{0:T(128)} %bitcast.place_ref, ...), custom_call_target="tpu_custom_call" | custom-call | flops 1 | bytes 25165824 | tf_op jit(solution)/shard_map/pallas_call | solution.py:83
  46.5 48.7 %collective-permute-done.rest_1_.rest_9_ = bf16[35,32,128]{2,1,0:T(8,128)(2,1)S(1)} collective-permute-done((bf16[35,32,128]{2,1,0:T(8,128)(2,1)S(1)}, bf16[35,32,128]{2,1,0:T(8,128)(2,1)S(1)}, u32[]{:S(2)}, u32[]{:S(2)}) %collective-permute-start) | collective-permute-done | bytes 286752 | tf_op jit(solution)/shard_map/ppermute | solution.py:337
  96.1 4.4 collective-permute-start.6
  100.6 40.7 %collective-permute-done.2.rest_3_.rest_11_ = bf16[35,32,128]{2,1,0:T(8,128)(2,1)S(1)} collective-permute-done((bf16[35,32,128]{2,1,0:T(8,128)(2,1)S(1)}, bf16[35,32,128]{2,1,0:T(8,128)(2,1)S(1)}, u32[]{:S(2)}, u32[]{:S(2)}) %collective-permute-start.2) | collective-permute-done | bytes 286752 | tf_op jit(solution)/shard_map/ppermute | solution.py:337
  142.3 10.3 %collective-permute-start.15 = (bf16[96,32,128]{2,1,0:T(8,128)(2,1)}, bf16[96,32,128]{2,1,0:T(8,128)(2,1)}, u32[]{:S(2)}, u32[]{:S(2)}) collective-permute-start(bf16[96,32,128]{2,1,0:T(8,128)(2,1)} %copy-done.32), channel_id=1, source_target_pairs={{0,2},{1,3},{2,4},{3,5},{4,6},{5,7},{6,0},{7,1},{8,10},{9,11},{10,... | collective-permute-start | bytes 2359304 | tf_op jit(solution)/shard_map/ppermute | solution.py:337
  152.6 5.9 %collective-permute-start.16 = (bf16[96,32,128]{2,1,0:T(8,128)(2,1)}, bf16[96,32,128]{2,1,0:T(8,128)(2,1)}, u32[]{:S(2)}, u32[]{:S(2)}) collective-permute-start(bf16[96,32,128]{2,1,0:T(8,128)(2,1)} %copy-done.31), channel_id=1, source_target_pairs={{0,3},{1,4},{2,5},{3,6},{4,7},{5,0},{6,1},{7,2},{8,11},{9,12},{10,... | collective-permute-start | bytes 2359304 | tf_op jit(solution)/shard_map/ppermute | solution.py:337
  158.5 29.4 %collective-permute-start.17 = (bf16[96,32,128]{2,1,0:T(8,128)(2,1)}, bf16[96,32,128]{2,1,0:T(8,128)(2,1)}, u32[]{:S(2)}, u32[]{:S(2)}) collective-permute-start(bf16[96,32,128]{2,1,0:T(8,128)(2,1)} %copy-done.30), channel_id=1, source_target_pairs={{0,4},{1,5},{2,6},{3,7},{4,0},{5,1},{6,2},{7,3},{8,12},{9,13},{10,... | collective-permute-start | bytes 2359304 | tf_op jit(solution)/shard_map/ppermute | solution.py:337
  187.9 21.8 %collective-permute-start.18 = (bf16[96,32,128]{2,1,0:T(8,128)(2,1)}, bf16[96,32,128]{2,1,0:T(8,128)(2,1)}, u32[]{:S(2)}, u32[]{:S(2)}) collective-permute-start(bf16[96,32,128]{2,1,0:T(8,128)(2,1)} %copy-done.29), channel_id=1, source_target_pairs={{0,5},{1,6},{2,7},{3,0},{4,1},{5,2},{6,3},{7,4},{8,13},{9,14},{10,... | collective-permute-start | bytes 2359304 | tf_op jit(solution)/shard_map/ppermute | solution.py:337
  213.1 6.7 %shard_map.136 = (bf16[16,32,128]{2,1,0:T(8,128)(2,1)S(1)}, bf16[16,32,128]{2,1,0:T(8,128)(2,1)}, bf16[16,32,128]{2,1,0:T(8,128)(2,1)S(1)}, bf16[16,32,128]{2,1,...) custom-call(s32[1]{0:T(128)} %bitcast.place_ref, ...), custom_call_target="tpu_custom_call" | custom-call | flops 8388608000 | bytes 1024 | tf_op jit(solution)/shard_map/pallas_call | solution.py:222
  225.2 3.8 collective-permute-start.19
  229.0 13.8 %shard_map.139 = (bf16[8,32,32,128]{3,2,1,0:T(8,128)(2,1)S(1)}, f32[928,128]{1,0:T(8,128)S(1)}) custom-call(s32[1]{0:T(128)} %bitcast.place_ref, f32[768]{0:T(1024)S(1)} %copy-done.47, f32[768]{0:T(1024)S(1)} %copy-done.48, f32[768]{0:T(1024)S(1)} %copy-done.49, bf16[8,64,32,128]{3,2,1,0:T(8,128)(2,1)} %all-to-all-done.rest_0_.rest_1_, ...), custom_call_target="tpu_custom_call" | custom-call | flops 16777216000 | bytes 1024 | tf_op jit(solution)/shard_map/pallas_call | solution.py:222
  245.1 30.4 %collective-permute-done.19.refs_6_.rest_6_.rest_14_ = bf16[96,32,128]{2,1,0:T(8,128)(2,1)S(1)} collective-permute-done((bf16[96,32,128]{2,1,0:T(8,128)(2,1)}, bf16[96,32,128]{2,1,0:T(8,128)(2,1)S(1)}, u32[]{:S(2)}, u32[]{:S(2)}) %collective-permute-start.19) | collective-permute-done | bytes 786464 | tf_op jit(solution)/shard_map/ppermute | solution.py:337
  276.7 21.7 %all-to-all-start.1 = ((bf16[8,32,32,128]{3,2,1,0:T(8,128)(2,1)}), bf16[8,32,32,128]{3,2,1,0:T(8,128)(2,1)S(1)}, u32[]{:S(2)}, u32[]{:S(2)}) async-start(bf16[8,32,32,128]{3,2,1,0:T(8,128)(2,1)} %shard_map.140.rest_21_), calls=%async_computation.1 | async-start | bytes 4194304 | tf_op jit(solution)/shard_map/all_to_all | solution.py:333
  299.5 19.4 %shard_map.141 = (bf16[48,32,128]{2,1,0:T(8,128)(2,1)S(1)}, bf16[48,32,128]{2,1,0:T(8,128)(2,1)S(1)}, bf16[48,32,128]{2,1,0:T(8,128)(2,1)S(1)}, bf16[48,32,128]{...) custom-call(s32[1]{0:T(128)} %bitcast.place_ref, ...), custom_call_target="tpu_custom_call" | custom-call | flops 25165824000 | bytes 1024 | tf_op jit(solution)/shard_map/pallas_call | solution.py:222
  325.7 2.2 shard_map.145
  332.6 4.6 %collective-permute-done.28 = f32[464,128]{1,0:T(8,128)S(1)} collective-permute-done((f32[464,128]{1,0:T(8,128)S(1)}, f32[464,128]{1,0:T(8,128)S(1)}, u32[]{:S(2)}, u32[]{:S(2)}) %collective-permute-start.28) | collective-permute-done | bytes 237600 | tf_op jit(solution)/shard_map/ppermute | solution.py:292
  339.9 2.2 collective-permute-start.21
  346.2 7.5 %collective-permute-done.27.rest_7_.refs_2_ = bf16[48,32,128]{2,1,0:T(8,128)(2,1)} collective-permute-done((bf16[48,32,128]{2,1,0:T(8,128)(2,1)}, bf16[48,32,128]{2,1,0:T(8,128)(2,1)}, u32[]{:S(2)}, u32[]{:S(2)}) %collective-permute-start.27) | collective-permute-done | bytes 393248 | tf_op jit(solution)/shard_map/ppermute | solution.py:337
  353.7 19.6 %collective-permute-start.23 = (bf16[48,32,128]{2,1,0:T(8,128)(2,1)}, bf16[48,32,128]{2,1,0:T(8,128)(2,1)S(1)}, u32[]{:S(2)}, u32[]{:S(2)}) collective-permute-start(bf16[48,32,128]{2,1,0:T(8,128)(2,1)} %copy-done.36), channel_id=1, source_target_pairs={{0,5},{1,6},{2,7},{3,0},{4,1},{5,2},{6,3},{7,4},{8,13},{9,14},{10,... | collective-permute-start | bytes 1179656 | tf_op jit(solution)/shard_map/ppermute | solution.py:337
  377.4 22.2 %collective-permute-done.31 = f32[232,128]{1,0:T(8,128)S(1)} collective-permute-done((f32[232,128]{1,0:T(8,128)}, f32[232,128]{1,0:T(8,128)S(1)}, u32[]{:S(2)}, u32[]{:S(2)}) %collective-permute-start.31) | collective-permute-done | bytes 118816 | tf_op jit(solution)/shard_map/ppermute | solution.py:292
  401.9 3.2 collective-permute-start.32
  405.2 12.8 %collective-permute-done.32 = f32[232,128]{1,0:T(8,128)S(1)} collective-permute-done((f32[232,128]{1,0:T(8,128)}, f32[232,128]{1,0:T(8,128)S(1)}, u32[]{:S(2)}, u32[]{:S(2)}) %collective-permute-start.32) | collective-permute-done | bytes 118816 | tf_op jit(solution)/shard_map/ppermute | solution.py:292
  422.3 4.4 collective-permute-start.8
  428.4 4.0 collective-permute-done.8.rest_2_.refs_2_
  436.3 2.6 collective-permute-start.12
  443.9 3.0 shard_map.142.rest_8_
  446.9 6.0 %shard_map.143.rest_8_ = bf16[32,128,768]{2,1,0:T(8,128)(2,1)} custom-call(s32[1]{0:T(128)} %bitcast.place_ref, bf16[48,32,128]{2,1,0:T(8,128)(2,1)S(1)} %copy-done.20, bf16[48,32,128]{2,1,0:T(8,128)(2,1)S(1)} %copy-done.3, bf16[48,32,128]{2,1,0:T(8,128)(2,1)S(1)} %copy-done.5, bf16[48,32,128]{2,1,0:T(8,128)(2,1)S(1)} %copy-done.9, ...), custom_call_target="tpu_custom_call", output_to_operand_aliasing={{}: (9, {})} | custom-call | flops 1 | bytes 12582912 | tf_op jit(solution)/shard_map/pallas_call | solution.py:117
  455.4 2.6 shard_map.144
  (194 shorter events, 69.6 us)
Async XLA Ops:
  10.5 218.5 %all-to-all-start = ((bf16[8,64,32,128]{3,2,1,0:T(8,128)(2,1)}), bf16[8,64,32,128]{3,2,1,0:T(8,128)(2,1)}, u32[]{:S(2)}, u32[]{:S(2)}) async-start(bf16[8,64,32,128]{3,2,1,0:T(8,128)(2,1)} %copy-done), calls=%async_computation | async-start | bytes 8388608 | tf_op jit(solution)/shard_map/all_to_all | solution.py:333
  22.2 73.0 %collective-permute-start = (bf16[35,32,128]{2,1,0:T(8,128)(2,1)S(1)}, bf16[35,32,128]{2,1,0:T(8,128)(2,1)S(1)}, u32[]{:S(2)}, u32[]{:S(2)}) collective-permute-start(bf16[35,32,128]{2,1,0:T(8,128)(2,1)S(1)} %get-tuple-element.44), channel_id=1, source_target_pairs={{0,1},{1,2},{2,3},{3,4},{4,5},{5,6},{6,7},{7,0},{8,9},{9,10},{10,1... | collective-permute-start | bytes 860168 | tf_op jit(solution)/shard_map/ppermute | solution.py:337
  22.7 73.4 %collective-permute-start.1 = (bf16[35,32,128]{2,1,0:T(8,128)(2,1)S(1)}, bf16[35,32,128]{2,1,0:T(8,128)(2,1)S(1)}, u32[]{:S(2)}, u32[]{:S(2)}) collective-permute-start(bf16[35,32,128]{2,1,0:T(8,128)(2,1)S(1)} %get-tuple-element.45), channel_id=1, source_target_pairs={{0,2},{1,3},{2,4},{3,5},{4,6},{5,7},{6,0},{7,1},{8,10},{9,11},{10,... | collective-permute-start | bytes 860168 | tf_op jit(solution)/shard_map/ppermute | solution.py:337
  24.4 116.9 %collective-permute-start.2 = (bf16[35,32,128]{2,1,0:T(8,128)(2,1)S(1)}, bf16[35,32,128]{2,1,0:T(8,128)(2,1)S(1)}, u32[]{:S(2)}, u32[]{:S(2)}) collective-permute-start(bf16[35,32,128]{2,1,0:T(8,128)(2,1)S(1)} %get-tuple-element.46), channel_id=1, source_target_pairs={{0,3},{1,4},{2,5},{3,6},{4,7},{5,0},{6,1},{7,2},{8,11},{9,12},{10,... | collective-permute-start | bytes 860168 | tf_op jit(solution)/shard_map/ppermute | solution.py:337
  26.6 115.7 %collective-permute-start.3 = (bf16[35,32,128]{2,1,0:T(8,128)(2,1)}, bf16[35,32,128]{2,1,0:T(8,128)(2,1)S(1)}, u32[]{:S(2)}, u32[]{:S(2)}) collective-permute-start(bf16[35,32,128]{2,1,0:T(8,128)(2,1)} %get-tuple-element.47), channel_id=1, source_target_pairs={{0,4},{1,5},{2,6},{3,7},{4,0},{5,1},{6,2},{7,3},{8,12},{9,13},{10,... | collective-permute-start | bytes 860168 | tf_op jit(solution)/shard_map/ppermute | solution.py:337
  28.1 124.5 %collective-permute-start.4 = (bf16[35,32,128]{2,1,0:T(8,128)(2,1)}, bf16[35,32,128]{2,1,0:T(8,128)(2,1)S(1)}, u32[]{:S(2)}, u32[]{:S(2)}) collective-permute-start(bf16[35,32,128]{2,1,0:T(8,128)(2,1)} %get-tuple-element.48), channel_id=1, source_target_pairs={{0,5},{1,6},{2,7},{3,0},{4,1},{5,2},{6,3},{7,4},{8,13},{9,14},{10,... | collective-permute-start | bytes 860168 | tf_op jit(solution)/shard_map/ppermute | solution.py:337
  95.2 63.3 %collective-permute-start.5 = (bf16[35,32,128]{2,1,0:T(8,128)(2,1)}, bf16[35,32,128]{2,1,0:T(8,128)(2,1)S(1)}, u32[]{:S(2)}, u32[]{:S(2)}) collective-permute-start(bf16[35,32,128]{2,1,0:T(8,128)(2,1)} %get-tuple-element.49), channel_id=1, source_target_pairs={{0,6},{1,7},{2,0},{3,1},{4,2},{5,3},{6,4},{7,5},{8,14},{9,15},{10,... | collective-permute-start | bytes 860168 | tf_op jit(solution)/shard_map/ppermute | solution.py:337
  96.1 91.8 %collective-permute-start.6 = (bf16[35,32,128]{2,1,0:T(8,128)(2,1)}, bf16[35,32,128]{2,1,0:T(8,128)(2,1)S(1)}, u32[]{:S(2)}, u32[]{:S(2)}) collective-permute-start(bf16[35,32,128]{2,1,0:T(8,128)(2,1)} %get-tuple-element.50), channel_id=1, source_target_pairs={{0,7},{1,0},{2,1},{3,2},{4,3},{5,4},{6,5},{7,6},{8,15},{9,8},{10,9... | collective-permute-start | bytes 860168 | tf_op jit(solution)/shard_map/ppermute | solution.py:337
  141.2 83.9 %collective-permute-start.14 = (bf16[96,32,128]{2,1,0:T(8,128)(2,1)}, bf16[96,32,128]{2,1,0:T(8,128)(2,1)S(1)}, u32[]{:S(2)}, u32[]{:S(2)}) collective-permute-start(bf16[96,32,128]{2,1,0:T(8,128)(2,1)} %copy-done.33), channel_id=1, source_target_pairs={{0,1},{1,2},{2,3},{3,4},{4,5},{5,6},{6,7},{7,0},{8,9},{9,10},{10,1... | collective-permute-start | bytes 2359304 | tf_op jit(solution)/shard_map/ppermute | solution.py:337
  142.3 86.7 %collective-permute-start.15 = (bf16[96,32,128]{2,1,0:T(8,128)(2,1)}, bf16[96,32,128]{2,1,0:T(8,128)(2,1)}, u32[]{:S(2)}, u32[]{:S(2)}) collective-permute-start(bf16[96,32,128]{2,1,0:T(8,128)(2,1)} %copy-done.32), channel_id=1, source_target_pairs={{0,2},{1,3},{2,4},{3,5},{4,6},{5,7},{6,0},{7,1},{8,10},{9,11},{10,... | collective-permute-start | bytes 2359304 | tf_op jit(solution)/shard_map/ppermute | solution.py:337
  152.6 92.3 %collective-permute-start.16 = (bf16[96,32,128]{2,1,0:T(8,128)(2,1)}, bf16[96,32,128]{2,1,0:T(8,128)(2,1)}, u32[]{:S(2)}, u32[]{:S(2)}) collective-permute-start(bf16[96,32,128]{2,1,0:T(8,128)(2,1)} %copy-done.31), channel_id=1, source_target_pairs={{0,3},{1,4},{2,5},{3,6},{4,7},{5,0},{6,1},{7,2},{8,11},{9,12},{10,... | collective-permute-start | bytes 2359304 | tf_op jit(solution)/shard_map/ppermute | solution.py:337
  158.5 86.7 %collective-permute-start.17 = (bf16[96,32,128]{2,1,0:T(8,128)(2,1)}, bf16[96,32,128]{2,1,0:T(8,128)(2,1)}, u32[]{:S(2)}, u32[]{:S(2)}) collective-permute-start(bf16[96,32,128]{2,1,0:T(8,128)(2,1)} %copy-done.30), channel_id=1, source_target_pairs={{0,4},{1,5},{2,6},{3,7},{4,0},{5,1},{6,2},{7,3},{8,12},{9,13},{10,... | collective-permute-start | bytes 2359304 | tf_op jit(solution)/shard_map/ppermute | solution.py:337
  187.9 57.2 %collective-permute-start.18 = (bf16[96,32,128]{2,1,0:T(8,128)(2,1)}, bf16[96,32,128]{2,1,0:T(8,128)(2,1)}, u32[]{:S(2)}, u32[]{:S(2)}) collective-permute-start(bf16[96,32,128]{2,1,0:T(8,128)(2,1)} %copy-done.29), channel_id=1, source_target_pairs={{0,5},{1,6},{2,7},{3,0},{4,1},{5,2},{6,3},{7,4},{8,13},{9,14},{10,... | collective-permute-start | bytes 2359304 | tf_op jit(solution)/shard_map/ppermute | solution.py:337
  225.2 50.3 %collective-permute-start.19 = (bf16[96,32,128]{2,1,0:T(8,128)(2,1)}, bf16[96,32,128]{2,1,0:T(8,128)(2,1)S(1)}, u32[]{:S(2)}, u32[]{:S(2)}) collective-permute-start(bf16[96,32,128]{2,1,0:T(8,128)(2,1)} %get-tuple-element.65), channel_id=1, source_target_pairs={{0,6},{1,7},{2,0},{3,1},{4,2},{5,3},{6,4},{7,5},{8,14},{9,15},{10,... | collective-permute-start | bytes 2359304 | tf_op jit(solution)/shard_map/ppermute | solution.py:337
  229.0 46.5 %collective-permute-start.20 = (bf16[96,32,128]{2,1,0:T(8,128)(2,1)}, bf16[96,32,128]{2,1,0:T(8,128)(2,1)S(1)}, u32[]{:S(2)}, u32[]{:S(2)}) collective-permute-start(bf16[96,32,128]{2,1,0:T(8,128)(2,1)} %get-tuple-element.66), channel_id=1, source_target_pairs={{0,7},{1,0},{2,1},{3,2},{4,3},{5,4},{6,5},{7,6},{8,15},{9,8},{10,9... | collective-permute-start | bytes 2359304 | tf_op jit(solution)/shard_map/ppermute | solution.py:337
  276.7 167.2 %all-to-all-start.1 = ((bf16[8,32,32,128]{3,2,1,0:T(8,128)(2,1)}), bf16[8,32,32,128]{3,2,1,0:T(8,128)(2,1)S(1)}, u32[]{:S(2)}, u32[]{:S(2)}) async-start(bf16[8,32,32,128]{3,2,1,0:T(8,128)(2,1)} %shard_map.140.rest_21_), calls=%async_computation.1 | async-start | bytes 4194304 | tf_op jit(solution)/shard_map/all_to_all | solution.py:333
  330.6 15.6 %collective-permute-start.26 = (bf16[48,32,128]{2,1,0:T(8,128)(2,1)}, bf16[48,32,128]{2,1,0:T(8,128)(2,1)S(1)}, u32[]{:S(2)}, u32[]{:S(2)}) collective-permute-start(bf16[48,32,128]{2,1,0:T(8,128)(2,1)} %copy-done.40), channel_id=1, source_target_pairs={{0,2},{1,3},{2,4},{3,5},{4,6},{5,7},{6,0},{7,1},{8,10},{9,11},{10,... | collective-permute-start | bytes 1179656 | tf_op jit(solution)/shard_map/ppermute | solution.py:337
  332.6 21.1 %collective-permute-start.27 = (bf16[48,32,128]{2,1,0:T(8,128)(2,1)}, bf16[48,32,128]{2,1,0:T(8,128)(2,1)}, u32[]{:S(2)}, u32[]{:S(2)}) collective-permute-start(bf16[48,32,128]{2,1,0:T(8,128)(2,1)} %copy-done.39), channel_id=1, source_target_pairs={{0,1},{1,2},{2,3},{3,4},{4,5},{5,6},{6,7},{7,0},{8,9},{9,10},{10,1... | collective-permute-start | bytes 1179656 | tf_op jit(solution)/shard_map/ppermute | solution.py:337
  339.9 36.4 %collective-permute-start.21 = (bf16[48,32,128]{2,1,0:T(8,128)(2,1)}, bf16[48,32,128]{2,1,0:T(8,128)(2,1)S(1)}, u32[]{:S(2)}, u32[]{:S(2)}) collective-permute-start(bf16[48,32,128]{2,1,0:T(8,128)(2,1)} %copy-done.38), channel_id=1, source_target_pairs={{0,7},{1,0},{2,1},{3,2},{4,3},{5,4},{6,5},{7,6},{8,15},{9,8},{10,9... | collective-permute-start | bytes 1179656 | tf_op jit(solution)/shard_map/ppermute | solution.py:337
  342.1 59.1 %collective-permute-start.22 = (bf16[48,32,128]{2,1,0:T(8,128)(2,1)}, bf16[48,32,128]{2,1,0:T(8,128)(2,1)S(1)}, u32[]{:S(2)}, u32[]{:S(2)}) collective-permute-start(bf16[48,32,128]{2,1,0:T(8,128)(2,1)} %copy-done.37), channel_id=1, source_target_pairs={{0,6},{1,7},{2,0},{3,1},{4,2},{5,3},{6,4},{7,5},{8,14},{9,15},{10,... | collective-permute-start | bytes 1179656 | tf_op jit(solution)/shard_map/ppermute | solution.py:337
  353.7 19.7 %collective-permute-start.30 = (f32[232,128]{1,0:T(8,128)}, f32[232,128]{1,0:T(8,128)S(1)}, u32[]{:S(2)}, u32[]{:S(2)}) collective-permute-start(f32[232,128]{1,0:T(8,128)} %shard_map.146), channel_id=1, source_target_pairs={{0,1},{1,0},{2,3},{3,2},{4,5},{5,4},{6,7},{7,6},{8,9},{9,8},{10,11... | collective-permute-start | bytes 356360 | tf_op jit(solution)/shard_map/ppermute | solution.py:292
  353.7 65.8 %collective-permute-start.23 = (bf16[48,32,128]{2,1,0:T(8,128)(2,1)}, bf16[48,32,128]{2,1,0:T(8,128)(2,1)S(1)}, u32[]{:S(2)}, u32[]{:S(2)}) collective-permute-start(bf16[48,32,128]{2,1,0:T(8,128)(2,1)} %copy-done.36), channel_id=1, source_target_pairs={{0,5},{1,6},{2,7},{3,0},{4,1},{5,2},{6,3},{7,4},{8,13},{9,14},{10,... | collective-permute-start | bytes 1179656 | tf_op jit(solution)/shard_map/ppermute | solution.py:337
  373.3 46.2 %collective-permute-start.24 = (bf16[48,32,128]{2,1,0:T(8,128)(2,1)}, bf16[48,32,128]{2,1,0:T(8,128)(2,1)}, u32[]{:S(2)}, u32[]{:S(2)}) collective-permute-start(bf16[48,32,128]{2,1,0:T(8,128)(2,1)} %copy-done.35), channel_id=1, source_target_pairs={{0,4},{1,5},{2,6},{3,7},{4,0},{5,1},{6,2},{7,3},{8,12},{9,13},{10,... | collective-permute-start | bytes 1179656 | tf_op jit(solution)/shard_map/ppermute | solution.py:337
  373.3 47.5 %collective-permute-start.25 = (bf16[48,32,128]{2,1,0:T(8,128)(2,1)}, bf16[48,32,128]{2,1,0:T(8,128)(2,1)}, u32[]{:S(2)}, u32[]{:S(2)}) collective-permute-start(bf16[48,32,128]{2,1,0:T(8,128)(2,1)} %copy-done.34), channel_id=1, source_target_pairs={{0,3},{1,4},{2,5},{3,6},{4,7},{5,0},{6,1},{7,2},{8,11},{9,12},{10,... | collective-permute-start | bytes 1179656 | tf_op jit(solution)/shard_map/ppermute | solution.py:337
  377.0 22.6 %collective-permute-start.31 = (f32[232,128]{1,0:T(8,128)}, f32[232,128]{1,0:T(8,128)S(1)}, u32[]{:S(2)}, u32[]{:S(2)}) collective-permute-start(f32[232,128]{1,0:T(8,128)} %shard_map.147), channel_id=1, source_target_pairs={{0,2},{1,3},{2,0},{3,1},{4,6},{5,7},{6,4},{7,5},{8,10},{9,11},{10,... | collective-permute-start | bytes 356360 | tf_op jit(solution)/shard_map/ppermute | solution.py:292
  401.9 16.0 %collective-permute-start.32 = (f32[232,128]{1,0:T(8,128)}, f32[232,128]{1,0:T(8,128)S(1)}, u32[]{:S(2)}, u32[]{:S(2)}) collective-permute-start(f32[232,128]{1,0:T(8,128)} %shard_map.148), channel_id=1, source_target_pairs={{0,4},{1,5},{2,6},{3,7},{4,0},{5,1},{6,2},{7,3},{8,12},{9,13},{10,... | collective-permute-start | bytes 356360 | tf_op jit(solution)/shard_map/ppermute | solution.py:292
  422.3 10.1 %collective-permute-start.8 = (bf16[16,32,128]{2,1,0:T(8,128)(2,1)}, bf16[16,32,128]{2,1,0:T(8,128)(2,1)S(1)}, u32[]{:S(2)}, u32[]{:S(2)}) collective-permute-start(bf16[16,32,128]{2,1,0:T(8,128)(2,1)} %copy-done.46), channel_id=1, source_target_pairs={{0,6},{1,7},{2,0},{3,1},{4,2},{5,3},{6,4},{7,5},{8,14},{9,15},{10,... | collective-permute-start | bytes 393224 | tf_op jit(solution)/shard_map/ppermute | solution.py:337
  434.6 18.3 %collective-permute-start.9 = (bf16[16,32,128]{2,1,0:T(8,128)(2,1)}, bf16[16,32,128]{2,1,0:T(8,128)(2,1)S(1)}, u32[]{:S(2)}, u32[]{:S(2)}) collective-permute-start(bf16[16,32,128]{2,1,0:T(8,128)(2,1)} %copy-done.45), channel_id=1, source_target_pairs={{0,5},{1,6},{2,7},{3,0},{4,1},{5,2},{6,3},{7,4},{8,13},{9,14},{10,... | collective-permute-start | bytes 393224 | tf_op jit(solution)/shard_map/ppermute | solution.py:337
  434.6 19.9 %collective-permute-start.10 = (bf16[16,32,128]{2,1,0:T(8,128)(2,1)}, bf16[16,32,128]{2,1,0:T(8,128)(2,1)S(1)}, u32[]{:S(2)}, u32[]{:S(2)}) collective-permute-start(bf16[16,32,128]{2,1,0:T(8,128)(2,1)} %copy-done.44), channel_id=1, source_target_pairs={{0,4},{1,5},{2,6},{3,7},{4,0},{5,1},{6,2},{7,3},{8,12},{9,13},{10,... | collective-permute-start | bytes 393224 | tf_op jit(solution)/shard_map/ppermute | solution.py:337
  435.9 19.4 %collective-permute-start.11 = (bf16[16,32,128]{2,1,0:T(8,128)(2,1)}, bf16[16,32,128]{2,1,0:T(8,128)(2,1)}, u32[]{:S(2)}, u32[]{:S(2)}) collective-permute-start(bf16[16,32,128]{2,1,0:T(8,128)(2,1)} %copy-done.43), channel_id=1, source_target_pairs={{0,3},{1,4},{2,5},{3,6},{4,7},{5,0},{6,1},{7,2},{8,11},{9,12},{10,... | collective-permute-start | bytes 393224 | tf_op jit(solution)/shard_map/ppermute | solution.py:337
  436.3 19.0 %collective-permute-start.12 = (bf16[16,32,128]{2,1,0:T(8,128)(2,1)}, bf16[16,32,128]{2,1,0:T(8,128)(2,1)}, u32[]{:S(2)}, u32[]{:S(2)}) collective-permute-start(bf16[16,32,128]{2,1,0:T(8,128)(2,1)} %copy-done.42), channel_id=1, source_target_pairs={{0,2},{1,3},{2,4},{3,5},{4,6},{5,7},{6,0},{7,1},{8,10},{9,11},{10,... | collective-permute-start | bytes 393224 | tf_op jit(solution)/shard_map/ppermute | solution.py:337
  440.1 15.2 %collective-permute-start.13 = (bf16[16,32,128]{2,1,0:T(8,128)(2,1)}, bf16[16,32,128]{2,1,0:T(8,128)(2,1)}, u32[]{:S(2)}, u32[]{:S(2)}) collective-permute-start(bf16[16,32,128]{2,1,0:T(8,128)(2,1)} %copy-done.41), channel_id=1, source_target_pairs={{0,1},{1,2},{2,3},{3,4},{4,5},{5,6},{6,7},{7,0},{8,9},{9,10},{10,1... | collective-permute-start | bytes 393224 | tf_op jit(solution)/shard_map/ppermute | solution.py:337
  (58 other events, 797.2 us)

commit v15 on v14

--- a/solution.py
+++ b/solution.py
@@ -369,7 +369,7 @@
         leaving.append(returned)
 
     back, first = leaving[-1][2], leaving[-1][0]
-    sums = sum_over_mesh(add(terms, []), [None, back[-2:], back[1:2], back[2:3], back[3:-2], first[1:3]])
+    sums = sum_over_mesh(add(terms, []), [None, back[-2:], back[1:2], back[2:3], back[3:-2] + first[3:6]])
     grads = []
     for returned in leaving:
         held = None

time: 461 us -> 471 us (1.022)
  starting transfers between devices: 156 us -> 168 us
    ppermute x28, starting transfers between devices: 118 us -> 133 us  [exchange(): moved.append(lax.ppermute(parts[shift], 'ctx', pairs))]
    unnamed x115 -> x131, local copies, waits for them, and re-layouts: 28 us -> 30.1 us
  transfers between devices with their start and end apart: 37 -> 37, of which waited for: 16 -> 15; matrix products, arithmetic and copies ran while one was open for 3% -> 3% of each run, Pallas kernels for 15% -> 14%
where the time goes in v15:
time: 471 us; the launch traced here: 468 us
  waiting for transfers between devices  177 us (38%)
  starting transfers between devices  168 us (36%)
  Pallas kernels  77.8 us (17%)
  local copies, waits for them, and re-layouts  30.8 us (7%)
  other arithmetic  13.9 us (3%)
    ppermute x28, waiting for transfers between devices, exchange(): moved.append(lax.ppermute(parts[shift], 'ctx', pairs))  140 us
    ppermute x28, starting transfers between devices, exchange(): moved.append(lax.ppermute(parts[shift], 'ctx', pairs))  133 us
    pallas_call x3, Pallas kernels, mix(): pl.pallas_call(functools.partial(mix_kernel, parts=len(parts), tile=tile,...  39.3 us
    ppermute x7, waiting for transfers between devices, exchange_with(): lax.ppermute(array, axis, [(i, i ^ bit) for i in range(size)])  37.1 us
    unnamed x131, local copies, waits for them, and re-layouts  30.1 us
    all_to_all x2, starting transfers between devices, exchange(): lax.all_to_all(parts[0], 'ctx', split_axis=0, concat_axis=0, tiled=True)  28.1 us
    pallas_call x3, Pallas kernels, split_channels(): pl.pallas_call(functools.partial(kernel, rotated=rotated), grid=(tiles, r...  24.8 us
    pallas_call x3, Pallas kernels, merge_channels(): pl.pallas_call(functools.partial(merge_kernel, parts=len(parts), rotated=...  11.5 us
  transfers between devices with their start and end apart: 37, of which 15 were waited for; matrix products, arithmetic and copies ran while one was open for 3% of the time, Pallas kernels for 14%

profile of v15, /device:TPU:0, one launch (start us, length us, event | category | flops | bytes accessed | tf_op | source)
XLA Modules:
  0.0 468.0 jit_solution(2977172882496494651)
XLA Ops:
  0.6 7.8 %shard_map.138 = bf16[8,64,32,128]{3,2,1,0:T(8,128)(2,1)S(1)} custom-call(s32[1]{0:T(128)} %bitcast.place_ref, bf16[32,128,768]{2,1,0:T(8,128)(2,1)} %bitcast.51, bf16[32,128,768]{2,1,0:T(8,128)(2,1)} %bitcast.54), custom_call_target="tpu_custom_call" | custom-call | flops 1 | bytes 16777216 | tf_op jit(solution)/shard_map/pallas_call | solution.py:83
  10.5 6.5 %all-to-all-start = ((bf16[8,64,32,128]{3,2,1,0:T(8,128)(2,1)}), bf16[8,64,32,128]{3,2,1,0:T(8,128)(2,1)}, u32[]{:S(2)}, u32[]{:S(2)}) async-start(bf16[8,64,32,128]{3,2,1,0:T(8,128)(2,1)} %copy-done), calls=%async_computation | async-start | bytes 8388608 | tf_op jit(solution)/shard_map/all_to_all | solution.py:333
  17.0 5.3 %shard_map.135 = (bf16[35,32,128]{2,1,0:T(8,128)(2,1)S(1)}, bf16[35,32,128]{2,1,0:T(8,128)(2,1)S(1)}, bf16[35,32,128]{2,1,0:T(8,128)(2,1)S(1)}, bf16[35,32,128]{...) custom-call(s32[1]{0:T(128)} %bitcast.place_ref, ...), custom_call_target="tpu_custom_call" | custom-call | flops 1 | bytes 8388608 | tf_op jit(solution)/shard_map/pallas_call | solution.py:83
  24.4 2.2 collective-permute-start.2
  29.2 11.7 %shard_map.137 = (bf16[96,32,128]{2,1,0:T(8,128)(2,1)S(1)}, bf16[96,32,128]{2,1,0:T(8,128)(2,1)S(1)}, bf16[96,32,128]{2,1,0:T(8,128)(2,1)S(1)}, bf16[96,32,128]{...) custom-call(s32[1]{0:T(128)} %bitcast.place_ref, ...), custom_call_target="tpu_custom_call" | custom-call | flops 1 | bytes 25165824 | tf_op jit(solution)/shard_map/pallas_call | solution.py:83
  46.6 48.6 %collective-permute-done.rest_1_.rest_9_ = bf16[35,32,128]{2,1,0:T(8,128)(2,1)S(1)} collective-permute-done((bf16[35,32,128]{2,1,0:T(8,128)(2,1)S(1)}, bf16[35,32,128]{2,1,0:T(8,128)(2,1)S(1)}, u32[]{:S(2)}, u32[]{:S(2)}) %collective-permute-start) | collective-permute-done | bytes 286752 | tf_op jit(solution)/shard_map/ppermute | solution.py:337
  96.1 4.4 collective-permute-start.6
  100.6 40.7 %collective-permute-done.2.rest_3_.rest_11_ = bf16[35,32,128]{2,1,0:T(8,128)(2,1)S(1)} collective-permute-done((bf16[35,32,128]{2,1,0:T(8,128)(2,1)S(1)}, bf16[35,32,128]{2,1,0:T(8,128)(2,1)S(1)}, u32[]{:S(2)}, u32[]{:S(2)}) %collective-permute-start.2) | collective-permute-done | bytes 286752 | tf_op jit(solution)/shard_map/ppermute | solution.py:337
  142.3 10.3 %collective-permute-start.15 = (bf16[96,32,128]{2,1,0:T(8,128)(2,1)}, bf16[96,32,128]{2,1,0:T(8,128)(2,1)}, u32[]{:S(2)}, u32[]{:S(2)}) collective-permute-start(bf16[96,32,128]{2,1,0:T(8,128)(2,1)} %copy-done.36), channel_id=1, source_target_pairs={{0,2},{1,3},{2,4},{3,5},{4,6},{5,7},{6,0},{7,1},{8,10},{9,11},{10,... | collective-permute-start | bytes 2359304 | tf_op jit(solution)/shard_map/ppermute | solution.py:337
  152.6 5.9 %collective-permute-start.16 = (bf16[96,32,128]{2,1,0:T(8,128)(2,1)}, bf16[96,32,128]{2,1,0:T(8,128)(2,1)}, u32[]{:S(2)}, u32[]{:S(2)}) collective-permute-start(bf16[96,32,128]{2,1,0:T(8,128)(2,1)} %copy-done.35), channel_id=1, source_target_pairs={{0,3},{1,4},{2,5},{3,6},{4,7},{5,0},{6,1},{7,2},{8,11},{9,12},{10,... | collective-permute-start | bytes 2359304 | tf_op jit(solution)/shard_map/ppermute | solution.py:337
  158.5 29.4 %collective-permute-start.17 = (bf16[96,32,128]{2,1,0:T(8,128)(2,1)}, bf16[96,32,128]{2,1,0:T(8,128)(2,1)}, u32[]{:S(2)}, u32[]{:S(2)}) collective-permute-start(bf16[96,32,128]{2,1,0:T(8,128)(2,1)} %copy-done.34), channel_id=1, source_target_pairs={{0,4},{1,5},{2,6},{3,7},{4,0},{5,1},{6,2},{7,3},{8,12},{9,13},{10,... | collective-permute-start | bytes 2359304 | tf_op jit(solution)/shard_map/ppermute | solution.py:337
  187.9 21.8 %collective-permute-start.18 = (bf16[96,32,128]{2,1,0:T(8,128)(2,1)}, bf16[96,32,128]{2,1,0:T(8,128)(2,1)}, u32[]{:S(2)}, u32[]{:S(2)}) collective-permute-start(bf16[96,32,128]{2,1,0:T(8,128)(2,1)} %copy-done.33), channel_id=1, source_target_pairs={{0,5},{1,6},{2,7},{3,0},{4,1},{5,2},{6,3},{7,4},{8,13},{9,14},{10,... | collective-permute-start | bytes 2359304 | tf_op jit(solution)/shard_map/ppermute | solution.py:337
  213.1 6.1 %shard_map.136 = (bf16[16,32,128]{2,1,0:T(8,128)(2,1)S(1)}, bf16[16,32,128]{2,1,0:T(8,128)(2,1)S(1)}, bf16[16,32,128]{2,1,0:T(8,128)(2,1)S(1)}, bf16[16,32,128]{...) custom-call(s32[1]{0:T(128)} %bitcast.place_ref, ...), custom_call_target="tpu_custom_call" | custom-call | flops 8388608000 | bytes 1024 | tf_op jit(solution)/shard_map/pallas_call | solution.py:222
  225.2 3.8 collective-permute-start.19
  229.0 13.8 %shard_map.139 = (bf16[8,32,32,128]{3,2,1,0:T(8,128)(2,1)S(1)}, f32[928,128]{1,0:T(8,128)S(1)}) custom-call(s32[1]{0:T(128)} %bitcast.place_ref, f32[768]{0:T(1024)S(1)} %copy-done.53, f32[768]{0:T(1024)S(1)} %copy-done.54, f32[768]{0:T(1024)S(1)} %copy-done.55, bf16[8,64,32,128]{3,2,1,0:T(8,128)(2,1)} %all-to-all-done.rest_0_.rest_1_, ...), custom_call_target="tpu_custom_call" | custom-call | flops 16777216000 | bytes 1024 | tf_op jit(solution)/shard_map/pallas_call | solution.py:222
  245.1 30.4 %collective-permute-done.19.refs_6_.rest_6_.rest_14_ = bf16[96,32,128]{2,1,0:T(8,128)(2,1)S(1)} collective-permute-done((bf16[96,32,128]{2,1,0:T(8,128)(2,1)}, bf16[96,32,128]{2,1,0:T(8,128)(2,1)S(1)}, u32[]{:S(2)}, u32[]{:S(2)}) %collective-permute-start.19) | collective-permute-done | bytes 786464 | tf_op jit(solution)/shard_map/ppermute | solution.py:337
  276.7 21.6 %all-to-all-start.1 = ((bf16[8,32,32,128]{3,2,1,0:T(8,128)(2,1)}), bf16[8,32,32,128]{3,2,1,0:T(8,128)(2,1)S(1)}, u32[]{:S(2)}, u32[]{:S(2)}) async-start(bf16[8,32,32,128]{3,2,1,0:T(8,128)(2,1)} %shard_map.140.rest_21_), calls=%async_computation.1 | async-start | bytes 4194304 | tf_op jit(solution)/shard_map/all_to_all | solution.py:333
  299.5 19.4 %shard_map.141 = (bf16[48,32,128]{2,1,0:T(8,128)(2,1)S(1)}, bf16[48,32,128]{2,1,0:T(8,128)(2,1)S(1)}, bf16[48,32,128]{2,1,0:T(8,128)(2,1)S(1)}, bf16[48,32,128]{...) custom-call(s32[1]{0:T(128)} %bitcast.place_ref, ...), custom_call_target="tpu_custom_call" | custom-call | flops 25165824000 | bytes 1024 | tf_op jit(solution)/shard_map/pallas_call | solution.py:222
  332.6 4.6 collective-permute-done.28
  346.2 7.4 %collective-permute-done.27.rest_7_.refs_2_ = bf16[48,32,128]{2,1,0:T(8,128)(2,1)S(1)} collective-permute-done((bf16[48,32,128]{2,1,0:T(8,128)(2,1)}, bf16[48,32,128]{2,1,0:T(8,128)(2,1)S(1)}, u32[]{:S(2)}, u32[]{:S(2)}) %collective-permute-start.27) | collective-permute-done | bytes 393248 | tf_op jit(solution)/shard_map/ppermute | solution.py:337
  354.3 19.6 %collective-permute-start.23 = (bf16[48,32,128]{2,1,0:T(8,128)(2,1)}, bf16[48,32,128]{2,1,0:T(8,128)(2,1)S(1)}, u32[]{:S(2)}, u32[]{:S(2)}) collective-permute-start(bf16[48,32,128]{2,1,0:T(8,128)(2,1)} %copy-done.40), channel_id=1, source_target_pairs={{0,5},{1,6},{2,7},{3,0},{4,1},{5,2},{6,3},{7,4},{8,13},{9,14},{10,... | collective-permute-start | bytes 1179656 | tf_op jit(solution)/shard_map/ppermute | solution.py:337
  377.3 23.0 %collective-permute-done.31 = f32[232,128]{1,0:T(8,128)S(1)} collective-permute-done((f32[232,128]{1,0:T(8,128)}, f32[232,128]{1,0:T(8,128)S(1)}, u32[]{:S(2)}, u32[]{:S(2)}) %collective-permute-start.31) | collective-permute-done | bytes 118816 | tf_op jit(solution)/shard_map/ppermute | solution.py:292
  400.3 3.4 collective-permute-start.9
  406.2 13.6 %collective-permute-start.10 = (bf16[16,32,128]{2,1,0:T(8,128)(2,1)}, bf16[16,32,128]{2,1,0:T(8,128)(2,1)S(1)}, u32[]{:S(2)}, u32[]{:S(2)}) collective-permute-start(bf16[16,32,128]{2,1,0:T(8,128)(2,1)} %copy-done.50), channel_id=1, source_target_pairs={{0,4},{1,5},{2,6},{3,7},{4,0},{5,1},{6,2},{7,3},{8,12},{9,13},{10,... | collective-permute-start | bytes 393224 | tf_op jit(solution)/shard_map/ppermute | solution.py:337
  419.8 3.0 collective-permute-done.32
  422.8 4.8 %collective-permute-start.11 = (bf16[16,32,128]{2,1,0:T(8,128)(2,1)}, bf16[16,32,128]{2,1,0:T(8,128)(2,1)S(1)}, u32[]{:S(2)}, u32[]{:S(2)}) collective-permute-start(bf16[16,32,128]{2,1,0:T(8,128)(2,1)} %copy-done.49), channel_id=1, source_target_pairs={{0,3},{1,4},{2,5},{3,6},{4,7},{5,0},{6,1},{7,2},{8,11},{9,12},{10,... | collective-permute-start | bytes 393224 | tf_op jit(solution)/shard_map/ppermute | solution.py:337
  429.2 7.5 %collective-permute-done.11.rest_5_.refs_6_ = bf16[16,32,128]{2,1,0:T(8,128)(2,1)S(1)} collective-permute-done((bf16[16,32,128]{2,1,0:T(8,128)(2,1)}, bf16[16,32,128]{2,1,0:T(8,128)(2,1)S(1)}, u32[]{:S(2)}, u32[]{:S(2)}) %collective-permute-start.11) | collective-permute-done | bytes 131104 | tf_op jit(solution)/shard_map/ppermute | solution.py:337
  440.4 3.6 collective-permute-done.33
  449.7 2.9 collective-permute-done.34
  456.4 3.0 shard_map.142.rest_8_
  459.4 5.9 %shard_map.143.rest_8_ = bf16[32,128,768]{2,1,0:T(8,128)(2,1)} custom-call(s32[1]{0:T(128)} %bitcast.place_ref, bf16[48,32,128]{2,1,0:T(8,128)(2,1)S(1)} %copy-done.24, bf16[48,32,128]{2,1,0:T(8,128)(2,1)} %collective-permute-done.21.rest_1_.refs_1_, bf16[48,32,128]{2,1,0:T(8,128)(2,1)} %collective-permute-done.22.rest_2_.refs_1_, ...), custom_call_target="tpu_custom_call", output_to_operand_aliasing={{}: (9, {})} | custom-call | flops 1 | bytes 12582912 | tf_op jit(solution)/shard_map/pallas_call | solution.py:117
  465.4 2.6 shard_map.144
  (209 shorter events, 72.3 us)
Async XLA Ops:
  10.5 218.6 %all-to-all-start = ((bf16[8,64,32,128]{3,2,1,0:T(8,128)(2,1)}), bf16[8,64,32,128]{3,2,1,0:T(8,128)(2,1)}, u32[]{:S(2)}, u32[]{:S(2)}) async-start(bf16[8,64,32,128]{3,2,1,0:T(8,128)(2,1)} %copy-done), calls=%async_computation | async-start | bytes 8388608 | tf_op jit(solution)/shard_map/all_to_all | solution.py:333
  22.2 72.9 %collective-permute-start = (bf16[35,32,128]{2,1,0:T(8,128)(2,1)S(1)}, bf16[35,32,128]{2,1,0:T(8,128)(2,1)S(1)}, u32[]{:S(2)}, u32[]{:S(2)}) collective-permute-start(bf16[35,32,128]{2,1,0:T(8,128)(2,1)S(1)} %get-tuple-element.44), channel_id=1, source_target_pairs={{0,1},{1,2},{2,3},{3,4},{4,5},{5,6},{6,7},{7,0},{8,9},{9,10},{10,1... | collective-permute-start | bytes 860168 | tf_op jit(solution)/shard_map/ppermute | solution.py:337
  22.7 73.4 %collective-permute-start.1 = (bf16[35,32,128]{2,1,0:T(8,128)(2,1)S(1)}, bf16[35,32,128]{2,1,0:T(8,128)(2,1)S(1)}, u32[]{:S(2)}, u32[]{:S(2)}) collective-permute-start(bf16[35,32,128]{2,1,0:T(8,128)(2,1)S(1)} %get-tuple-element.45), channel_id=1, source_target_pairs={{0,2},{1,3},{2,4},{3,5},{4,6},{5,7},{6,0},{7,1},{8,10},{9,11},{10,... | collective-permute-start | bytes 860168 | tf_op jit(solution)/shard_map/ppermute | solution.py:337
  24.4 116.9 %collective-permute-start.2 = (bf16[35,32,128]{2,1,0:T(8,128)(2,1)S(1)}, bf16[35,32,128]{2,1,0:T(8,128)(2,1)S(1)}, u32[]{:S(2)}, u32[]{:S(2)}) collective-permute-start(bf16[35,32,128]{2,1,0:T(8,128)(2,1)S(1)} %get-tuple-element.46), channel_id=1, source_target_pairs={{0,3},{1,4},{2,5},{3,6},{4,7},{5,0},{6,1},{7,2},{8,11},{9,12},{10,... | collective-permute-start | bytes 860168 | tf_op jit(solution)/shard_map/ppermute | solution.py:337
  26.6 115.7 %collective-permute-start.3 = (bf16[35,32,128]{2,1,0:T(8,128)(2,1)}, bf16[35,32,128]{2,1,0:T(8,128)(2,1)S(1)}, u32[]{:S(2)}, u32[]{:S(2)}) collective-permute-start(bf16[35,32,128]{2,1,0:T(8,128)(2,1)} %get-tuple-element.47), channel_id=1, source_target_pairs={{0,4},{1,5},{2,6},{3,7},{4,0},{5,1},{6,2},{7,3},{8,12},{9,13},{10,... | collective-permute-start | bytes 860168 | tf_op jit(solution)/shard_map/ppermute | solution.py:337
  28.1 124.5 %collective-permute-start.4 = (bf16[35,32,128]{2,1,0:T(8,128)(2,1)}, bf16[35,32,128]{2,1,0:T(8,128)(2,1)S(1)}, u32[]{:S(2)}, u32[]{:S(2)}) collective-permute-start(bf16[35,32,128]{2,1,0:T(8,128)(2,1)} %get-tuple-element.48), channel_id=1, source_target_pairs={{0,5},{1,6},{2,7},{3,0},{4,1},{5,2},{6,3},{7,4},{8,13},{9,14},{10,... | collective-permute-start | bytes 860168 | tf_op jit(solution)/shard_map/ppermute | solution.py:337
  95.2 63.3 %collective-permute-start.5 = (bf16[35,32,128]{2,1,0:T(8,128)(2,1)}, bf16[35,32,128]{2,1,0:T(8,128)(2,1)S(1)}, u32[]{:S(2)}, u32[]{:S(2)}) collective-permute-start(bf16[35,32,128]{2,1,0:T(8,128)(2,1)} %get-tuple-element.49), channel_id=1, source_target_pairs={{0,6},{1,7},{2,0},{3,1},{4,2},{5,3},{6,4},{7,5},{8,14},{9,15},{10,... | collective-permute-start | bytes 860168 | tf_op jit(solution)/shard_map/ppermute | solution.py:337
  96.1 91.8 %collective-permute-start.6 = (bf16[35,32,128]{2,1,0:T(8,128)(2,1)}, bf16[35,32,128]{2,1,0:T(8,128)(2,1)S(1)}, u32[]{:S(2)}, u32[]{:S(2)}) collective-permute-start(bf16[35,32,128]{2,1,0:T(8,128)(2,1)} %get-tuple-element.50), channel_id=1, source_target_pairs={{0,7},{1,0},{2,1},{3,2},{4,3},{5,4},{6,5},{7,6},{8,15},{9,8},{10,9... | collective-permute-start | bytes 860168 | tf_op jit(solution)/shard_map/ppermute | solution.py:337
  141.2 83.9 %collective-permute-start.14 = (bf16[96,32,128]{2,1,0:T(8,128)(2,1)}, bf16[96,32,128]{2,1,0:T(8,128)(2,1)S(1)}, u32[]{:S(2)}, u32[]{:S(2)}) collective-permute-start(bf16[96,32,128]{2,1,0:T(8,128)(2,1)} %copy-done.37), channel_id=1, source_target_pairs={{0,1},{1,2},{2,3},{3,4},{4,5},{5,6},{6,7},{7,0},{8,9},{9,10},{10,1... | collective-permute-start | bytes 2359304 | tf_op jit(solution)/shard_map/ppermute | solution.py:337
  142.3 86.7 %collective-permute-start.15 = (bf16[96,32,128]{2,1,0:T(8,128)(2,1)}, bf16[96,32,128]{2,1,0:T(8,128)(2,1)}, u32[]{:S(2)}, u32[]{:S(2)}) collective-permute-start(bf16[96,32,128]{2,1,0:T(8,128)(2,1)} %copy-done.36), channel_id=1, source_target_pairs={{0,2},{1,3},{2,4},{3,5},{4,6},{5,7},{6,0},{7,1},{8,10},{9,11},{10,... | collective-permute-start | bytes 2359304 | tf_op jit(solution)/shard_map/ppermute | solution.py:337
  152.6 92.4 %collective-permute-start.16 = (bf16[96,32,128]{2,1,0:T(8,128)(2,1)}, bf16[96,32,128]{2,1,0:T(8,128)(2,1)}, u32[]{:S(2)}, u32[]{:S(2)}) collective-permute-start(bf16[96,32,128]{2,1,0:T(8,128)(2,1)} %copy-done.35), channel_id=1, source_target_pairs={{0,3},{1,4},{2,5},{3,6},{4,7},{5,0},{6,1},{7,2},{8,11},{9,12},{10,... | collective-permute-start | bytes 2359304 | tf_op jit(solution)/shard_map/ppermute | solution.py:337
  158.5 86.7 %collective-permute-start.17 = (bf16[96,32,128]{2,1,0:T(8,128)(2,1)}, bf16[96,32,128]{2,1,0:T(8,128)(2,1)}, u32[]{:S(2)}, u32[]{:S(2)}) collective-permute-start(bf16[96,32,128]{2,1,0:T(8,128)(2,1)} %copy-done.34), channel_id=1, source_target_pairs={{0,4},{1,5},{2,6},{3,7},{4,0},{5,1},{6,2},{7,3},{8,12},{9,13},{10,... | collective-permute-start | bytes 2359304 | tf_op jit(solution)/shard_map/ppermute | solution.py:337
  187.9 57.2 %collective-permute-start.18 = (bf16[96,32,128]{2,1,0:T(8,128)(2,1)}, bf16[96,32,128]{2,1,0:T(8,128)(2,1)}, u32[]{:S(2)}, u32[]{:S(2)}) collective-permute-start(bf16[96,32,128]{2,1,0:T(8,128)(2,1)} %copy-done.33), channel_id=1, source_target_pairs={{0,5},{1,6},{2,7},{3,0},{4,1},{5,2},{6,3},{7,4},{8,13},{9,14},{10,... | collective-permute-start | bytes 2359304 | tf_op jit(solution)/shard_map/ppermute | solution.py:337
  225.2 50.3 %collective-permute-start.19 = (bf16[96,32,128]{2,1,0:T(8,128)(2,1)}, bf16[96,32,128]{2,1,0:T(8,128)(2,1)S(1)}, u32[]{:S(2)}, u32[]{:S(2)}) collective-permute-start(bf16[96,32,128]{2,1,0:T(8,128)(2,1)} %get-tuple-element.65), channel_id=1, source_target_pairs={{0,6},{1,7},{2,0},{3,1},{4,2},{5,3},{6,4},{7,5},{8,14},{9,15},{10,... | collective-permute-start | bytes 2359304 | tf_op jit(solution)/shard_map/ppermute | solution.py:337
  229.0 46.5 %collective-permute-start.20 = (bf16[96,32,128]{2,1,0:T(8,128)(2,1)}, bf16[96,32,128]{2,1,0:T(8,128)(2,1)S(1)}, u32[]{:S(2)}, u32[]{:S(2)}) collective-permute-start(bf16[96,32,128]{2,1,0:T(8,128)(2,1)} %get-tuple-element.66), channel_id=1, source_target_pairs={{0,7},{1,0},{2,1},{3,2},{4,3},{5,4},{6,5},{7,6},{8,15},{9,8},{10,9... | collective-permute-start | bytes 2359304 | tf_op jit(solution)/shard_map/ppermute | solution.py:337
  276.7 179.7 %all-to-all-start.1 = ((bf16[8,32,32,128]{3,2,1,0:T(8,128)(2,1)}), bf16[8,32,32,128]{3,2,1,0:T(8,128)(2,1)S(1)}, u32[]{:S(2)}, u32[]{:S(2)}) async-start(bf16[8,32,32,128]{3,2,1,0:T(8,128)(2,1)} %shard_map.140.rest_21_), calls=%async_computation.1 | async-start | bytes 4194304 | tf_op jit(solution)/shard_map/all_to_all | solution.py:333
  330.6 15.6 %collective-permute-start.26 = (bf16[48,32,128]{2,1,0:T(8,128)(2,1)}, bf16[48,32,128]{2,1,0:T(8,128)(2,1)S(1)}, u32[]{:S(2)}, u32[]{:S(2)}) collective-permute-start(bf16[48,32,128]{2,1,0:T(8,128)(2,1)} %copy-done.44), channel_id=1, source_target_pairs={{0,2},{1,3},{2,4},{3,5},{4,6},{5,7},{6,0},{7,1},{8,10},{9,11},{10,... | collective-permute-start | bytes 1179656 | tf_op jit(solution)/shard_map/ppermute | solution.py:337
  332.6 21.0 %collective-permute-start.27 = (bf16[48,32,128]{2,1,0:T(8,128)(2,1)}, bf16[48,32,128]{2,1,0:T(8,128)(2,1)S(1)}, u32[]{:S(2)}, u32[]{:S(2)}) collective-permute-start(bf16[48,32,128]{2,1,0:T(8,128)(2,1)} %copy-done.43), channel_id=1, source_target_pairs={{0,1},{1,2},{2,3},{3,4},{4,5},{5,6},{6,7},{7,0},{8,9},{9,10},{10,1... | collective-permute-start | bytes 1179656 | tf_op jit(solution)/shard_map/ppermute | solution.py:337
  339.9 37.0 %collective-permute-start.21 = (bf16[48,32,128]{2,1,0:T(8,128)(2,1)}, bf16[48,32,128]{2,1,0:T(8,128)(2,1)}, u32[]{:S(2)}, u32[]{:S(2)}) collective-permute-start(bf16[48,32,128]{2,1,0:T(8,128)(2,1)} %copy-done.42), channel_id=1, source_target_pairs={{0,7},{1,0},{2,1},{3,2},{4,3},{5,4},{6,5},{7,6},{8,15},{9,8},{10,9... | collective-permute-start | bytes 1179656 | tf_op jit(solution)/shard_map/ppermute | solution.py:337
  342.1 63.1 %collective-permute-start.22 = (bf16[48,32,128]{2,1,0:T(8,128)(2,1)}, bf16[48,32,128]{2,1,0:T(8,128)(2,1)}, u32[]{:S(2)}, u32[]{:S(2)}) collective-permute-start(bf16[48,32,128]{2,1,0:T(8,128)(2,1)} %copy-done.41), channel_id=1, source_target_pairs={{0,6},{1,7},{2,0},{3,1},{4,2},{5,3},{6,4},{7,5},{8,14},{9,15},{10,... | collective-permute-start | bytes 1179656 | tf_op jit(solution)/shard_map/ppermute | solution.py:337
  354.3 19.6 %collective-permute-start.30 = (f32[232,128]{1,0:T(8,128)}, f32[232,128]{1,0:T(8,128)S(1)}, u32[]{:S(2)}, u32[]{:S(2)}) collective-permute-start(f32[232,128]{1,0:T(8,128)} %shard_map.146), channel_id=1, source_target_pairs={{0,1},{1,0},{2,3},{3,2},{4,5},{5,4},{6,7},{7,6},{8,9},{9,8},{10,11... | collective-permute-start | bytes 356360 | tf_op jit(solution)/shard_map/ppermute | solution.py:292
  354.3 82.4 %collective-permute-start.23 = (bf16[48,32,128]{2,1,0:T(8,128)(2,1)}, bf16[48,32,128]{2,1,0:T(8,128)(2,1)S(1)}, u32[]{:S(2)}, u32[]{:S(2)}) collective-permute-start(bf16[48,32,128]{2,1,0:T(8,128)(2,1)} %copy-done.40), channel_id=1, source_target_pairs={{0,5},{1,6},{2,7},{3,0},{4,1},{5,2},{6,3},{7,4},{8,13},{9,14},{10,... | collective-permute-start | bytes 1179656 | tf_op jit(solution)/shard_map/ppermute | solution.py:337
  374.0 62.7 %collective-permute-start.24 = (bf16[48,32,128]{2,1,0:T(8,128)(2,1)}, bf16[48,32,128]{2,1,0:T(8,128)(2,1)S(1)}, u32[]{:S(2)}, u32[]{:S(2)}) collective-permute-start(bf16[48,32,128]{2,1,0:T(8,128)(2,1)} %copy-done.39), channel_id=1, source_target_pairs={{0,4},{1,5},{2,6},{3,7},{4,0},{5,1},{6,2},{7,3},{8,12},{9,13},{10,... | collective-permute-start | bytes 1179656 | tf_op jit(solution)/shard_map/ppermute | solution.py:337
  374.0 63.4 %collective-permute-start.25 = (bf16[48,32,128]{2,1,0:T(8,128)(2,1)}, bf16[48,32,128]{2,1,0:T(8,128)(2,1)S(1)}, u32[]{:S(2)}, u32[]{:S(2)}) collective-permute-start(bf16[48,32,128]{2,1,0:T(8,128)(2,1)} %copy-done.38), channel_id=1, source_target_pairs={{0,3},{1,4},{2,5},{3,6},{4,7},{5,0},{6,1},{7,2},{8,11},{9,12},{10,... | collective-permute-start | bytes 1179656 | tf_op jit(solution)/shard_map/ppermute | solution.py:337
  376.9 23.4 %collective-permute-start.31 = (f32[232,128]{1,0:T(8,128)}, f32[232,128]{1,0:T(8,128)S(1)}, u32[]{:S(2)}, u32[]{:S(2)}) collective-permute-start(f32[232,128]{1,0:T(8,128)} %shard_map.147), channel_id=1, source_target_pairs={{0,2},{1,3},{2,0},{3,1},{4,6},{5,7},{6,4},{7,5},{8,10},{9,11},{10,... | collective-permute-start | bytes 356360 | tf_op jit(solution)/shard_map/ppermute | solution.py:292
  405.3 17.6 %collective-permute-start.32 = (f32[232,128]{1,0:T(8,128)}, f32[232,128]{1,0:T(8,128)S(1)}, u32[]{:S(2)}, u32[]{:S(2)}) collective-permute-start(f32[232,128]{1,0:T(8,128)} %shard_map.148), channel_id=1, source_target_pairs={{0,4},{1,5},{2,6},{3,7},{4,0},{5,1},{6,2},{7,3},{8,12},{9,13},{10,... | collective-permute-start | bytes 356360 | tf_op jit(solution)/shard_map/ppermute | solution.py:292
  406.2 23.0 %collective-permute-start.10 = (bf16[16,32,128]{2,1,0:T(8,128)(2,1)}, bf16[16,32,128]{2,1,0:T(8,128)(2,1)S(1)}, u32[]{:S(2)}, u32[]{:S(2)}) collective-permute-start(bf16[16,32,128]{2,1,0:T(8,128)(2,1)} %copy-done.50), channel_id=1, source_target_pairs={{0,4},{1,5},{2,6},{3,7},{4,0},{5,1},{6,2},{7,3},{8,12},{9,13},{10,... | collective-permute-start | bytes 393224 | tf_op jit(solution)/shard_map/ppermute | solution.py:337
  422.8 13.9 %collective-permute-start.11 = (bf16[16,32,128]{2,1,0:T(8,128)(2,1)}, bf16[16,32,128]{2,1,0:T(8,128)(2,1)S(1)}, u32[]{:S(2)}, u32[]{:S(2)}) collective-permute-start(bf16[16,32,128]{2,1,0:T(8,128)(2,1)} %copy-done.49), channel_id=1, source_target_pairs={{0,3},{1,4},{2,5},{3,6},{4,7},{5,0},{6,1},{7,2},{8,11},{9,12},{10,... | collective-permute-start | bytes 393224 | tf_op jit(solution)/shard_map/ppermute | solution.py:337
  447.7 17.6 %collective-permute-start.7 = (bf16[16,32,128]{2,1,0:T(8,128)(2,1)}, bf16[16,32,128]{2,1,0:T(8,128)(2,1)S(1)}, u32[]{:S(2)}, u32[]{:S(2)}) collective-permute-start(bf16[16,32,128]{2,1,0:T(8,128)(2,1)} %copy-done.48), channel_id=1, source_target_pairs={{0,7},{1,0},{2,1},{3,2},{4,3},{5,4},{6,5},{7,6},{8,15},{9,8},{10,9... | collective-permute-start | bytes 393224 | tf_op jit(solution)/shard_map/ppermute | solution.py:337
  447.7 17.6 %collective-permute-start.8 = (bf16[16,32,128]{2,1,0:T(8,128)(2,1)}, bf16[16,32,128]{2,1,0:T(8,128)(2,1)S(1)}, u32[]{:S(2)}, u32[]{:S(2)}) collective-permute-start(bf16[16,32,128]{2,1,0:T(8,128)(2,1)} %copy-done.47), channel_id=1, source_target_pairs={{0,6},{1,7},{2,0},{3,1},{4,2},{5,3},{6,4},{7,5},{8,14},{9,15},{10,... | collective-permute-start | bytes 393224 | tf_op jit(solution)/shard_map/ppermute | solution.py:337
  449.4 15.9 %collective-permute-start.12 = (bf16[16,32,128]{2,1,0:T(8,128)(2,1)}, bf16[16,32,128]{2,1,0:T(8,128)(2,1)}, u32[]{:S(2)}, u32[]{:S(2)}) collective-permute-start(bf16[16,32,128]{2,1,0:T(8,128)(2,1)} %copy-done.46), channel_id=1, source_target_pairs={{0,2},{1,3},{2,4},{3,5},{4,6},{5,7},{6,0},{7,1},{8,10},{9,11},{10,... | collective-permute-start | bytes 393224 | tf_op jit(solution)/shard_map/ppermute | solution.py:337
  449.7 15.6 %collective-permute-start.13 = (bf16[16,32,128]{2,1,0:T(8,128)(2,1)}, bf16[16,32,128]{2,1,0:T(8,128)(2,1)}, u32[]{:S(2)}, u32[]{:S(2)}) collective-permute-start(bf16[16,32,128]{2,1,0:T(8,128)(2,1)} %copy-done.45), channel_id=1, source_target_pairs={{0,1},{1,2},{2,3},{3,4},{4,5},{5,6},{6,7},{7,0},{8,9},{9,10},{10,1... | collective-permute-start | bytes 393224 | tf_op jit(solution)/shard_map/ppermute | solution.py:337
  (66 other events, 913.6 us)

commit v16 on v15

--- a/solution.py
+++ b/solution.py
@@ -86,7 +86,7 @@
         in_specs=specs,
         out_specs=part_specs(devices, rotated, (planes, step, B), lambda t, i: (t, i, 0)),
         out_shape=part_shapes(devices, rotated, (tiles * planes, rows, B)),
-        scratch_shapes=[pltpu.VMEM((step * LANES, B), jnp.float32)],
+        scratch_shapes=[pltpu.VMEM(((step + 1) * LANES, B), jnp.float32)],
         compiler_params=pltpu.CompilerParams(vmem_limit_bytes=VMEM_BYTES),
         cost_estimate=pl.CostEstimate(flops=1, bytes_accessed=16 * rows * B * LANES * tiles, transcendentals=0),
     )(*given)
@@ -120,7 +120,7 @@
         in_specs=specs,
         out_specs=pl.BlockSpec((step, B, LANES), lambda t, i: (i, 0, tile + t)),
         out_shape=jax.ShapeDtypeStruct((rows, B, width), jnp.bfloat16),
-        scratch_shapes=[pltpu.VMEM((step * LANES, B), jnp.float32)],
+        scratch_shapes=[pltpu.VMEM(((step + 1) * LANES, B), jnp.float32)],
         input_output_aliases={} if held is None else {len(parts) + 1: 0},
         compiler_params=pltpu.CompilerParams(vmem_limit_bytes=VMEM_BYTES),
         cost_estimate=pl.CostEstimate(flops=1, bytes_accessed=8 * rows * B * LANES * tiles, transcendentals=0),
@@ -369,7 +369,7 @@
         leaving.append(returned)
 
     back, first = leaving[-1][2], leaving[-1][0]
-    sums = sum_over_mesh(add(terms, []), [None, back[-2:], back[1:2], back[2:3], back[3:-2] + first[3:6]])
+    sums = sum_over_mesh(add(terms, []), [None, back[-2:], back[1:2], back[2:3], back[3:-2], first[3:5]])
     grads = []
     for returned in leaving:
         held = None

time: 471 us -> 462 us (0.981)
  starting transfers between devices: 168 us -> 154 us
  waiting for transfers between devices: 177 us -> 183 us
    ppermute x28, starting transfers between devices: 133 us -> 117 us  [exchange(): moved.append(lax.ppermute(parts[shift], 'ctx', pairs))]
    ppermute x7, waiting for transfers between devices: 37.1 us -> 43.4 us  [exchange_with(): lax.ppermute(array, axis, [(i, i ^ bit) for i in range(size)])]
    unnamed x131 -> x115, local copies, waits for them, and re-layouts: 30.1 us -> 28 us
  transfers between devices with their start and end apart: 37 -> 37, of which waited for: 15 -> 14; matrix products, arithmetic and copies ran while one was open for 3% -> 3% of each run, Pallas kernels for 14% -> 15%
where the time goes in v16:
time: 462 us; the launch traced here: 460 us
  waiting for transfers between devices  183 us (40%)
  starting transfers between devices  154 us (33%)
  Pallas kernels  78.5 us (17%)
  local copies, waits for them, and re-layouts  28.7 us (6%)
  other arithmetic  13.9 us (3%)
    ppermute x28, waiting for transfers between devices, exchange(): moved.append(lax.ppermute(parts[shift], 'ctx', pairs))  140 us
    ppermute x28, starting transfers between devices, exchange(): moved.append(lax.ppermute(parts[shift], 'ctx', pairs))  117 us
    ppermute x7, waiting for transfers between devices, exchange_with(): lax.ppermute(array, axis, [(i, i ^ bit) for i in range(size)])  43.4 us
    pallas_call x3, Pallas kernels, mix(): pl.pallas_call(functools.partial(mix_kernel, parts=len(parts), tile=tile,...  39.9 us
    all_to_all x2, starting transfers between devices, exchange(): lax.all_to_all(parts[0], 'ctx', split_axis=0, concat_axis=0, tiled=True)  28.1 us
    unnamed x115, local copies, waits for them, and re-layouts  28 us
    pallas_call x3, Pallas kernels, split_channels(): pl.pallas_call(functools.partial(kernel, rotated=rotated), grid=(tiles, r...  24.8 us
    pallas_call x3, Pallas kernels, merge_channels(): pl.pallas_call(functools.partial(merge_kernel, parts=len(parts), rotated=...  11.6 us
  transfers between devices with their start and end apart: 37, of which 14 were waited for; matrix products, arithmetic and copies ran while one was open for 3% of the time, Pallas kernels for 15%

profile of v16, /device:TPU:0, one launch (start us, length us, event | category | flops | bytes accessed | tf_op | source)
XLA Modules:
  0.0 459.6 jit_solution(14801359217829987443)
XLA Ops:
  0.6 7.8 %shard_map.138 = bf16[8,64,32,128]{3,2,1,0:T(8,128)(2,1)S(1)} custom-call(s32[1]{0:T(128)} %bitcast.place_ref, bf16[32,128,768]{2,1,0:T(8,128)(2,1)} %bitcast.51, bf16[32,128,768]{2,1,0:T(8,128)(2,1)} %bitcast.54), custom_call_target="tpu_custom_call" | custom-call | flops 1 | bytes 16777216 | tf_op jit(solution)/shard_map/pallas_call | solution.py:83
  10.5 6.5 %all-to-all-start = ((bf16[8,64,32,128]{3,2,1,0:T(8,128)(2,1)}), bf16[8,64,32,128]{3,2,1,0:T(8,128)(2,1)}, u32[]{:S(2)}, u32[]{:S(2)}) async-start(bf16[8,64,32,128]{3,2,1,0:T(8,128)(2,1)} %copy-done), calls=%async_computation | async-start | bytes 8388608 | tf_op jit(solution)/shard_map/all_to_all | solution.py:333
  17.0 5.3 %shard_map.135 = (bf16[35,32,128]{2,1,0:T(8,128)(2,1)S(1)}, bf16[35,32,128]{2,1,0:T(8,128)(2,1)S(1)}, bf16[35,32,128]{2,1,0:T(8,128)(2,1)S(1)}, bf16[35,32,128]{...) custom-call(s32[1]{0:T(128)} %bitcast.place_ref, ...), custom_call_target="tpu_custom_call" | custom-call | flops 1 | bytes 8388608 | tf_op jit(solution)/shard_map/pallas_call | solution.py:83
  24.4 2.2 collective-permute-start.2
  29.2 11.7 %shard_map.137 = (bf16[96,32,128]{2,1,0:T(8,128)(2,1)S(1)}, bf16[96,32,128]{2,1,0:T(8,128)(2,1)S(1)}, bf16[96,32,128]{2,1,0:T(8,128)(2,1)S(1)}, bf16[96,32,128]{...) custom-call(s32[1]{0:T(128)} %bitcast.place_ref, ...), custom_call_target="tpu_custom_call" | custom-call | flops 1 | bytes 25165824 | tf_op jit(solution)/shard_map/pallas_call | solution.py:83
  46.5 48.7 %collective-permute-done.rest_1_.rest_9_ = bf16[35,32,128]{2,1,0:T(8,128)(2,1)S(1)} collective-permute-done((bf16[35,32,128]{2,1,0:T(8,128)(2,1)S(1)}, bf16[35,32,128]{2,1,0:T(8,128)(2,1)S(1)}, u32[]{:S(2)}, u32[]{:S(2)}) %collective-permute-start) | collective-permute-done | bytes 286752 | tf_op jit(solution)/shard_map/ppermute | solution.py:337
  96.1 4.4 collective-permute-start.6
  100.6 40.7 %collective-permute-done.2.rest_3_.rest_11_ = bf16[35,32,128]{2,1,0:T(8,128)(2,1)S(1)} collective-permute-done((bf16[35,32,128]{2,1,0:T(8,128)(2,1)S(1)}, bf16[35,32,128]{2,1,0:T(8,128)(2,1)S(1)}, u32[]{:S(2)}, u32[]{:S(2)}) %collective-permute-start.2) | collective-permute-done | bytes 286752 | tf_op jit(solution)/shard_map/ppermute | solution.py:337
  142.3 10.3 %collective-permute-start.15 = (bf16[96,32,128]{2,1,0:T(8,128)(2,1)}, bf16[96,32,128]{2,1,0:T(8,128)(2,1)}, u32[]{:S(2)}, u32[]{:S(2)}) collective-permute-start(bf16[96,32,128]{2,1,0:T(8,128)(2,1)} %copy-done.32), channel_id=1, source_target_pairs={{0,2},{1,3},{2,4},{3,5},{4,6},{5,7},{6,0},{7,1},{8,10},{9,11},{10,... | collective-permute-start | bytes 2359304 | tf_op jit(solution)/shard_map/ppermute | solution.py:337
  152.6 5.9 %collective-permute-start.16 = (bf16[96,32,128]{2,1,0:T(8,128)(2,1)}, bf16[96,32,128]{2,1,0:T(8,128)(2,1)}, u32[]{:S(2)}, u32[]{:S(2)}) collective-permute-start(bf16[96,32,128]{2,1,0:T(8,128)(2,1)} %copy-done.31), channel_id=1, source_target_pairs={{0,3},{1,4},{2,5},{3,6},{4,7},{5,0},{6,1},{7,2},{8,11},{9,12},{10,... | collective-permute-start | bytes 2359304 | tf_op jit(solution)/shard_map/ppermute | solution.py:337
  158.5 29.4 %collective-permute-start.17 = (bf16[96,32,128]{2,1,0:T(8,128)(2,1)}, bf16[96,32,128]{2,1,0:T(8,128)(2,1)}, u32[]{:S(2)}, u32[]{:S(2)}) collective-permute-start(bf16[96,32,128]{2,1,0:T(8,128)(2,1)} %copy-done.30), channel_id=1, source_target_pairs={{0,4},{1,5},{2,6},{3,7},{4,0},{5,1},{6,2},{7,3},{8,12},{9,13},{10,... | collective-permute-start | bytes 2359304 | tf_op jit(solution)/shard_map/ppermute | solution.py:337
  187.9 21.8 %collective-permute-start.18 = (bf16[96,32,128]{2,1,0:T(8,128)(2,1)}, bf16[96,32,128]{2,1,0:T(8,128)(2,1)}, u32[]{:S(2)}, u32[]{:S(2)}) collective-permute-start(bf16[96,32,128]{2,1,0:T(8,128)(2,1)} %copy-done.29), channel_id=1, source_target_pairs={{0,5},{1,6},{2,7},{3,0},{4,1},{5,2},{6,3},{7,4},{8,13},{9,14},{10,... | collective-permute-start | bytes 2359304 | tf_op jit(solution)/shard_map/ppermute | solution.py:337
  213.1 6.7 %shard_map.136 = (bf16[16,32,128]{2,1,0:T(8,128)(2,1)S(1)}, bf16[16,32,128]{2,1,0:T(8,128)(2,1)S(1)}, bf16[16,32,128]{2,1,0:T(8,128)(2,1)S(1)}, bf16[16,32,128]{...) custom-call(s32[1]{0:T(128)} %bitcast.place_ref, ...), custom_call_target="tpu_custom_call" | custom-call | flops 8388608000 | bytes 1024 | tf_op jit(solution)/shard_map/pallas_call | solution.py:222
  225.2 3.8 collective-permute-start.19
  229.0 13.8 %shard_map.139 = (bf16[8,32,32,128]{3,2,1,0:T(8,128)(2,1)S(1)}, f32[928,128]{1,0:T(8,128)S(1)}) custom-call(s32[1]{0:T(128)} %bitcast.place_ref, f32[768]{0:T(1024)S(1)} %copy-done.47, f32[768]{0:T(1024)S(1)} %copy-done.48, f32[768]{0:T(1024)S(1)} %copy-done.49, bf16[8,64,32,128]{3,2,1,0:T(8,128)(2,1)} %all-to-all-done.rest_0_.rest_1_, ...), custom_call_target="tpu_custom_call" | custom-call | flops 16777216000 | bytes 1024 | tf_op jit(solution)/shard_map/pallas_call | solution.py:222
  245.1 30.4 %collective-permute-done.19.refs_6_.rest_6_.rest_14_ = bf16[96,32,128]{2,1,0:T(8,128)(2,1)S(1)} collective-permute-done((bf16[96,32,128]{2,1,0:T(8,128)(2,1)}, bf16[96,32,128]{2,1,0:T(8,128)(2,1)S(1)}, u32[]{:S(2)}, u32[]{:S(2)}) %collective-permute-start.19) | collective-permute-done | bytes 786464 | tf_op jit(solution)/shard_map/ppermute | solution.py:337
  276.7 21.7 %all-to-all-start.1 = ((bf16[8,32,32,128]{3,2,1,0:T(8,128)(2,1)}), bf16[8,32,32,128]{3,2,1,0:T(8,128)(2,1)S(1)}, u32[]{:S(2)}, u32[]{:S(2)}) async-start(bf16[8,32,32,128]{3,2,1,0:T(8,128)(2,1)} %shard_map.140.rest_21_), calls=%async_computation.1 | async-start | bytes 4194304 | tf_op jit(solution)/shard_map/all_to_all | solution.py:333
  299.5 19.4 %shard_map.141 = (bf16[48,32,128]{2,1,0:T(8,128)(2,1)S(1)}, bf16[48,32,128]{2,1,0:T(8,128)(2,1)S(1)}, bf16[48,32,128]{2,1,0:T(8,128)(2,1)S(1)}, bf16[48,32,128]{...) custom-call(s32[1]{0:T(128)} %bitcast.place_ref, ...), custom_call_target="tpu_custom_call" | custom-call | flops 25165824000 | bytes 1024 | tf_op jit(solution)/shard_map/pallas_call | solution.py:222
  332.6 4.6 %collective-permute-done.28 = f32[464,128]{1,0:T(8,128)S(1)} collective-permute-done((f32[464,128]{1,0:T(8,128)S(1)}, f32[464,128]{1,0:T(8,128)S(1)}, u32[]{:S(2)}, u32[]{:S(2)}) %collective-permute-start.28) | collective-permute-done | bytes 237600 | tf_op jit(solution)/shard_map/ppermute | solution.py:292
  339.9 2.2 collective-permute-start.21
  346.2 7.5 %collective-permute-done.27.rest_7_.refs_2_ = bf16[48,32,128]{2,1,0:T(8,128)(2,1)} collective-permute-done((bf16[48,32,128]{2,1,0:T(8,128)(2,1)}, bf16[48,32,128]{2,1,0:T(8,128)(2,1)}, u32[]{:S(2)}, u32[]{:S(2)}) %collective-permute-start.27) | collective-permute-done | bytes 393248 | tf_op jit(solution)/shard_map/ppermute | solution.py:337
  353.7 19.6 %collective-permute-start.23 = (bf16[48,32,128]{2,1,0:T(8,128)(2,1)}, bf16[48,32,128]{2,1,0:T(8,128)(2,1)S(1)}, u32[]{:S(2)}, u32[]{:S(2)}) collective-permute-start(bf16[48,32,128]{2,1,0:T(8,128)(2,1)} %copy-done.36), channel_id=1, source_target_pairs={{0,5},{1,6},{2,7},{3,0},{4,1},{5,2},{6,3},{7,4},{8,13},{9,14},{10,... | collective-permute-start | bytes 1179656 | tf_op jit(solution)/shard_map/ppermute | solution.py:337
  377.4 22.2 %collective-permute-done.31 = f32[232,128]{1,0:T(8,128)S(1)} collective-permute-done((f32[232,128]{1,0:T(8,128)}, f32[232,128]{1,0:T(8,128)S(1)}, u32[]{:S(2)}, u32[]{:S(2)}) %collective-permute-start.31) | collective-permute-done | bytes 118816 | tf_op jit(solution)/shard_map/ppermute | solution.py:292
  401.9 3.2 collective-permute-start.32
  405.2 12.8 %collective-permute-done.32 = f32[232,128]{1,0:T(8,128)S(1)} collective-permute-done((f32[232,128]{1,0:T(8,128)}, f32[232,128]{1,0:T(8,128)S(1)}, u32[]{:S(2)}, u32[]{:S(2)}) %collective-permute-start.32) | collective-permute-done | bytes 118816 | tf_op jit(solution)/shard_map/ppermute | solution.py:292
  422.3 2.6 collective-permute-start.9
  424.9 3.0 collective-permute-start.10
  429.6 6.9 %collective-permute-done.10.rest_4_.refs_2_ = bf16[16,32,128]{2,1,0:T(8,128)(2,1)S(1)} collective-permute-done((bf16[16,32,128]{2,1,0:T(8,128)(2,1)}, bf16[16,32,128]{2,1,0:T(8,128)(2,1)S(1)}, u32[]{:S(2)}, u32[]{:S(2)}) %collective-permute-start.10) | collective-permute-done | bytes 131104 | tf_op jit(solution)/shard_map/ppermute | solution.py:337
  440.4 3.7 collective-permute-done.34
  447.9 3.0 shard_map.142.rest_8_
  450.9 6.0 %shard_map.143.rest_8_ = bf16[32,128,768]{2,1,0:T(8,128)(2,1)} custom-call(s32[1]{0:T(128)} %bitcast.place_ref, bf16[48,32,128]{2,1,0:T(8,128)(2,1)S(1)} %copy-done.20, bf16[48,32,128]{2,1,0:T(8,128)(2,1)S(1)} %copy-done.3, bf16[48,32,128]{2,1,0:T(8,128)(2,1)S(1)} %copy-done.5, bf16[48,32,128]{2,1,0:T(8,128)(2,1)S(1)} %copy-done.9, ...), custom_call_target="tpu_custom_call", output_to_operand_aliasing={{}: (9, {})} | custom-call | flops 1 | bytes 12582912 | tf_op jit(solution)/shard_map/pallas_call | solution.py:117
  457.0 2.6 shard_map.144
  (194 shorter events, 68.1 us)
Async XLA Ops:
  10.5 218.5 %all-to-all-start = ((bf16[8,64,32,128]{3,2,1,0:T(8,128)(2,1)}), bf16[8,64,32,128]{3,2,1,0:T(8,128)(2,1)}, u32[]{:S(2)}, u32[]{:S(2)}) async-start(bf16[8,64,32,128]{3,2,1,0:T(8,128)(2,1)} %copy-done), calls=%async_computation | async-start | bytes 8388608 | tf_op jit(solution)/shard_map/all_to_all | solution.py:333
  22.2 73.0 %collective-permute-start = (bf16[35,32,128]{2,1,0:T(8,128)(2,1)S(1)}, bf16[35,32,128]{2,1,0:T(8,128)(2,1)S(1)}, u32[]{:S(2)}, u32[]{:S(2)}) collective-permute-start(bf16[35,32,128]{2,1,0:T(8,128)(2,1)S(1)} %get-tuple-element.44), channel_id=1, source_target_pairs={{0,1},{1,2},{2,3},{3,4},{4,5},{5,6},{6,7},{7,0},{8,9},{9,10},{10,1... | collective-permute-start | bytes 860168 | tf_op jit(solution)/shard_map/ppermute | solution.py:337
  22.7 73.4 %collective-permute-start.1 = (bf16[35,32,128]{2,1,0:T(8,128)(2,1)S(1)}, bf16[35,32,128]{2,1,0:T(8,128)(2,1)S(1)}, u32[]{:S(2)}, u32[]{:S(2)}) collective-permute-start(bf16[35,32,128]{2,1,0:T(8,128)(2,1)S(1)} %get-tuple-element.45), channel_id=1, source_target_pairs={{0,2},{1,3},{2,4},{3,5},{4,6},{5,7},{6,0},{7,1},{8,10},{9,11},{10,... | collective-permute-start | bytes 860168 | tf_op jit(solution)/shard_map/ppermute | solution.py:337
  24.4 116.9 %collective-permute-start.2 = (bf16[35,32,128]{2,1,0:T(8,128)(2,1)S(1)}, bf16[35,32,128]{2,1,0:T(8,128)(2,1)S(1)}, u32[]{:S(2)}, u32[]{:S(2)}) collective-permute-start(bf16[35,32,128]{2,1,0:T(8,128)(2,1)S(1)} %get-tuple-element.46), channel_id=1, source_target_pairs={{0,3},{1,4},{2,5},{3,6},{4,7},{5,0},{6,1},{7,2},{8,11},{9,12},{10,... | collective-permute-start | bytes 860168 | tf_op jit(solution)/shard_map/ppermute | solution.py:337
  26.6 115.7 %collective-permute-start.3 = (bf16[35,32,128]{2,1,0:T(8,128)(2,1)}, bf16[35,32,128]{2,1,0:T(8,128)(2,1)S(1)}, u32[]{:S(2)}, u32[]{:S(2)}) collective-permute-start(bf16[35,32,128]{2,1,0:T(8,128)(2,1)} %get-tuple-element.47), channel_id=1, source_target_pairs={{0,4},{1,5},{2,6},{3,7},{4,0},{5,1},{6,2},{7,3},{8,12},{9,13},{10,... | collective-permute-start | bytes 860168 | tf_op jit(solution)/shard_map/ppermute | solution.py:337
  28.1 124.5 %collective-permute-start.4 = (bf16[35,32,128]{2,1,0:T(8,128)(2,1)}, bf16[35,32,128]{2,1,0:T(8,128)(2,1)S(1)}, u32[]{:S(2)}, u32[]{:S(2)}) collective-permute-start(bf16[35,32,128]{2,1,0:T(8,128)(2,1)} %get-tuple-element.48), channel_id=1, source_target_pairs={{0,5},{1,6},{2,7},{3,0},{4,1},{5,2},{6,3},{7,4},{8,13},{9,14},{10,... | collective-permute-start | bytes 860168 | tf_op jit(solution)/shard_map/ppermute | solution.py:337
  95.2 63.3 %collective-permute-start.5 = (bf16[35,32,128]{2,1,0:T(8,128)(2,1)}, bf16[35,32,128]{2,1,0:T(8,128)(2,1)S(1)}, u32[]{:S(2)}, u32[]{:S(2)}) collective-permute-start(bf16[35,32,128]{2,1,0:T(8,128)(2,1)} %get-tuple-element.49), channel_id=1, source_target_pairs={{0,6},{1,7},{2,0},{3,1},{4,2},{5,3},{6,4},{7,5},{8,14},{9,15},{10,... | collective-permute-start | bytes 860168 | tf_op jit(solution)/shard_map/ppermute | solution.py:337
  96.1 91.8 %collective-permute-start.6 = (bf16[35,32,128]{2,1,0:T(8,128)(2,1)}, bf16[35,32,128]{2,1,0:T(8,128)(2,1)S(1)}, u32[]{:S(2)}, u32[]{:S(2)}) collective-permute-start(bf16[35,32,128]{2,1,0:T(8,128)(2,1)} %get-tuple-element.50), channel_id=1, source_target_pairs={{0,7},{1,0},{2,1},{3,2},{4,3},{5,4},{6,5},{7,6},{8,15},{9,8},{10,9... | collective-permute-start | bytes 860168 | tf_op jit(solution)/shard_map/ppermute | solution.py:337
  141.2 83.9 %collective-permute-start.14 = (bf16[96,32,128]{2,1,0:T(8,128)(2,1)}, bf16[96,32,128]{2,1,0:T(8,128)(2,1)S(1)}, u32[]{:S(2)}, u32[]{:S(2)}) collective-permute-start(bf16[96,32,128]{2,1,0:T(8,128)(2,1)} %copy-done.33), channel_id=1, source_target_pairs={{0,1},{1,2},{2,3},{3,4},{4,5},{5,6},{6,7},{7,0},{8,9},{9,10},{10,1... | collective-permute-start | bytes 2359304 | tf_op jit(solution)/shard_map/ppermute | solution.py:337
  142.3 86.7 %collective-permute-start.15 = (bf16[96,32,128]{2,1,0:T(8,128)(2,1)}, bf16[96,32,128]{2,1,0:T(8,128)(2,1)}, u32[]{:S(2)}, u32[]{:S(2)}) collective-permute-start(bf16[96,32,128]{2,1,0:T(8,128)(2,1)} %copy-done.32), channel_id=1, source_target_pairs={{0,2},{1,3},{2,4},{3,5},{4,6},{5,7},{6,0},{7,1},{8,10},{9,11},{10,... | collective-permute-start | bytes 2359304 | tf_op jit(solution)/shard_map/ppermute | solution.py:337
  152.6 92.3 %collective-permute-start.16 = (bf16[96,32,128]{2,1,0:T(8,128)(2,1)}, bf16[96,32,128]{2,1,0:T(8,128)(2,1)}, u32[]{:S(2)}, u32[]{:S(2)}) collective-permute-start(bf16[96,32,128]{2,1,0:T(8,128)(2,1)} %copy-done.31), channel_id=1, source_target_pairs={{0,3},{1,4},{2,5},{3,6},{4,7},{5,0},{6,1},{7,2},{8,11},{9,12},{10,... | collective-permute-start | bytes 2359304 | tf_op jit(solution)/shard_map/ppermute | solution.py:337
  158.5 86.7 %collective-permute-start.17 = (bf16[96,32,128]{2,1,0:T(8,128)(2,1)}, bf16[96,32,128]{2,1,0:T(8,128)(2,1)}, u32[]{:S(2)}, u32[]{:S(2)}) collective-permute-start(bf16[96,32,128]{2,1,0:T(8,128)(2,1)} %copy-done.30), channel_id=1, source_target_pairs={{0,4},{1,5},{2,6},{3,7},{4,0},{5,1},{6,2},{7,3},{8,12},{9,13},{10,... | collective-permute-start | bytes 2359304 | tf_op jit(solution)/shard_map/ppermute | solution.py:337
  187.9 57.2 %collective-permute-start.18 = (bf16[96,32,128]{2,1,0:T(8,128)(2,1)}, bf16[96,32,128]{2,1,0:T(8,128)(2,1)}, u32[]{:S(2)}, u32[]{:S(2)}) collective-permute-start(bf16[96,32,128]{2,1,0:T(8,128)(2,1)} %copy-done.29), channel_id=1, source_target_pairs={{0,5},{1,6},{2,7},{3,0},{4,1},{5,2},{6,3},{7,4},{8,13},{9,14},{10,... | collective-permute-start | bytes 2359304 | tf_op jit(solution)/shard_map/ppermute | solution.py:337
  225.2 50.3 %collective-permute-start.19 = (bf16[96,32,128]{2,1,0:T(8,128)(2,1)}, bf16[96,32,128]{2,1,0:T(8,128)(2,1)S(1)}, u32[]{:S(2)}, u32[]{:S(2)}) collective-permute-start(bf16[96,32,128]{2,1,0:T(8,128)(2,1)} %get-tuple-element.65), channel_id=1, source_target_pairs={{0,6},{1,7},{2,0},{3,1},{4,2},{5,3},{6,4},{7,5},{8,14},{9,15},{10,... | collective-permute-start | bytes 2359304 | tf_op jit(solution)/shard_map/ppermute | solution.py:337
  229.0 46.5 %collective-permute-start.20 = (bf16[96,32,128]{2,1,0:T(8,128)(2,1)}, bf16[96,32,128]{2,1,0:T(8,128)(2,1)S(1)}, u32[]{:S(2)}, u32[]{:S(2)}) collective-permute-start(bf16[96,32,128]{2,1,0:T(8,128)(2,1)} %get-tuple-element.66), channel_id=1, source_target_pairs={{0,7},{1,0},{2,1},{3,2},{4,3},{5,4},{6,5},{7,6},{8,15},{9,8},{10,9... | collective-permute-start | bytes 2359304 | tf_op jit(solution)/shard_map/ppermute | solution.py:337
  276.7 171.2 %all-to-all-start.1 = ((bf16[8,32,32,128]{3,2,1,0:T(8,128)(2,1)}), bf16[8,32,32,128]{3,2,1,0:T(8,128)(2,1)S(1)}, u32[]{:S(2)}, u32[]{:S(2)}) async-start(bf16[8,32,32,128]{3,2,1,0:T(8,128)(2,1)} %shard_map.140.rest_21_), calls=%async_computation.1 | async-start | bytes 4194304 | tf_op jit(solution)/shard_map/all_to_all | solution.py:333
  330.6 15.6 %collective-permute-start.26 = (bf16[48,32,128]{2,1,0:T(8,128)(2,1)}, bf16[48,32,128]{2,1,0:T(8,128)(2,1)S(1)}, u32[]{:S(2)}, u32[]{:S(2)}) collective-permute-start(bf16[48,32,128]{2,1,0:T(8,128)(2,1)} %copy-done.40), channel_id=1, source_target_pairs={{0,2},{1,3},{2,4},{3,5},{4,6},{5,7},{6,0},{7,1},{8,10},{9,11},{10,... | collective-permute-start | bytes 1179656 | tf_op jit(solution)/shard_map/ppermute | solution.py:337
  332.6 21.1 %collective-permute-start.27 = (bf16[48,32,128]{2,1,0:T(8,128)(2,1)}, bf16[48,32,128]{2,1,0:T(8,128)(2,1)}, u32[]{:S(2)}, u32[]{:S(2)}) collective-permute-start(bf16[48,32,128]{2,1,0:T(8,128)(2,1)} %copy-done.39), channel_id=1, source_target_pairs={{0,1},{1,2},{2,3},{3,4},{4,5},{5,6},{6,7},{7,0},{8,9},{9,10},{10,1... | collective-permute-start | bytes 1179656 | tf_op jit(solution)/shard_map/ppermute | solution.py:337
  339.9 36.4 %collective-permute-start.21 = (bf16[48,32,128]{2,1,0:T(8,128)(2,1)}, bf16[48,32,128]{2,1,0:T(8,128)(2,1)S(1)}, u32[]{:S(2)}, u32[]{:S(2)}) collective-permute-start(bf16[48,32,128]{2,1,0:T(8,128)(2,1)} %copy-done.38), channel_id=1, source_target_pairs={{0,7},{1,0},{2,1},{3,2},{4,3},{5,4},{6,5},{7,6},{8,15},{9,8},{10,9... | collective-permute-start | bytes 1179656 | tf_op jit(solution)/shard_map/ppermute | solution.py:337
  342.1 59.1 %collective-permute-start.22 = (bf16[48,32,128]{2,1,0:T(8,128)(2,1)}, bf16[48,32,128]{2,1,0:T(8,128)(2,1)S(1)}, u32[]{:S(2)}, u32[]{:S(2)}) collective-permute-start(bf16[48,32,128]{2,1,0:T(8,128)(2,1)} %copy-done.37), channel_id=1, source_target_pairs={{0,6},{1,7},{2,0},{3,1},{4,2},{5,3},{6,4},{7,5},{8,14},{9,15},{10,... | collective-permute-start | bytes 1179656 | tf_op jit(solution)/shard_map/ppermute | solution.py:337
  353.7 19.7 %collective-permute-start.30 = (f32[232,128]{1,0:T(8,128)}, f32[232,128]{1,0:T(8,128)S(1)}, u32[]{:S(2)}, u32[]{:S(2)}) collective-permute-start(f32[232,128]{1,0:T(8,128)} %shard_map.146), channel_id=1, source_target_pairs={{0,1},{1,0},{2,3},{3,2},{4,5},{5,4},{6,7},{7,6},{8,9},{9,8},{10,11... | collective-permute-start | bytes 356360 | tf_op jit(solution)/shard_map/ppermute | solution.py:292
  353.7 65.8 %collective-permute-start.23 = (bf16[48,32,128]{2,1,0:T(8,128)(2,1)}, bf16[48,32,128]{2,1,0:T(8,128)(2,1)S(1)}, u32[]{:S(2)}, u32[]{:S(2)}) collective-permute-start(bf16[48,32,128]{2,1,0:T(8,128)(2,1)} %copy-done.36), channel_id=1, source_target_pairs={{0,5},{1,6},{2,7},{3,0},{4,1},{5,2},{6,3},{7,4},{8,13},{9,14},{10,... | collective-permute-start | bytes 1179656 | tf_op jit(solution)/shard_map/ppermute | solution.py:337
  373.3 46.2 %collective-permute-start.24 = (bf16[48,32,128]{2,1,0:T(8,128)(2,1)}, bf16[48,32,128]{2,1,0:T(8,128)(2,1)}, u32[]{:S(2)}, u32[]{:S(2)}) collective-permute-start(bf16[48,32,128]{2,1,0:T(8,128)(2,1)} %copy-done.35), channel_id=1, source_target_pairs={{0,4},{1,5},{2,6},{3,7},{4,0},{5,1},{6,2},{7,3},{8,12},{9,13},{10,... | collective-permute-start | bytes 1179656 | tf_op jit(solution)/shard_map/ppermute | solution.py:337
  373.3 47.5 %collective-permute-start.25 = (bf16[48,32,128]{2,1,0:T(8,128)(2,1)}, bf16[48,32,128]{2,1,0:T(8,128)(2,1)}, u32[]{:S(2)}, u32[]{:S(2)}) collective-permute-start(bf16[48,32,128]{2,1,0:T(8,128)(2,1)} %copy-done.34), channel_id=1, source_target_pairs={{0,3},{1,4},{2,5},{3,6},{4,7},{5,0},{6,1},{7,2},{8,11},{9,12},{10,... | collective-permute-start | bytes 1179656 | tf_op jit(solution)/shard_map/ppermute | solution.py:337
  377.0 22.6 %collective-permute-start.31 = (f32[232,128]{1,0:T(8,128)}, f32[232,128]{1,0:T(8,128)S(1)}, u32[]{:S(2)}, u32[]{:S(2)}) collective-permute-start(f32[232,128]{1,0:T(8,128)} %shard_map.147), channel_id=1, source_target_pairs={{0,2},{1,3},{2,0},{3,1},{4,6},{5,7},{6,4},{7,5},{8,10},{9,11},{10,... | collective-permute-start | bytes 356360 | tf_op jit(solution)/shard_map/ppermute | solution.py:292
  401.9 16.0 %collective-permute-start.32 = (f32[232,128]{1,0:T(8,128)}, f32[232,128]{1,0:T(8,128)S(1)}, u32[]{:S(2)}, u32[]{:S(2)}) collective-permute-start(f32[232,128]{1,0:T(8,128)} %shard_map.148), channel_id=1, source_target_pairs={{0,4},{1,5},{2,6},{3,7},{4,0},{5,1},{6,2},{7,3},{8,12},{9,13},{10,... | collective-permute-start | bytes 356360 | tf_op jit(solution)/shard_map/ppermute | solution.py:292
  424.9 11.6 %collective-permute-start.10 = (bf16[16,32,128]{2,1,0:T(8,128)(2,1)}, bf16[16,32,128]{2,1,0:T(8,128)(2,1)S(1)}, u32[]{:S(2)}, u32[]{:S(2)}) collective-permute-start(bf16[16,32,128]{2,1,0:T(8,128)(2,1)} %copy-done.46), channel_id=1, source_target_pairs={{0,4},{1,5},{2,6},{3,7},{4,0},{5,1},{6,2},{7,3},{8,12},{9,13},{10,... | collective-permute-start | bytes 393224 | tf_op jit(solution)/shard_map/ppermute | solution.py:337
  438.4 18.5 %collective-permute-start.7 = (bf16[16,32,128]{2,1,0:T(8,128)(2,1)}, bf16[16,32,128]{2,1,0:T(8,128)(2,1)S(1)}, u32[]{:S(2)}, u32[]{:S(2)}) collective-permute-start(bf16[16,32,128]{2,1,0:T(8,128)(2,1)} %copy-done.45), channel_id=1, source_target_pairs={{0,7},{1,0},{2,1},{3,2},{4,3},{5,4},{6,5},{7,6},{8,15},{9,8},{10,9... | collective-permute-start | bytes 393224 | tf_op jit(solution)/shard_map/ppermute | solution.py:337
  438.4 18.5 %collective-permute-start.8 = (bf16[16,32,128]{2,1,0:T(8,128)(2,1)}, bf16[16,32,128]{2,1,0:T(8,128)(2,1)S(1)}, u32[]{:S(2)}, u32[]{:S(2)}) collective-permute-start(bf16[16,32,128]{2,1,0:T(8,128)(2,1)} %copy-done.44), channel_id=1, source_target_pairs={{0,6},{1,7},{2,0},{3,1},{4,2},{5,3},{6,4},{7,5},{8,14},{9,15},{10,... | collective-permute-start | bytes 393224 | tf_op jit(solution)/shard_map/ppermute | solution.py:337
  439.7 17.2 %collective-permute-start.11 = (bf16[16,32,128]{2,1,0:T(8,128)(2,1)}, bf16[16,32,128]{2,1,0:T(8,128)(2,1)}, u32[]{:S(2)}, u32[]{:S(2)}) collective-permute-start(bf16[16,32,128]{2,1,0:T(8,128)(2,1)} %copy-done.43), channel_id=1, source_target_pairs={{0,3},{1,4},{2,5},{3,6},{4,7},{5,0},{6,1},{7,2},{8,11},{9,12},{10,... | collective-permute-start | bytes 393224 | tf_op jit(solution)/shard_map/ppermute | solution.py:337
  440.2 16.7 %collective-permute-start.12 = (bf16[16,32,128]{2,1,0:T(8,128)(2,1)}, bf16[16,32,128]{2,1,0:T(8,128)(2,1)}, u32[]{:S(2)}, u32[]{:S(2)}) collective-permute-start(bf16[16,32,128]{2,1,0:T(8,128)(2,1)} %copy-done.42), channel_id=1, source_target_pairs={{0,2},{1,3},{2,4},{3,5},{4,6},{5,7},{6,0},{7,1},{8,10},{9,11},{10,... | collective-permute-start | bytes 393224 | tf_op jit(solution)/shard_map/ppermute | solution.py:337
  444.1 12.8 %collective-permute-start.13 = (bf16[16,32,128]{2,1,0:T(8,128)(2,1)}, bf16[16,32,128]{2,1,0:T(8,128)(2,1)}, u32[]{:S(2)}, u32[]{:S(2)}) collective-permute-start(bf16[16,32,128]{2,1,0:T(8,128)(2,1)} %copy-done.41), channel_id=1, source_target_pairs={{0,1},{1,2},{2,3},{3,4},{4,5},{5,6},{6,7},{7,0},{8,9},{9,10},{10,1... | collective-permute-start | bytes 393224 | tf_op jit(solution)/shard_map/ppermute | solution.py:337
  (58 other events, 803.7 us)
